TPU v7x, 128 devices: a whole 4x4x4 slice. The times are simulated.
128 devices in a mesh: batch: 4 (over y), seq: 32 (over z, x, core).
Axes of the slice: x: 4, y: 4, z: 4, core: 2. Of those that a mesh axis runs over, the one named last changes fastest.
Arguments:
- tokens: bfloat16 [2, 4, 8192, 640], P(None, 'batch', 'seq'), may hold values from -6 to 6
- lengths: int32 [2, 4, 64], P(None, 'batch'), may hold values from 1 to 1024, 8192 in all within a row
- gain_one: bfloat16 [640], P('batch'), may hold values from 0.5 to 1.5
- bias_one: bfloat16 [640], P('batch'), may hold values from -3 to 3
- w_qkv: bfloat16 [640, 1920], P('batch'), may hold values from -0.25 to 0.25
- w_out: bfloat16 [640, 640], P('batch'), may hold values from -1 to 1
- gain_two: bfloat16 [640], P('batch'), may hold values from 0.5 to 1.5
- bias_two: bfloat16 [640], P('batch'), may hold values from -3 to 3
- w_up: bfloat16 [640, 5120], P('batch'), may hold values from -0.25 to 0.25
- w_down: bfloat16 [5120, 640], P('batch'), may hold values from -0.078125 to 0.078125
- cotangent: bfloat16 [2, 4, 8192, 640], P(None, 'batch', 'seq'), may hold values from -6 to 6
Outputs:
- block_out: bfloat16 [2, 4, 8192, 640], P(None, 'batch', 'seq')
- grad_tokens: bfloat16 [2, 4, 8192, 640], P(None, 'batch', 'seq')
- grad_gain_one: float32 [640], P('batch')
- grad_bias_one: float32 [640], P('batch')
- grad_qkv: float32 [640, 1920], P('batch')
- grad_out_proj: float32 [640, 640], P('batch')
- grad_gain_two: float32 [640], P('batch')
- grad_bias_two: float32 [640], P('batch')
- grad_up: float32 [640, 5120], P('batch')
- grad_down: float32 [5120, 640], P('batch')
Inputs may be any that keep to these rules, and one draw needn't show every extreme that they name: Each stream's row of 64 lengths sums to 8192; the largest in each row is 1024.
All inputs are finite; a program needn't handle non-finite values.
Results may differ from a plain program's by a relative error of at most 0.029.
Values may be sent and summed in bfloat16 or wider, within the bound.
No kernel may reach another device: no remote copies, remote signals or barrier semaphores. Data moves between devices by JAX's collectives and lax.ppermute only.
A program may use at most 192 MiB of HBM per device.

v0:
```python
import math

import jax
import jax.numpy as jnp
from jax import lax
from jax.experimental import pallas as pl
from jax.experimental.pallas import tpu as pltpu
from jax.sharding import Mesh
from jax.sharding import PartitionSpec as P

HEAD_DIM = 32
SCALE = HEAD_DIM ** -0.5
LOG2E = math.log2(math.e)
C2 = SCALE * LOG2E
BIG = 1e30
TILE = 256
EPSILON = 1e-05
PAIRS = 5
SHORT, LONG = 384, 1152
f32, bf16 = jnp.float32, jnp.bfloat16
NT = (((1,), (1,)), ((), ()))


def pair_offset(info_ref):
    p = pl.program_id(0)
    sub = jnp.where(p == PAIRS - 1, info_ref[0], lax.rem(p, 2))
    return sub * (2 * HEAD_DIM)


def split3(v):
    a = v.astype(bf16)
    r = v - a.astype(f32)
    b = r.astype(bf16)
    d = (r - b.astype(f32)).astype(bf16)
    return a, b, d


def rows_masked(xT, off):
    row = lax.broadcasted_iota(jnp.int32, xT.shape, 0) - off
    xf = xT.astype(f32)
    return [jnp.where((row >= HEAD_DIM * j) & (row < HEAD_DIM * (j + 1)), xf, 0.0).astype(bf16) for j in range(2)]


def lanes_masked(x, off):
    lane = lax.broadcasted_iota(jnp.int32, x.shape, 1) - off
    xf = x.astype(f32)
    return [jnp.where((lane >= HEAD_DIM * j) & (lane < HEAD_DIM * (j + 1)), xf, 0.0).astype(bf16) for j in range(2)]


def attend_kernel(info_ref, qT_ref, k_ref, vT_ref, kaug_ref, qaugT_ref, oT_ref, o_ref, l_ref, rhs):
    off = pair_offset(info_ref)
    oT_ref[...] = jnp.where(lax.rem(pl.program_id(0), 2) == 0, 0.0, oT_ref[...])
    for t in range(2):
        cols = slice(t * TILE, (t + 1) * TILE)
        masked = rows_masked(qT_ref[:, cols], off)
        for j in range(2):
            rhs[0:128, j * TILE:(j + 1) * TILE] = masked[j]
            rhs[128:256, j * TILE:(j + 1) * TILE] = qaugT_ref[:, cols]
        start = info_ref[1 + t]
        need = info_ref[3 + t]

        def block(first, size):
            def step(i, carry):
                row = pl.multiple_of(first + i * size, 128)
                lhs = jnp.concatenate([k_ref[pl.ds(row, size), :], kaug_ref[pl.ds(row, size), :]], axis=1)
                raw = [jnp.dot(lhs, rhs[:, j * TILE:(j + 1) * TILE], preferred_element_type=f32) for j in range(2)]
                out = []
                for j in range(2):
                    m, l, o = carry[j]
                    s = raw[j] * C2
                    m_new = jnp.maximum(m, jnp.max(s, axis=0, keepdims=True))
                    alpha = jnp.exp2(m - m_new)
                    p = jnp.exp2(s - m_new)
                    vT = vT_ref[pl.ds(pl.multiple_of(off + j * HEAD_DIM, HEAD_DIM), HEAD_DIM), pl.ds(row, size)]
                    out.append((m_new, l * alpha + jnp.sum(p, axis=0, keepdims=True),
                                o * alpha + jnp.dot(vT, p.astype(bf16), preferred_element_type=f32)))
                return tuple(out)
            return step

        def finish(state):
            for j in range(2):
                m, l, o = state[j]
                oT_ref[pl.ds(pl.multiple_of(off + j * HEAD_DIM, HEAD_DIM), HEAD_DIM), cols] = o * (1.0 / l)
                l_ref[0, j:j + 1, cols] = m + jnp.log2(l)

        init = tuple((jnp.full((1, TILE), -1e38, f32), jnp.zeros((1, TILE), f32), jnp.zeros((HEAD_DIM, TILE), f32)) for _ in range(2))

        longs = lax.div(need, LONG)
        state = lax.fori_loop(0, longs, block(start, LONG), init)
        finish(lax.fori_loop(0, lax.div(need - longs * LONG, SHORT), block(start + longs * LONG, SHORT), state))

    o_ref[...] = oT_ref[...].T.astype(bf16)


def attend(info, qT, k, vT, kaug, qaugT):
    win = k.shape[0]
    nq = qT.shape[1]
    group = lambda p, *_: p // 2
    return pl.pallas_call(
        attend_kernel,
        out_shape=(jax.ShapeDtypeStruct((384, nq), f32), jax.ShapeDtypeStruct((nq, 384), bf16), jax.ShapeDtypeStruct((PAIRS, 8, nq), f32)),
        grid_spec=pltpu.PrefetchScalarGridSpec(
            num_scalar_prefetch=1, grid=(PAIRS,),
            in_specs=[
                pl.BlockSpec((128, nq), lambda p, *_: (p // 2, 0)),
                pl.BlockSpec((win, 128), lambda p, *_: (0, p // 2)),
                pl.BlockSpec((128, win), lambda p, *_: (p // 2, 0)),
                pl.BlockSpec((win, 128), lambda p, *_: (0, 0)),
                pl.BlockSpec((128, nq), lambda p, *_: (0, 0)),
            ],
            out_specs=[
                pl.BlockSpec((128, nq), lambda p, *_: (p // 2, 0)),
                pl.BlockSpec((nq, 128), lambda p, *_: (0, p // 2)),
                pl.BlockSpec((1, 8, nq), lambda p, *_: (p, 0, 0)),
            ],
            scratch_shapes=[pltpu.VMEM((256, 2 * TILE), bf16)],
        ),
        compiler_params=pltpu.CompilerParams(vmem_limit_bytes=28 << 20),
        cost_estimate=pl.CostEstimate(flops=20 * 10**9, bytes_accessed=6 << 20, transcendentals=5 * 10**6),
        name="attend",
    )(info, qT, k, vT, kaug, qaugT)


def attend_back_kernel(info_ref, qT_ref, q_ref, k_ref, kT_ref, v_ref, doT_ref, do_ref, oT_ref, l_ref, kaug_ref, qaugT_ref,
                       dq_ref, dk_ref, dv_ref, dqT_ref, rhs_s, rhs_d, q_stk, do_stk, dk_acc, dv_acc):
    p_id = pl.program_id(0)
    off = pair_offset(info_ref)

    @pl.when(lax.rem(p_id, 2) == 0)
    def _():
        dqT_ref[...] = jnp.zeros_like(dqT_ref)
        dk_acc[...] = jnp.zeros_like(dk_acc)
        dv_acc[...] = jnp.zeros_like(dv_acc)

    for t in range(2):
        cols = slice(t * TILE, (t + 1) * TILE)
        masked_q = rows_masked(qT_ref[:, cols], off)
        masked_do = rows_masked(doT_ref[:, cols], off)
        lane_q = lanes_masked(q_ref[cols, :], off)
        lane_do = lanes_masked(do_ref[cols, :], off)
        for j in range(2):
            part = slice(j * TILE, (j + 1) * TILE)
            head = pl.ds(pl.multiple_of(off + j * HEAD_DIM, HEAD_DIM), HEAD_DIM)
            delta = jnp.sum(doT_ref[head, cols].astype(f32) * oT_ref[head, cols], axis=0, keepdims=True)
            total = l_ref[0, j:j + 1, cols] * (1.0 / C2)
            rowid = lax.broadcasted_iota(jnp.int32, (64, TILE), 0)
            lp, dp = split3(-total), split3(-delta)
            def pieces(parts):
                x = jnp.zeros((64, TILE), f32)
                for n in range(3):
                    x = jnp.where(rowid == n, parts[n].astype(f32), x)
                return x.astype(bf16)
            rhs_s[0:128, part] = masked_q[j]
            rhs_s[128:192, part] = qaugT_ref[0:64, cols]
            rhs_s[192:256, part] = pieces(lp)
            rhs_d[0:128, part] = masked_do[j]
            rhs_d[128:192, part] = jnp.zeros((64, TILE), bf16)
            rhs_d[192:256, part] = pieces(dp)
            q_stk[part, :] = lane_q[j]
            do_stk[part, :] = lane_do[j]
        start = info_ref[1 + t]
        need = info_ref[3 + t]

        def block(first, size):
            def step(i, carry):
                row = pl.multiple_of(first + i * size, 128)
                rows = pl.ds(row, size)
                aug = kaug_ref[rows, :]
                lhs_k = jnp.concatenate([k_ref[rows, :], aug], axis=1)
                lhs_v = jnp.concatenate([v_ref[rows, :], aug], axis=1)
                out, dv, dk = [], dv_acc[rows, :], dk_acc[rows, :]
                for j in range(2):
                    part = slice(j * TILE, (j + 1) * TILE)
                    s = jnp.dot(lhs_k, rhs_s[:, part], preferred_element_type=f32)
                    dp = jnp.dot(lhs_v, rhs_d[:, part], preferred_element_type=f32)
                    p = jnp.exp2(s * C2)
                    ds = (p * dp).astype(bf16)
                    dv = dv + jnp.dot(p.astype(bf16), do_stk[part, :], preferred_element_type=f32)
                    dk = dk + jnp.dot(ds, q_stk[part, :], preferred_element_type=f32)
                    kT = kT_ref[pl.ds(pl.multiple_of(off + j * HEAD_DIM, HEAD_DIM), HEAD_DIM), rows]
                    out.append(carry[j] + jnp.dot(kT, ds, preferred_element_type=f32))
                dv_acc[rows, :] = dv
                dk_acc[rows, :] = dk
                return tuple(out)
            return step

        def finish(dqs):
            for j in range(2):
                dqT_ref[pl.ds(pl.multiple_of(off + j * HEAD_DIM, HEAD_DIM), HEAD_DIM), cols] = dqs[j] * SCALE

        init = tuple(jnp.zeros((HEAD_DIM, TILE), f32) for _ in range(2))

        longs = lax.div(need, LONG)
        state = lax.fori_loop(0, longs, block(start, LONG), init)
        finish(lax.fori_loop(0, lax.div(need - longs * LONG, SHORT), block(start + longs * LONG, SHORT), state))
    @pl.when((lax.rem(p_id, 2) == 1) | (p_id == PAIRS - 1))
    def _():
        dq_ref[...] = dqT_ref[...].T.astype(bf16)
        dk_ref[...] = (dk_acc[...] * SCALE).astype(bf16)
        dv_ref[...] = dv_acc[...].astype(bf16)


def attend_back(m, info, qT, q, k, kT, v, doT, do, oT, lse, kaug, qaugT):
    win, nq = k.shape[0], qT.shape[1]
    wide = pl.BlockSpec((128, nq), lambda p, *_: (p // 2, 0))
    tall = pl.BlockSpec((nq, 128), lambda p, *_: (0, p // 2))
    keys = pl.BlockSpec((win, 128), lambda p, *_: (0, p // 2))
    return pl.pallas_call(
        attend_back_kernel,
        out_shape=(jax.ShapeDtypeStruct((nq, 384), bf16), jax.ShapeDtypeStruct((win, 384), bf16), jax.ShapeDtypeStruct((win, 384), bf16)),
        grid_spec=pltpu.PrefetchScalarGridSpec(
            num_scalar_prefetch=1, grid=(PAIRS,),
            in_specs=[wide, tall, keys, pl.BlockSpec((128, win), lambda p, *_: (p // 2, 0)), keys,
                      pl.BlockSpec((128, nq), lambda p, *_: (p // 2, m)), pl.BlockSpec((nq, 128), lambda p, *_: (m, p // 2)), wide,
                      pl.BlockSpec((1, 8, nq), lambda p, *_: (p, 0, 0)),
                      pl.BlockSpec((win, 128), lambda p, *_: (0, 0)), pl.BlockSpec((128, nq), lambda p, *_: (0, 0))],
            out_specs=[tall, keys, keys],
            scratch_shapes=[pltpu.VMEM((128, nq), f32), pltpu.VMEM((256, 2 * TILE), bf16), pltpu.VMEM((256, 2 * TILE), bf16),
                            pltpu.VMEM((2 * TILE, 128), bf16), pltpu.VMEM((2 * TILE, 128), bf16),
                            pltpu.VMEM((win, 128), f32), pltpu.VMEM((win, 128), f32)],
        ),
        compiler_params=pltpu.CompilerParams(vmem_limit_bytes=32 << 20),
        cost_estimate=pl.CostEstimate(flops=40 * 10**9, bytes_accessed=12 << 20, transcendentals=5 * 10**6),
        name="attend_back",
    )(info, qT, q, k, kT, v, doT, do, oT, lse, kaug, qaugT)


def moments(x):
    centred = x - jnp.mean(x, axis=-1, keepdims=True)
    r = lax.rsqrt(jnp.mean(centred * centred, axis=-1, keepdims=True) + EPSILON)
    return centred * r, r


def norm_back(grad, n, r, gain):
    e = grad * gain
    return r * (e - jnp.mean(e, axis=-1, keepdims=True) - n * jnp.mean(e * n, axis=-1, keepdims=True))


def call(kernel, out_shape, name, flops=10**9, limit=48, **spec):
    return pl.pallas_call(
        kernel, out_shape=out_shape, name=name,
        compiler_params=pltpu.CompilerParams(vmem_limit_bytes=limit << 20),
        cost_estimate=pl.CostEstimate(flops=flops, bytes_accessed=8 << 20, transcendentals=0), **spec)


def shape(*dims, dtype=bf16):
    return jax.ShapeDtypeStruct(dims, dtype)


def scalar_first(grid, in_specs, out_specs, scratch=()):
    return dict(grid_spec=pltpu.PrefetchScalarGridSpec(
        num_scalar_prefetch=1, grid=grid, in_specs=in_specs, out_specs=out_specs, scratch_shapes=list(scratch)))


def full(*dims):
    return pl.BlockSpec(dims, lambda *_: (0,) * len(dims))


def pack_heads_kernel(core_ref, qkv_ref, vec_ref, heads_ref):
    for part in range(3):
        near = pl.ds(pl.multiple_of(640 * part + 256 * core_ref[0], 128), 256)
        heads_ref[0:160, 384 * part:384 * part + 256] = qkv_ref[:, near]
        heads_ref[0:160, 384 * part + 256:384 * (part + 1)] = qkv_ref[:, 640 * part + 512:640 * (part + 1)]
    heads_ref[160:176, :] = jnp.zeros((16, 1152), bf16)
    heads_ref[160:176, 0:160] = vec_ref[...]


def pack_heads(core, w_qkv, vectors):
    return call(pack_heads_kernel, shape(176, 1152), "pack_heads", 10**6, 8, **scalar_first(
        (1,), [full(160, 1920), full(16, 160)], full(176, 1152)))(core, w_qkv, vectors)


def pack_feed_kernel(core_ref, out_ref, up_ref, down_ref, feed_ref):
    core = core_ref[0]
    for f in range(4):
        feed_ref[:, 640 * f:640 * (f + 1)] = up_ref[:, pl.ds(pl.multiple_of(1280 * f + 640 * core, 128), 640)]
        feed_ref[:, 2560 + 640 * f:2560 + 640 * (f + 1)] = down_ref[pl.ds(pl.multiple_of(640 * core + 160 * f, 32), 160), :]
    feed_ref[:, 5120:5760] = out_ref[...]


def pack_feed(core, w_out, w_up, w_down):
    args = (w_out, w_up, w_down)
    return call(pack_feed_kernel, shape(160, 5760), "pack_feed", 10**6, 16, **scalar_first(
        (1,), [full(*a.shape) for a in args], full(160, 5760)))(core, *args)


def assemble_kernel(y_ref, own_ref, before_ref, after_ref, near_ref, far_ref, heads_ref, vec_ref):
    total = jnp.zeros((16, 640), f32)

    def place(by, top, bottom, vec):
        nonlocal total
        row = lax.rem(y_ref[0] + by, 4) * 160
        for part, base in ((top, 0), (bottom, top.shape[0])):
            heads_ref[pl.ds(pl.multiple_of(row + base, 32), part.shape[0]), :] = part
        total = total + pltpu.roll(vec[:, :640].astype(f32), row, 1)

    for by, ref in ((0, own_ref), (3, before_ref), (1, after_ref)):
        place(by, ref[0:96, :], ref[96:160, :], ref[160:176, :])
    place(2, near_ref[...], far_ref[0:64, :], far_ref[64:80, :])
    vec_ref[...] = total


def assemble(y, *parts):
    return call(assemble_kernel, (shape(640, 1152), shape(16, 640, dtype=f32)), "assemble", 10**6, 12, **scalar_first(
        (1,), [full(*a.shape) for a in parts], [full(640, 1152), full(16, 640)]))(y, *parts)


def rows_in_order(core, mine, theirs, x_ref):
    mine, theirs = mine.astype(f32), theirs.astype(f32)
    x_ref[0:256, :] = jnp.where(core == 0, mine, theirs)
    x_ref[256:512, :] = jnp.where(core == 0, theirs, mine)


def window_rows(core, own_refs, other_refs, m, block, x_ref):
    for j in range(len(own_refs)):
        @pl.when(block == j)
        def _():
            rows_in_order(core, own_refs[j][m], other_refs[j][m], x_ref)


def project_kernel(m, chips, place_ref, *refs):
    n = len(chips)
    own_refs, other_refs = refs[:n], refs[n:2 * n]
    vec_ref, w_ref = refs[2 * n:2 * n + 2]
    k_ref, v_ref, kT_ref, vT_ref = refs[-6 - 2 * (n == 3):][:4]
    x_ref, hid_ref = refs[-2:]
    step = pl.program_id(0)
    block = sum(jnp.where(step == i, chip, 0) for i, chip in enumerate(chips))
    needed = (block >= place_ref[1 + 2 * m]) & (block < place_ref[2 + 2 * m])

    @pl.when(jnp.logical_not(needed))
    def _():
        for ref in (k_ref, v_ref, kT_ref, vT_ref):
            ref[...] = jnp.zeros_like(ref)

    @pl.when(needed)
    def _():
        window_rows(place_ref[0], own_refs, other_refs, m, step, x_ref)
        hidden = (moments(x_ref[...])[0] * vec_ref[0:1, :] + vec_ref[1:2, :]).astype(bf16)
        hid_ref[...] = hidden
        kv = jnp.dot(hidden, w_ref[:, 384:], preferred_element_type=f32)
        low = kv.astype(bf16)
        k_ref[...] = low[:, :384]
        v_ref[...] = low[:, 384:]
        turned = kv.T.astype(bf16)
        kT_ref[...] = turned[:384]
        vT_ref[...] = turned[384:]

    if n == 3:
        q_ref, qT_ref = refs[-4:-2]

        @pl.when(step == 1)
        def _():
            q = jnp.dot(hid_ref[...], w_ref[:, :384], preferred_element_type=f32)
            q_ref[...] = q.astype(bf16)
            qT_ref[...] = q.T.astype(bf16)


def project(m, chips, place, own, other, vec, w, earlier=()):
    n = len(chips)
    chip = (lambda b: b + 1) if n == 3 else (lambda b: 4 * b)
    tall, wide = pl.BlockSpec((512, 384), lambda b, *_: (chip(b), 0)), pl.BlockSpec((384, 512), lambda b, *_: (0, chip(b)))
    shapes = [shape(2560, 384), shape(2560, 384), shape(384, 2560), shape(384, 2560)]
    specs = [tall, tall, wide, wide]
    if n == 3:
        shapes, specs = shapes + [shape(512, 384), shape(384, 512)], specs + [full(512, 384), full(384, 512)]
    own, other = [own[c] for c in chips], [other[c] for c in chips]
    return call(
        lambda *refs: project_kernel(m, chips, *refs), shapes, "project", 5 * 10**9, 28,
        input_output_aliases={2 * n + 3 + i: i for i in range(len(earlier))}, **scalar_first(
            (n,), [full(2, 256, 640)] * (2 * n) + [full(16, 640), full(640, 1152)] + [pl.BlockSpec(memory_space=pl.ANY)] * len(earlier),
            specs, [pltpu.VMEM((512, 640), f32), pltpu.VMEM((512, 640), bf16)]))(place, *own, *other, vec, w, *earlier)


def heads_joined(core, mine, theirs):
    first, second = (jnp.where(core == 0, a, b) for a, b in ((mine, theirs), (theirs, mine)))
    return jnp.concatenate([first[:, :256], second[:, :256], first[:, 256:] + second[:, 256:]], axis=1)


def middle_kernel(core_ref, low_ref, theirs_ref, tok_ref, w_ref, vec_ref, mid_ref, hid_ref):
    core = core_ref[0]
    rows = pl.ds(pl.multiple_of(256 * core, 256), 256)
    for m in range(2):
        attended = heads_joined(core, low_ref[m, rows, :].astype(f32), theirs_ref[m, rows, :].astype(f32)).astype(bf16)
        part = slice(256 * m, 256 * (m + 1))
        middle = tok_ref[m].astype(f32) + jnp.dot(attended, w_ref[...], preferred_element_type=f32)
        mid_ref[part, :] = middle
        hid_ref[part, :] = (moments(middle)[0] * vec_ref[2:3, :] + vec_ref[3:4, :]).astype(bf16)


def middle_step(core, low, theirs, tok, w, vec):
    args = (low, theirs, tok, w, vec)
    specs = [full(*a.shape) for a in args]
    return call(middle_kernel, (shape(512, 640, dtype=f32), shape(512, 640)), "middle", 10**9, 16, **scalar_first(
        (1,), specs, [full(512, 640), full(512, 640)]))(core, *args)


def feed_kernel(h_ref, h2_ref, cot_ref, cot2_ref, up_ref, down_ref, out_ref, dh_ref, theirs_ref, g_ref, h, cot, hT, cT, out, dh):
    chunk = pl.program_id(0)

    @pl.when(chunk == 0)
    def _():
        h[0:512, :], h[512:1024, :] = h_ref[...], h2_ref[...]
        cot[0:512, :], cot[512:1024, :] = cot_ref[...], cot2_ref[...]
        hT[...] = h[...].astype(f32).T.astype(bf16)
        cT[...] = cot[...].astype(f32).T.astype(bf16)
        out[...] = jnp.zeros_like(out)
        dh[...] = jnp.zeros_like(dh)

    up_w = up_ref[...]
    down_w = jnp.concatenate([down_ref[160 * y:160 * (y + 1), 640 * i:640 * (i + 1)] for y in range(2) for i in range(4)], axis=0)
    acts, d_ups = [], []
    for t in range(4):
        rows = slice(256 * t, 256 * (t + 1))
        u = jnp.dot(h[rows, :], up_w, preferred_element_type=f32)
        d_act = lax.dot_general(cot[rows, :], down_w, NT, preferred_element_type=f32)
        cdf = 0.5 * (1.0 + lax.erf(u * (2.0 ** -0.5)))
        pdf = jnp.exp(u * u * -0.5) * ((2.0 * math.pi) ** -0.5)
        act = (u * cdf).astype(bf16)
        d_up = (d_act * (cdf + u * pdf)).astype(bf16)
        out[rows, :] += jnp.dot(act, down_w, preferred_element_type=f32)
        dh[rows, :] += lax.dot_general(d_up, up_w, NT, preferred_element_type=f32)
        acts.append(act)
        d_ups.append(d_up)
    g_up = jnp.dot(hT[...], jnp.concatenate(d_ups, axis=0), preferred_element_type=f32).astype(bf16)
    g_down = jnp.dot(cT[...], jnp.concatenate(acts, axis=0), preferred_element_type=f32).T.astype(bf16)
    for f in range(2):
        for y in range(4):
            for i in range(2):
                g_ref[4 * chunk + 2 * f + i, y] = g_up[160 * y + 80 * i:160 * y + 80 * (i + 1), 640 * f:640 * (f + 1)]
        for i in range(8):
            g_ref[8 + i, 2 * chunk + f] = g_down[640 * f + 80 * i:640 * f + 80 * (i + 1)]

    @pl.when(chunk == 1)
    def _():
        out_ref[...], dh_ref[...] = out[0:512, :], dh[0:512, :]
        theirs_ref[0], theirs_ref[1] = out[512:1024, :].astype(bf16), dh[512:1024, :].astype(bf16)


def feed_forward(h, h2, cot, cot2, weights):
    return call(
        feed_kernel,
        (shape(512, 640, dtype=f32), shape(512, 640, dtype=f32), shape(2, 512, 640), shape(16, 4, 80, 640)),
        "feed_forward", 30 * 10**9, 52, grid=(2,),
        in_specs=[full(512, 640)] * 4 + [pl.BlockSpec((640, 1280), lambda f: (0, f)), pl.BlockSpec((320, 2560), lambda f: (f, 1))],
        out_specs=[full(512, 640), full(512, 640), full(2, 512, 640), full(16, 4, 80, 640)],
        scratch_shapes=[pltpu.VMEM((1024, 640), bf16), pltpu.VMEM((1024, 640), bf16), pltpu.VMEM((640, 1024), bf16), pltpu.VMEM((640, 1024), bf16),
                        pltpu.VMEM((1024, 640), f32), pltpu.VMEM((1024, 640), f32)],
    )(h, h2, cot, cot2, weights, weights)


def after_kernel(mid_ref, out_ref, dh_ref, theirs_ref, cot_ref, vec_ref, block_ref, grad_ref, branch_ref, g_ref):
    middle = mid_ref[...]
    block_ref[...] = (middle + out_ref[...] + theirs_ref[0].astype(f32)).astype(bf16)
    d_hidden = dh_ref[...] + theirs_ref[1].astype(f32)
    n, r = moments(middle)
    g_ref[...] = jnp.zeros_like(g_ref)
    g_ref[0:1, :] = jnp.sum(d_hidden * n, axis=0, keepdims=True)
    g_ref[1:2, :] = jnp.sum(d_hidden, axis=0, keepdims=True)
    grad = cot_ref[...].astype(f32) + norm_back(d_hidden, n, r, vec_ref[2:3, :])
    grad_ref[...] = grad
    branch_ref[...] = grad.astype(bf16)


def after_feed(middle, out, dh, theirs, cot, vec):
    args = (middle, out, dh, theirs, cot, vec)
    return call(
        after_kernel, (shape(512, 640), shape(512, 640, dtype=f32), shape(512, 640), shape(8, 640, dtype=f32)), "after_feed", 10**9, 24,
        in_specs=[pl.BlockSpec(memory_space=pltpu.VMEM)] * 6, out_specs=[pl.BlockSpec(memory_space=pltpu.VMEM)] * 4)(*args)


def branch_kernel(core_ref, own_ref, their_ref, w_ref, low_ref, theirs_ref, do_ref, doT_ref, g_ref):
    core = core_ref[0]
    w = jnp.concatenate([w_ref[pl.ds(pl.multiple_of(256 * core, 256), 256), :], w_ref[512:640, :]], axis=0)
    g = jnp.zeros((640, 384), f32)
    for m in range(2):
        part = slice(256 * m, 256 * (m + 1))
        mine, theirs = own_ref[part, :].astype(f32), their_ref[part, :].astype(f32)
        branch = jnp.concatenate([jnp.where(core == 0, mine, theirs), jnp.where(core == 0, theirs, mine)], axis=0)
        kept = jnp.where(core == 0, branch[:, :384], branch[:, 256:]).astype(bf16)
        branch = branch.astype(bf16)
        rows = slice(512 * m, 512 * (m + 1))
        do = lax.dot_general(branch, w, NT, preferred_element_type=f32)
        do_ref[rows, :] = do.astype(bf16)
        doT_ref[:, rows] = do.T.astype(bf16)
        attended = heads_joined(core, low_ref[m].astype(f32), theirs_ref[m].astype(f32))
        g = g + jnp.dot(attended.T.astype(bf16), kept, preferred_element_type=f32)
    g_ref[...] = g


def branch_step(core, own, their, w, low, theirs):
    args = (own, their, w, low, theirs)
    specs = [full(*a.shape) for a in args]
    return call(
        branch_kernel, (shape(1024, 384), shape(384, 1024), shape(640, 384, dtype=f32)), "branch", 10**9, 24, **scalar_first(
            (1,), specs, [full(1024, 384), full(384, 1024), full(640, 384)]))(core, *args)


def project_back_kernel(core_ref, *refs):
    own_refs, other_refs = refs[:5], refs[5:10]
    (vec_ref, w_ref, dq0_ref, dq1_ref, dk0_ref, dk1_ref, dv0_ref, dv1_ref, g_out_ref, g_two_ref,
     mine_ref, theirs_ref, tail_ref, x_ref, d_kv, d_q, d_hid, g_ref, g_vec) = refs[10:]
    step, core = pl.program_id(0), core_ref[0]
    block = lax.rem(step, 5)

    @pl.when(step == 0)
    def _():
        g_ref[...] = jnp.zeros_like(g_ref)
        g_vec[...] = jnp.zeros_like(g_vec)
        g_vec[2:4, :] = g_two_ref[0:2, :]

    second = lax.div(step, 5)
    needed = (block >= core_ref[1 + 2 * second]) & (block < core_ref[2 + 2 * second])

    @pl.when(jnp.logical_not(needed))
    def _():
        mine_ref[...] = jnp.zeros_like(mine_ref)
        theirs_ref[...] = jnp.zeros_like(theirs_ref)

    for m, (dq, dk, dv) in enumerate(((dq0_ref, dk0_ref, dv0_ref), (dq1_ref, dk1_ref, dv1_ref))):
        @pl.when(needed & (second == m))
        def _():
            window_rows(core, own_refs, other_refs, m, block, x_ref)
            d_kv[:, :384], d_kv[:, 384:] = dk[...], dv[...]
            d_q[...] = dq[...]

    @pl.when(needed)
    def _():
        n = moments(x_ref[...])[0]
        hiddenT = (n * vec_ref[0:1, :] + vec_ref[1:2, :]).T.astype(bf16)
        d_hid[...] = lax.dot_general(d_kv[...], w_ref[:, 384:], NT, preferred_element_type=f32)
        g_ref[:, 384:] += jnp.dot(hiddenT, d_kv[...], preferred_element_type=f32)

        @pl.when(block == 2)
        def _():
            g_ref[:, :384] += jnp.dot(hiddenT, d_q[...], preferred_element_type=f32)
            d_hid[...] += lax.dot_general(d_q[...], w_ref[:, :384], NT, preferred_element_type=f32)

        dh = d_hid[...]
        mine_ref[0, 0] = jnp.where(core == 0, dh[:256], dh[256:]).astype(bf16)
        theirs_ref[0, 0] = jnp.where(core == 0, dh[256:], dh[:256]).astype(bf16)
        g_vec[0:1, :] += jnp.sum(dh * n, axis=0, keepdims=True)
        g_vec[1:2, :] += jnp.sum(dh, axis=0, keepdims=True)

    @pl.when(step == 9)
    def _():
        turned = g_vec[...].T
        lane = lax.broadcasted_iota(jnp.int32, (640, 128), 1) - 64 * (1 - core)
        spare = g_ref[:, 256:384]
        for i in range(4):
            spare = jnp.where(lane == i, turned[:, i:i + 1], spare)
        g_ref[:, 256:384] = spare
        for y in range(4):
            for z in range(4):
                rows = slice(160 * y + 40 * z, 160 * y + 40 * (z + 1))
                for x in range(3):
                    tail_ref[16 * y + 4 * z + x] = g_ref[rows, 384 * x:384 * (x + 1)].astype(bf16)
                tail_ref[16 * y + 4 * z + 3] = g_out_ref[rows, :].astype(bf16)


def project_back(core, own, other, vec, w, dq, dk, dv, g_out, g_two):
    first = pl.BlockSpec((512, 384), lambda b, *_: (jnp.minimum(b, 4), 0))
    second = pl.BlockSpec((512, 384), lambda b, *_: (jnp.maximum(b - 5, 0), 0))
    return call(
        project_back_kernel, (shape(5, 2, 256, 640), shape(5, 2, 256, 640), shape(64, 40, 384)), "project_back", 10**10, 36, **scalar_first(
            (10,), [full(2, 256, 640)] * 10 + [full(16, 640), full(640, 1152), full(512, 384), full(512, 384), first, second, first, second,
                                               full(640, 384), full(8, 640)],
            [pl.BlockSpec((1, 1, 256, 640), lambda b, *_: (lax.rem(b, 5), b // 5, 0, 0))] * 2 + [full(64, 40, 384)],
            [pltpu.VMEM((512, 640), f32), pltpu.VMEM((512, 768), bf16), pltpu.VMEM((512, 384), bf16),
             pltpu.VMEM((512, 640), f32), pltpu.VMEM((640, 1152), f32), pltpu.VMEM((8, 640), f32)]))(core, *own, *other, vec, w, *dq, *dk, *dv, g_out, g_two)


def in_core_order(core_ref, mine, theirs):
    core, mine, theirs = core_ref[0], mine.astype(f32), theirs.astype(f32)
    return jnp.where(core == 0, mine, theirs), jnp.where(core == 0, theirs, mine)


def final_feed_kernel(core_ref, mine_ref, theirs_ref, up_ref, down_ref):
    for i in range(16):
        for c, piece in enumerate(in_core_order(core_ref, mine_ref[i], theirs_ref[i])):
            if i < 8:
                base = 1280 * (i // 2) + 640 * c
                up_ref[80 * (i % 2):80 * (i % 2 + 1), base:base + 640] = piece
            else:
                base = 640 * c + 80 * (i - 8)
                down_ref[base:base + 80, :] = piece


def final_feed(core, mine, theirs):
    return call(final_feed_kernel, (shape(160, 5120, dtype=f32), shape(1280, 640, dtype=f32)), "final_feed", 10**6, 32, **scalar_first(
        (1,), [full(16, 80, 640)] * 2, [full(160, 5120), full(1280, 640)]))(core, mine, theirs)


def final_heads_kernel(core_ref, mine_ref, theirs_ref, qkv_ref, out_ref, vec_ref):
    lane = lax.broadcasted_iota(jnp.int32, (40, 128), 1)
    for z in range(4):
        rows = slice(40 * z, 40 * (z + 1))
        for x in range(4):
            a, b = in_core_order(core_ref, mine_ref[4 * z + x], theirs_ref[4 * z + x])
            if x < 3:
                last = jnp.where(lane < 64, a[:, 256:], b[:, 256:])
                qkv_ref[rows, 640 * x:640 * (x + 1)] = jnp.concatenate([a[:, :256], b[:, :256], last], axis=1)
            else:
                out_ref[rows, :] = jnp.concatenate([a, b[:, 128:]], axis=1)
            if x == 0:
                vec_ref[rows, :] = pltpu.roll(a[:, 256:], 64, 1) + b[:, 256:]


def final_heads(core, mine, theirs):
    return call(
        final_heads_kernel, (shape(160, 1920, dtype=f32), shape(160, 640, dtype=f32), shape(160, 128, dtype=f32)), "final_heads", 10**6, 16,
        **scalar_first((1,), [full(16, 40, 384)] * 2, [full(160, 1920), full(160, 640), full(160, 128)]))(core, mine, theirs)


def shifted(array, axis, by):
    devices = lax.axis_size(axis)
    return lax.ppermute(array, axis, [(i, (i + by) % devices) for i in range(devices)])


def passed_along(array, by):
    devices = lax.axis_size(("z", "x"))
    return lax.ppermute(array, ("z", "x"), [(i, i + by) for i in range(devices) if 0 <= i + by < devices])


def swapped(array):
    return lax.ppermute(array, "core", [(0, 1), (1, 0)])


def pick(array, index):
    return lax.dynamic_index_in_dim(array, index, 0, keepdims=False)


def summed_share(array, axis):
    me, devices = lax.axis_index(axis), lax.axis_size(axis)
    total = pick(array, me).astype(f32)
    for by in (1, devices - 1, 2):
        total = total + shifted(pick(array, (me + by) % devices), axis, by).astype(f32)
    return total.astype(bf16)


def gathered(array, axis):
    me, devices = lax.axis_index(axis), lax.axis_size(axis)
    out = jnp.zeros((devices,) + array.shape, array.dtype)
    out = lax.dynamic_update_index_in_dim(out, array, me, 0)
    for by in (1, devices - 1, 2):
        out = lax.dynamic_update_index_in_dim(out, shifted(array, axis, by), (me + devices - by) % devices, 0)
    return out


def gathered_ring(array, axis):
    me, half = lax.axis_index(axis), array.shape[0] // 2
    before, after = shifted(array, axis, 1), shifted(array, axis, -1)
    far = jnp.concatenate([shifted(before[:half], axis, 1), shifted(after[half:], axis, -1)])
    out = jnp.zeros((4,) + array.shape, array.dtype)
    for by, part in ((0, array), (3, before), (1, after), (2, far)):
        out = lax.dynamic_update_index_in_dim(out, part, (me + by) % 4, 0)
    return out


def window_info(length_row, chip, core, win):
    ends = jnp.cumsum(length_row)
    starts = ends - length_row
    base = chip * 512 - 1024
    places = base + jnp.arange(win, dtype=jnp.int32)
    inside = (places[:, None] >= starts[None, :]) & (places[:, None] < ends[None, :])
    ones = jnp.broadcast_to(jnp.arange(64) < 3, (win, 64)).astype(bf16)
    key_rows = jnp.concatenate([jnp.where(inside, 0.0, -BIG).astype(bf16), ones], axis=1)
    own = chip * 512 + jnp.arange(512, dtype=jnp.int32)
    inside_q = (own[None, :] >= starts[:, None]) & (own[None, :] < ends[:, None])
    query_rows = jnp.concatenate([inside_q.astype(bf16), jnp.zeros((64, 512), bf16)], axis=0)
    info = [core]
    sizes = []
    for t in range(2):
        first = chip * 512 + t * TILE
        low = jnp.max(jnp.where(starts <= first, starts, 0)) - base
        high = jnp.min(jnp.where(ends > first + TILE - 1, ends, 1 << 30)) - base
        start = low // 128 * 128
        need = high - start
        size = (need + SHORT - 1) // SHORT * SHORT
        info.append(jnp.minimum(start, win - size))
        sizes.append(size)
    low = jnp.minimum(info[1], info[2]) // 512
    high = (jnp.maximum(info[1] + sizes[0], info[2] + sizes[1]) + 511) // 512
    return jnp.stack(info + sizes).astype(jnp.int32), key_rows, query_rows, [low, high]


def body(tokens, lengths, gain_one, bias_one, w_qkv, w_out, gain_two, bias_two, w_up, w_down, cotangent):
    core, chip = lax.axis_index("core"), lax.axis_index(("z", "x"))
    core_arg, y_arg = core[None].astype(jnp.int32), lax.axis_index("batch")[None].astype(jnp.int32)
    tok, cot = tokens[:, 0], cotangent[:, 0].reshape(512, 640)

    before, after = passed_along(tok, 1), passed_along(tok, -1)
    vectors = jnp.pad(jnp.stack([gain_one, bias_one, gain_two, bias_two]), ((0, 12), (0, 0)))
    heads = pack_heads(core_arg, w_qkv, vectors)
    heads_before, heads_after = shifted(heads, "batch", 1), shifted(heads, "batch", -1)
    feed_weights = lax.all_gather(pack_feed(core_arg, w_out, w_up, w_down), "batch", axis=0, tiled=True)
    w_out_all = feed_weights[:, 5120:]
    own = (passed_along(before, 1), before, tok, after, passed_along(after, -1))
    near, far = shifted(heads_before[:96], "batch", 1), shifted(heads_after[96:], "batch", -1)
    other = tuple(swapped(a) for a in own)
    w_heads, vec = assemble(y_arg, heads, heads_before, heads_after, near, far)

    windows = [window_info(lengths[m, 0], chip, core, 2560) for m in range(2)]
    place = jnp.stack([core] + windows[0][3] + windows[1][3]).astype(jnp.int32)
    forward = []
    near_parts = [project(m, (1, 2, 3), place, own, other, vec, w_heads) for m in range(2)]
    for m in range(2):
        k, v, kT, vT = project(m, (0, 4), place, own, other, vec, w_heads, near_parts[m][:4])
        q, qT = near_parts[m][4:]
        info, key_rows, query_rows, _ = windows[m]
        oT, low, lse = attend(info, qT, k, vT, key_rows, query_rows)
        forward.append((info, qT, q, k, kT, v, oT, lse, key_rows, query_rows, low))

    low = jnp.stack([f[-1] for f in forward])
    theirs = swapped(low)
    middle, hidden_two = middle_step(core_arg, low, theirs, tok, w_out_all, vec)
    out, d_hidden, partial, feed_grads = feed_forward(hidden_two, swapped(hidden_two), cot, swapped(cot), feed_weights)
    feed_grads = lax.psum_scatter(feed_grads.reshape(5120, 640), ("z", "x"), scatter_dimension=0, tiled=True).reshape(4, 80, 640)
    block_out, grad_middle, branch, g_two = after_feed(middle, out, d_hidden, swapped(partial), cot, vec)

    do, doT, g_out = branch_step(core_arg, branch, swapped(branch), w_out_all, low, theirs)
    grads = []
    for m in range(2):
        info, qT, q, k, kT, v, oT, lse, key_rows, query_rows, _ = forward[m]
        grads.append(attend_back(m, info, qT, q, k, kT, v, doT, do, oT, lse, key_rows, query_rows))
    dq, dk, dv = zip(*grads)
    mine, theirs, tail = project_back(place, own, other, vec, w_heads, dq, dk, dv, g_out, g_two)
    tail = lax.all_to_all(tail, ("batch", "z", "x"), 0, 0, tiled=True)

    theirs = swapped(theirs)
    sums = [mine[j].astype(f32) + theirs[j].astype(f32) for j in range(5)]
    right = passed_along(sums[4].astype(bf16), 1).astype(f32) + sums[3]
    left = passed_along(sums[0].astype(bf16), -1).astype(f32) + sums[1]
    d_one = sums[2] + passed_along(right.astype(bf16), 1).astype(f32) + passed_along(left.astype(bf16), -1).astype(f32)
    n_one, r_one = moments(tok.reshape(512, 640).astype(f32))
    grad_tokens = (grad_middle + norm_back(d_one.reshape(512, 640), n_one, r_one, vec[0:1])).astype(bf16)

    feed = lax.all_gather(summed_share(feed_grads, "batch"), ("z", "x"), axis=0, tiled=True).reshape(16, 80, 640)
    grad_up, grad_down = final_feed(core_arg, feed, swapped(feed))
    tail, grad_tokens = lax.optimization_barrier((tail, grad_tokens))
    tail = jnp.sum(tail.astype(f32), axis=0).astype(bf16)
    tail = gathered(gathered(tail, "x").reshape(160, 384), "z").reshape(16, 40, 384)
    grad_qkv, grad_out, spare = final_heads(core_arg, tail, swapped(tail))
    return (
        block_out.reshape(2, 1, 256, 640), grad_tokens.reshape(2, 1, 256, 640), spare[:, 0], spare[:, 1], grad_qkv, grad_out,
        spare[:, 2], spare[:, 3], grad_up, grad_down)


def solution(mesh):
    fine = Mesh(mesh.devices.reshape(4, 4, 4, 2), ("batch", "z", "x", "core"))
    rows = P(None, "batch", ("z", "x", "core"), None)
    one, two = P("batch"), P("batch", None)
    return jax.shard_map(
        body,
        mesh=fine,
        in_specs=(rows, P(None, "batch", None), one, one, two, two, one, one, two, two, rows),
        out_specs=(rows, rows, one, one, two, two, one, one, two, two),
        check_vma=False,
    )
```

profile of v0, /device:TPU:1, one launch (start us, length us, event | category | flops | bytes accessed | tf_op | source)
XLA Modules:
  0.0 388.4 jit_solution(17618172509109661157)
XLA Ops:
  13.5 4.0 %collective-permute-start = (bf16[2,256,640]{2,1,0:T(8,128)(2,1)S(1)}, bf16[2,256,640]{2,1,0:T(8,128)(2,1)S(1)}, u32[]{:S(2)}, u32[]{:S(2)}) collective-permute-start(bf16[2,256,640]{2,1,0:T(8,128)(2,1)S(1)} %bitcast.115), channel_id=1, source_target_pairs={{0,2},{2,4},{4,6},{6,8},{8,10},{10,12},{12,14},{14,16},{16,18},{18... | collective-permute-start | bytes 1966088 | tf_op jit(solution)/shard_map/ppermute | solution.py:622
  40.4 5.0 %collective-permute-done.8.far_ref = bf16[80,1152]{1,0:T(8,128)(2,1)S(1)} collective-permute-done((bf16[80,1152]{1,0:T(8,128)(2,1)S(1)}, bf16[80,1152]{1,0:T(8,128)(2,1)S(1)}, u32[]{:S(2)}, u32[]{:S(2)}) %collective-permute-start.8) | collective-permute-done | bytes 184352 | tf_op jit(solution)/shard_map/ppermute | solution.py:617
  45.4 5.2 %collective-permute-start.9 = (bf16[2,256,640]{2,1,0:T(8,128)(2,1)S(1)}, bf16[2,256,640]{2,1,0:T(8,128)(2,1)S(1)}, u32[]{:S(2)}, u32[]{:S(2)}) collective-permute-start(bf16[2,256,640]{2,1,0:T(8,128)(2,1)S(1)} %collective-permute-done.refs_1_), channel_id=1, source_target_pairs={{0,2},{2,4},{4,6},{6,8},{8,10},{10,12},{12,14},{14,16},{16,18},{18... | collective-permute-start | bytes 1966088 | tf_op jit(solution)/shard_map/ppermute | solution.py:622
  56.8 5.1 %collective-permute-done.9.refs_1_.refs_0_ = bf16[2,256,640]{2,1,0:T(8,128)(2,1)S(1)} collective-permute-done((bf16[2,256,640]{2,1,0:T(8,128)(2,1)S(1)}, bf16[2,256,640]{2,1,0:T(8,128)(2,1)S(1)}, u32[]{:S(2)}, u32[]{:S(2)}) %collective-permute-start.9) | collective-permute-done | bytes 655392 | tf_op jit(solution)/shard_map/ppermute | solution.py:622
  61.9 3.6 collective-permute-start.11
  65.5 6.7 %collective-permute-done.10.refs_2_.refs_4_ = bf16[2,256,640]{2,1,0:T(8,128)(2,1)S(1)} collective-permute-done((bf16[2,256,640]{2,1,0:T(8,128)(2,1)}, bf16[2,256,640]{2,1,0:T(8,128)(2,1)S(1)}, u32[]{:S(2)}, u32[]{:S(2)}) %collective-permute-start.10) | collective-permute-done | bytes 655392 | tf_op jit(solution)/shard_map/ppermute | solution.py:622
  73.0 5.6 %project.6 = (bf16[2560,384]{1,0:T(8,128)(2,1)S(1)}, bf16[2560,384]{1,0:T(8,128)(2,1)S(1)}, bf16[384,2560]{1,0:T(8,128)(2,1)S(1)}, bf16[384,2560]{1,0:T(8,128)(2...) custom-call(s32[5]{0:T(128)S(1)} %stack.81.refs_0_.core_ref, ...), custom_call_target="tpu_custom_call" | custom-call | flops 5000000000 | bytes 8388608 | tf_op jit(solution)/shard_map/project/pallas_call | solution.py:368
  79.4 5.5 %project.4 = (bf16[2560,384]{1,0:T(8,128)(2,1)S(1)}, bf16[2560,384]{1,0:T(8,128)(2,1)S(1)}, bf16[384,2560]{1,0:T(8,128)(2,1)S(1)}, bf16[384,2560]{1,0:T(8,128)(2...) custom-call(s32[5]{0:T(128)S(1)} %stack.81.refs_0_.core_ref, ...), custom_call_target="tpu_custom_call" | custom-call | flops 5000000000 | bytes 8388608 | tf_op jit(solution)/shard_map/project/pallas_call | solution.py:368
  88.5 13.4 %attend.3 = (f32[384,512]{1,0:T(8,128)S(1)}, bf16[512,384]{1,0:T(8,128)(2,1)S(1)}, f32[5,8,512]{2,1,0:T(8,128)S(1)}) custom-call(s32[5]{0:T(128)S(1)} %stack.92.info_ref, bf16[384,512]{1,0:T(8,128)(2,1)S(1)} %get-tuple-element.77.qT_ref, bf16[2560,384]{1,0:T(8,128)(2,1)S(1)} %get-tuple-element.82.k_ref, bf16[384,2560]{1,0:T(8,128)(2,1)S(1)} %get-tuple-element.83.vT_ref, ...), custom_call_target="tpu_custom_call" | custom-call | flops 20000000000 | bytes 6291456 | tf_op jit(solution)/shard_map/attend/pallas_call | solution.py:99
  102.0 11.0 %attend.2 = (f32[384,512]{1,0:T(8,128)S(1)}, bf16[512,384]{1,0:T(8,128)(2,1)S(1)}, f32[5,8,512]{2,1,0:T(8,128)S(1)}) custom-call(s32[5]{0:T(128)S(1)} %stack.76.info_ref, bf16[384,512]{1,0:T(8,128)(2,1)S(1)} %get-tuple-element.69.qT_ref, bf16[2560,384]{1,0:T(8,128)(2,1)S(1)} %get-tuple-element.74.k_ref, bf16[384,2560]{1,0:T(8,128)(2,1)S(1)} %get-tuple-element.75.vT_ref, ...), custom_call_target="tpu_custom_call" | custom-call | flops 20000000000 | bytes 6291456 | tf_op jit(solution)/shard_map/attend/pallas_call | solution.py:99
  120.9 31.8 %feed_forward.1 = (f32[512,640]{1,0:T(8,128)}, f32[512,640]{1,0:T(8,128)}, bf16[2,512,640]{2,1,0:T(8,128)(2,1)}, bf16[16,4,80,640]{3,2,1,0:T(8,128)(2,1)}) custom-call(bf16[512,640]{1,0:T(8,128)(2,1)S(1)} %get-tuple-element.86.h_ref, bf16[512,640]{1,0:T(8,128)(2,1)S(1)} %collective-permute-done.14.h2_ref, bf16[512,640]{1,0:T(8,128)(2,1)} %bitcast.21.cot_ref, ...), custom_call_target="tpu_custom_call" | custom-call | flops 30000001024 | bytes 8388608 | tf_op jit(solution)/shard_map/feed_forward/pallas_call | solution.py:441
  168.2 15.8 %attend_back.2 = (bf16[512,384]{1,0:T(8,128)(2,1)S(1)}, bf16[2560,384]{1,0:T(8,128)(2,1)S(1)}, bf16[2560,384]{1,0:T(8,128)(2,1)S(1)}) custom-call(s32[5]{0:T(128)S(1)} %stack.76.info_ref, bf16[384,512]{1,0:T(8,128)(2,1)S(1)} %copy-done.58, bf16[512,384]{1,0:T(8,128)(2,1)S(1)} %copy-done.56, bf16[2560,384]{1,0:T(8,128)(2,1)S(1)} %copy-done.35, ...), custom_call_target="tpu_custom_call" | custom-call | flops 40000000000 | bytes 12582912 | tf_op jit(solution)/shard_map/attend_back/pallas_call | solution.py:208
  186.6 19.3 %attend_back.3 = (bf16[512,384]{1,0:T(8,128)(2,1)S(1)}, bf16[2560,384]{1,0:T(8,128)(2,1)S(1)}, bf16[2560,384]{1,0:T(8,128)(2,1)S(1)}) custom-call(s32[5]{0:T(128)S(1)} %stack.92.info_ref, bf16[384,512]{1,0:T(8,128)(2,1)S(1)} %copy-done.54, bf16[512,384]{1,0:T(8,128)(2,1)S(1)} %copy-done.52, bf16[2560,384]{1,0:T(8,128)(2,1)S(1)} %copy-done.41, ...), custom_call_target="tpu_custom_call" | custom-call | flops 40000000000 | bytes 12582912 | tf_op jit(solution)/shard_map/attend_back/pallas_call | solution.py:208
  210.4 17.4 %project_back.1 = (bf16[5,2,256,640]{3,2,1,0:T(8,128)(2,1)}, bf16[5,2,256,640]{3,2,1,0:T(8,128)(2,1)}, bf16[64,40,384]{2,1,0:T(8,128)(2,1)}) custom-call(s32[5]{0:T(128)S(1)} %copy-done.17, bf16[2,256,640]{2,1,0:T(8,128)(2,1)S(1)} %copy-done.25, bf16[2,256,640]{2,1,0:T(8,128)(2,1)S(1)} %copy-done.21, bf16[2,256,640]{2,1,0:T(8,128)(2,1)S(1)} %bitcast.121, ...), custom_call_target="tpu_custom_call" | custom-call | flops 10000000000 | bytes 8388608 | tf_op jit(solution)/shard_map/project_back/pallas_call | solution.py:564
  228.1 6.0 %collective-permute-done.18 = bf16[5,2,256,640]{3,2,1,0:T(8,128)(2,1)} collective-permute-done((bf16[5,2,256,640]{3,2,1,0:T(8,128)(2,1)}, bf16[5,2,256,640]{3,2,1,0:T(8,128)(2,1)}, u32[]{:S(2)}, u32[]{:S(2)}) %collective-permute-start.18) | collective-permute-done | bytes 3276832 | tf_op jit(solution)/shard_map/ppermute | solution.py:626
  237.2 15.7 %collective-permute-start.19 = (bf16[2,256,640]{2,1,0:T(8,128)(2,1)}, bf16[2,256,640]{2,1,0:T(8,128)(2,1)S(1)}, u32[]{:S(2)}, u32[]{:S(2)}) collective-permute-start(bf16[2,256,640]{2,1,0:T(8,128)(2,1)} %get-tuple-element.163), channel_id=1, source_target_pairs={{0,2},{2,4},{4,6},{6,8},{8,10},{10,12},{12,14},{14,16},{16,18},{18... | collective-permute-start | bytes 1966088 | tf_op jit(solution)/shard_map/ppermute | solution.py:622
  258.1 9.3 %collective-permute-start.31 = (bf16[80,640]{1,0:T(8,128)(2,1)S(1)}, bf16[80,640]{1,0:T(8,128)(2,1)S(1)}, u32[]{:S(2)}, u32[]{:S(2)}) collective-permute-start(bf16[80,640]{1,0:T(8,128)(2,1)S(1)} %get-tuple-element.167), channel_id=1, source_target_pairs={{0,96},{32,0},{64,32},{96,64},{1,97},{33,1},{65,33},{97,65},{2,98}... | collective-permute-start | bytes 307208 | tf_op jit(solution)/shard_map/ppermute | solution.py:617
  267.9 4.8 %collective-permute-done.31 = bf16[80,640]{1,0:T(8,128)(2,1)S(1)} collective-permute-done((bf16[80,640]{1,0:T(8,128)(2,1)S(1)}, bf16[80,640]{1,0:T(8,128)(2,1)S(1)}, u32[]{:S(2)}, u32[]{:S(2)}) %collective-permute-start.31) | collective-permute-done | bytes 102432 | tf_op jit(solution)/shard_map/ppermute | solution.py:617
  274.5 26.7 %all-to-all-start = ((bf16[64,40,384]{2,1,0:T(8,128)(2,1)}), bf16[64,40,384]{2,1,0:T(8,128)(2,1)S(1)}, u32[]{:S(2)}, u32[]{:S(2)}) async-start(bf16[64,40,384]{2,1,0:T(8,128)(2,1)} %get-tuple-element.112), calls=%async_computation | async-start | bytes 3932160 | tf_op jit(solution)/shard_map/all_to_all | solution.py:728
  301.3 3.5 fusion.8
  306.0 4.9 %collective-permute-start.20 = (bf16[2,256,640]{2,1,0:T(8,128)(2,1)}, bf16[2,256,640]{2,1,0:T(8,128)(2,1)}, u32[]{:S(2)}, u32[]{:S(2)}) collective-permute-start(bf16[2,256,640]{2,1,0:T(8,128)(2,1)} %get-tuple-element.161), channel_id=1, source_target_pairs={{0,2},{2,4},{4,6},{6,8},{8,10},{10,12},{12,14},{14,16},{16,18},{18... | collective-permute-start | bytes 1966088 | tf_op jit(solution)/shard_map/ppermute | solution.py:622
  311.3 27.5 %collective-permute-done.22 = bf16[2,256,640]{2,1,0:T(8,128)(2,1)S(1)} collective-permute-done((bf16[2,256,640]{2,1,0:T(8,128)(2,1)}, bf16[2,256,640]{2,1,0:T(8,128)(2,1)S(1)}, u32[]{:S(2)}, u32[]{:S(2)}) %collective-permute-start.22) | collective-permute-done | bytes 655392 | tf_op jit(solution)/shard_map/ppermute | solution.py:622
  347.3 15.3 %all-gather.5.cloned.1.call-done = bf16[1280,640]{1,0:T(8,128)(2,1)} async-done(((bf16[80,640]{1,0:T(8,128)(2,1)}), bf16[1280,640]{1,0:T(8,128)(2,1)}) %all-gather.5.cloned.1.call-update) | async-done | bytes 1638416 | tf_op jit(solution)/shard_map/all_gather | solution.py:738
  378.5 3.1 final_feed.1
  (266 shorter events, 101.6 us)
Async XLA Ops:
  7.2 107.3 %all-gather.3.cloned.1.call-start = ((), (), s32[]{:S(2)}) async-start(), calls=%async_computation.2 | async-start | bytes 9216000 | tf_op jit(solution)/shard_map/all_gather | solution.py:696
  12.5 241.7 %reduce-scatter.2.cloned.1.call-start = ((), (), s32[]{:S(2)}) async-start(), calls=%async_computation.3 | async-start | bytes 6963200 | tf_op jit(solution)/shard_map/reduce_scatter | solution.py:718
  13.5 24.4 %collective-permute-start = (bf16[2,256,640]{2,1,0:T(8,128)(2,1)S(1)}, bf16[2,256,640]{2,1,0:T(8,128)(2,1)S(1)}, u32[]{:S(2)}, u32[]{:S(2)}) collective-permute-start(bf16[2,256,640]{2,1,0:T(8,128)(2,1)S(1)} %bitcast.115), channel_id=1, source_target_pairs={{0,2},{2,4},{4,6},{6,8},{8,10},{10,12},{12,14},{14,16},{16,18},{18... | collective-permute-start | bytes 1966088 | tf_op jit(solution)/shard_map/ppermute | solution.py:622
  17.5 33.1 %collective-permute-start.1 = (bf16[2,256,640]{2,1,0:T(8,128)(2,1)S(1)}, bf16[2,256,640]{2,1,0:T(8,128)(2,1)}, u32[]{:S(2)}, u32[]{:S(2)}) collective-permute-start(bf16[2,256,640]{2,1,0:T(8,128)(2,1)S(1)} %bitcast.116), channel_id=1, source_target_pairs={{2,0},{4,2},{6,4},{8,6},{10,8},{12,10},{14,12},{16,14},{18,16},{20... | collective-permute-start | bytes 1966088 | tf_op jit(solution)/shard_map/ppermute | solution.py:622
  18.8 54.2 %collective-permute-start.3 = (bf16[2,256,640]{2,1,0:T(8,128)(2,1)S(1)}, bf16[2,256,640]{2,1,0:T(8,128)(2,1)}, u32[]{:S(2)}, u32[]{:S(2)}) collective-permute-start(bf16[2,256,640]{2,1,0:T(8,128)(2,1)S(1)} %bitcast.117), channel_id=1, source_target_pairs={{0,1},{1,0},{2,3},{3,2},{4,5},{5,4},{6,7},{7,6},{8,9},{9,8},{10,11... | collective-permute-start | bytes 1966088 | tf_op jit(solution)/shard_map/ppermute | solution.py:626
  20.0 13.5 %collective-permute-start.5 = (bf16[176,1152]{1,0:T(8,128)(2,1)S(1)}, bf16[176,1152]{1,0:T(8,128)(2,1)S(1)}, u32[]{:S(2)}, u32[]{:S(2)}) collective-permute-start(bf16[176,1152]{1,0:T(8,128)(2,1)S(1)} %pack_heads.1.own_ref), channel_id=1, source_target_pairs={{0,32},{32,64},{64,96},{96,0},{1,33},{33,65},{65,97},{97,1},{2,34}... | collective-permute-start | bytes 1216520 | tf_op jit(solution)/shard_map/ppermute | solution.py:617
  21.4 14.0 %collective-permute-start.6 = (bf16[176,1152]{1,0:T(8,128)(2,1)S(1)}, bf16[176,1152]{1,0:T(8,128)(2,1)S(1)}, u32[]{:S(2)}, u32[]{:S(2)}) collective-permute-start(bf16[176,1152]{1,0:T(8,128)(2,1)S(1)} %pack_heads.1.own_ref), channel_id=1, source_target_pairs={{0,96},{32,0},{64,32},{96,64},{1,97},{33,1},{65,33},{97,65},{2,98}... | collective-permute-start | bytes 1216520 | tf_op jit(solution)/shard_map/ppermute | solution.py:617
  34.2 19.4 %collective-permute-start.7 = (bf16[96,1152]{1,0:T(8,128)(2,1)}, bf16[96,1152]{1,0:T(8,128)(2,1)S(1)}, u32[]{:S(2)}, u32[]{:S(2)}) collective-permute-start(bf16[96,1152]{1,0:T(8,128)(2,1)} %slice.80), channel_id=1, source_target_pairs={{0,32},{32,64},{64,96},{96,0},{1,33},{33,65},{65,97},{97,1},{2,34}... | collective-permute-start | bytes 663560 | tf_op jit(solution)/shard_map/ppermute | solution.py:617
  38.0 35.0 %collective-permute-start.2 = (bf16[2,256,640]{2,1,0:T(8,128)(2,1)S(1)}, bf16[2,256,640]{2,1,0:T(8,128)(2,1)S(1)}, u32[]{:S(2)}, u32[]{:S(2)}) collective-permute-start(bf16[2,256,640]{2,1,0:T(8,128)(2,1)S(1)} %collective-permute-done.refs_1_), channel_id=1, source_target_pairs={{0,1},{1,0},{2,3},{3,2},{4,5},{5,4},{6,7},{7,6},{8,9},{9,8},{10,11... | collective-permute-start | bytes 1966088 | tf_op jit(solution)/shard_map/ppermute | solution.py:626
  45.4 16.5 %collective-permute-start.9 = (bf16[2,256,640]{2,1,0:T(8,128)(2,1)S(1)}, bf16[2,256,640]{2,1,0:T(8,128)(2,1)S(1)}, u32[]{:S(2)}, u32[]{:S(2)}) collective-permute-start(bf16[2,256,640]{2,1,0:T(8,128)(2,1)S(1)} %collective-permute-done.refs_1_), channel_id=1, source_target_pairs={{0,2},{2,4},{4,6},{6,8},{8,10},{10,12},{12,14},{14,16},{16,18},{18... | collective-permute-start | bytes 1966088 | tf_op jit(solution)/shard_map/ppermute | solution.py:622
  50.6 22.4 %collective-permute-start.4 = (bf16[2,256,640]{2,1,0:T(8,128)(2,1)}, bf16[2,256,640]{2,1,0:T(8,128)(2,1)S(1)}, u32[]{:S(2)}, u32[]{:S(2)}) collective-permute-start(bf16[2,256,640]{2,1,0:T(8,128)(2,1)} %collective-permute-done.1.refs_3_), channel_id=1, source_target_pairs={{0,1},{1,0},{2,3},{3,2},{4,5},{5,4},{6,7},{7,6},{8,9},{9,8},{10,11... | collective-permute-start | bytes 1966088 | tf_op jit(solution)/shard_map/ppermute | solution.py:626
  53.6 18.5 %collective-permute-start.10 = (bf16[2,256,640]{2,1,0:T(8,128)(2,1)}, bf16[2,256,640]{2,1,0:T(8,128)(2,1)S(1)}, u32[]{:S(2)}, u32[]{:S(2)}) collective-permute-start(bf16[2,256,640]{2,1,0:T(8,128)(2,1)} %collective-permute-done.1.refs_3_), channel_id=1, source_target_pairs={{2,0},{4,2},{6,4},{8,6},{10,8},{12,10},{14,12},{16,14},{18,16},{20... | collective-permute-start | bytes 1966088 | tf_op jit(solution)/shard_map/ppermute | solution.py:622
  61.9 23.0 %collective-permute-start.11 = (bf16[2,256,640]{2,1,0:T(8,128)(2,1)S(1)}, bf16[2,256,640]{2,1,0:T(8,128)(2,1)S(1)}, u32[]{:S(2)}, u32[]{:S(2)}) collective-permute-start(bf16[2,256,640]{2,1,0:T(8,128)(2,1)S(1)} %collective-permute-done.9.refs_1_.refs_0_), channel_id=1, source_target_pairs={{0,1},{1,0},{2,3},{3,2},{4,5},{5,4},{6,7},{7,6},{8,9},{9,8},{10,11... | collective-permute-start | bytes 1966088 | tf_op jit(solution)/shard_map/ppermute | solution.py:626
  72.1 12.8 %collective-permute-start.12 = (bf16[2,256,640]{2,1,0:T(8,128)(2,1)S(1)}, bf16[2,256,640]{2,1,0:T(8,128)(2,1)S(1)}, u32[]{:S(2)}, u32[]{:S(2)}) collective-permute-start(bf16[2,256,640]{2,1,0:T(8,128)(2,1)S(1)} %collective-permute-done.10.refs_2_.refs_4_), channel_id=1, source_target_pairs={{0,1},{1,0},{2,3},{3,2},{4,5},{5,4},{6,7},{7,6},{8,9},{9,8},{10,11... | collective-permute-start | bytes 1966088 | tf_op jit(solution)/shard_map/ppermute | solution.py:626
  152.9 209.7 %all-gather.5.cloned.1.call-start = ((), (), s32[]{:S(2)}) async-start(), calls=%async_computation.4 | async-start | bytes 1740800 | tf_op jit(solution)/shard_map/all_gather | solution.py:738
  237.2 64.1 %collective-permute-start.19 = (bf16[2,256,640]{2,1,0:T(8,128)(2,1)}, bf16[2,256,640]{2,1,0:T(8,128)(2,1)S(1)}, u32[]{:S(2)}, u32[]{:S(2)}) collective-permute-start(bf16[2,256,640]{2,1,0:T(8,128)(2,1)} %get-tuple-element.163), channel_id=1, source_target_pairs={{0,2},{2,4},{4,6},{6,8},{8,10},{10,12},{12,14},{14,16},{16,18},{18... | collective-permute-start | bytes 1966088 | tf_op jit(solution)/shard_map/ppermute | solution.py:622
  252.8 48.4 %collective-permute-start.21 = (bf16[2,256,640]{2,1,0:T(8,128)(2,1)}, bf16[2,256,640]{2,1,0:T(8,128)(2,1)}, u32[]{:S(2)}, u32[]{:S(2)}) collective-permute-start(bf16[2,256,640]{2,1,0:T(8,128)(2,1)} %get-tuple-element.164), channel_id=1, source_target_pairs={{2,0},{4,2},{6,4},{8,6},{10,8},{12,10},{14,12},{16,14},{18,16},{20... | collective-permute-start | bytes 1966088 | tf_op jit(solution)/shard_map/ppermute | solution.py:622
  255.2 12.6 %collective-permute-start.32 = (bf16[80,640]{1,0:T(8,128)(2,1)S(1)}, bf16[80,640]{1,0:T(8,128)(2,1)S(1)}, u32[]{:S(2)}, u32[]{:S(2)}) collective-permute-start(bf16[80,640]{1,0:T(8,128)(2,1)S(1)} %get-tuple-element.166), channel_id=1, source_target_pairs={{0,64},{32,96},{64,0},{96,32},{1,65},{33,97},{65,1},{97,33},{2,66}... | collective-permute-start | bytes 307208 | tf_op jit(solution)/shard_map/ppermute | solution.py:617
  258.1 14.6 %collective-permute-start.31 = (bf16[80,640]{1,0:T(8,128)(2,1)S(1)}, bf16[80,640]{1,0:T(8,128)(2,1)S(1)}, u32[]{:S(2)}, u32[]{:S(2)}) collective-permute-start(bf16[80,640]{1,0:T(8,128)(2,1)S(1)} %get-tuple-element.167), channel_id=1, source_target_pairs={{0,96},{32,0},{64,32},{96,64},{1,97},{33,1},{65,33},{97,65},{2,98}... | collective-permute-start | bytes 307208 | tf_op jit(solution)/shard_map/ppermute | solution.py:617
  274.5 68.1 %all-to-all-start = ((bf16[64,40,384]{2,1,0:T(8,128)(2,1)}), bf16[64,40,384]{2,1,0:T(8,128)(2,1)S(1)}, u32[]{:S(2)}, u32[]{:S(2)}) async-start(bf16[64,40,384]{2,1,0:T(8,128)(2,1)} %get-tuple-element.112), calls=%async_computation | async-start | bytes 3932160 | tf_op jit(solution)/shard_map/all_to_all | solution.py:728
  304.7 34.1 %collective-permute-start.22 = (bf16[2,256,640]{2,1,0:T(8,128)(2,1)}, bf16[2,256,640]{2,1,0:T(8,128)(2,1)S(1)}, u32[]{:S(2)}, u32[]{:S(2)}) collective-permute-start(bf16[2,256,640]{2,1,0:T(8,128)(2,1)} %get-tuple-element.162), channel_id=1, source_target_pairs={{2,0},{4,2},{6,4},{8,6},{10,8},{12,10},{14,12},{16,14},{18,16},{20... | collective-permute-start | bytes 1966088 | tf_op jit(solution)/shard_map/ppermute | solution.py:622
  306.0 32.8 %collective-permute-start.20 = (bf16[2,256,640]{2,1,0:T(8,128)(2,1)}, bf16[2,256,640]{2,1,0:T(8,128)(2,1)}, u32[]{:S(2)}, u32[]{:S(2)}) collective-permute-start(bf16[2,256,640]{2,1,0:T(8,128)(2,1)} %get-tuple-element.161), channel_id=1, source_target_pairs={{0,2},{2,4},{4,6},{6,8},{8,10},{10,12},{12,14},{14,16},{16,18},{18... | collective-permute-start | bytes 1966088 | tf_op jit(solution)/shard_map/ppermute | solution.py:622
  346.1 18.5 %collective-permute-start.25 = (bf16[40,384]{1,0:T(8,128)(2,1)S(1)}, bf16[40,384]{1,0:T(8,128)(2,1)S(1)}, u32[]{:S(2)}, u32[]{:S(2)}) collective-permute-start(bf16[40,384]{1,0:T(8,128)(2,1)S(1)} %reduce_sum.52), channel_id=1, source_target_pairs={{0,4},{2,6},{4,0},{6,2},{1,5},{3,7},{5,1},{7,3},{8,12},{10,14},{12... | collective-permute-start | bytes 92168 | tf_op jit(solution)/shard_map/ppermute | solution.py:617
  362.6 16.0 %collective-permute-start.33 = (bf16[16,80,640]{2,1,0:T(8,128)(2,1)}, bf16[16,80,640]{2,1,0:T(8,128)(2,1)S(1)}, u32[]{:S(2)}, u32[]{:S(2)}) collective-permute-start(bf16[16,80,640]{2,1,0:T(8,128)(2,1)} %bitcast.124), channel_id=1, source_target_pairs={{0,1},{1,0},{2,3},{3,2},{4,5},{5,4},{6,7},{7,6},{8,9},{9,8},{10,11... | collective-permute-start | bytes 4915208 | tf_op jit(solution)/shard_map/ppermute | solution.py:626
  (82 other events, 831.6 us)
Sparse Core Ops, SparseCore 0:
  12.6 84.3 all-gather.2
  153.0 101.1 reduce-scatter.1
  274.4 88.0 all-gather.4
where the time goes:
time: 394 us; the launch traced here: 388 us
  Pallas kernels  133 us (34%)
  starting transfers between devices  104 us (26%)
  waiting for transfers between devices  86.9 us (22%)
  local copies, waits for them, and re-layouts  25.8 us (7%)
  between operations  20.7 us (5%)
  other arithmetic  17.7 us (4%)
    ppermute x8, waiting for transfers between devices, passed_along(): lax.ppermute(array, ('z', 'x'), [(i, i + by) for i in range(devices) if 0...  39.3 us
    pallas_call x2, Pallas kernels, attend_back(): pl.pallas_call(attend_back_kernel, out_shape=(jax.ShapeDtypeStruct((nq, 3...  35 us
    ppermute x8, starting transfers between devices, passed_along(): lax.ppermute(array, ('z', 'x'), [(i, i + by) for i in range(devices) if 0...  34.9 us
    pallas_call x1, Pallas kernels, feed_forward(): call(feed_kernel, (shape(512, 640, dtype=f32), shape(512, 640, dtype=f32)...  31.8 us
    all_to_all x1, starting transfers between devices, body(): tail = lax.all_to_all(tail, ('batch', 'z', 'x'), 0, 0, tiled=True)  26.7 us
    ppermute x13, starting transfers between devices, shifted(): lax.ppermute(array, axis, [(i, (i + by) % devices) for i in range(devices)])  26.3 us
    pallas_call x2, Pallas kernels, attend(): pl.pallas_call(attend_kernel, out_shape=(jax.ShapeDtypeStruct((384, nq),...  24.4 us
    unnamed x140, local copies, waits for them, and re-layouts  21.2 us
  transfers between devices with their start and end apart: 38, of which 17 were waited for; matrix products, arithmetic and copies ran while one was open for 6% of the time, Pallas kernels for 25%

commit v1 on v0

--- a/solution.py
+++ b/solution.py
@@ -92,19 +92,18 @@
     o_ref[...] = oT_ref[...].T.astype(bf16)
 
 
-def attend(info, qT, k, vT, kaug, qaugT):
-    win = k.shape[0]
-    nq = qT.shape[1]
-    group = lambda p, *_: p // 2
+def attend(m, info, qT, k, vT, kaug, qaugT):
+    win = k.shape[1]
+    nq = qT.shape[2]
     return pl.pallas_call(
         attend_kernel,
         out_shape=(jax.ShapeDtypeStruct((384, nq), f32), jax.ShapeDtypeStruct((nq, 384), bf16), jax.ShapeDtypeStruct((PAIRS, 8, nq), f32)),
         grid_spec=pltpu.PrefetchScalarGridSpec(
             num_scalar_prefetch=1, grid=(PAIRS,),
             in_specs=[
-                pl.BlockSpec((128, nq), lambda p, *_: (p // 2, 0)),
-                pl.BlockSpec((win, 128), lambda p, *_: (0, p // 2)),
-                pl.BlockSpec((128, win), lambda p, *_: (p // 2, 0)),
+                pl.BlockSpec((None, 128, nq), lambda p, *_: (m, p // 2, 0)),
+                pl.BlockSpec((None, win, 128), lambda p, *_: (m, 0, p // 2)),
+                pl.BlockSpec((None, 128, win), lambda p, *_: (m, p // 2, 0)),
                 pl.BlockSpec((win, 128), lambda p, *_: (0, 0)),
                 pl.BlockSpec((128, nq), lambda p, *_: (0, 0)),
             ],
@@ -201,16 +200,19 @@
 
 
 def attend_back(m, info, qT, q, k, kT, v, doT, do, oT, lse, kaug, qaugT):
-    win, nq = k.shape[0], qT.shape[1]
+    win, nq = k.shape[1], qT.shape[2]
     wide = pl.BlockSpec((128, nq), lambda p, *_: (p // 2, 0))
     tall = pl.BlockSpec((nq, 128), lambda p, *_: (0, p // 2))
     keys = pl.BlockSpec((win, 128), lambda p, *_: (0, p // 2))
+    wide_m = pl.BlockSpec((None, 128, nq), lambda p, *_: (m, p // 2, 0))
+    tall_m = pl.BlockSpec((None, nq, 128), lambda p, *_: (m, 0, p // 2))
+    keys_m = pl.BlockSpec((None, win, 128), lambda p, *_: (m, 0, p // 2))
     return pl.pallas_call(
         attend_back_kernel,
         out_shape=(jax.ShapeDtypeStruct((nq, 384), bf16), jax.ShapeDtypeStruct((win, 384), bf16), jax.ShapeDtypeStruct((win, 384), bf16)),
         grid_spec=pltpu.PrefetchScalarGridSpec(
             num_scalar_prefetch=1, grid=(PAIRS,),
-            in_specs=[wide, tall, keys, pl.BlockSpec((128, win), lambda p, *_: (p // 2, 0)), keys,
+            in_specs=[wide_m, tall_m, keys_m, pl.BlockSpec((None, 128, win), lambda p, *_: (m, p // 2, 0)), keys_m,
                       pl.BlockSpec((128, nq), lambda p, *_: (p // 2, m)), pl.BlockSpec((nq, 128), lambda p, *_: (m, p // 2)), wide,
                       pl.BlockSpec((1, 8, nq), lambda p, *_: (p, 0, 0)),
                       pl.BlockSpec((win, 128), lambda p, *_: (0, 0)), pl.BlockSpec((128, nq), lambda p, *_: (0, 0))],
@@ -318,13 +320,13 @@
             rows_in_order(core, own_refs[j][m], other_refs[j][m], x_ref)
 
 
-def project_kernel(m, chips, place_ref, *refs):
+def project_kernel(chips, place_ref, *refs):
     n = len(chips)
     own_refs, other_refs = refs[:n], refs[n:2 * n]
     vec_ref, w_ref = refs[2 * n:2 * n + 2]
     k_ref, v_ref, kT_ref, vT_ref = refs[-6 - 2 * (n == 3):][:4]
     x_ref, hid_ref = refs[-2:]
-    step = pl.program_id(0)
+    m, step = pl.program_id(0), pl.program_id(1)
     block = sum(jnp.where(step == i, chip, 0) for i, chip in enumerate(chips))
     needed = (block >= place_ref[1 + 2 * m]) & (block < place_ref[2 + 2 * m])
 
@@ -340,11 +342,11 @@
         hid_ref[...] = hidden
         kv = jnp.dot(hidden, w_ref[:, 384:], preferred_element_type=f32)
         low = kv.astype(bf16)
-        k_ref[...] = low[:, :384]
-        v_ref[...] = low[:, 384:]
+        k_ref[0] = low[:, :384]
+        v_ref[0] = low[:, 384:]
         turned = kv.T.astype(bf16)
-        kT_ref[...] = turned[:384]
-        vT_ref[...] = turned[384:]
+        kT_ref[0] = turned[:384]
+        vT_ref[0] = turned[384:]
 
     if n == 3:
         q_ref, qT_ref = refs[-4:-2]
@@ -352,23 +354,25 @@
         @pl.when(step == 1)
         def _():
             q = jnp.dot(hid_ref[...], w_ref[:, :384], preferred_element_type=f32)
-            q_ref[...] = q.astype(bf16)
-            qT_ref[...] = q.T.astype(bf16)
-
-
-def project(m, chips, place, own, other, vec, w, earlier=()):
+            q_ref[0] = q.astype(bf16)
+            qT_ref[0] = q.T.astype(bf16)
+
+
+def project(chips, place, own, other, vec, w, earlier=()):
     n = len(chips)
     chip = (lambda b: b + 1) if n == 3 else (lambda b: 4 * b)
-    tall, wide = pl.BlockSpec((512, 384), lambda b, *_: (chip(b), 0)), pl.BlockSpec((384, 512), lambda b, *_: (0, chip(b)))
-    shapes = [shape(2560, 384), shape(2560, 384), shape(384, 2560), shape(384, 2560)]
+    tall = pl.BlockSpec((1, 512, 384), lambda m, b, *_: (m, chip(b), 0))
+    wide = pl.BlockSpec((1, 384, 512), lambda m, b, *_: (m, 0, chip(b)))
+    shapes = [shape(2, 2560, 384), shape(2, 2560, 384), shape(2, 384, 2560), shape(2, 384, 2560)]
     specs = [tall, tall, wide, wide]
     if n == 3:
-        shapes, specs = shapes + [shape(512, 384), shape(384, 512)], specs + [full(512, 384), full(384, 512)]
+        shapes += [shape(2, 512, 384), shape(2, 384, 512)]
+        specs += [pl.BlockSpec((1, 512, 384), lambda m, *_: (m, 0, 0)), pl.BlockSpec((1, 384, 512), lambda m, *_: (m, 0, 0))]
     own, other = [own[c] for c in chips], [other[c] for c in chips]
     return call(
-        lambda *refs: project_kernel(m, chips, *refs), shapes, "project", 5 * 10**9, 28,
+        lambda *refs: project_kernel(chips, *refs), shapes, "project", 5 * 10**9, 28,
         input_output_aliases={2 * n + 3 + i: i for i in range(len(earlier))}, **scalar_first(
-            (n,), [full(2, 256, 640)] * (2 * n) + [full(16, 640), full(640, 1152)] + [pl.BlockSpec(memory_space=pl.ANY)] * len(earlier),
+            (2, n), [full(2, 256, 640)] * (2 * n) + [full(16, 640), full(640, 1152)] + [pl.BlockSpec(memory_space=pl.ANY)] * len(earlier),
             specs, [pltpu.VMEM((512, 640), f32), pltpu.VMEM((512, 640), bf16)]))(place, *own, *other, vec, w, *earlier)
 
 
@@ -377,25 +381,25 @@
     return jnp.concatenate([first[:, :256], second[:, :256], first[:, 256:] + second[:, 256:]], axis=1)
 
 
-def middle_kernel(core_ref, low_ref, theirs_ref, tok_ref, w_ref, vec_ref, mid_ref, hid_ref):
+def middle_kernel(core_ref, low0_ref, low1_ref, theirs_ref, tok_ref, tok2_ref, w_ref, vec_ref, mid_ref, hid_ref, hid2_ref):
     core = core_ref[0]
-    rows = pl.ds(pl.multiple_of(256 * core, 256), 256)
-    for m in range(2):
-        attended = heads_joined(core, low_ref[m, rows, :].astype(f32), theirs_ref[m, rows, :].astype(f32)).astype(bf16)
+    for m, low_ref in enumerate((low0_ref, low1_ref)):
+        attended = heads_joined(core, low_ref[...].astype(f32), theirs_ref[m].astype(f32)).astype(bf16)
+        branch = jnp.dot(attended, w_ref[...], preferred_element_type=f32)
+        mine = jnp.where(core == 0, branch[:256], branch[256:]) + tok_ref[m].astype(f32)
+        theirs = jnp.where(core == 0, branch[256:], branch[:256]) + tok2_ref[m].astype(f32)
         part = slice(256 * m, 256 * (m + 1))
-        middle = tok_ref[m].astype(f32) + jnp.dot(attended, w_ref[...], preferred_element_type=f32)
-        mid_ref[part, :] = middle
-        hid_ref[part, :] = (moments(middle)[0] * vec_ref[2:3, :] + vec_ref[3:4, :]).astype(bf16)
-
-
-def middle_step(core, low, theirs, tok, w, vec):
-    args = (low, theirs, tok, w, vec)
-    specs = [full(*a.shape) for a in args]
-    return call(middle_kernel, (shape(512, 640, dtype=f32), shape(512, 640)), "middle", 10**9, 16, **scalar_first(
-        (1,), specs, [full(512, 640), full(512, 640)]))(core, *args)
-
-
-def feed_kernel(h_ref, h2_ref, cot_ref, cot2_ref, up_ref, down_ref, out_ref, dh_ref, theirs_ref, g_ref, h, cot, hT, cT, out, dh):
+        mid_ref[part, :] = mine
+        hid_ref[part, :] = (moments(mine)[0] * vec_ref[2:3, :] + vec_ref[3:4, :]).astype(bf16)
+        hid2_ref[part, :] = (moments(theirs)[0] * vec_ref[2:3, :] + vec_ref[3:4, :]).astype(bf16)
+
+
+def middle_step(core, *args):
+    return call(middle_kernel, (shape(512, 640, dtype=f32), shape(512, 640), shape(512, 640)), "middle", 10**9, 20, **scalar_first(
+        (1,), [full(*a.shape) for a in args], [full(512, 640)] * 3))(core, *args)
+
+
+def feed_kernel(h_ref, h2_ref, cot_ref, cot2_ref, up_ref, down_ref, mine_ref, theirs_ref, g_ref, h, cot, hT, cT, out, dh):
     chunk = pl.program_id(0)
 
     @pl.when(chunk == 0)
@@ -433,26 +437,26 @@
 
     @pl.when(chunk == 1)
     def _():
-        out_ref[...], dh_ref[...] = out[0:512, :], dh[0:512, :]
+        mine_ref[0], mine_ref[1] = out[0:512, :].astype(bf16), dh[0:512, :].astype(bf16)
         theirs_ref[0], theirs_ref[1] = out[512:1024, :].astype(bf16), dh[512:1024, :].astype(bf16)
 
 
 def feed_forward(h, h2, cot, cot2, weights):
     return call(
         feed_kernel,
-        (shape(512, 640, dtype=f32), shape(512, 640, dtype=f32), shape(2, 512, 640), shape(16, 4, 80, 640)),
+        (shape(2, 512, 640), shape(2, 512, 640), shape(16, 4, 80, 640)),
         "feed_forward", 30 * 10**9, 52, grid=(2,),
         in_specs=[full(512, 640)] * 4 + [pl.BlockSpec((640, 1280), lambda f: (0, f)), pl.BlockSpec((320, 2560), lambda f: (f, 1))],
-        out_specs=[full(512, 640), full(512, 640), full(2, 512, 640), full(16, 4, 80, 640)],
+        out_specs=[full(2, 512, 640), full(2, 512, 640), full(16, 4, 80, 640)],
         scratch_shapes=[pltpu.VMEM((1024, 640), bf16), pltpu.VMEM((1024, 640), bf16), pltpu.VMEM((640, 1024), bf16), pltpu.VMEM((640, 1024), bf16),
                         pltpu.VMEM((1024, 640), f32), pltpu.VMEM((1024, 640), f32)],
     )(h, h2, cot, cot2, weights, weights)
 
 
-def after_kernel(mid_ref, out_ref, dh_ref, theirs_ref, cot_ref, vec_ref, block_ref, grad_ref, branch_ref, g_ref):
+def after_kernel(mid_ref, mine_ref, theirs_ref, cot_ref, vec_ref, block_ref, grad_ref, branch_ref, g_ref):
     middle = mid_ref[...]
-    block_ref[...] = (middle + out_ref[...] + theirs_ref[0].astype(f32)).astype(bf16)
-    d_hidden = dh_ref[...] + theirs_ref[1].astype(f32)
+    block_ref[...] = (middle + mine_ref[0].astype(f32) + theirs_ref[0].astype(f32)).astype(bf16)
+    d_hidden = mine_ref[1].astype(f32) + theirs_ref[1].astype(f32)
     n, r = moments(middle)
     g_ref[...] = jnp.zeros_like(g_ref)
     g_ref[0:1, :] = jnp.sum(d_hidden * n, axis=0, keepdims=True)
@@ -462,14 +466,13 @@
     branch_ref[...] = grad.astype(bf16)
 
 
-def after_feed(middle, out, dh, theirs, cot, vec):
-    args = (middle, out, dh, theirs, cot, vec)
+def after_feed(*args):
     return call(
         after_kernel, (shape(512, 640), shape(512, 640, dtype=f32), shape(512, 640), shape(8, 640, dtype=f32)), "after_feed", 10**9, 24,
-        in_specs=[pl.BlockSpec(memory_space=pltpu.VMEM)] * 6, out_specs=[pl.BlockSpec(memory_space=pltpu.VMEM)] * 4)(*args)
-
-
-def branch_kernel(core_ref, own_ref, their_ref, w_ref, low_ref, theirs_ref, do_ref, doT_ref, g_ref):
+        in_specs=[pl.BlockSpec(memory_space=pltpu.VMEM)] * 5, out_specs=[pl.BlockSpec(memory_space=pltpu.VMEM)] * 4)(*args)
+
+
+def branch_kernel(core_ref, own_ref, their_ref, w_ref, low0_ref, low1_ref, theirs_ref, do_ref, doT_ref, g_ref):
     core = core_ref[0]
     w = jnp.concatenate([w_ref[pl.ds(pl.multiple_of(256 * core, 256), 256), :], w_ref[512:640, :]], axis=0)
     g = jnp.zeros((640, 384), f32)
@@ -483,13 +486,12 @@
         do = lax.dot_general(branch, w, NT, preferred_element_type=f32)
         do_ref[rows, :] = do.astype(bf16)
         doT_ref[:, rows] = do.T.astype(bf16)
-        attended = heads_joined(core, low_ref[m].astype(f32), theirs_ref[m].astype(f32))
+        attended = heads_joined(core, (low0_ref, low1_ref)[m][...].astype(f32), theirs_ref[m].astype(f32))
         g = g + jnp.dot(attended.T.astype(bf16), kept, preferred_element_type=f32)
     g_ref[...] = g
 
 
-def branch_step(core, own, their, w, low, theirs):
-    args = (own, their, w, low, theirs)
+def branch_step(core, *args):
     specs = [full(*a.shape) for a in args]
     return call(
         branch_kernel, (shape(1024, 384), shape(384, 1024), shape(640, 384, dtype=f32)), "branch", 10**9, 24, **scalar_first(
@@ -570,46 +572,38 @@
              pltpu.VMEM((512, 640), f32), pltpu.VMEM((640, 1152), f32), pltpu.VMEM((8, 640), f32)]))(core, *own, *other, vec, w, *dq, *dk, *dv, g_out, g_two)
 
 
-def in_core_order(core_ref, mine, theirs):
-    core, mine, theirs = core_ref[0], mine.astype(f32), theirs.astype(f32)
-    return jnp.where(core == 0, mine, theirs), jnp.where(core == 0, theirs, mine)
-
-
-def final_feed_kernel(core_ref, mine_ref, theirs_ref, up_ref, down_ref):
+def final_kernel(core_ref, mine_ref, theirs_ref, up_ref, down_ref, qkv_ref, out_ref, vec_ref):
+    core = core_ref[0]
+    lane = lax.broadcasted_iota(jnp.int32, (40, 128), 1)
     for i in range(16):
-        for c, piece in enumerate(in_core_order(core_ref, mine_ref[i], theirs_ref[i])):
+        mine, theirs = mine_ref[i].astype(f32), theirs_ref[i].astype(f32)
+        pair = [jnp.where(core == 0, mine, theirs), jnp.where(core == 0, theirs, mine)]
+        for c in range(2):
+            piece = jnp.concatenate([pair[c][80 * t:80 * (t + 1)] for t in range(5)], axis=1)
             if i < 8:
                 base = 1280 * (i // 2) + 640 * c
                 up_ref[80 * (i % 2):80 * (i % 2 + 1), base:base + 640] = piece
             else:
                 base = 640 * c + 80 * (i - 8)
                 down_ref[base:base + 80, :] = piece
-
-
-def final_feed(core, mine, theirs):
-    return call(final_feed_kernel, (shape(160, 5120, dtype=f32), shape(1280, 640, dtype=f32)), "final_feed", 10**6, 32, **scalar_first(
-        (1,), [full(16, 80, 640)] * 2, [full(160, 5120), full(1280, 640)]))(core, mine, theirs)
-
-
-def final_heads_kernel(core_ref, mine_ref, theirs_ref, qkv_ref, out_ref, vec_ref):
-    lane = lax.broadcasted_iota(jnp.int32, (40, 128), 1)
-    for z in range(4):
-        rows = slice(40 * z, 40 * (z + 1))
-        for x in range(4):
-            a, b = in_core_order(core_ref, mine_ref[4 * z + x], theirs_ref[4 * z + x])
-            if x < 3:
-                last = jnp.where(lane < 64, a[:, 256:], b[:, 256:])
-                qkv_ref[rows, 640 * x:640 * (x + 1)] = jnp.concatenate([a[:, :256], b[:, :256], last], axis=1)
-            else:
-                out_ref[rows, :] = jnp.concatenate([a, b[:, 128:]], axis=1)
-            if x == 0:
-                vec_ref[rows, :] = pltpu.roll(a[:, 256:], 64, 1) + b[:, 256:]
-
-
-def final_heads(core, mine, theirs):
+        a, b = ([pair[c][400 + 40 * t:440 + 40 * t] for t in range(3)] for c in range(2))
+        rows, x = slice(40 * (i // 4), 40 * (i // 4 + 1)), i % 4
+        if x < 3:
+            last = jnp.where(lane < 64, a[2], b[2])
+            qkv_ref[rows, 640 * x:640 * (x + 1)] = jnp.concatenate([a[0], a[1], b[0], b[1], last], axis=1)
+        else:
+            out_ref[rows, :] = jnp.concatenate([a[0], a[1], a[2], b[1], b[2]], axis=1)
+        if x == 0:
+            vec_ref[rows, :] = pltpu.roll(a[2], 64, 1) + b[2]
+
+
+def final_step(core, mine, theirs):
     return call(
-        final_heads_kernel, (shape(160, 1920, dtype=f32), shape(160, 640, dtype=f32), shape(160, 128, dtype=f32)), "final_heads", 10**6, 16,
-        **scalar_first((1,), [full(16, 40, 384)] * 2, [full(160, 1920), full(160, 640), full(160, 128)]))(core, mine, theirs)
+        final_kernel,
+        (shape(160, 5120, dtype=f32), shape(1280, 640, dtype=f32), shape(160, 1920, dtype=f32), shape(160, 640, dtype=f32),
+         shape(160, 128, dtype=f32)), "final", 10**6, 32, **scalar_first(
+            (1,), [full(16, 520, 128)] * 2, [full(160, 5120), full(1280, 640), full(160, 1920), full(160, 640), full(160, 128)]))(
+                core, mine, theirs)
 
 
 def shifted(array, axis, by):
@@ -684,63 +678,64 @@
     return jnp.stack(info + sizes).astype(jnp.int32), key_rows, query_rows, [low, high]
 
 
+def lane_tiles_down(array):
+    return jnp.concatenate([array[:, 128 * t:128 * (t + 1)] for t in range(array.shape[1] // 128)], axis=0)
+
+
 def body(tokens, lengths, gain_one, bias_one, w_qkv, w_out, gain_two, bias_two, w_up, w_down, cotangent):
     core, chip = lax.axis_index("core"), lax.axis_index(("z", "x"))
     core_arg, y_arg = core[None].astype(jnp.int32), lax.axis_index("batch")[None].astype(jnp.int32)
     tok, cot = tokens[:, 0], cotangent[:, 0].reshape(512, 640)
 
-    before, after = passed_along(tok, 1), passed_along(tok, -1)
+    together = lambda *arrays: lax.optimization_barrier(arrays)
+    before, after, tok_other = passed_along(tok, 1), passed_along(tok, -1), swapped(tok)
     vectors = jnp.pad(jnp.stack([gain_one, bias_one, gain_two, bias_two]), ((0, 12), (0, 0)))
     heads = pack_heads(core_arg, w_qkv, vectors)
     heads_before, heads_after = shifted(heads, "batch", 1), shifted(heads, "batch", -1)
+    heads, w_out, w_up, w_down = together(heads, w_out, w_up, w_down)
     feed_weights = lax.all_gather(pack_feed(core_arg, w_out, w_up, w_down), "batch", axis=0, tiled=True)
     w_out_all = feed_weights[:, 5120:]
+    before, after, heads_before, heads_after = together(before, after, heads_before, heads_after)
     own = (passed_along(before, 1), before, tok, after, passed_along(after, -1))
     near, far = shifted(heads_before[:96], "batch", 1), shifted(heads_after[96:], "batch", -1)
-    other = tuple(swapped(a) for a in own)
+    other = (swapped(own[0]), swapped(before), tok_other, swapped(after), swapped(own[4]))
     w_heads, vec = assemble(y_arg, heads, heads_before, heads_after, near, far)
 
     windows = [window_info(lengths[m, 0], chip, core, 2560) for m in range(2)]
     place = jnp.stack([core] + windows[0][3] + windows[1][3]).astype(jnp.int32)
-    forward = []
-    near_parts = [project(m, (1, 2, 3), place, own, other, vec, w_heads) for m in range(2)]
-    for m in range(2):
-        k, v, kT, vT = project(m, (0, 4), place, own, other, vec, w_heads, near_parts[m][:4])
-        q, qT = near_parts[m][4:]
-        info, key_rows, query_rows, _ = windows[m]
-        oT, low, lse = attend(info, qT, k, vT, key_rows, query_rows)
-        forward.append((info, qT, q, k, kT, v, oT, lse, key_rows, query_rows, low))
-
-    low = jnp.stack([f[-1] for f in forward])
-    theirs = swapped(low)
-    middle, hidden_two = middle_step(core_arg, low, theirs, tok, w_out_all, vec)
-    out, d_hidden, partial, feed_grads = feed_forward(hidden_two, swapped(hidden_two), cot, swapped(cot), feed_weights)
+    *near_parts, q, qT = project((1, 2, 3), place, own, other, vec, w_heads)
+    k, v, kT, vT = project((0, 4), place, own, other, vec, w_heads, near_parts)
+    (oT0, low0, lse0), (oT1, low1, lse1) = (
+        attend(m, info, qT, k, vT, key_rows, query_rows) for m, (info, key_rows, query_rows, _) in enumerate(windows))
+
+    theirs = swapped(jnp.stack([low0, low1]))
+    middle, hidden_two, hidden_other = middle_step(core_arg, low0, low1, theirs, tok, tok_other, w_out_all, vec)
+    mine, partial, feed_grads = feed_forward(hidden_two, hidden_other, cot, swapped(cot), feed_weights)
     feed_grads = lax.psum_scatter(feed_grads.reshape(5120, 640), ("z", "x"), scatter_dimension=0, tiled=True).reshape(4, 80, 640)
-    block_out, grad_middle, branch, g_two = after_feed(middle, out, d_hidden, swapped(partial), cot, vec)
-
-    do, doT, g_out = branch_step(core_arg, branch, swapped(branch), w_out_all, low, theirs)
-    grads = []
-    for m in range(2):
-        info, qT, q, k, kT, v, oT, lse, key_rows, query_rows, _ = forward[m]
-        grads.append(attend_back(m, info, qT, q, k, kT, v, doT, do, oT, lse, key_rows, query_rows))
-    dq, dk, dv = zip(*grads)
+    block_out, grad_middle, branch, g_two = after_feed(middle, mine, swapped(partial), cot, vec)
+
+    do, doT, g_out = branch_step(core_arg, branch, swapped(branch), w_out_all, low0, low1, theirs)
+    dq, dk, dv = zip(*(
+        attend_back(m, info, qT, q, k, kT, v, doT, do, oT, lse, key_rows, query_rows)
+        for m, ((info, key_rows, query_rows, _), oT, lse) in enumerate(zip(windows, (oT0, oT1), (lse0, lse1)))))
     mine, theirs, tail = project_back(place, own, other, vec, w_heads, dq, dk, dv, g_out, g_two)
+
     tail = lax.all_to_all(tail, ("batch", "z", "x"), 0, 0, tiled=True)
-
+    tail = jnp.sum(tail.astype(f32), axis=0).astype(bf16)
+    feed = summed_share(feed_grads, "batch")
     theirs = swapped(theirs)
     sums = [mine[j].astype(f32) + theirs[j].astype(f32) for j in range(5)]
-    right = passed_along(sums[4].astype(bf16), 1).astype(f32) + sums[3]
-    left = passed_along(sums[0].astype(bf16), -1).astype(f32) + sums[1]
-    d_one = sums[2] + passed_along(right.astype(bf16), 1).astype(f32) + passed_along(left.astype(bf16), -1).astype(f32)
+    shares = jnp.concatenate([lane_tiles_down(feed), lane_tiles_down(tail)], axis=0)
+    shares, right, left = together(shares, sums[4].astype(bf16), sums[0].astype(bf16))
+    shares = gathered(shares, "x").reshape(2080, 128)
+    right = (passed_along(right, 1).astype(f32) + sums[3]).astype(bf16)
+    left = (passed_along(left, -1).astype(f32) + sums[1]).astype(bf16)
+    shares, right, left = together(shares, right, left)
+    d_one = sums[2] + passed_along(right, 1).astype(f32) + passed_along(left, -1).astype(f32)
     n_one, r_one = moments(tok.reshape(512, 640).astype(f32))
     grad_tokens = (grad_middle + norm_back(d_one.reshape(512, 640), n_one, r_one, vec[0:1])).astype(bf16)
-
-    feed = lax.all_gather(summed_share(feed_grads, "batch"), ("z", "x"), axis=0, tiled=True).reshape(16, 80, 640)
-    grad_up, grad_down = final_feed(core_arg, feed, swapped(feed))
-    tail, grad_tokens = lax.optimization_barrier((tail, grad_tokens))
-    tail = jnp.sum(tail.astype(f32), axis=0).astype(bf16)
-    tail = gathered(gathered(tail, "x").reshape(160, 384), "z").reshape(16, 40, 384)
-    grad_qkv, grad_out, spare = final_heads(core_arg, tail, swapped(tail))
+    shares = gathered_ring(shares, "z").reshape(16, 520, 128)
+    grad_up, grad_down, grad_qkv, grad_out, spare = final_step(core_arg, shares, swapped(shares))
     return (
         block_out.reshape(2, 1, 256, 640), grad_tokens.reshape(2, 1, 256, 640), spare[:, 0], spare[:, 1], grad_qkv, grad_out,
         spare[:, 2], spare[:, 3], grad_up, grad_down)

time: 394 us -> 428 us (1.086)
  waiting for transfers between devices: 86.9 us -> 103 us
  local copies, waits for them, and re-layouts: 25.8 us -> 39.2 us
  starting transfers between devices: 104 us -> 109 us
    all_to_all x1, waiting for transfers between devices: 0.01 us -> 27.7 us  [body(): tail = lax.all_to_all(tail, ('batch', 'z', 'x'), 0, 0, tiled=True)]
    all_to_all x1, starting transfers between devices: 26.7 us -> 50.9 us  [body(): tail = lax.all_to_all(tail, ('batch', 'z', 'x'), 0, 0, tiled=True)]
    all_gather x1 -> x0, waiting for transfers between devices: 15.3 us -> none  [body(): lax.all_gather(summed_share(feed_grads, 'batch'), ('z', 'x'), axis=0, til...]
    ppermute x8, starting transfers between devices: 34.9 us -> 23.2 us  [passed_along(): lax.ppermute(array, ('z', 'x'), [(i, i + by) for i in range(devices) if 0...]
    unnamed x140 -> x99, local copies, waits for them, and re-layouts: 21.2 us -> 32.1 us
    ppermute x13 -> x14, starting transfers between devices: 26.3 us -> 16.6 us  [shifted(): lax.ppermute(array, axis, [(i, (i + by) % devices) for i in range(devices)])]
    ppermute x13 -> x11, waiting for transfers between devices: 15.3 us -> 6.9 us  [swapped(): return lax.ppermute(array, 'core', [(0, 1), (1, 0)])]
    ppermute x13 -> x14, waiting for transfers between devices: 16.9 us -> 24.5 us  [shifted(): lax.ppermute(array, axis, [(i, (i + by) % devices) for i in range(devices)])]
  transfers between devices with their start and end apart: 38 -> 36, of which waited for: 17 -> 17; matrix products, arithmetic and copies ran while one was open for 6% -> 3% of each run, Pallas kernels for 25% -> 23%
where the time goes in v1:
time: 428 us; the launch traced here: 419 us
  Pallas kernels  134 us (31%)
  starting transfers between devices  109 us (25%)
  waiting for transfers between devices  103 us (24%)
  local copies, waits for them, and re-layouts  39.2 us (9%)
  between operations  20.7 us (5%)
  other arithmetic  13.9 us (3%)
    all_to_all x1, starting transfers between devices, body(): tail = lax.all_to_all(tail, ('batch', 'z', 'x'), 0, 0, tiled=True)  50.9 us
    ppermute x8, waiting for transfers between devices, passed_along(): lax.ppermute(array, ('z', 'x'), [(i, i + by) for i in range(devices) if 0...  43.8 us
    pallas_call x2, Pallas kernels, attend_back(): pl.pallas_call(attend_back_kernel, out_shape=(jax.ShapeDtypeStruct((nq, 3...  32.3 us
    unnamed x99, local copies, waits for them, and re-layouts  32.1 us
    pallas_call x1, Pallas kernels, feed_forward(): call(feed_kernel, (shape(2, 512, 640), shape(2, 512, 640), shape(16, 4, 8...  31.9 us
    all_to_all x1, waiting for transfers between devices, body(): tail = lax.all_to_all(tail, ('batch', 'z', 'x'), 0, 0, tiled=True)  27.7 us
    ppermute x14, waiting for transfers between devices, shifted(): lax.ppermute(array, axis, [(i, (i + by) % devices) for i in range(devices)])  24.5 us
    ppermute x8, starting transfers between devices, passed_along(): lax.ppermute(array, ('z', 'x'), [(i, i + by) for i in range(devices) if 0...  23.2 us
  transfers between devices with their start and end apart: 36, of which 17 were waited for; matrix products, arithmetic and copies ran while one was open for 3% of the time, Pallas kernels for 23%

profile of v1, /device:TPU:1, one launch (start us, length us, event | category | flops | bytes accessed | tf_op | source)
XLA Modules:
  0.0 419.3 jit_solution(6154709471811838140)
XLA Ops:
  17.3 4.8 %collective-permute-start = (bf16[2,256,640]{2,1,0:T(8,128)(2,1)S(1)}, bf16[2,256,640]{2,1,0:T(8,128)(2,1)}, u32[]{:S(2)}, u32[]{:S(2)}) collective-permute-start(bf16[2,256,640]{2,1,0:T(8,128)(2,1)S(1)} %bitcast.115), channel_id=1, source_target_pairs={{0,2},{2,4},{4,6},{6,8},{8,10},{10,12},{12,14},{14,16},{16,18},{18... | collective-permute-start | bytes 1966088 | tf_op jit(solution)/shard_map/ppermute | solution.py:616
  29.1 5.6 %collective-permute-done.2.before_ref = bf16[176,1152]{1,0:T(8,128)(2,1)S(1)} collective-permute-done((bf16[176,1152]{1,0:T(8,128)(2,1)S(1)}, bf16[176,1152]{1,0:T(8,128)(2,1)S(1)}, u32[]{:S(2)}, u32[]{:S(2)}) %collective-permute-start.2) | collective-permute-done | bytes 405536 | tf_op jit(solution)/shard_map/ppermute | solution.py:611
  34.9 4.4 %collective-permute-done.1.refs_3_ = bf16[2,256,640]{2,1,0:T(8,128)(2,1)} collective-permute-done((bf16[2,256,640]{2,1,0:T(8,128)(2,1)S(1)}, bf16[2,256,640]{2,1,0:T(8,128)(2,1)}, u32[]{:S(2)}, u32[]{:S(2)}) %collective-permute-start.1) | collective-permute-done | bytes 655392 | tf_op jit(solution)/shard_map/ppermute | solution.py:616
  45.9 5.2 %collective-permute-start.9 = (bf16[2,256,640]{2,1,0:T(8,128)(2,1)}, bf16[2,256,640]{2,1,0:T(8,128)(2,1)}, u32[]{:S(2)}, u32[]{:S(2)}) collective-permute-start(bf16[2,256,640]{2,1,0:T(8,128)(2,1)} %collective-permute-done.refs_1_), channel_id=1, source_target_pairs={{0,2},{2,4},{4,6},{6,8},{8,10},{10,12},{12,14},{14,16},{16,18},{18... | collective-permute-start | bytes 1966088 | tf_op jit(solution)/shard_map/ppermute | solution.py:616
  56.0 8.8 %collective-permute-done.9.refs_1_.refs_0_ = bf16[2,256,640]{2,1,0:T(8,128)(2,1)} collective-permute-done((bf16[2,256,640]{2,1,0:T(8,128)(2,1)}, bf16[2,256,640]{2,1,0:T(8,128)(2,1)}, u32[]{:S(2)}, u32[]{:S(2)}) %collective-permute-start.9) | collective-permute-done | bytes 655392 | tf_op jit(solution)/shard_map/ppermute | solution.py:616
  65.5 5.1 %collective-permute-done.10.refs_2_.refs_4_ = bf16[2,256,640]{2,1,0:T(8,128)(2,1)} collective-permute-done((bf16[2,256,640]{2,1,0:T(8,128)(2,1)}, bf16[2,256,640]{2,1,0:T(8,128)(2,1)}, u32[]{:S(2)}, u32[]{:S(2)}) %collective-permute-start.10) | collective-permute-done | bytes 655392 | tf_op jit(solution)/shard_map/ppermute | solution.py:616
  79.2 10.0 %project.2 = (bf16[2,2560,384]{2,1,0:T(8,128)(2,1)S(1)}, bf16[2,2560,384]{2,1,0:T(8,128)(2,1)S(1)}, bf16[2,384,2560]{2,1,0:T(8,128)(2,1)S(1)}, bf16[2,384,2560]{...) custom-call(s32[5]{0:T(128)S(1)} %stack.81.refs_0_.core_ref, ...), custom_call_target="tpu_custom_call" | custom-call | flops 5000000000 | bytes 8388608 | tf_op jit(solution)/shard_map/project/pallas_call | solution.py:372
  89.3 4.4 %project.3 = (bf16[2,2560,384]{2,1,0:T(8,128)(2,1)S(1)}, bf16[2,2560,384]{2,1,0:T(8,128)(2,1)S(1)}, bf16[2,384,2560]{2,1,0:T(8,128)(2,1)S(1)}, bf16[2,384,2560]{2,1,0:T(8,128)(2,1)S(1)}) custom-call(s32[5]{0:T(128)S(1)} %stack.81.refs_0_.core_ref, ...), custom_call_target="tpu_custom_call", output_to_operand_aliasing={{0}: (7, {}), {1}: (8, {}), {2}: (9, {}), {3}: (10, {})} | custom-call | flops 5000000000 | bytes 8388608 | tf_op jit(solution)/shard_map/project/pallas_call | solution.py:372
  97.5 10.6 %attend.2 = (f32[384,512]{1,0:T(8,128)S(1)}, bf16[512,384]{1,0:T(8,128)(2,1)S(1)}, f32[5,8,512]{2,1,0:T(8,128)S(1)}) custom-call(s32[5]{0:T(128)S(1)} %stack.76.info_ref, bf16[2,384,512]{2,1,0:T(8,128)(2,1)S(1)} %get-tuple-element.76.qT_ref, bf16[2,2560,384]{2,1,0:T(8,128)(2,1)S(1)} %get-tuple-element.81.k_ref, ...), custom_call_target="tpu_custom_call" | custom-call | flops 20000000000 | bytes 6291456 | tf_op jit(solution)/shard_map/attend/pallas_call | solution.py:98
  108.2 10.4 %attend.3 = (f32[384,512]{1,0:T(8,128)S(1)}, bf16[512,384]{1,0:T(8,128)(2,1)S(1)}, f32[5,8,512]{2,1,0:T(8,128)S(1)}) custom-call(s32[5]{0:T(128)S(1)} %stack.91.info_ref, bf16[2,384,512]{2,1,0:T(8,128)(2,1)S(1)} %get-tuple-element.76.qT_ref, bf16[2,2560,384]{2,1,0:T(8,128)(2,1)S(1)} %get-tuple-element.81.k_ref, ...), custom_call_target="tpu_custom_call" | custom-call | flops 20000000000 | bytes 6291456 | tf_op jit(solution)/shard_map/attend/pallas_call | solution.py:98
  127.3 31.9 %feed_forward.1 = (bf16[2,512,640]{2,1,0:T(8,128)(2,1)}, bf16[2,512,640]{2,1,0:T(8,128)(2,1)}, bf16[16,4,80,640]{3,2,1,0:T(8,128)(2,1)}) custom-call(bf16[512,640]{1,0:T(8,128)(2,1)S(1)} %get-tuple-element.89.h_ref, bf16[512,640]{1,0:T(8,128)(2,1)S(1)} %get-tuple-element.90.h2_ref, bf16[512,640]{1,0:T(8,128)(2,1)} %bitcast.21.cot_ref, ...), custom_call_target="tpu_custom_call" | custom-call | flops 30000001024 | bytes 8388608 | tf_op jit(solution)/shard_map/feed_forward/pallas_call | solution.py:445
  181.2 15.8 %attend_back.2 = (bf16[512,384]{1,0:T(8,128)(2,1)S(1)}, bf16[2560,384]{1,0:T(8,128)(2,1)S(1)}, bf16[2560,384]{1,0:T(8,128)(2,1)S(1)}) custom-call(s32[5]{0:T(128)S(1)} %stack.76.info_ref, bf16[2,384,512]{2,1,0:T(8,128)(2,1)S(1)} %copy-done.36, bf16[2,512,384]{2,1,0:T(8,128)(2,1)S(1)} %copy-done.34, bf16[2,2560,384]{2,1,0:T(8,128)(2,1)S(1)} %copy-done.2, ...), custom_call_target="tpu_custom_call" | custom-call | flops 40000000000 | bytes 12582912 | tf_op jit(solution)/shard_map/attend_back/pallas_call | solution.py:210
  199.5 16.6 %attend_back.3 = (bf16[512,384]{1,0:T(8,128)(2,1)S(1)}, bf16[2560,384]{1,0:T(8,128)(2,1)S(1)}, bf16[2560,384]{1,0:T(8,128)(2,1)S(1)}) custom-call(s32[5]{0:T(128)S(1)} %stack.91.info_ref, bf16[2,384,512]{2,1,0:T(8,128)(2,1)S(1)} %copy-done.37, bf16[2,512,384]{2,1,0:T(8,128)(2,1)S(1)} %copy-done.34, bf16[2,2560,384]{2,1,0:T(8,128)(2,1)S(1)} %copy-done.2, ...), custom_call_target="tpu_custom_call" | custom-call | flops 40000000000 | bytes 12582912 | tf_op jit(solution)/shard_map/attend_back/pallas_call | solution.py:210
  223.5 20.8 %project_back.1 = (bf16[5,2,256,640]{3,2,1,0:T(8,128)(2,1)}, bf16[5,2,256,640]{3,2,1,0:T(8,128)(2,1)}, bf16[64,40,384]{2,1,0:T(8,128)(2,1)}) custom-call(s32[5]{0:T(128)S(1)} %copy-done.23, bf16[2,256,640]{2,1,0:T(8,128)(2,1)} %collective-permute-done.9.refs_1_.refs_0_, bf16[2,256,640]{2,1,0:T(8,128)(2,1)} %collective-permute-done.refs_1_, ...), custom_call_target="tpu_custom_call" | custom-call | flops 10000000000 | bytes 8388608 | tf_op jit(solution)/shard_map/project_back/pallas_call | solution.py:566
  244.7 50.9 %all-to-all-start = ((bf16[64,40,384]{2,1,0:T(8,128)(2,1)}), bf16[64,40,384]{2,1,0:T(8,128)(2,1)S(1)}, u32[]{:S(2)}, u32[]{:S(2)}) async-start(bf16[64,40,384]{2,1,0:T(8,128)(2,1)} %get-tuple-element.116), calls=%async_computation.1 | async-start | bytes 3932160 | tf_op jit(solution)/shard_map/all_to_all | solution.py:723
  295.8 27.7 %all-to-all-done = bf16[64,40,384]{2,1,0:T(8,128)(2,1)S(1)} async-done(((bf16[64,40,384]{2,1,0:T(8,128)(2,1)}), bf16[64,40,384]{2,1,0:T(8,128)(2,1)S(1)}, u32[]{:S(2)}, u32[]{:S(2)}) %all-to-all-start) | async-done | bytes 1966112 | tf_op jit(solution)/shard_map/all_to_all | solution.py:723
  338.4 4.0 collective-permute-start.24
  342.7 12.1 %collective-permute-done.25 = bf16[2,256,640]{2,1,0:T(8,128)(2,1)S(1)} collective-permute-done((bf16[2,256,640]{2,1,0:T(8,128)(2,1)S(1)}, bf16[2,256,640]{2,1,0:T(8,128)(2,1)S(1)}, u32[]{:S(2)}, u32[]{:S(2)}) %collective-permute-start.25) | collective-permute-done | bytes 655392 | tf_op jit(solution)/shard_map/ppermute | solution.py:616
  360.4 8.7 %collective-permute-done.29 = bf16[2080,128]{1,0:T(8,128)(2,1)S(1)} collective-permute-done((bf16[2080,128]{1,0:T(8,128)(2,1)S(1)}, bf16[2080,128]{1,0:T(8,128)(2,1)S(1)}, u32[]{:S(2)}, u32[]{:S(2)}) %collective-permute-start.29) | collective-permute-done | bytes 532512 | tf_op jit(solution)/shard_map/ppermute | solution.py:611
  371.3 5.5 %collective-permute-done.31 = bf16[1040,128]{1,0:T(8,128)(2,1)S(1)} collective-permute-done((bf16[1040,128]{1,0:T(8,128)(2,1)S(1)}, bf16[1040,128]{1,0:T(8,128)(2,1)S(1)}, u32[]{:S(2)}, u32[]{:S(2)}) %collective-permute-start.31) | collective-permute-done | bytes 266272 | tf_op jit(solution)/shard_map/ppermute | solution.py:611
  377.6 7.4 %collective-permute-start.32 = (bf16[16,520,128]{2,1,0:T(8,128)(2,1)S(1)}, bf16[16,520,128]{2,1,0:T(8,128)(2,1)S(1)}, u32[]{:S(2)}, u32[]{:S(2)}) collective-permute-start(bf16[16,520,128]{2,1,0:T(8,128)(2,1)S(1)} %bitcast.121), channel_id=1, source_target_pairs={{0,1},{1,0},{2,3},{3,2},{4,5},{5,4},{6,7},{7,6},{8,9},{9,8},{10,11... | collective-permute-start | bytes 6389768 | tf_op jit(solution)/shard_map/ppermute | solution.py:620
  386.5 4.0 collective-permute-start.26
  390.9 12.5 %collective-permute-done.27 = bf16[2,256,640]{2,1,0:T(8,128)(2,1)S(1)} collective-permute-done((bf16[2,256,640]{2,1,0:T(8,128)(2,1)S(1)}, bf16[2,256,640]{2,1,0:T(8,128)(2,1)S(1)}, u32[]{:S(2)}, u32[]{:S(2)}) %collective-permute-start.27) | collective-permute-done | bytes 655392 | tf_op jit(solution)/shard_map/ppermute | solution.py:616
  407.6 3.6 final.1
  (220 shorter events, 107.7 us)
Async XLA Ops:
  7.2 113.1 %all-gather.2.cloned.1.call-start = ((), (), s32[]{:S(2)}) async-start(), calls=%async_computation.2 | async-start | bytes 9216000 | tf_op jit(solution)/shard_map/all_gather | solution.py:696
  16.2 307.5 %reduce-scatter.2.cloned.1.call-start = ((), (), s32[]{:S(2)}) async-start(), calls=%async_computation.3 | async-start | bytes 6963200 | tf_op jit(solution)/shard_map/reduce_scatter | solution.py:714
  17.3 17.7 %collective-permute-start = (bf16[2,256,640]{2,1,0:T(8,128)(2,1)S(1)}, bf16[2,256,640]{2,1,0:T(8,128)(2,1)}, u32[]{:S(2)}, u32[]{:S(2)}) collective-permute-start(bf16[2,256,640]{2,1,0:T(8,128)(2,1)S(1)} %bitcast.115), channel_id=1, source_target_pairs={{0,2},{2,4},{4,6},{6,8},{8,10},{10,12},{12,14},{14,16},{16,18},{18... | collective-permute-start | bytes 1966088 | tf_op jit(solution)/shard_map/ppermute | solution.py:616
  22.1 17.3 %collective-permute-start.1 = (bf16[2,256,640]{2,1,0:T(8,128)(2,1)S(1)}, bf16[2,256,640]{2,1,0:T(8,128)(2,1)}, u32[]{:S(2)}, u32[]{:S(2)}) collective-permute-start(bf16[2,256,640]{2,1,0:T(8,128)(2,1)S(1)} %bitcast.116), channel_id=1, source_target_pairs={{2,0},{4,2},{6,4},{8,6},{10,8},{12,10},{14,12},{16,14},{18,16},{20... | collective-permute-start | bytes 1966088 | tf_op jit(solution)/shard_map/ppermute | solution.py:616
  23.3 11.3 %collective-permute-start.2 = (bf16[176,1152]{1,0:T(8,128)(2,1)S(1)}, bf16[176,1152]{1,0:T(8,128)(2,1)S(1)}, u32[]{:S(2)}, u32[]{:S(2)}) collective-permute-start(bf16[176,1152]{1,0:T(8,128)(2,1)S(1)} %pack_heads.1.own_ref), channel_id=1, source_target_pairs={{0,32},{32,64},{64,96},{96,0},{1,33},{33,65},{65,97},{97,1},{2,34}... | collective-permute-start | bytes 1216520 | tf_op jit(solution)/shard_map/ppermute | solution.py:611
  24.7 10.2 %collective-permute-start.3 = (bf16[176,1152]{1,0:T(8,128)(2,1)S(1)}, bf16[176,1152]{1,0:T(8,128)(2,1)S(1)}, u32[]{:S(2)}, u32[]{:S(2)}) collective-permute-start(bf16[176,1152]{1,0:T(8,128)(2,1)S(1)} %pack_heads.1.own_ref), channel_id=1, source_target_pairs={{0,96},{32,0},{64,32},{96,64},{1,97},{33,1},{65,33},{97,65},{2,98}... | collective-permute-start | bytes 1216520 | tf_op jit(solution)/shard_map/ppermute | solution.py:611
  26.2 52.9 %collective-permute-start.5 = (bf16[2,256,640]{2,1,0:T(8,128)(2,1)S(1)}, bf16[2,256,640]{2,1,0:T(8,128)(2,1)}, u32[]{:S(2)}, u32[]{:S(2)}) collective-permute-start(bf16[2,256,640]{2,1,0:T(8,128)(2,1)S(1)} %bitcast.117), channel_id=1, source_target_pairs={{0,1},{1,0},{2,3},{3,2},{4,5},{5,4},{6,7},{7,6},{8,9},{9,8},{10,11... | collective-permute-start | bytes 1966088 | tf_op jit(solution)/shard_map/ppermute | solution.py:620
  39.4 14.2 %collective-permute-start.7 = (bf16[96,1152]{1,0:T(8,128)(2,1)S(1)}, bf16[96,1152]{1,0:T(8,128)(2,1)S(1)}, u32[]{:S(2)}, u32[]{:S(2)}) collective-permute-start(bf16[96,1152]{1,0:T(8,128)(2,1)S(1)} %slice.92), channel_id=1, source_target_pairs={{0,32},{32,64},{64,96},{96,0},{1,33},{33,65},{65,97},{97,1},{2,34}... | collective-permute-start | bytes 663560 | tf_op jit(solution)/shard_map/ppermute | solution.py:611
  40.7 10.4 %collective-permute-start.8 = (bf16[80,1152]{1,0:T(8,128)(2,1)S(1)}, bf16[80,1152]{1,0:T(8,128)(2,1)S(1)}, u32[]{:S(2)}, u32[]{:S(2)}) collective-permute-start(bf16[80,1152]{1,0:T(8,128)(2,1)S(1)} %slice.93), channel_id=1, source_target_pairs={{0,96},{32,0},{64,32},{96,64},{1,97},{33,1},{65,33},{97,65},{2,98}... | collective-permute-start | bytes 552968 | tf_op jit(solution)/shard_map/ppermute | solution.py:611
  43.5 35.6 %collective-permute-start.4 = (bf16[2,256,640]{2,1,0:T(8,128)(2,1)}, bf16[2,256,640]{2,1,0:T(8,128)(2,1)}, u32[]{:S(2)}, u32[]{:S(2)}) collective-permute-start(bf16[2,256,640]{2,1,0:T(8,128)(2,1)} %collective-permute-done.refs_1_), channel_id=1, source_target_pairs={{0,1},{1,0},{2,3},{3,2},{4,5},{5,4},{6,7},{7,6},{8,9},{9,8},{10,11... | collective-permute-start | bytes 1966088 | tf_op jit(solution)/shard_map/ppermute | solution.py:620
  45.9 18.8 %collective-permute-start.9 = (bf16[2,256,640]{2,1,0:T(8,128)(2,1)}, bf16[2,256,640]{2,1,0:T(8,128)(2,1)}, u32[]{:S(2)}, u32[]{:S(2)}) collective-permute-start(bf16[2,256,640]{2,1,0:T(8,128)(2,1)} %collective-permute-done.refs_1_), channel_id=1, source_target_pairs={{0,2},{2,4},{4,6},{6,8},{8,10},{10,12},{12,14},{14,16},{16,18},{18... | collective-permute-start | bytes 1966088 | tf_op jit(solution)/shard_map/ppermute | solution.py:616
  51.1 28.0 %collective-permute-start.6 = (bf16[2,256,640]{2,1,0:T(8,128)(2,1)}, bf16[2,256,640]{2,1,0:T(8,128)(2,1)}, u32[]{:S(2)}, u32[]{:S(2)}) collective-permute-start(bf16[2,256,640]{2,1,0:T(8,128)(2,1)} %collective-permute-done.1.refs_3_), channel_id=1, source_target_pairs={{0,1},{1,0},{2,3},{3,2},{4,5},{5,4},{6,7},{7,6},{8,9},{9,8},{10,11... | collective-permute-start | bytes 1966088 | tf_op jit(solution)/shard_map/ppermute | solution.py:620
  53.5 17.1 %collective-permute-start.10 = (bf16[2,256,640]{2,1,0:T(8,128)(2,1)}, bf16[2,256,640]{2,1,0:T(8,128)(2,1)}, u32[]{:S(2)}, u32[]{:S(2)}) collective-permute-start(bf16[2,256,640]{2,1,0:T(8,128)(2,1)} %collective-permute-done.1.refs_3_), channel_id=1, source_target_pairs={{2,0},{4,2},{6,4},{8,6},{10,8},{12,10},{14,12},{16,14},{18,16},{20... | collective-permute-start | bytes 1966088 | tf_op jit(solution)/shard_map/ppermute | solution.py:616
  64.7 24.5 %collective-permute-start.11 = (bf16[2,256,640]{2,1,0:T(8,128)(2,1)}, bf16[2,256,640]{2,1,0:T(8,128)(2,1)}, u32[]{:S(2)}, u32[]{:S(2)}) collective-permute-start(bf16[2,256,640]{2,1,0:T(8,128)(2,1)} %collective-permute-done.9.refs_1_.refs_0_), channel_id=1, source_target_pairs={{0,1},{1,0},{2,3},{3,2},{4,5},{5,4},{6,7},{7,6},{8,9},{9,8},{10,11... | collective-permute-start | bytes 1966088 | tf_op jit(solution)/shard_map/ppermute | solution.py:620
  70.7 18.6 %collective-permute-start.12 = (bf16[2,256,640]{2,1,0:T(8,128)(2,1)}, bf16[2,256,640]{2,1,0:T(8,128)(2,1)}, u32[]{:S(2)}, u32[]{:S(2)}) collective-permute-start(bf16[2,256,640]{2,1,0:T(8,128)(2,1)} %collective-permute-done.10.refs_2_.refs_4_), channel_id=1, source_target_pairs={{0,1},{1,0},{2,3},{3,2},{4,5},{5,4},{6,7},{7,6},{8,9},{9,8},{10,11... | collective-permute-start | bytes 1966088 | tf_op jit(solution)/shard_map/ppermute | solution.py:620
  244.4 82.9 %collective-permute-start.17 = (bf16[5,2,256,640]{3,2,1,0:T(8,128)(2,1)}, bf16[5,2,256,640]{3,2,1,0:T(8,128)(2,1)}, u32[]{:S(2)}, u32[]{:S(2)}) collective-permute-start(bf16[5,2,256,640]{3,2,1,0:T(8,128)(2,1)} %get-tuple-element.114), channel_id=1, source_target_pairs={{0,1},{1,0},{2,3},{3,2},{4,5},{5,4},{6,7},{7,6},{8,9},{9,8},{10,11... | collective-permute-start | bytes 9830408 | tf_op jit(solution)/shard_map/ppermute | solution.py:620
  244.7 78.7 %all-to-all-start = ((bf16[64,40,384]{2,1,0:T(8,128)(2,1)}), bf16[64,40,384]{2,1,0:T(8,128)(2,1)S(1)}, u32[]{:S(2)}, u32[]{:S(2)}) async-start(bf16[64,40,384]{2,1,0:T(8,128)(2,1)} %get-tuple-element.116), calls=%async_computation.1 | async-start | bytes 3932160 | tf_op jit(solution)/shard_map/all_to_all | solution.py:723
  337.1 17.7 %collective-permute-start.25 = (bf16[2,256,640]{2,1,0:T(8,128)(2,1)S(1)}, bf16[2,256,640]{2,1,0:T(8,128)(2,1)S(1)}, u32[]{:S(2)}, u32[]{:S(2)}) collective-permute-start(bf16[2,256,640]{2,1,0:T(8,128)(2,1)S(1)} %get-tuple-element.119), channel_id=1, source_target_pairs={{2,0},{4,2},{6,4},{8,6},{10,8},{12,10},{14,12},{16,14},{18,16},{20... | collective-permute-start | bytes 1966088 | tf_op jit(solution)/shard_map/ppermute | solution.py:616
  338.4 16.4 %collective-permute-start.24 = (bf16[2,256,640]{2,1,0:T(8,128)(2,1)S(1)}, bf16[2,256,640]{2,1,0:T(8,128)(2,1)S(1)}, u32[]{:S(2)}, u32[]{:S(2)}) collective-permute-start(bf16[2,256,640]{2,1,0:T(8,128)(2,1)S(1)} %get-tuple-element.118), channel_id=1, source_target_pairs={{0,2},{2,4},{4,6},{6,8},{8,10},{10,12},{12,14},{14,16},{16,18},{18... | collective-permute-start | bytes 1966088 | tf_op jit(solution)/shard_map/ppermute | solution.py:616
  356.6 14.2 %collective-permute-start.28 = (bf16[2080,128]{1,0:T(8,128)(2,1)S(1)}, bf16[2080,128]{1,0:T(8,128)(2,1)S(1)}, u32[]{:S(2)}, u32[]{:S(2)}) collective-permute-start(bf16[2080,128]{1,0:T(8,128)(2,1)S(1)} %bitcast.126), channel_id=1, source_target_pairs={{0,8},{8,16},{16,24},{24,0},{1,9},{9,17},{17,25},{25,1},{2,10},{10... | collective-permute-start | bytes 1597448 | tf_op jit(solution)/shard_map/ppermute | solution.py:611
  360.1 9.1 %collective-permute-start.29 = (bf16[2080,128]{1,0:T(8,128)(2,1)S(1)}, bf16[2080,128]{1,0:T(8,128)(2,1)S(1)}, u32[]{:S(2)}, u32[]{:S(2)}) collective-permute-start(bf16[2080,128]{1,0:T(8,128)(2,1)S(1)} %bitcast.127), channel_id=1, source_target_pairs={{0,24},{8,0},{16,8},{24,16},{1,25},{9,1},{17,9},{25,17},{2,26},{10... | collective-permute-start | bytes 1597448 | tf_op jit(solution)/shard_map/ppermute | solution.py:611
  377.6 30.0 %collective-permute-start.32 = (bf16[16,520,128]{2,1,0:T(8,128)(2,1)S(1)}, bf16[16,520,128]{2,1,0:T(8,128)(2,1)S(1)}, u32[]{:S(2)}, u32[]{:S(2)}) collective-permute-start(bf16[16,520,128]{2,1,0:T(8,128)(2,1)S(1)} %bitcast.121), channel_id=1, source_target_pairs={{0,1},{1,0},{2,3},{3,2},{4,5},{5,4},{6,7},{7,6},{8,9},{9,8},{10,11... | collective-permute-start | bytes 6389768 | tf_op jit(solution)/shard_map/ppermute | solution.py:620
  385.2 18.2 %collective-permute-start.27 = (bf16[2,256,640]{2,1,0:T(8,128)(2,1)S(1)}, bf16[2,256,640]{2,1,0:T(8,128)(2,1)S(1)}, u32[]{:S(2)}, u32[]{:S(2)}) collective-permute-start(bf16[2,256,640]{2,1,0:T(8,128)(2,1)S(1)} %get-tuple-element.121), channel_id=1, source_target_pairs={{2,0},{4,2},{6,4},{8,6},{10,8},{12,10},{14,12},{16,14},{18,16},{20... | collective-permute-start | bytes 1966088 | tf_op jit(solution)/shard_map/ppermute | solution.py:616
  386.5 17.8 %collective-permute-start.26 = (bf16[2,256,640]{2,1,0:T(8,128)(2,1)S(1)}, bf16[2,256,640]{2,1,0:T(8,128)(2,1)S(1)}, u32[]{:S(2)}, u32[]{:S(2)}) collective-permute-start(bf16[2,256,640]{2,1,0:T(8,128)(2,1)S(1)} %get-tuple-element.120), channel_id=1, source_target_pairs={{0,2},{2,4},{4,6},{6,8},{8,10},{10,12},{12,14},{14,16},{16,18},{18... | collective-permute-start | bytes 1966088 | tf_op jit(solution)/shard_map/ppermute | solution.py:616
  (56 other events, 399.9 us)
Sparse Core Ops, SparseCore 0:
  16.3 84.0 all-gather.1
  159.6 99.0 reduce-scatter.1

commit v2 on v1

--- a/solution.py
+++ b/solution.py
@@ -209,7 +209,7 @@
     keys_m = pl.BlockSpec((None, win, 128), lambda p, *_: (m, 0, p // 2))
     return pl.pallas_call(
         attend_back_kernel,
-        out_shape=(jax.ShapeDtypeStruct((nq, 384), bf16), jax.ShapeDtypeStruct((win, 384), bf16), jax.ShapeDtypeStruct((win, 384), bf16)),
+        out_shape=(far(nq, 384), far(win, 384), far(win, 384)),
         grid_spec=pltpu.PrefetchScalarGridSpec(
             num_scalar_prefetch=1, grid=(PAIRS,),
             in_specs=[wide_m, tall_m, keys_m, pl.BlockSpec((None, 128, win), lambda p, *_: (m, p // 2, 0)), keys_m,
@@ -249,6 +249,10 @@
     return jax.ShapeDtypeStruct(dims, dtype)
 
 
+def far(*dims):
+    return pltpu.MemorySpace.HBM(dims, bf16)
+
+
 def scalar_first(grid, in_specs, out_specs, scratch=()):
     return dict(grid_spec=pltpu.PrefetchScalarGridSpec(
         num_scalar_prefetch=1, grid=grid, in_specs=in_specs, out_specs=out_specs, scratch_shapes=list(scratch)))
@@ -363,10 +367,10 @@
     chip = (lambda b: b + 1) if n == 3 else (lambda b: 4 * b)
     tall = pl.BlockSpec((1, 512, 384), lambda m, b, *_: (m, chip(b), 0))
     wide = pl.BlockSpec((1, 384, 512), lambda m, b, *_: (m, 0, chip(b)))
-    shapes = [shape(2, 2560, 384), shape(2, 2560, 384), shape(2, 384, 2560), shape(2, 384, 2560)]
+    shapes = [far(2, 2560, 384), far(2, 2560, 384), far(2, 384, 2560), far(2, 384, 2560)]
     specs = [tall, tall, wide, wide]
     if n == 3:
-        shapes += [shape(2, 512, 384), shape(2, 384, 512)]
+        shapes += [far(2, 512, 384), far(2, 384, 512)]
         specs += [pl.BlockSpec((1, 512, 384), lambda m, *_: (m, 0, 0)), pl.BlockSpec((1, 384, 512), lambda m, *_: (m, 0, 0))]
     own, other = [own[c] for c in chips], [other[c] for c in chips]
     return call(
@@ -454,22 +458,26 @@
 
 
 def after_kernel(mid_ref, mine_ref, theirs_ref, cot_ref, vec_ref, block_ref, grad_ref, branch_ref, g_ref):
+    @pl.when(pl.program_id(0) == 0)
+    def _():
+        g_ref[...] = jnp.zeros_like(g_ref)
+
     middle = mid_ref[...]
     block_ref[...] = (middle + mine_ref[0].astype(f32) + theirs_ref[0].astype(f32)).astype(bf16)
     d_hidden = mine_ref[1].astype(f32) + theirs_ref[1].astype(f32)
     n, r = moments(middle)
-    g_ref[...] = jnp.zeros_like(g_ref)
-    g_ref[0:1, :] = jnp.sum(d_hidden * n, axis=0, keepdims=True)
-    g_ref[1:2, :] = jnp.sum(d_hidden, axis=0, keepdims=True)
+    g_ref[0:1, :] += jnp.sum(d_hidden * n, axis=0, keepdims=True)
+    g_ref[1:2, :] += jnp.sum(d_hidden, axis=0, keepdims=True)
     grad = cot_ref[...].astype(f32) + norm_back(d_hidden, n, r, vec_ref[2:3, :])
     grad_ref[...] = grad
     branch_ref[...] = grad.astype(bf16)
 
 
 def after_feed(*args):
+    rows, pair = pl.BlockSpec((128, 640), lambda i: (i, 0)), pl.BlockSpec((2, 128, 640), lambda i: (0, i, 0))
     return call(
-        after_kernel, (shape(512, 640), shape(512, 640, dtype=f32), shape(512, 640), shape(8, 640, dtype=f32)), "after_feed", 10**9, 24,
-        in_specs=[pl.BlockSpec(memory_space=pltpu.VMEM)] * 5, out_specs=[pl.BlockSpec(memory_space=pltpu.VMEM)] * 4)(*args)
+        after_kernel, (shape(512, 640), shape(512, 640, dtype=f32), shape(512, 640), shape(8, 640, dtype=f32)), "after_feed", 10**9, 16,
+        grid=(4,), in_specs=[rows, pair, pair, rows, full(16, 640)], out_specs=[rows, rows, rows, full(8, 640)])(*args)
 
 
 def branch_kernel(core_ref, own_ref, their_ref, w_ref, low0_ref, low1_ref, theirs_ref, do_ref, doT_ref, g_ref):
@@ -498,112 +506,124 @@
             (1,), specs, [full(1024, 384), full(384, 1024), full(640, 384)]))(core, *args)
 
 
-def project_back_kernel(core_ref, *refs):
+def project_back_kernel(m, place_ref, *refs):
     own_refs, other_refs = refs[:5], refs[5:10]
-    (vec_ref, w_ref, dq0_ref, dq1_ref, dk0_ref, dk1_ref, dv0_ref, dv1_ref, g_out_ref, g_two_ref,
-     mine_ref, theirs_ref, tail_ref, x_ref, d_kv, d_q, d_hid, g_ref, g_vec) = refs[10:]
-    step, core = pl.program_id(0), core_ref[0]
-    block = lax.rem(step, 5)
-
-    @pl.when(step == 0)
-    def _():
-        g_ref[...] = jnp.zeros_like(g_ref)
-        g_vec[...] = jnp.zeros_like(g_vec)
-        g_vec[2:4, :] = g_two_ref[0:2, :]
-
-    second = lax.div(step, 5)
-    needed = (block >= core_ref[1 + 2 * second]) & (block < core_ref[2 + 2 * second])
+    vec_ref, w_ref, dq_ref, dk_ref, dv_ref = refs[10:15]
+    x_ref, d_hid = refs[-2:]
+    if m == 0:
+        mine_ref, theirs_ref, g_ref, g_vec = refs[15:19]
+    else:
+        g0_ref, g_vec0_ref, g_out_ref, g_two_ref, mine_ref, theirs_ref, tail_ref, g_ref, g_vec = refs[15:24]
+    block, core = pl.program_id(0), place_ref[0]
+    needed = (block >= place_ref[1 + 2 * m]) & (block < place_ref[2 + 2 * m])
+
+    @pl.when(block == 0)
+    def _():
+        if m == 0:
+            g_ref[...] = jnp.zeros_like(g_ref)
+            g_vec[...] = jnp.zeros_like(g_vec)
+        else:
+            g_ref[...] = g0_ref[...]
+            g_vec[...] = g_vec0_ref[...]
+            g_vec[2:4, :] = g_two_ref[0:2, :]
 
     @pl.when(jnp.logical_not(needed))
     def _():
         mine_ref[...] = jnp.zeros_like(mine_ref)
         theirs_ref[...] = jnp.zeros_like(theirs_ref)
 
-    for m, (dq, dk, dv) in enumerate(((dq0_ref, dk0_ref, dv0_ref), (dq1_ref, dk1_ref, dv1_ref))):
-        @pl.when(needed & (second == m))
-        def _():
-            window_rows(core, own_refs, other_refs, m, block, x_ref)
-            d_kv[:, :384], d_kv[:, 384:] = dk[...], dv[...]
-            d_q[...] = dq[...]
-
     @pl.when(needed)
     def _():
+        window_rows(core, own_refs, other_refs, 0, block, x_ref)
         n = moments(x_ref[...])[0]
         hiddenT = (n * vec_ref[0:1, :] + vec_ref[1:2, :]).T.astype(bf16)
-        d_hid[...] = lax.dot_general(d_kv[...], w_ref[:, 384:], NT, preferred_element_type=f32)
-        g_ref[:, 384:] += jnp.dot(hiddenT, d_kv[...], preferred_element_type=f32)
+        d_kv = jnp.concatenate([dk_ref[...], dv_ref[...]], axis=1)
+        d_hid[...] = lax.dot_general(d_kv, w_ref[:, 384:], NT, preferred_element_type=f32)
+        g_ref[:, 384:] += jnp.dot(hiddenT, d_kv, preferred_element_type=f32)
 
         @pl.when(block == 2)
         def _():
-            g_ref[:, :384] += jnp.dot(hiddenT, d_q[...], preferred_element_type=f32)
-            d_hid[...] += lax.dot_general(d_q[...], w_ref[:, :384], NT, preferred_element_type=f32)
+            g_ref[:, :384] += jnp.dot(hiddenT, dq_ref[...], preferred_element_type=f32)
+            d_hid[...] += lax.dot_general(dq_ref[...], w_ref[:, :384], NT, preferred_element_type=f32)
 
         dh = d_hid[...]
-        mine_ref[0, 0] = jnp.where(core == 0, dh[:256], dh[256:]).astype(bf16)
-        theirs_ref[0, 0] = jnp.where(core == 0, dh[256:], dh[:256]).astype(bf16)
+        mine_ref[0] = jnp.where(core == 0, dh[:256], dh[256:]).astype(bf16)
+        theirs_ref[0] = jnp.where(core == 0, dh[256:], dh[:256]).astype(bf16)
         g_vec[0:1, :] += jnp.sum(dh * n, axis=0, keepdims=True)
         g_vec[1:2, :] += jnp.sum(dh, axis=0, keepdims=True)
 
-    @pl.when(step == 9)
-    def _():
-        turned = g_vec[...].T
-        lane = lax.broadcasted_iota(jnp.int32, (640, 128), 1) - 64 * (1 - core)
-        spare = g_ref[:, 256:384]
-        for i in range(4):
-            spare = jnp.where(lane == i, turned[:, i:i + 1], spare)
-        g_ref[:, 256:384] = spare
-        for y in range(4):
-            for z in range(4):
-                rows = slice(160 * y + 40 * z, 160 * y + 40 * (z + 1))
-                for x in range(3):
-                    tail_ref[16 * y + 4 * z + x] = g_ref[rows, 384 * x:384 * (x + 1)].astype(bf16)
-                tail_ref[16 * y + 4 * z + 3] = g_out_ref[rows, :].astype(bf16)
-
-
-def project_back(core, own, other, vec, w, dq, dk, dv, g_out, g_two):
-    first = pl.BlockSpec((512, 384), lambda b, *_: (jnp.minimum(b, 4), 0))
-    second = pl.BlockSpec((512, 384), lambda b, *_: (jnp.maximum(b - 5, 0), 0))
+    if m == 1:
+        @pl.when(block == 4)
+        def _():
+            turned = g_vec[...].T
+            lane = lax.broadcasted_iota(jnp.int32, (640, 128), 1) - 64 * (1 - core)
+            spare = g_ref[:, 256:384]
+            for i in range(4):
+                spare = jnp.where(lane == i, turned[:, i:i + 1], spare)
+            g_ref[:, 256:384] = spare
+            for y in range(4):
+                for z in range(4):
+                    rows = slice(160 * y + 40 * z, 160 * y + 40 * (z + 1))
+                    for x in range(3):
+                        tail_ref[16 * y + 4 * z + x] = g_ref[rows, 384 * x:384 * (x + 1)].astype(bf16)
+                    tail_ref[16 * y + 4 * z + 3] = g_out_ref[rows, :].astype(bf16)
+
+
+def project_back(m, place, own, other, vec, w, dq, dk, dv, *rest):
+    keys = pl.BlockSpec((512, 384), lambda b, *_: (b, 0))
+    tokens = pl.BlockSpec((1, 256, 640), lambda *_: (m, 0, 0))
+    part = pl.BlockSpec((1, 256, 640), lambda b, *_: (b, 0, 0))
+    sums, sum_specs = (shape(640, 1152, dtype=f32), shape(8, 640, dtype=f32)), [full(640, 1152), full(8, 640)]
+    scratch = [pltpu.VMEM((512, 640), f32), pltpu.VMEM((512, 640), f32)]
+    if m == 1:
+        scratch = [pltpu.VMEM(a.shape, f32) for a in sums] + scratch
+        sums, sum_specs = (shape(64, 40, 384),), [full(64, 40, 384)]
     return call(
-        project_back_kernel, (shape(5, 2, 256, 640), shape(5, 2, 256, 640), shape(64, 40, 384)), "project_back", 10**10, 36, **scalar_first(
-            (10,), [full(2, 256, 640)] * 10 + [full(16, 640), full(640, 1152), full(512, 384), full(512, 384), first, second, first, second,
-                                               full(640, 384), full(8, 640)],
-            [pl.BlockSpec((1, 1, 256, 640), lambda b, *_: (lax.rem(b, 5), b // 5, 0, 0))] * 2 + [full(64, 40, 384)],
-            [pltpu.VMEM((512, 640), f32), pltpu.VMEM((512, 768), bf16), pltpu.VMEM((512, 384), bf16),
-             pltpu.VMEM((512, 640), f32), pltpu.VMEM((640, 1152), f32), pltpu.VMEM((8, 640), f32)]))(core, *own, *other, vec, w, *dq, *dk, *dv, g_out, g_two)
-
-
-def final_kernel(core_ref, mine_ref, theirs_ref, up_ref, down_ref, qkv_ref, out_ref, vec_ref):
-    core = core_ref[0]
-    lane = lax.broadcasted_iota(jnp.int32, (40, 128), 1)
+        lambda *refs: project_back_kernel(m, *refs), (shape(5, 256, 640), shape(5, 256, 640)) + sums, "project_back", 5 * 10**9, 32,
+        **scalar_first((5,), [tokens] * 10 + [full(16, 640), full(640, 1152), full(512, 384), keys, keys] + [full(*a.shape) for a in rest],
+                       [part, part] + sum_specs, scratch))(place, *own, *other, vec, w, dq, dk, dv, *rest)
+
+
+def in_core_order(core_ref, mine, theirs):
+    core, mine, theirs = core_ref[0], mine.astype(f32), theirs.astype(f32)
+    return jnp.where(core == 0, mine, theirs), jnp.where(core == 0, theirs, mine)
+
+
+def final_feed_kernel(core_ref, mine_ref, theirs_ref, up_ref, down_ref):
     for i in range(16):
-        mine, theirs = mine_ref[i].astype(f32), theirs_ref[i].astype(f32)
-        pair = [jnp.where(core == 0, mine, theirs), jnp.where(core == 0, theirs, mine)]
-        for c in range(2):
-            piece = jnp.concatenate([pair[c][80 * t:80 * (t + 1)] for t in range(5)], axis=1)
+        for c, piece in enumerate(in_core_order(core_ref, mine_ref[i], theirs_ref[i])):
             if i < 8:
                 base = 1280 * (i // 2) + 640 * c
                 up_ref[80 * (i % 2):80 * (i % 2 + 1), base:base + 640] = piece
             else:
                 base = 640 * c + 80 * (i - 8)
                 down_ref[base:base + 80, :] = piece
-        a, b = ([pair[c][400 + 40 * t:440 + 40 * t] for t in range(3)] for c in range(2))
-        rows, x = slice(40 * (i // 4), 40 * (i // 4 + 1)), i % 4
-        if x < 3:
-            last = jnp.where(lane < 64, a[2], b[2])
-            qkv_ref[rows, 640 * x:640 * (x + 1)] = jnp.concatenate([a[0], a[1], b[0], b[1], last], axis=1)
-        else:
-            out_ref[rows, :] = jnp.concatenate([a[0], a[1], a[2], b[1], b[2]], axis=1)
-        if x == 0:
-            vec_ref[rows, :] = pltpu.roll(a[2], 64, 1) + b[2]
-
-
-def final_step(core, mine, theirs):
+
+
+def final_feed(core, mine, theirs):
+    return call(final_feed_kernel, (shape(160, 5120, dtype=f32), shape(1280, 640, dtype=f32)), "final_feed", 10**6, 32, **scalar_first(
+        (1,), [full(16, 80, 640)] * 2, [full(160, 5120), full(1280, 640)]))(core, mine, theirs)
+
+
+def final_heads_kernel(core_ref, mine_ref, theirs_ref, qkv_ref, out_ref, vec_ref):
+    lane = lax.broadcasted_iota(jnp.int32, (40, 128), 1)
+    for z in range(4):
+        rows = slice(40 * z, 40 * (z + 1))
+        for x in range(4):
+            a, b = in_core_order(core_ref, mine_ref[4 * z + x], theirs_ref[4 * z + x])
+            if x < 3:
+                last = jnp.where(lane < 64, a[:, 256:], b[:, 256:])
+                qkv_ref[rows, 640 * x:640 * (x + 1)] = jnp.concatenate([a[:, :256], b[:, :256], last], axis=1)
+            else:
+                out_ref[rows, :] = jnp.concatenate([a, b[:, 128:]], axis=1)
+            if x == 0:
+                vec_ref[rows, :] = pltpu.roll(a[:, 256:], 64, 1) + b[:, 256:]
+
+
+def final_heads(core, mine, theirs):
     return call(
-        final_kernel,
-        (shape(160, 5120, dtype=f32), shape(1280, 640, dtype=f32), shape(160, 1920, dtype=f32), shape(160, 640, dtype=f32),
-         shape(160, 128, dtype=f32)), "final", 10**6, 32, **scalar_first(
-            (1,), [full(16, 520, 128)] * 2, [full(160, 5120), full(1280, 640), full(160, 1920), full(160, 640), full(160, 128)]))(
-                core, mine, theirs)
+        final_heads_kernel, (shape(160, 1920, dtype=f32), shape(160, 640, dtype=f32), shape(160, 128, dtype=f32)), "final_heads", 10**6, 16,
+        **scalar_first((1,), [full(16, 40, 384)] * 2, [full(160, 1920), full(160, 640), full(160, 128)]))(core, mine, theirs)
 
 
 def shifted(array, axis, by):
@@ -678,10 +698,6 @@
     return jnp.stack(info + sizes).astype(jnp.int32), key_rows, query_rows, [low, high]
 
 
-def lane_tiles_down(array):
-    return jnp.concatenate([array[:, 128 * t:128 * (t + 1)] for t in range(array.shape[1] // 128)], axis=0)
-
-
 def body(tokens, lengths, gain_one, bias_one, w_qkv, w_out, gain_two, bias_two, w_up, w_down, cotangent):
     core, chip = lax.axis_index("core"), lax.axis_index(("z", "x"))
     core_arg, y_arg = core[None].astype(jnp.int32), lax.axis_index("batch")[None].astype(jnp.int32)
@@ -692,7 +708,7 @@
     vectors = jnp.pad(jnp.stack([gain_one, bias_one, gain_two, bias_two]), ((0, 12), (0, 0)))
     heads = pack_heads(core_arg, w_qkv, vectors)
     heads_before, heads_after = shifted(heads, "batch", 1), shifted(heads, "batch", -1)
-    heads, w_out, w_up, w_down = together(heads, w_out, w_up, w_down)
+    heads, tok_other, w_out, w_up, w_down = together(heads, tok_other, w_out, w_up, w_down)
     feed_weights = lax.all_gather(pack_feed(core_arg, w_out, w_up, w_down), "batch", axis=0, tiled=True)
     w_out_all = feed_weights[:, 5120:]
     before, after, heads_before, heads_after = together(before, after, heads_before, heads_after)
@@ -715,27 +731,36 @@
     block_out, grad_middle, branch, g_two = after_feed(middle, mine, swapped(partial), cot, vec)
 
     do, doT, g_out = branch_step(core_arg, branch, swapped(branch), w_out_all, low0, low1, theirs)
-    dq, dk, dv = zip(*(
-        attend_back(m, info, qT, q, k, kT, v, doT, do, oT, lse, key_rows, query_rows)
-        for m, ((info, key_rows, query_rows, _), oT, lse) in enumerate(zip(windows, (oT0, oT1), (lse0, lse1)))))
-    mine, theirs, tail = project_back(place, own, other, vec, w_heads, dq, dk, dv, g_out, g_two)
+    back = [
+        lambda m=m, info=info, rows=(key_rows, query_rows), oT=oT, lse=lse: attend_back(m, info, qT, q, k, kT, v, doT, do, oT, lse, *rows)
+        for m, ((info, key_rows, query_rows, _), oT, lse) in enumerate(zip(windows, (oT0, oT1), (lse0, lse1)))]
+    mine0, theirs0, g_sum, g_vec = project_back(0, place, own, other, vec, w_heads, *back[0]())
+    feed = summed_share(feed_grads, "batch")
+    dq, dk, dv, feed = together(*back[1](), feed)
+    mine1, theirs1, tail = project_back(1, place, own, other, vec, w_heads, dq, dk, dv, g_sum, g_vec, g_out, g_two)
 
     tail = lax.all_to_all(tail, ("batch", "z", "x"), 0, 0, tiled=True)
-    tail = jnp.sum(tail.astype(f32), axis=0).astype(bf16)
-    feed = summed_share(feed_grads, "batch")
-    theirs = swapped(theirs)
-    sums = [mine[j].astype(f32) + theirs[j].astype(f32) for j in range(5)]
-    shares = jnp.concatenate([lane_tiles_down(feed), lane_tiles_down(tail)], axis=0)
-    shares, right, left = together(shares, sums[4].astype(bf16), sums[0].astype(bf16))
-    shares = gathered(shares, "x").reshape(2080, 128)
-    right = (passed_along(right, 1).astype(f32) + sums[3]).astype(bf16)
-    left = (passed_along(left, -1).astype(f32) + sums[1]).astype(bf16)
-    shares, right, left = together(shares, right, left)
-    d_one = sums[2] + passed_along(right, 1).astype(f32) + passed_along(left, -1).astype(f32)
+    feed = lax.all_gather(feed, ("z", "x"), axis=0, tiled=True).reshape(16, 80, 640)
+    sums = []
+    for mine, theirs in ((mine0, theirs0), (mine1, theirs1)):
+        theirs = swapped(theirs)
+        sums.append([mine[j].astype(f32) + theirs[j].astype(f32) for j in range(5)])
+    handed = []
+    for m in range(2):
+        right, left = sums[m][4].astype(bf16), sums[m][0].astype(bf16)
+        if m == 1:
+            tail, right, left = together(tail, right, left)
+            tail = gathered(jnp.sum(tail.astype(f32), axis=0).astype(bf16), "x").reshape(160, 384)
+        right = (passed_along(right, 1).astype(f32) + sums[m][3]).astype(bf16)
+        left = (passed_along(left, -1).astype(f32) + sums[m][1]).astype(bf16)
+        if m == 1:
+            tail, right, left = together(tail, right, left)
+        handed.append(sums[m][2] + passed_along(right, 1).astype(f32) + passed_along(left, -1).astype(f32))
     n_one, r_one = moments(tok.reshape(512, 640).astype(f32))
-    grad_tokens = (grad_middle + norm_back(d_one.reshape(512, 640), n_one, r_one, vec[0:1])).astype(bf16)
-    shares = gathered_ring(shares, "z").reshape(16, 520, 128)
-    grad_up, grad_down, grad_qkv, grad_out, spare = final_step(core_arg, shares, swapped(shares))
+    grad_tokens = (grad_middle + norm_back(jnp.concatenate(handed), n_one, r_one, vec[0:1])).astype(bf16)
+    tail = gathered(tail, "z").reshape(16, 40, 384)
+    grad_qkv, grad_out, spare = final_heads(core_arg, tail, swapped(tail))
+    grad_up, grad_down = final_feed(core_arg, feed, swapped(feed))
     return (
         block_out.reshape(2, 1, 256, 640), grad_tokens.reshape(2, 1, 256, 640), spare[:, 0], spare[:, 1], grad_qkv, grad_out,
         spare[:, 2], spare[:, 3], grad_up, grad_down)

time: 428 us -> 458 us (1.070)
  the two profiles are of different devices: /device:TPU:1 before, /device:TPU:32 now
where the time goes in v2:
time: 458 us; the launch traced here: 449 us
  Pallas kernels  154 us (34%)
  waiting for transfers between devices  107 us (23%)
  starting transfers between devices  80.5 us (18%)
  local copies, waits for them, and re-layouts  64.8 us (14%)
  other arithmetic  22.2 us (5%)
  between operations  20.5 us (4%)
    unnamed x137, local copies, waits for them, and re-layouts  57.5 us
    ppermute x12, waiting for transfers between devices, passed_along(): lax.ppermute(array, ('z', 'x'), [(i, i + by) for i in range(devices) if 0...  46.8 us
    ppermute x12, starting transfers between devices, passed_along(): lax.ppermute(array, ('z', 'x'), [(i, i + by) for i in range(devices) if 0...  41.6 us
    pallas_call x2, Pallas kernels, attend_back(): pl.pallas_call(attend_back_kernel, out_shape=(far(nq, 384), far(win, 384)...  40.8 us
    pallas_call x1, Pallas kernels, feed_forward(): call(feed_kernel, (shape(2, 512, 640), shape(2, 512, 640), shape(16, 4, 8...  31.9 us
    ppermute x13, waiting for transfers between devices, shifted(): lax.ppermute(array, axis, [(i, (i + by) % devices) for i in range(devices)])  26.9 us
    pallas_call x2, Pallas kernels, attend(): pl.pallas_call(attend_kernel, out_shape=(jax.ShapeDtypeStruct((384, nq),...  26.5 us
    reduce_scatter x1, waiting for transfers between devices, body(): lax.psum_scatter(feed_grads.reshape(5120, 640), ('z', 'x'), scatter_dimen...  26.2 us
  transfers between devices with their start and end apart: 42, of which 17 were waited for; matrix products, arithmetic and copies ran while one was open for 7% of the time, Pallas kernels for 26%

profile of v2, /device:TPU:32, one launch (start us, length us, event | category | flops | bytes accessed | tf_op | source)
XLA Modules:
  0.0 449.3 jit_solution(947331144038225176)
XLA Ops:
  20.8 4.6 %collective-permute-start.1 = (bf16[2,256,640]{2,1,0:T(8,128)(2,1)S(1)}, bf16[2,256,640]{2,1,0:T(8,128)(2,1)}, u32[]{:S(2)}, u32[]{:S(2)}) collective-permute-start(bf16[2,256,640]{2,1,0:T(8,128)(2,1)S(1)} %bitcast.124), channel_id=1, source_target_pairs={{2,0},{4,2},{6,4},{8,6},{10,8},{12,10},{14,12},{16,14},{18,16},{20... | collective-permute-start | bytes 1966088 | tf_op jit(solution)/shard_map/ppermute | solution.py:636
  31.4 11.6 %collective-permute-done.2.before_ref = bf16[176,1152]{1,0:T(8,128)(2,1)S(1)} collective-permute-done((bf16[176,1152]{1,0:T(8,128)(2,1)S(1)}, bf16[176,1152]{1,0:T(8,128)(2,1)S(1)}, u32[]{:S(2)}, u32[]{:S(2)}) %collective-permute-start.2) | collective-permute-done | bytes 405536 | tf_op jit(solution)/shard_map/ppermute | solution.py:631
  46.5 5.7 %collective-permute-start.10 = (bf16[2,256,640]{2,1,0:T(8,128)(2,1)}, bf16[2,256,640]{2,1,0:T(8,128)(2,1)}, u32[]{:S(2)}, u32[]{:S(2)}) collective-permute-start(bf16[2,256,640]{2,1,0:T(8,128)(2,1)} %collective-permute-done.1.refs_3_.refs_4_), channel_id=1, source_target_pairs={{2,0},{4,2},{6,4},{8,6},{10,8},{12,10},{14,12},{16,14},{18,16},{20... | collective-permute-start | bytes 1966088 | tf_op jit(solution)/shard_map/ppermute | solution.py:636
  57.2 7.5 %collective-permute-done.8.far_ref = bf16[80,1152]{1,0:T(8,128)(2,1)S(1)} collective-permute-done((bf16[80,1152]{1,0:T(8,128)(2,1)S(1)}, bf16[80,1152]{1,0:T(8,128)(2,1)S(1)}, u32[]{:S(2)}, u32[]{:S(2)}) %collective-permute-start.8) | collective-permute-done | bytes 184352 | tf_op jit(solution)/shard_map/ppermute | solution.py:631
  73.0 6.8 %collective-permute-done.7.near_ref = bf16[96,1152]{1,0:T(8,128)(2,1)S(1)} collective-permute-done((bf16[96,1152]{1,0:T(8,128)(2,1)}, bf16[96,1152]{1,0:T(8,128)(2,1)S(1)}, u32[]{:S(2)}, u32[]{:S(2)}) %collective-permute-start.7) | collective-permute-done | bytes 221216 | tf_op jit(solution)/shard_map/ppermute | solution.py:631
  80.9 13.3 %project.2 = (bf16[2,2560,384]{2,1,0:T(8,128)(2,1)}, bf16[2,2560,384]{2,1,0:T(8,128)(2,1)}, bf16[2,384,2560]{2,1,0:T(8,128)(2,1)}, bf16[2,384,2560]{2,1,0:T(8,12...) custom-call(s32[5]{0:T(128)S(1)} %stack.81.refs_0_, ...), custom_call_target="tpu_custom_call" | custom-call | flops 5000000000 | bytes 8388608 | tf_op jit(solution)/shard_map/project/pallas_call | solution.py:376
  94.3 5.5 %project.3 = (bf16[2,2560,384]{2,1,0:T(8,128)(2,1)}, bf16[2,2560,384]{2,1,0:T(8,128)(2,1)}, bf16[2,384,2560]{2,1,0:T(8,128)(2,1)}, bf16[2,384,2560]{2,1,0:T(8,128)(2,1)}) custom-call(s32[5]{0:T(128)S(1)} %stack.81.refs_0_, ...), custom_call_target="tpu_custom_call", output_to_operand_aliasing={{0}: (7, {}), {1}: (8, {}), {2}: (9, {}), {3}: (10, {})} | custom-call | flops 5000000000 | bytes 8388608 | tf_op jit(solution)/shard_map/project/pallas_call | solution.py:376
  104.0 13.4 %attend.2 = (f32[384,512]{1,0:T(8,128)S(1)}, bf16[512,384]{1,0:T(8,128)(2,1)S(1)}, f32[5,8,512]{2,1,0:T(8,128)S(1)}) custom-call(s32[5]{0:T(128)S(1)} %stack.76.info_ref, bf16[2,384,512]{2,1,0:T(8,128)(2,1)S(1)} %copy-done.54, bf16[2,2560,384]{2,1,0:T(8,128)(2,1)S(1)} %copy-done.1, bf16[2,384,2560]{2,1,0:T(8,128)(2,1)S(1)} %copy-done.8, ...), custom_call_target="tpu_custom_call" | custom-call | flops 20000000000 | bytes 6291456 | tf_op jit(solution)/shard_map/attend/pallas_call | solution.py:98
  118.4 13.0 %attend.3 = (f32[384,512]{1,0:T(8,128)S(1)}, bf16[512,384]{1,0:T(8,128)(2,1)S(1)}, f32[5,8,512]{2,1,0:T(8,128)S(1)}) custom-call(s32[5]{0:T(128)S(1)} %stack.91.info_ref, bf16[2,384,512]{2,1,0:T(8,128)(2,1)S(1)} %copy-done.54, bf16[2,2560,384]{2,1,0:T(8,128)(2,1)S(1)} %copy-done.1, bf16[2,384,2560]{2,1,0:T(8,128)(2,1)S(1)} %copy-done.8, ...), custom_call_target="tpu_custom_call" | custom-call | flops 20000000000 | bytes 6291456 | tf_op jit(solution)/shard_map/attend/pallas_call | solution.py:98
  141.6 31.9 %feed_forward.1 = (bf16[2,512,640]{2,1,0:T(8,128)(2,1)}, bf16[2,512,640]{2,1,0:T(8,128)(2,1)}, bf16[16,4,80,640]{3,2,1,0:T(8,128)(2,1)}) custom-call(bf16[512,640]{1,0:T(8,128)(2,1)S(1)} %get-tuple-element.99.h_ref, bf16[512,640]{1,0:T(8,128)(2,1)S(1)} %get-tuple-element.100.h2_ref, bf16[512,640]{1,0:T(8,128)(2,1)} %bitcast.21.cot_ref, ...), custom_call_target="tpu_custom_call" | custom-call | flops 30000001024 | bytes 8388608 | tf_op jit(solution)/shard_map/feed_forward/pallas_call | solution.py:449
  179.5 4.1 after_feed.1
  198.3 19.6 %attend_back.2 = (bf16[512,384]{1,0:T(8,128)(2,1)}, bf16[2560,384]{1,0:T(8,128)(2,1)}, bf16[2560,384]{1,0:T(8,128)(2,1)}) custom-call(s32[5]{0:T(128)S(1)} %stack.76.info_ref, bf16[2,384,512]{2,1,0:T(8,128)(2,1)S(1)} %copy-done.55, bf16[2,512,384]{2,1,0:T(8,128)(2,1)S(1)} %copy-done.52, bf16[2,2560,384]{2,1,0:T(8,128)(2,1)S(1)} %copy-done.2, ...), custom_call_target="tpu_custom_call" | custom-call | flops 40000000000 | bytes 12582912 | tf_op jit(solution)/shard_map/attend_back/pallas_call | solution.py:210
  222.1 9.8 %project_back.2 = (bf16[5,256,640]{2,1,0:T(8,128)(2,1)S(1)}, bf16[5,256,640]{2,1,0:T(8,128)(2,1)}, f32[640,1152]{1,0:T(8,128)S(1)}, f32[8,640]{1,0:T(8,128)S(1)}) custom-call(s32[5]{0:T(128)S(1)} %stack.81.refs_0_, bf16[2,256,640]{2,1,0:T(8,128)(2,1)} %collective-permute-done.9.refs_1_, bf16[2,256,640]{2,1,0:T(8,128)(2,1)} %collective-permute-done.refs_1_.refs_2_, ...), custom_call_target="tpu_custom_call" | custom-call | flops 5000000000 | bytes 8388608 | tf_op jit(solution)/shard_map/project_back/pallas_call | solution.py:581
  235.0 26.2 %reduce-scatter.2.cloned.1.call-done = bf16[320,640]{1,0:T(8,128)(2,1)} async-done(((bf16[5120,640]{1,0:T(8,128)(2,1)}), bf16[320,640]{1,0:T(8,128)(2,1)}) %reduce-scatter.2.cloned.1.call-update) | async-done | bytes 409616 | tf_op jit(solution)/shard_map/reduce_scatter | solution.py:730
  279.5 21.2 %attend_back.3 = (bf16[512,384]{1,0:T(8,128)(2,1)}, bf16[2560,384]{1,0:T(8,128)(2,1)}, bf16[2560,384]{1,0:T(8,128)(2,1)}) custom-call(s32[5]{0:T(128)S(1)} %stack.91.info_ref, bf16[2,384,512]{2,1,0:T(8,128)(2,1)S(1)} %copy-done.56, bf16[2,512,384]{2,1,0:T(8,128)(2,1)S(1)} %copy-done.53, bf16[2,2560,384]{2,1,0:T(8,128)(2,1)S(1)} %copy-done.3, ...), custom_call_target="tpu_custom_call" | custom-call | flops 40000000000 | bytes 12582912 | tf_op jit(solution)/shard_map/attend_back/pallas_call | solution.py:210
  310.8 11.0 %project_back.3 = (bf16[5,256,640]{2,1,0:T(8,128)(2,1)S(1)}, bf16[5,256,640]{2,1,0:T(8,128)(2,1)S(1)}, bf16[64,40,384]{2,1,0:T(8,128)(2,1)}) custom-call(s32[5]{0:T(128)S(1)} %stack.81.refs_0_, bf16[2,256,640]{2,1,0:T(8,128)(2,1)} %collective-permute-done.9.refs_1_, bf16[2,256,640]{2,1,0:T(8,128)(2,1)} %collective-permute-done.refs_1_.refs_2_, ...), custom_call_target="tpu_custom_call" | custom-call | flops 5000000000 | bytes 8388608 | tf_op jit(solution)/shard_map/project_back/pallas_call | solution.py:581
  323.0 13.4 %all-to-all-start = ((bf16[64,40,384]{2,1,0:T(8,128)(2,1)}), bf16[64,40,384]{2,1,0:T(8,128)(2,1)}, u32[]{:S(2)}, u32[]{:S(2)}) async-start(bf16[64,40,384]{2,1,0:T(8,128)(2,1)} %get-tuple-element.133), calls=%async_computation.1 | async-start | bytes 3932160 | tf_op jit(solution)/shard_map/all_to_all | solution.py:742
  342.3 4.6 %collective-permute-start.20 = (bf16[256,640]{1,0:T(8,128)(2,1)S(1)}, bf16[256,640]{1,0:T(8,128)(2,1)S(1)}, u32[]{:S(2)}, u32[]{:S(2)}) collective-permute-start(bf16[256,640]{1,0:T(8,128)(2,1)S(1)} %get-tuple-element.183), channel_id=1, source_target_pairs={{2,0},{4,2},{6,4},{8,6},{10,8},{12,10},{14,12},{16,14},{18,16},{20... | collective-permute-start | bytes 983048 | tf_op jit(solution)/shard_map/ppermute | solution.py:636
  347.3 19.2 %collective-permute-done.18 = bf16[256,640]{1,0:T(8,128)(2,1)S(1)} collective-permute-done((bf16[256,640]{1,0:T(8,128)(2,1)}, bf16[256,640]{1,0:T(8,128)(2,1)S(1)}, u32[]{:S(2)}, u32[]{:S(2)}) %collective-permute-start.18) | collective-permute-done | bytes 327712 | tf_op jit(solution)/shard_map/ppermute | solution.py:636
  368.8 4.5 collective-permute-start.21
  378.9 7.7 %collective-permute-done.19 = bf16[256,640]{1,0:T(8,128)(2,1)S(1)} collective-permute-done((bf16[256,640]{1,0:T(8,128)(2,1)S(1)}, bf16[256,640]{1,0:T(8,128)(2,1)S(1)}, u32[]{:S(2)}, u32[]{:S(2)}) %collective-permute-start.19) | collective-permute-done | bytes 327712 | tf_op jit(solution)/shard_map/ppermute | solution.py:636
  397.0 3.9 collective-permute-start.29
  404.1 4.1 collective-permute-done.29
  426.5 5.0 %collective-permute-done.31 = bf16[256,640]{1,0:T(8,128)(2,1)} collective-permute-done((bf16[256,640]{1,0:T(8,128)(2,1)}, bf16[256,640]{1,0:T(8,128)(2,1)}, u32[]{:S(2)}, u32[]{:S(2)}) %collective-permute-start.31) | collective-permute-done | bytes 327712 | tf_op jit(solution)/shard_map/ppermute | solution.py:636
  (275 shorter events, 161.0 us)
Async XLA Ops:
  7.2 127.3 %all-gather.3.cloned.1.call-start = ((), (), s32[]{:S(2)}) async-start(), calls=%async_computation.2 | async-start | bytes 9216000 | tf_op jit(solution)/shard_map/all_gather | solution.py:712
  16.4 244.8 %reduce-scatter.2.cloned.1.call-start = ((), (), s32[]{:S(2)}) async-start(), calls=%async_computation.3 | async-start | bytes 6963200 | tf_op jit(solution)/shard_map/reduce_scatter | solution.py:730
  17.4 26.6 %collective-permute-start = (bf16[2,256,640]{2,1,0:T(8,128)(2,1)S(1)}, bf16[2,256,640]{2,1,0:T(8,128)(2,1)}, u32[]{:S(2)}, u32[]{:S(2)}) collective-permute-start(bf16[2,256,640]{2,1,0:T(8,128)(2,1)S(1)} %bitcast.123), channel_id=1, source_target_pairs={{0,2},{2,4},{4,6},{6,8},{8,10},{10,12},{12,14},{14,16},{16,18},{18... | collective-permute-start | bytes 1966088 | tf_op jit(solution)/shard_map/ppermute | solution.py:636
  20.8 23.2 %collective-permute-start.1 = (bf16[2,256,640]{2,1,0:T(8,128)(2,1)S(1)}, bf16[2,256,640]{2,1,0:T(8,128)(2,1)}, u32[]{:S(2)}, u32[]{:S(2)}) collective-permute-start(bf16[2,256,640]{2,1,0:T(8,128)(2,1)S(1)} %bitcast.124), channel_id=1, source_target_pairs={{2,0},{4,2},{6,4},{8,6},{10,8},{12,10},{14,12},{16,14},{18,16},{20... | collective-permute-start | bytes 1966088 | tf_op jit(solution)/shard_map/ppermute | solution.py:636
  25.4 17.6 %collective-permute-start.2 = (bf16[176,1152]{1,0:T(8,128)(2,1)S(1)}, bf16[176,1152]{1,0:T(8,128)(2,1)S(1)}, u32[]{:S(2)}, u32[]{:S(2)}) collective-permute-start(bf16[176,1152]{1,0:T(8,128)(2,1)S(1)} %pack_heads.1.own_ref), channel_id=1, source_target_pairs={{0,32},{32,64},{64,96},{96,0},{1,33},{33,65},{65,97},{97,1},{2,34}... | collective-permute-start | bytes 1216520 | tf_op jit(solution)/shard_map/ppermute | solution.py:631
  27.0 17.0 %collective-permute-start.3 = (bf16[176,1152]{1,0:T(8,128)(2,1)S(1)}, bf16[176,1152]{1,0:T(8,128)(2,1)S(1)}, u32[]{:S(2)}, u32[]{:S(2)}) collective-permute-start(bf16[176,1152]{1,0:T(8,128)(2,1)S(1)} %pack_heads.1.own_ref), channel_id=1, source_target_pairs={{0,96},{32,0},{64,32},{96,64},{1,97},{33,1},{65,33},{97,65},{2,98}... | collective-permute-start | bytes 1216520 | tf_op jit(solution)/shard_map/ppermute | solution.py:631
  44.0 36.9 %collective-permute-start.4 = (bf16[2,256,640]{2,1,0:T(8,128)(2,1)}, bf16[2,256,640]{2,1,0:T(8,128)(2,1)}, u32[]{:S(2)}, u32[]{:S(2)}) collective-permute-start(bf16[2,256,640]{2,1,0:T(8,128)(2,1)} %collective-permute-done.refs_1_.refs_2_), channel_id=1, source_target_pairs={{0,1},{1,0},{2,3},{3,2},{4,5},{5,4},{6,7},{7,6},{8,9},{9,8},{10,11... | collective-permute-start | bytes 1966088 | tf_op jit(solution)/shard_map/ppermute | solution.py:640
  44.0 21.5 %collective-permute-start.9 = (bf16[2,256,640]{2,1,0:T(8,128)(2,1)}, bf16[2,256,640]{2,1,0:T(8,128)(2,1)}, u32[]{:S(2)}, u32[]{:S(2)}) collective-permute-start(bf16[2,256,640]{2,1,0:T(8,128)(2,1)} %collective-permute-done.refs_1_.refs_2_), channel_id=1, source_target_pairs={{0,2},{2,4},{4,6},{6,8},{8,10},{10,12},{12,14},{14,16},{16,18},{18... | collective-permute-start | bytes 1966088 | tf_op jit(solution)/shard_map/ppermute | solution.py:636
  46.0 35.0 %collective-permute-start.6 = (bf16[2,256,640]{2,1,0:T(8,128)(2,1)}, bf16[2,256,640]{2,1,0:T(8,128)(2,1)}, u32[]{:S(2)}, u32[]{:S(2)}) collective-permute-start(bf16[2,256,640]{2,1,0:T(8,128)(2,1)} %collective-permute-done.1.refs_3_.refs_4_), channel_id=1, source_target_pairs={{0,1},{1,0},{2,3},{3,2},{4,5},{5,4},{6,7},{7,6},{8,9},{9,8},{10,11... | collective-permute-start | bytes 1966088 | tf_op jit(solution)/shard_map/ppermute | solution.py:640
  46.5 20.5 %collective-permute-start.10 = (bf16[2,256,640]{2,1,0:T(8,128)(2,1)}, bf16[2,256,640]{2,1,0:T(8,128)(2,1)}, u32[]{:S(2)}, u32[]{:S(2)}) collective-permute-start(bf16[2,256,640]{2,1,0:T(8,128)(2,1)} %collective-permute-done.1.refs_3_.refs_4_), channel_id=1, source_target_pairs={{2,0},{4,2},{6,4},{8,6},{10,8},{12,10},{14,12},{16,14},{18,16},{20... | collective-permute-start | bytes 1966088 | tf_op jit(solution)/shard_map/ppermute | solution.py:636
  65.4 14.4 %collective-permute-start.7 = (bf16[96,1152]{1,0:T(8,128)(2,1)}, bf16[96,1152]{1,0:T(8,128)(2,1)S(1)}, u32[]{:S(2)}, u32[]{:S(2)}) collective-permute-start(bf16[96,1152]{1,0:T(8,128)(2,1)} %slice.92), channel_id=1, source_target_pairs={{0,32},{32,64},{64,96},{96,0},{1,33},{33,65},{65,97},{97,1},{2,34}... | collective-permute-start | bytes 663560 | tf_op jit(solution)/shard_map/ppermute | solution.py:631
  65.5 28.8 %collective-permute-start.11 = (bf16[2,256,640]{2,1,0:T(8,128)(2,1)}, bf16[2,256,640]{2,1,0:T(8,128)(2,1)}, u32[]{:S(2)}, u32[]{:S(2)}) collective-permute-start(bf16[2,256,640]{2,1,0:T(8,128)(2,1)} %collective-permute-done.9.refs_1_), channel_id=1, source_target_pairs={{0,1},{1,0},{2,3},{3,2},{4,5},{5,4},{6,7},{7,6},{8,9},{9,8},{10,11... | collective-permute-start | bytes 1966088 | tf_op jit(solution)/shard_map/ppermute | solution.py:640
  67.0 27.3 %collective-permute-start.12 = (bf16[2,256,640]{2,1,0:T(8,128)(2,1)}, bf16[2,256,640]{2,1,0:T(8,128)(2,1)}, u32[]{:S(2)}, u32[]{:S(2)}) collective-permute-start(bf16[2,256,640]{2,1,0:T(8,128)(2,1)} %collective-permute-done.10.refs_2_.refs_5_), channel_id=1, source_target_pairs={{0,1},{1,0},{2,3},{3,2},{4,5},{5,4},{6,7},{7,6},{8,9},{9,8},{10,11... | collective-permute-start | bytes 1966088 | tf_op jit(solution)/shard_map/ppermute | solution.py:640
  234.6 102.1 %collective-permute-start.17 = (bf16[5,256,640]{2,1,0:T(8,128)(2,1)}, bf16[5,256,640]{2,1,0:T(8,128)(2,1)}, u32[]{:S(2)}, u32[]{:S(2)}) collective-permute-start(bf16[5,256,640]{2,1,0:T(8,128)(2,1)} %get-tuple-element.117), channel_id=1, source_target_pairs={{0,1},{1,0},{2,3},{3,2},{4,5},{5,4},{6,7},{7,6},{8,9},{9,8},{10,11... | collective-permute-start | bytes 4915208 | tf_op jit(solution)/shard_map/ppermute | solution.py:640
  262.2 38.5 %collective-permute-start.24 = (bf16[80,640]{1,0:T(8,128)(2,1)S(1)}, bf16[80,640]{1,0:T(8,128)(2,1)S(1)}, u32[]{:S(2)}, u32[]{:S(2)}) collective-permute-start(bf16[80,640]{1,0:T(8,128)(2,1)S(1)} %get-tuple-element.191), channel_id=1, source_target_pairs={{0,64},{32,96},{64,0},{96,32},{1,65},{33,97},{65,1},{97,33},{2,66}... | collective-permute-start | bytes 307208 | tf_op jit(solution)/shard_map/ppermute | solution.py:631
  265.2 35.5 %collective-permute-start.23 = (bf16[80,640]{1,0:T(8,128)(2,1)S(1)}, bf16[80,640]{1,0:T(8,128)(2,1)S(1)}, u32[]{:S(2)}, u32[]{:S(2)}) collective-permute-start(bf16[80,640]{1,0:T(8,128)(2,1)S(1)} %get-tuple-element.192), channel_id=1, source_target_pairs={{0,96},{32,0},{64,32},{96,64},{1,97},{33,1},{65,33},{97,65},{2,98}... | collective-permute-start | bytes 307208 | tf_op jit(solution)/shard_map/ppermute | solution.py:631
  266.6 34.1 %collective-permute-start.22 = (bf16[80,640]{1,0:T(8,128)(2,1)S(1)}, bf16[80,640]{1,0:T(8,128)(2,1)S(1)}, u32[]{:S(2)}, u32[]{:S(2)}) collective-permute-start(bf16[80,640]{1,0:T(8,128)(2,1)S(1)} %get-tuple-element.190), channel_id=1, source_target_pairs={{0,32},{32,64},{64,96},{96,0},{1,33},{33,65},{65,97},{97,1},{2,34}... | collective-permute-start | bytes 307208 | tf_op jit(solution)/shard_map/ppermute | solution.py:631
  323.0 66.9 %all-to-all-start = ((bf16[64,40,384]{2,1,0:T(8,128)(2,1)}), bf16[64,40,384]{2,1,0:T(8,128)(2,1)}, u32[]{:S(2)}, u32[]{:S(2)}) async-start(bf16[64,40,384]{2,1,0:T(8,128)(2,1)} %get-tuple-element.133), calls=%async_computation.1 | async-start | bytes 3932160 | tf_op jit(solution)/shard_map/all_to_all | solution.py:742
  336.4 86.9 %all-gather.5.cloned.1.call-start = ((), (), s32[]{:S(2)}) async-start(), calls=%async_computation.4 | async-start | bytes 1740800 | tf_op jit(solution)/shard_map/all_gather | solution.py:743
  336.5 52.2 %collective-permute-start.25 = (bf16[5,256,640]{2,1,0:T(8,128)(2,1)}, bf16[5,256,640]{2,1,0:T(8,128)(2,1)}, u32[]{:S(2)}, u32[]{:S(2)}) collective-permute-start(bf16[5,256,640]{2,1,0:T(8,128)(2,1)} %copy-done.37), channel_id=1, source_target_pairs={{0,1},{1,0},{2,3},{3,2},{4,5},{5,4},{6,7},{7,6},{8,9},{9,8},{10,11... | collective-permute-start | bytes 4915208 | tf_op jit(solution)/shard_map/ppermute | solution.py:640
  338.9 27.7 %collective-permute-start.18 = (bf16[256,640]{1,0:T(8,128)(2,1)}, bf16[256,640]{1,0:T(8,128)(2,1)S(1)}, u32[]{:S(2)}, u32[]{:S(2)}) collective-permute-start(bf16[256,640]{1,0:T(8,128)(2,1)} %get-tuple-element.182), channel_id=1, source_target_pairs={{0,2},{2,4},{4,6},{6,8},{8,10},{10,12},{12,14},{14,16},{16,18},{18... | collective-permute-start | bytes 983048 | tf_op jit(solution)/shard_map/ppermute | solution.py:636
  342.3 24.3 %collective-permute-start.20 = (bf16[256,640]{1,0:T(8,128)(2,1)S(1)}, bf16[256,640]{1,0:T(8,128)(2,1)S(1)}, u32[]{:S(2)}, u32[]{:S(2)}) collective-permute-start(bf16[256,640]{1,0:T(8,128)(2,1)S(1)} %get-tuple-element.183), channel_id=1, source_target_pairs={{2,0},{4,2},{6,4},{8,6},{10,8},{12,10},{14,12},{16,14},{18,16},{20... | collective-permute-start | bytes 983048 | tf_op jit(solution)/shard_map/ppermute | solution.py:636
  423.3 15.9 %collective-permute-start.37 = (bf16[16,80,640]{2,1,0:T(8,128)(2,1)}, bf16[16,80,640]{2,1,0:T(8,128)(2,1)S(1)}, u32[]{:S(2)}, u32[]{:S(2)}) collective-permute-start(bf16[16,80,640]{2,1,0:T(8,128)(2,1)} %bitcast.133), channel_id=1, source_target_pairs={{0,1},{1,0},{2,3},{3,2},{4,5},{5,4},{6,7},{7,6},{8,9},{9,8},{10,11... | collective-permute-start | bytes 4915208 | tf_op jit(solution)/shard_map/ppermute | solution.py:640
  423.5 13.5 %collective-permute-start.36 = (bf16[16,40,384]{2,1,0:T(8,128)(2,1)S(1)}, bf16[16,40,384]{2,1,0:T(8,128)(2,1)S(1)}, u32[]{:S(2)}, u32[]{:S(2)}) collective-permute-start(bf16[16,40,384]{2,1,0:T(8,128)(2,1)S(1)} %bitcast.131), channel_id=1, source_target_pairs={{0,1},{1,0},{2,3},{3,2},{4,5},{5,4},{6,7},{7,6},{8,9},{9,8},{10,11... | collective-permute-start | bytes 1474568 | tf_op jit(solution)/shard_map/ppermute | solution.py:640
  (85 other events, 715.8 us)
Sparse Core Ops, SparseCore 0:
  16.5 85.7 all-gather.2
  173.6 87.5 reduce-scatter.1
  347.0 47.5 all-gather.4

commit v3 on v1

--- a/solution.py
+++ b/solution.py
@@ -93,8 +93,8 @@
 
 
 def attend(m, info, qT, k, vT, kaug, qaugT):
-    win = k.shape[1]
-    nq = qT.shape[2]
+    win, nq = k.shape[1], qT.shape[2]
+    qT, k, vT = stay(qT, k, vT)
     return pl.pallas_call(
         attend_kernel,
         out_shape=(jax.ShapeDtypeStruct((384, nq), f32), jax.ShapeDtypeStruct((nq, 384), bf16), jax.ShapeDtypeStruct((PAIRS, 8, nq), f32)),
@@ -201,6 +201,7 @@
 
 def attend_back(m, info, qT, q, k, kT, v, doT, do, oT, lse, kaug, qaugT):
     win, nq = k.shape[1], qT.shape[2]
+    qT, q, k, kT, v = stay(qT, q, k, kT, v)
     wide = pl.BlockSpec((128, nq), lambda p, *_: (p // 2, 0))
     tall = pl.BlockSpec((nq, 128), lambda p, *_: (0, p // 2))
     keys = pl.BlockSpec((win, 128), lambda p, *_: (0, p // 2))
@@ -209,7 +210,7 @@
     keys_m = pl.BlockSpec((None, win, 128), lambda p, *_: (m, 0, p // 2))
     return pl.pallas_call(
         attend_back_kernel,
-        out_shape=(jax.ShapeDtypeStruct((nq, 384), bf16), jax.ShapeDtypeStruct((win, 384), bf16), jax.ShapeDtypeStruct((win, 384), bf16)),
+        out_shape=(far(nq, 384), far(win, 384), far(win, 384)),
         grid_spec=pltpu.PrefetchScalarGridSpec(
             num_scalar_prefetch=1, grid=(PAIRS,),
             in_specs=[wide_m, tall_m, keys_m, pl.BlockSpec((None, 128, win), lambda p, *_: (m, p // 2, 0)), keys_m,
@@ -249,6 +250,14 @@
     return jax.ShapeDtypeStruct(dims, dtype)
 
 
+def far(*dims):
+    return pltpu.MemorySpace.HBM(dims, bf16)
+
+
+def stay(*arrays):
+    return [pltpu.with_memory_space_constraint(a, pltpu.MemorySpace.HBM) for a in arrays]
+
+
 def scalar_first(grid, in_specs, out_specs, scratch=()):
     return dict(grid_spec=pltpu.PrefetchScalarGridSpec(
         num_scalar_prefetch=1, grid=grid, in_specs=in_specs, out_specs=out_specs, scratch_shapes=list(scratch)))
@@ -261,50 +270,35 @@
 def pack_heads_kernel(core_ref, qkv_ref, vec_ref, heads_ref):
     for part in range(3):
         near = pl.ds(pl.multiple_of(640 * part + 256 * core_ref[0], 128), 256)
-        heads_ref[0:160, 384 * part:384 * part + 256] = qkv_ref[:, near]
-        heads_ref[0:160, 384 * part + 256:384 * (part + 1)] = qkv_ref[:, 640 * part + 512:640 * (part + 1)]
-    heads_ref[160:176, :] = jnp.zeros((16, 1152), bf16)
-    heads_ref[160:176, 0:160] = vec_ref[...]
+        heads_ref[:, 384 * part:384 * part + 256] = qkv_ref[:, near]
+        heads_ref[:, 384 * part + 256:384 * (part + 1)] = qkv_ref[:, 640 * part + 512:640 * (part + 1)]
+    heads_ref[:, 1152:1280] = vec_ref[...]
 
 
 def pack_heads(core, w_qkv, vectors):
-    return call(pack_heads_kernel, shape(176, 1152), "pack_heads", 10**6, 8, **scalar_first(
-        (1,), [full(160, 1920), full(16, 160)], full(176, 1152)))(core, w_qkv, vectors)
-
-
-def pack_feed_kernel(core_ref, out_ref, up_ref, down_ref, feed_ref):
+    return call(pack_heads_kernel, shape(160, 1280), "pack_heads", 10**6, 8, **scalar_first(
+        (1,), [full(160, 1920), full(160, 128)], full(160, 1280)))(core, w_qkv, vectors)
+
+
+def turn_kernel(vec_ref, rows_ref):
+    rows_ref[...] = vec_ref[...].astype(f32).T[:16]
+
+
+def vector_rows(heads):
+    return call(turn_kernel, shape(16, 640, dtype=f32), "vector_rows", 10**6, 8, grid=(1,),
+                in_specs=[pl.BlockSpec((640, 128), lambda i: (0, 9))], out_specs=full(16, 640))(heads)
+
+
+def pack_feed_kernel(core_ref, up_ref, down_ref, feed_ref):
     core = core_ref[0]
     for f in range(4):
         feed_ref[:, 640 * f:640 * (f + 1)] = up_ref[:, pl.ds(pl.multiple_of(1280 * f + 640 * core, 128), 640)]
         feed_ref[:, 2560 + 640 * f:2560 + 640 * (f + 1)] = down_ref[pl.ds(pl.multiple_of(640 * core + 160 * f, 32), 160), :]
-    feed_ref[:, 5120:5760] = out_ref[...]
-
-
-def pack_feed(core, w_out, w_up, w_down):
-    args = (w_out, w_up, w_down)
-    return call(pack_feed_kernel, shape(160, 5760), "pack_feed", 10**6, 16, **scalar_first(
-        (1,), [full(*a.shape) for a in args], full(160, 5760)))(core, *args)
-
-
-def assemble_kernel(y_ref, own_ref, before_ref, after_ref, near_ref, far_ref, heads_ref, vec_ref):
-    total = jnp.zeros((16, 640), f32)
-
-    def place(by, top, bottom, vec):
-        nonlocal total
-        row = lax.rem(y_ref[0] + by, 4) * 160
-        for part, base in ((top, 0), (bottom, top.shape[0])):
-            heads_ref[pl.ds(pl.multiple_of(row + base, 32), part.shape[0]), :] = part
-        total = total + pltpu.roll(vec[:, :640].astype(f32), row, 1)
-
-    for by, ref in ((0, own_ref), (3, before_ref), (1, after_ref)):
-        place(by, ref[0:96, :], ref[96:160, :], ref[160:176, :])
-    place(2, near_ref[...], far_ref[0:64, :], far_ref[64:80, :])
-    vec_ref[...] = total
-
-
-def assemble(y, *parts):
-    return call(assemble_kernel, (shape(640, 1152), shape(16, 640, dtype=f32)), "assemble", 10**6, 12, **scalar_first(
-        (1,), [full(*a.shape) for a in parts], [full(640, 1152), full(16, 640)]))(y, *parts)
+
+
+def pack_feed(core, w_up, w_down):
+    return call(pack_feed_kernel, shape(160, 5120), "pack_feed", 10**6, 16, **scalar_first(
+        (1,), [full(160, 5120), full(1280, 640)], full(160, 5120)))(core, w_up, w_down)
 
 
 def rows_in_order(core, mine, theirs, x_ref):
@@ -363,10 +357,10 @@
     chip = (lambda b: b + 1) if n == 3 else (lambda b: 4 * b)
     tall = pl.BlockSpec((1, 512, 384), lambda m, b, *_: (m, chip(b), 0))
     wide = pl.BlockSpec((1, 384, 512), lambda m, b, *_: (m, 0, chip(b)))
-    shapes = [shape(2, 2560, 384), shape(2, 2560, 384), shape(2, 384, 2560), shape(2, 384, 2560)]
+    shapes = [far(2, 2560, 384), far(2, 2560, 384), far(2, 384, 2560), far(2, 384, 2560)]
     specs = [tall, tall, wide, wide]
     if n == 3:
-        shapes += [shape(2, 512, 384), shape(2, 384, 512)]
+        shapes += [far(2, 512, 384), far(2, 384, 512)]
         specs += [pl.BlockSpec((1, 512, 384), lambda m, *_: (m, 0, 0)), pl.BlockSpec((1, 384, 512), lambda m, *_: (m, 0, 0))]
     own, other = [own[c] for c in chips], [other[c] for c in chips]
     return call(
@@ -381,8 +375,11 @@
     return jnp.concatenate([first[:, :256], second[:, :256], first[:, 256:] + second[:, 256:]], axis=1)
 
 
-def middle_kernel(core_ref, low0_ref, low1_ref, theirs_ref, tok_ref, tok2_ref, w_ref, vec_ref, mid_ref, hid_ref, hid2_ref):
-    core = core_ref[0]
+def middle_kernel(place_ref, low0_ref, low1_ref, theirs_ref, tok_ref, tok2_ref, vec_ref, w0_ref, w1_ref, w2_ref, w3_ref,
+                  mid_ref, hid_ref, hid2_ref, w_ref):
+    core = place_ref[0]
+    for by, part in enumerate((w0_ref, w1_ref, w2_ref, w3_ref)):
+        w_ref[pl.ds(pl.multiple_of(lax.rem(place_ref[5] + 4 - by, 4) * 160, 32), 160), :] = part[...]
     for m, low_ref in enumerate((low0_ref, low1_ref)):
         attended = heads_joined(core, low_ref[...].astype(f32), theirs_ref[m].astype(f32)).astype(bf16)
         branch = jnp.dot(attended, w_ref[...], preferred_element_type=f32)
@@ -394,9 +391,9 @@
         hid2_ref[part, :] = (moments(theirs)[0] * vec_ref[2:3, :] + vec_ref[3:4, :]).astype(bf16)
 
 
-def middle_step(core, *args):
-    return call(middle_kernel, (shape(512, 640, dtype=f32), shape(512, 640), shape(512, 640)), "middle", 10**9, 20, **scalar_first(
-        (1,), [full(*a.shape) for a in args], [full(512, 640)] * 3))(core, *args)
+def middle_step(place, *args):
+    return call(middle_kernel, (shape(512, 640, dtype=f32), shape(512, 640), shape(512, 640), shape(640, 640)), "middle", 10**9, 20, **scalar_first(
+        (1,), [full(*a.shape) for a in args], [full(512, 640)] * 3 + [full(640, 640)]))(place, *args)
 
 
 def feed_kernel(h_ref, h2_ref, cot_ref, cot2_ref, up_ref, down_ref, mine_ref, theirs_ref, g_ref, h, cot, hT, cT, out, dh):
@@ -561,6 +558,7 @@
 
 
 def project_back(core, own, other, vec, w, dq, dk, dv, g_out, g_two):
+    dk, dv = stay(*dk), stay(*dv)
     first = pl.BlockSpec((512, 384), lambda b, *_: (jnp.minimum(b, 4), 0))
     second = pl.BlockSpec((512, 384), lambda b, *_: (jnp.maximum(b - 5, 0), 0))
     return call(
@@ -572,38 +570,46 @@
              pltpu.VMEM((512, 640), f32), pltpu.VMEM((640, 1152), f32), pltpu.VMEM((8, 640), f32)]))(core, *own, *other, vec, w, *dq, *dk, *dv, g_out, g_two)
 
 
-def final_kernel(core_ref, mine_ref, theirs_ref, up_ref, down_ref, qkv_ref, out_ref, vec_ref):
-    core = core_ref[0]
-    lane = lax.broadcasted_iota(jnp.int32, (40, 128), 1)
+def in_core_order(core_ref, mine, theirs):
+    core, mine, theirs = core_ref[0], mine.astype(f32), theirs.astype(f32)
+    return jnp.where(core == 0, mine, theirs), jnp.where(core == 0, theirs, mine)
+
+
+def final_feed_kernel(core_ref, mine_ref, theirs_ref, up_ref, down_ref):
     for i in range(16):
-        mine, theirs = mine_ref[i].astype(f32), theirs_ref[i].astype(f32)
-        pair = [jnp.where(core == 0, mine, theirs), jnp.where(core == 0, theirs, mine)]
-        for c in range(2):
-            piece = jnp.concatenate([pair[c][80 * t:80 * (t + 1)] for t in range(5)], axis=1)
+        for c, piece in enumerate(in_core_order(core_ref, mine_ref[i], theirs_ref[i])):
             if i < 8:
                 base = 1280 * (i // 2) + 640 * c
                 up_ref[80 * (i % 2):80 * (i % 2 + 1), base:base + 640] = piece
             else:
                 base = 640 * c + 80 * (i - 8)
                 down_ref[base:base + 80, :] = piece
-        a, b = ([pair[c][400 + 40 * t:440 + 40 * t] for t in range(3)] for c in range(2))
-        rows, x = slice(40 * (i // 4), 40 * (i // 4 + 1)), i % 4
-        if x < 3:
-            last = jnp.where(lane < 64, a[2], b[2])
-            qkv_ref[rows, 640 * x:640 * (x + 1)] = jnp.concatenate([a[0], a[1], b[0], b[1], last], axis=1)
-        else:
-            out_ref[rows, :] = jnp.concatenate([a[0], a[1], a[2], b[1], b[2]], axis=1)
-        if x == 0:
-            vec_ref[rows, :] = pltpu.roll(a[2], 64, 1) + b[2]
-
-
-def final_step(core, mine, theirs):
+
+
+def final_feed(core, mine, theirs):
+    return call(final_feed_kernel, (shape(160, 5120, dtype=f32), shape(1280, 640, dtype=f32)), "final_feed", 10**6, 32, **scalar_first(
+        (1,), [full(16, 80, 640)] * 2, [full(160, 5120), full(1280, 640)]))(core, mine, theirs)
+
+
+def final_heads_kernel(core_ref, mine_ref, theirs_ref, qkv_ref, out_ref, vec_ref):
+    lane = lax.broadcasted_iota(jnp.int32, (40, 128), 1)
+    for z in range(4):
+        rows = slice(40 * z, 40 * (z + 1))
+        for x in range(4):
+            a, b = in_core_order(core_ref, mine_ref[4 * z + x], theirs_ref[4 * z + x])
+            if x < 3:
+                last = jnp.where(lane < 64, a[:, 256:], b[:, 256:])
+                qkv_ref[rows, 640 * x:640 * (x + 1)] = jnp.concatenate([a[:, :256], b[:, :256], last], axis=1)
+            else:
+                out_ref[rows, :] = jnp.concatenate([a, b[:, 128:]], axis=1)
+            if x == 0:
+                vec_ref[rows, :] = pltpu.roll(a[:, 256:], 64, 1) + b[:, 256:]
+
+
+def final_heads(core, mine, theirs):
     return call(
-        final_kernel,
-        (shape(160, 5120, dtype=f32), shape(1280, 640, dtype=f32), shape(160, 1920, dtype=f32), shape(160, 640, dtype=f32),
-         shape(160, 128, dtype=f32)), "final", 10**6, 32, **scalar_first(
-            (1,), [full(16, 520, 128)] * 2, [full(160, 5120), full(1280, 640), full(160, 1920), full(160, 640), full(160, 128)]))(
-                core, mine, theirs)
+        final_heads_kernel, (shape(160, 1920, dtype=f32), shape(160, 640, dtype=f32), shape(160, 128, dtype=f32)), "final_heads", 10**6, 16,
+        **scalar_first((1,), [full(16, 40, 384)] * 2, [full(160, 1920), full(160, 640), full(160, 128)]))(core, mine, theirs)
 
 
 def shifted(array, axis, by):
@@ -638,16 +644,6 @@
     out = lax.dynamic_update_index_in_dim(out, array, me, 0)
     for by in (1, devices - 1, 2):
         out = lax.dynamic_update_index_in_dim(out, shifted(array, axis, by), (me + devices - by) % devices, 0)
-    return out
-
-
-def gathered_ring(array, axis):
-    me, half = lax.axis_index(axis), array.shape[0] // 2
-    before, after = shifted(array, axis, 1), shifted(array, axis, -1)
-    far = jnp.concatenate([shifted(before[:half], axis, 1), shifted(after[half:], axis, -1)])
-    out = jnp.zeros((4,) + array.shape, array.dtype)
-    for by, part in ((0, array), (3, before), (1, after), (2, far)):
-        out = lax.dynamic_update_index_in_dim(out, part, (me + by) % 4, 0)
     return out
 
 
@@ -678,38 +674,31 @@
     return jnp.stack(info + sizes).astype(jnp.int32), key_rows, query_rows, [low, high]
 
 
-def lane_tiles_down(array):
-    return jnp.concatenate([array[:, 128 * t:128 * (t + 1)] for t in range(array.shape[1] // 128)], axis=0)
-
-
 def body(tokens, lengths, gain_one, bias_one, w_qkv, w_out, gain_two, bias_two, w_up, w_down, cotangent):
     core, chip = lax.axis_index("core"), lax.axis_index(("z", "x"))
-    core_arg, y_arg = core[None].astype(jnp.int32), lax.axis_index("batch")[None].astype(jnp.int32)
+    core_arg = core[None].astype(jnp.int32)
     tok, cot = tokens[:, 0], cotangent[:, 0].reshape(512, 640)
-
     together = lambda *arrays: lax.optimization_barrier(arrays)
+
+    vectors = jnp.pad(jnp.stack([gain_one, bias_one, gain_two, bias_two], axis=1), ((0, 0), (0, 124)))
+    heads = lax.all_gather(pack_heads(core_arg, w_qkv, vectors), "batch", axis=0, tiled=True)
     before, after, tok_other = passed_along(tok, 1), passed_along(tok, -1), swapped(tok)
-    vectors = jnp.pad(jnp.stack([gain_one, bias_one, gain_two, bias_two]), ((0, 12), (0, 0)))
-    heads = pack_heads(core_arg, w_qkv, vectors)
-    heads_before, heads_after = shifted(heads, "batch", 1), shifted(heads, "batch", -1)
-    heads, w_out, w_up, w_down = together(heads, w_out, w_up, w_down)
-    feed_weights = lax.all_gather(pack_feed(core_arg, w_out, w_up, w_down), "batch", axis=0, tiled=True)
-    w_out_all = feed_weights[:, 5120:]
-    before, after, heads_before, heads_after = together(before, after, heads_before, heads_after)
     own = (passed_along(before, 1), before, tok, after, passed_along(after, -1))
-    near, far = shifted(heads_before[:96], "batch", 1), shifted(heads_after[96:], "batch", -1)
     other = (swapped(own[0]), swapped(before), tok_other, swapped(after), swapped(own[4]))
-    w_heads, vec = assemble(y_arg, heads, heads_before, heads_after, near, far)
+    heads, w_up, w_down = together(heads, w_up, w_down)
+    feed_weights = lax.all_gather(pack_feed(core_arg, w_up, w_down), "batch", axis=0, tiled=True)
+    vec = vector_rows(heads)
 
     windows = [window_info(lengths[m, 0], chip, core, 2560) for m in range(2)]
-    place = jnp.stack([core] + windows[0][3] + windows[1][3]).astype(jnp.int32)
-    *near_parts, q, qT = project((1, 2, 3), place, own, other, vec, w_heads)
-    k, v, kT, vT = project((0, 4), place, own, other, vec, w_heads, near_parts)
+    place = jnp.stack([core] + windows[0][3] + windows[1][3] + [lax.axis_index("batch")]).astype(jnp.int32)
+    *near_parts, q, qT = project((1, 2, 3), place, own, other, vec, heads)
+    k, v, kT, vT = project((0, 4), place, own, other, vec, heads, near_parts)
     (oT0, low0, lse0), (oT1, low1, lse1) = (
         attend(m, info, qT, k, vT, key_rows, query_rows) for m, (info, key_rows, query_rows, _) in enumerate(windows))
 
     theirs = swapped(jnp.stack([low0, low1]))
-    middle, hidden_two, hidden_other = middle_step(core_arg, low0, low1, theirs, tok, tok_other, w_out_all, vec)
+    w_out_parts = [w_out] + [shifted(w_out, "batch", by) for by in (1, 2, 3)]
+    middle, hidden_two, hidden_other, w_out_all = middle_step(place, low0, low1, theirs, tok, tok_other, vec, *w_out_parts)
     mine, partial, feed_grads = feed_forward(hidden_two, hidden_other, cot, swapped(cot), feed_weights)
     feed_grads = lax.psum_scatter(feed_grads.reshape(5120, 640), ("z", "x"), scatter_dimension=0, tiled=True).reshape(4, 80, 640)
     block_out, grad_middle, branch, g_two = after_feed(middle, mine, swapped(partial), cot, vec)
@@ -718,24 +707,27 @@
     dq, dk, dv = zip(*(
         attend_back(m, info, qT, q, k, kT, v, doT, do, oT, lse, key_rows, query_rows)
         for m, ((info, key_rows, query_rows, _), oT, lse) in enumerate(zip(windows, (oT0, oT1), (lse0, lse1)))))
-    mine, theirs, tail = project_back(place, own, other, vec, w_heads, dq, dk, dv, g_out, g_two)
-
+    mine, theirs, tail = project_back(place, own, other, vec, heads, dq, dk, dv, g_out, g_two)
+
+    feed = summed_share(feed_grads, "batch")
+    tail, feed = together(tail, feed)
     tail = lax.all_to_all(tail, ("batch", "z", "x"), 0, 0, tiled=True)
-    tail = jnp.sum(tail.astype(f32), axis=0).astype(bf16)
-    feed = summed_share(feed_grads, "batch")
+    feed = lax.all_gather(feed, ("z", "x"), axis=0, tiled=True).reshape(16, 80, 640)
     theirs = swapped(theirs)
     sums = [mine[j].astype(f32) + theirs[j].astype(f32) for j in range(5)]
-    shares = jnp.concatenate([lane_tiles_down(feed), lane_tiles_down(tail)], axis=0)
-    shares, right, left = together(shares, sums[4].astype(bf16), sums[0].astype(bf16))
-    shares = gathered(shares, "x").reshape(2080, 128)
+    tail, right, left = together(tail, sums[4].astype(bf16), sums[0].astype(bf16))
+    tail = gathered(jnp.sum(tail.astype(f32), axis=0).astype(bf16), "x").reshape(160, 384)
     right = (passed_along(right, 1).astype(f32) + sums[3]).astype(bf16)
     left = (passed_along(left, -1).astype(f32) + sums[1]).astype(bf16)
-    shares, right, left = together(shares, right, left)
-    d_one = sums[2] + passed_along(right, 1).astype(f32) + passed_along(left, -1).astype(f32)
+    tail, right, left = together(tail, right, left)
+    tail = gathered(tail, "z").reshape(16, 40, 384)
+    right, left = passed_along(right, 1), passed_along(left, -1)
+    tail, right, left = together(tail, right, left)
+    d_one = (sums[2] + right.astype(f32) + left.astype(f32)).reshape(512, 640)
     n_one, r_one = moments(tok.reshape(512, 640).astype(f32))
-    grad_tokens = (grad_middle + norm_back(d_one.reshape(512, 640), n_one, r_one, vec[0:1])).astype(bf16)
-    shares = gathered_ring(shares, "z").reshape(16, 520, 128)
-    grad_up, grad_down, grad_qkv, grad_out, spare = final_step(core_arg, shares, swapped(shares))
+    grad_tokens = (grad_middle + norm_back(d_one, n_one, r_one, vec[0:1])).astype(bf16)
+    grad_qkv, grad_out, spare = final_heads(core_arg, tail, swapped(tail))
+    grad_up, grad_down = final_feed(core_arg, feed, swapped(feed))
     return (
         block_out.reshape(2, 1, 256, 640), grad_tokens.reshape(2, 1, 256, 640), spare[:, 0], spare[:, 1], grad_qkv, grad_out,
         spare[:, 2], spare[:, 3], grad_up, grad_down)

time: 428 us -> 431 us (level); the launches traced: 419 us -> 427 us
  waiting for transfers between devices: 103 us -> 143 us
  starting transfers between devices: 109 us -> 82 us
  local copies, waits for them, and re-layouts: 39.2 us -> 28.4 us
    all_gather x1 -> x3, waiting for transfers between devices: 0.01 us -> 30.4 us  [the longest x1 30.4 us: body(): lax.all_gather(pack_heads(core_arg, w_qkv, vectors), 'batch', axis=0, til...]
    all_to_all x1, starting transfers between devices: 50.9 us -> 22.2 us  [body(): tail = lax.all_to_all(tail, ('batch', 'z', 'x'), 0, 0, tiled=True)]
    reduce_scatter x1, waiting for transfers between devices: 0.01 us -> 24.3 us  [body(): lax.psum_scatter(feed_grads.reshape(5120, 640), ('z', 'x'), scatter_dimen...]
    ppermute x14 -> x12, waiting for transfers between devices: 24.5 us -> 14 us  [shifted(): lax.ppermute(array, axis, [(i, (i + by) % devices) for i in range(devices)])]
    unnamed x99 -> x86, local copies, waits for them, and re-layouts: 32.1 us -> 22.9 us
    ppermute x11 -> x12, starting transfers between devices: 17.9 us -> 23.5 us  [swapped(): return lax.ppermute(array, 'core', [(0, 1), (1, 0)])]
    ppermute x8, starting transfers between devices: 23.2 us -> 18.9 us  [passed_along(): lax.ppermute(array, ('z', 'x'), [(i, i + by) for i in range(devices) if 0...]
    all_to_all x1, waiting for transfers between devices: 27.7 us -> 23.3 us  [body(): tail = lax.all_to_all(tail, ('batch', 'z', 'x'), 0, 0, tiled=True)]
  transfers between devices with their start and end apart: 36 -> 37, of which waited for: 17 -> 17; matrix products, arithmetic and copies ran while one was open for 3% -> 4% of each run, Pallas kernels for 23% -> 24%
where the time goes in v3:
time: 431 us; the launch traced here: 427 us
  waiting for transfers between devices  143 us (33%)
  Pallas kernels  138 us (32%)
  starting transfers between devices  82 us (19%)
  local copies, waits for them, and re-layouts  28.4 us (7%)
  between operations  20.3 us (5%)
  other arithmetic  15.1 us (4%)
    ppermute x8, waiting for transfers between devices, passed_along(): lax.ppermute(array, ('z', 'x'), [(i, i + by) for i in range(devices) if 0...  46.1 us
    pallas_call x2, Pallas kernels, attend_back(): pl.pallas_call(attend_back_kernel, out_shape=(far(nq, 384), far(win, 384)...  33.9 us
    pallas_call x1, Pallas kernels, feed_forward(): call(feed_kernel, (shape(2, 512, 640), shape(2, 512, 640), shape(16, 4, 8...  31.7 us
    all_gather x1, waiting for transfers between devices, body(): lax.all_gather(pack_heads(core_arg, w_qkv, vectors), 'batch', axis=0, til...  30.4 us
    reduce_scatter x1, waiting for transfers between devices, body(): lax.psum_scatter(feed_grads.reshape(5120, 640), ('z', 'x'), scatter_dimen...  24.3 us
    ppermute x12, starting transfers between devices, swapped(): return lax.ppermute(array, 'core', [(0, 1), (1, 0)])  23.5 us
    pallas_call x2, Pallas kernels, attend(): pl.pallas_call(attend_kernel, out_shape=(jax.ShapeDtypeStruct((384, nq),...  23.4 us
    all_to_all x1, waiting for transfers between devices, body(): tail = lax.all_to_all(tail, ('batch', 'z', 'x'), 0, 0, tiled=True)  23.3 us
  transfers between devices with their start and end apart: 37, of which 17 were waited for; matrix products, arithmetic and copies ran while one was open for 4% of the time, Pallas kernels for 24%

profile of v3, /device:TPU:1, one launch (start us, length us, event | category | flops | bytes accessed | tf_op | source)
XLA Modules:
  0.0 427.3 jit_solution(1360035524865798866)
XLA Ops:
  12.0 30.4 %all-gather.4.cloned.1.call-done.vec_ref.refs_8_.refs_6_.refs_11_ = bf16[640,1280]{1,0:T(8,128)(2,1)} async-done(((bf16[160,1280]{1,0:T(8,128)(2,1)}), bf16[640,1280]{1,0:T(8,128)(2,1)}) %all-gather.4.cloned.1.call-update) | async-done | bytes 1638416 | tf_op jit(solution)/shard_map/all_gather | solution.py:684
  47.6 3.9 collective-permute-start
  56.5 7.6 %collective-permute-done.refs_1_ = bf16[2,256,640]{2,1,0:T(8,128)(2,1)} collective-permute-done((bf16[2,256,640]{2,1,0:T(8,128)(2,1)S(1)}, bf16[2,256,640]{2,1,0:T(8,128)(2,1)}, u32[]{:S(2)}, u32[]{:S(2)}) %collective-permute-start) | collective-permute-done | bytes 655392 | tf_op jit(solution)/shard_map/ppermute | solution.py:622
  65.6 5.1 %collective-permute-start.5 = (bf16[2,256,640]{2,1,0:T(8,128)(2,1)}, bf16[2,256,640]{2,1,0:T(8,128)(2,1)}, u32[]{:S(2)}, u32[]{:S(2)}) collective-permute-start(bf16[2,256,640]{2,1,0:T(8,128)(2,1)} %collective-permute-done.refs_1_), channel_id=1, source_target_pairs={{0,2},{2,4},{4,6},{6,8},{8,10},{10,12},{12,14},{14,16},{16,18},{18... | collective-permute-start | bytes 1966088 | tf_op jit(solution)/shard_map/ppermute | solution.py:622
  73.7 10.6 %collective-permute-done.5.refs_1_.refs_0_ = bf16[2,256,640]{2,1,0:T(8,128)(2,1)} collective-permute-done((bf16[2,256,640]{2,1,0:T(8,128)(2,1)}, bf16[2,256,640]{2,1,0:T(8,128)(2,1)}, u32[]{:S(2)}, u32[]{:S(2)}) %collective-permute-start.5) | collective-permute-done | bytes 655392 | tf_op jit(solution)/shard_map/ppermute | solution.py:622
  85.1 4.2 collective-permute-done.6.refs_2_.refs_4_
  96.6 12.3 %project.2 = (bf16[2,2560,384]{2,1,0:T(8,128)(2,1)}, bf16[2,2560,384]{2,1,0:T(8,128)(2,1)}, bf16[2,384,2560]{2,1,0:T(8,128)(2,1)}, bf16[2,384,2560]{2,1,0:T(8,12...) custom-call(s32[6]{0:T(128)S(1)} %stack.83.refs_0_.place_ref.core_ref, ...), custom_call_target="tpu_custom_call" | custom-call | flops 5000000000 | bytes 8388608 | tf_op jit(solution)/shard_map/project/pallas_call | solution.py:366
  108.8 5.4 %project.3 = (bf16[2,2560,384]{2,1,0:T(8,128)(2,1)}, bf16[2,2560,384]{2,1,0:T(8,128)(2,1)}, bf16[2,384,2560]{2,1,0:T(8,128)(2,1)}, bf16[2,384,2560]{2,1,0:T(8,128)(2,1)}) custom-call(s32[6]{0:T(128)S(1)} %stack.83.refs_0_.place_ref.core_ref, ...), custom_call_target="tpu_custom_call", output_to_operand_aliasing={{0}: (7, {}), {1}: (8, {}), {2}: (9, {}), {3}: (10, {})} | custom-call | flops 5000000000 | bytes 8388608 | tf_op jit(solution)/shard_map/project/pallas_call | solution.py:366
  114.3 11.7 %attend.3 = (f32[384,512]{1,0:T(8,128)S(1)}, bf16[512,384]{1,0:T(8,128)(2,1)S(1)}, f32[5,8,512]{2,1,0:T(8,128)S(1)}) custom-call(s32[5]{0:T(128)S(1)} %stack.98.info_ref, bf16[2,384,512]{2,1,0:T(8,128)(2,1)} %get-tuple-element.69.qT_ref, bf16[2,2560,384]{2,1,0:T(8,128)(2,1)} %get-tuple-element.74.k_ref, bf16[2,384,2560]{2,1,0:T(8,128)(2,1)} %get-tuple-element.75.vT_ref, ...), custom_call_target="tpu_custom_call" | custom-call | flops 20000000000 | bytes 6291456 | tf_op jit(solution)/shard_map/attend/pallas_call | solution.py:98
  126.9 11.7 %attend.2 = (f32[384,512]{1,0:T(8,128)S(1)}, bf16[512,384]{1,0:T(8,128)(2,1)S(1)}, f32[5,8,512]{2,1,0:T(8,128)S(1)}) custom-call(s32[5]{0:T(128)S(1)} %stack.88.info_ref, bf16[2,384,512]{2,1,0:T(8,128)(2,1)} %get-tuple-element.69.qT_ref, bf16[2,2560,384]{2,1,0:T(8,128)(2,1)} %get-tuple-element.74.k_ref, bf16[2,384,2560]{2,1,0:T(8,128)(2,1)} %get-tuple-element.75.vT_ref, ...), custom_call_target="tpu_custom_call" | custom-call | flops 20000000000 | bytes 6291456 | tf_op jit(solution)/shard_map/attend/pallas_call | solution.py:98
  145.5 3.8 collective-permute-done.10.w1_ref
  149.4 5.2 %collective-permute-done.11.w2_ref = bf16[160,640]{1,0:T(8,128)(2,1)S(1)} collective-permute-done((bf16[160,640]{1,0:T(8,128)(2,1)S(1)}, bf16[160,640]{1,0:T(8,128)(2,1)S(1)}, u32[]{:S(2)}, u32[]{:S(2)}) %collective-permute-start.11) | collective-permute-done | bytes 204832 | tf_op jit(solution)/shard_map/ppermute | solution.py:617
  164.2 31.7 %feed_forward.1 = (bf16[2,512,640]{2,1,0:T(8,128)(2,1)}, bf16[2,512,640]{2,1,0:T(8,128)(2,1)}, bf16[16,4,80,640]{3,2,1,0:T(8,128)(2,1)}) custom-call(bf16[512,640]{1,0:T(8,128)(2,1)S(1)} %copy-done.29, bf16[512,640]{1,0:T(8,128)(2,1)S(1)} %copy-done.31, bf16[512,640]{1,0:T(8,128)(2,1)S(1)} %bitcast.127, bf16[512,640]{1,0:T(8,128)(2,1)} %collective-permute-done.13.cot2_ref, ...), custom_call_target="tpu_custom_call" | custom-call | flops 30000001024 | bytes 8388608 | tf_op jit(solution)/shard_map/feed_forward/pallas_call | solution.py:442
  210.8 16.9 %attend_back.3 = (bf16[512,384]{1,0:T(8,128)(2,1)}, bf16[2560,384]{1,0:T(8,128)(2,1)}, bf16[2560,384]{1,0:T(8,128)(2,1)}) custom-call(s32[5]{0:T(128)S(1)} %stack.98.info_ref, bf16[2,384,512]{2,1,0:T(8,128)(2,1)} %get-tuple-element.69.qT_ref, bf16[2,512,384]{2,1,0:T(8,128)(2,1)} %get-tuple-element.87.q_ref, bf16[2,2560,384]{2,1,0:T(8,128)(2,1)} %get-tuple-element.74.k_ref, ...), custom_call_target="tpu_custom_call" | custom-call | flops 40000000000 | bytes 12582912 | tf_op jit(solution)/shard_map/attend_back/pallas_call | solution.py:211
  227.8 17.0 %attend_back.2 = (bf16[512,384]{1,0:T(8,128)(2,1)}, bf16[2560,384]{1,0:T(8,128)(2,1)}, bf16[2560,384]{1,0:T(8,128)(2,1)}) custom-call(s32[5]{0:T(128)S(1)} %stack.88.info_ref, bf16[2,384,512]{2,1,0:T(8,128)(2,1)} %get-tuple-element.69.qT_ref, bf16[2,512,384]{2,1,0:T(8,128)(2,1)} %get-tuple-element.87.q_ref, bf16[2,2560,384]{2,1,0:T(8,128)(2,1)} %get-tuple-element.74.k_ref, ...), custom_call_target="tpu_custom_call" | custom-call | flops 40000000000 | bytes 12582912 | tf_op jit(solution)/shard_map/attend_back/pallas_call | solution.py:211
  245.7 19.0 %project_back.1 = (bf16[5,2,256,640]{3,2,1,0:T(8,128)(2,1)S(1)}, bf16[5,2,256,640]{3,2,1,0:T(8,128)(2,1)}, bf16[64,40,384]{2,1,0:T(8,128)(2,1)S(1)}) custom-call(s32[6]{0:T(128)S(1)} %stack.83.refs_0_.place_ref.core_ref, bf16[2,256,640]{2,1,0:T(8,128)(2,1)} %collective-permute-done.5.refs_1_.refs_0_, bf16[2,256,640]{2,1,0:T(8,128)(2,1)} %collective-permute-done.refs_1_, ...), custom_call_target="tpu_custom_call" | custom-call | flops 10000000000 | bytes 8388608 | tf_op jit(solution)/shard_map/project_back/pallas_call | solution.py:564
  268.4 24.3 %reduce-scatter.2.cloned.1.call-done = bf16[320,640]{1,0:T(8,128)(2,1)} async-done(((bf16[5120,640]{1,0:T(8,128)(2,1)}), bf16[320,640]{1,0:T(8,128)(2,1)}) %reduce-scatter.2.cloned.1.call-update) | async-done | bytes 409616 | tf_op jit(solution)/shard_map/reduce_scatter | solution.py:703
  304.0 22.2 %all-to-all-start = ((bf16[64,40,384]{2,1,0:T(8,128)(2,1)}), bf16[64,40,384]{2,1,0:T(8,128)(2,1)S(1)}, u32[]{:S(2)}, u32[]{:S(2)}) async-start(bf16[64,40,384]{2,1,0:T(8,128)(2,1)} %copy-done.5), calls=%async_computation.1 | async-start | bytes 3932160 | tf_op jit(solution)/shard_map/all_to_all | solution.py:714
  330.3 23.3 %all-to-all-done = bf16[64,40,384]{2,1,0:T(8,128)(2,1)S(1)} async-done(((bf16[64,40,384]{2,1,0:T(8,128)(2,1)}), bf16[64,40,384]{2,1,0:T(8,128)(2,1)S(1)}, u32[]{:S(2)}, u32[]{:S(2)}) %all-to-all-start) | async-done | bytes 1966112 | tf_op jit(solution)/shard_map/all_to_all | solution.py:714
  361.1 12.1 %collective-permute-done.23 = bf16[2,256,640]{2,1,0:T(8,128)(2,1)S(1)} collective-permute-done((bf16[2,256,640]{2,1,0:T(8,128)(2,1)}, bf16[2,256,640]{2,1,0:T(8,128)(2,1)S(1)}, u32[]{:S(2)}, u32[]{:S(2)}) %collective-permute-start.23) | collective-permute-done | bytes 655392 | tf_op jit(solution)/shard_map/ppermute | solution.py:622
  373.2 6.6 %collective-permute-done.24 = bf16[2,256,640]{2,1,0:T(8,128)(2,1)S(1)} collective-permute-done((bf16[2,256,640]{2,1,0:T(8,128)(2,1)S(1)}, bf16[2,256,640]{2,1,0:T(8,128)(2,1)S(1)}, u32[]{:S(2)}, u32[]{:S(2)}) %collective-permute-start.24) | collective-permute-done | bytes 655392 | tf_op jit(solution)/shard_map/ppermute | solution.py:622
  390.5 5.8 %collective-permute-start.31 = (bf16[16,80,640]{2,1,0:T(8,128)(2,1)}, bf16[16,80,640]{2,1,0:T(8,128)(2,1)S(1)}, u32[]{:S(2)}, u32[]{:S(2)}) collective-permute-start(bf16[16,80,640]{2,1,0:T(8,128)(2,1)} %bitcast.124), channel_id=1, source_target_pairs={{0,1},{1,0},{2,3},{3,2},{4,5},{5,4},{6,7},{7,6},{8,9},{9,8},{10,11... | collective-permute-start | bytes 4915208 | tf_op jit(solution)/shard_map/ppermute | solution.py:626
  397.3 4.0 collective-permute-done.29
  401.3 10.1 %collective-permute-start.30 = (bf16[16,40,384]{2,1,0:T(8,128)(2,1)S(1)}, bf16[16,40,384]{2,1,0:T(8,128)(2,1)S(1)}, u32[]{:S(2)}, u32[]{:S(2)}) collective-permute-start(bf16[16,40,384]{2,1,0:T(8,128)(2,1)S(1)} %bitcast.122), channel_id=1, source_target_pairs={{0,1},{1,0},{2,3},{3,2},{4,5},{5,4},{6,7},{7,6},{8,9},{9,8},{10,11... | collective-permute-start | bytes 1474568 | tf_op jit(solution)/shard_map/ppermute | solution.py:626
  (208 shorter events, 101.9 us)
Async XLA Ops:
  7.2 35.2 %all-gather.4.cloned.1.call-start = ((), (), s32[]{:S(2)}) async-start(), calls=%async_computation.2 | async-start | bytes 2048000 | tf_op jit(solution)/shard_map/all_gather | solution.py:684
  11.9 149.0 %all-gather.6.cloned.1.call-start = ((), (), s32[]{:S(2)}) async-start(), calls=%async_computation.3 | async-start | bytes 8192000 | tf_op jit(solution)/shard_map/all_gather | solution.py:689
  46.6 246.1 %reduce-scatter.2.cloned.1.call-start = ((), (), s32[]{:S(2)}) async-start(), calls=%async_computation.4 | async-start | bytes 6963200 | tf_op jit(solution)/shard_map/reduce_scatter | solution.py:703
  47.6 16.5 %collective-permute-start = (bf16[2,256,640]{2,1,0:T(8,128)(2,1)S(1)}, bf16[2,256,640]{2,1,0:T(8,128)(2,1)}, u32[]{:S(2)}, u32[]{:S(2)}) collective-permute-start(bf16[2,256,640]{2,1,0:T(8,128)(2,1)S(1)} %bitcast.114), channel_id=1, source_target_pairs={{0,2},{2,4},{4,6},{6,8},{8,10},{10,12},{12,14},{14,16},{16,18},{18... | collective-permute-start | bytes 1966088 | tf_op jit(solution)/shard_map/ppermute | solution.py:622
  51.6 19.2 %collective-permute-start.1 = (bf16[2,256,640]{2,1,0:T(8,128)(2,1)S(1)}, bf16[2,256,640]{2,1,0:T(8,128)(2,1)}, u32[]{:S(2)}, u32[]{:S(2)}) collective-permute-start(bf16[2,256,640]{2,1,0:T(8,128)(2,1)S(1)} %bitcast.115), channel_id=1, source_target_pairs={{2,0},{4,2},{6,4},{8,6},{10,8},{12,10},{14,12},{16,14},{18,16},{20... | collective-permute-start | bytes 1966088 | tf_op jit(solution)/shard_map/ppermute | solution.py:622
  52.8 43.7 %collective-permute-start.3 = (bf16[2,256,640]{2,1,0:T(8,128)(2,1)S(1)}, bf16[2,256,640]{2,1,0:T(8,128)(2,1)S(1)}, u32[]{:S(2)}, u32[]{:S(2)}) collective-permute-start(bf16[2,256,640]{2,1,0:T(8,128)(2,1)S(1)} %bitcast.116), channel_id=1, source_target_pairs={{0,1},{1,0},{2,3},{3,2},{4,5},{5,4},{6,7},{7,6},{8,9},{9,8},{10,11... | collective-permute-start | bytes 1966088 | tf_op jit(solution)/shard_map/ppermute | solution.py:626
  64.1 32.4 %collective-permute-start.2 = (bf16[2,256,640]{2,1,0:T(8,128)(2,1)}, bf16[2,256,640]{2,1,0:T(8,128)(2,1)}, u32[]{:S(2)}, u32[]{:S(2)}) collective-permute-start(bf16[2,256,640]{2,1,0:T(8,128)(2,1)} %collective-permute-done.refs_1_), channel_id=1, source_target_pairs={{0,1},{1,0},{2,3},{3,2},{4,5},{5,4},{6,7},{7,6},{8,9},{9,8},{10,11... | collective-permute-start | bytes 1966088 | tf_op jit(solution)/shard_map/ppermute | solution.py:626
  65.6 18.7 %collective-permute-start.5 = (bf16[2,256,640]{2,1,0:T(8,128)(2,1)}, bf16[2,256,640]{2,1,0:T(8,128)(2,1)}, u32[]{:S(2)}, u32[]{:S(2)}) collective-permute-start(bf16[2,256,640]{2,1,0:T(8,128)(2,1)} %collective-permute-done.refs_1_), channel_id=1, source_target_pairs={{0,2},{2,4},{4,6},{6,8},{8,10},{10,12},{12,14},{14,16},{16,18},{18... | collective-permute-start | bytes 1966088 | tf_op jit(solution)/shard_map/ppermute | solution.py:622
  70.7 25.8 %collective-permute-start.4 = (bf16[2,256,640]{2,1,0:T(8,128)(2,1)}, bf16[2,256,640]{2,1,0:T(8,128)(2,1)}, u32[]{:S(2)}, u32[]{:S(2)}) collective-permute-start(bf16[2,256,640]{2,1,0:T(8,128)(2,1)} %collective-permute-done.1.refs_3_), channel_id=1, source_target_pairs={{0,1},{1,0},{2,3},{3,2},{4,5},{5,4},{6,7},{7,6},{8,9},{9,8},{10,11... | collective-permute-start | bytes 1966088 | tf_op jit(solution)/shard_map/ppermute | solution.py:626
  71.0 18.3 %collective-permute-start.6 = (bf16[2,256,640]{2,1,0:T(8,128)(2,1)}, bf16[2,256,640]{2,1,0:T(8,128)(2,1)}, u32[]{:S(2)}, u32[]{:S(2)}) collective-permute-start(bf16[2,256,640]{2,1,0:T(8,128)(2,1)} %collective-permute-done.1.refs_3_), channel_id=1, source_target_pairs={{2,0},{4,2},{6,4},{8,6},{10,8},{12,10},{14,12},{16,14},{18,16},{20... | collective-permute-start | bytes 1966088 | tf_op jit(solution)/shard_map/ppermute | solution.py:622
  84.3 24.5 %collective-permute-start.7 = (bf16[2,256,640]{2,1,0:T(8,128)(2,1)}, bf16[2,256,640]{2,1,0:T(8,128)(2,1)}, u32[]{:S(2)}, u32[]{:S(2)}) collective-permute-start(bf16[2,256,640]{2,1,0:T(8,128)(2,1)} %collective-permute-done.5.refs_1_.refs_0_), channel_id=1, source_target_pairs={{0,1},{1,0},{2,3},{3,2},{4,5},{5,4},{6,7},{7,6},{8,9},{9,8},{10,11... | collective-permute-start | bytes 1966088 | tf_op jit(solution)/shard_map/ppermute | solution.py:626
  89.3 19.5 %collective-permute-start.8 = (bf16[2,256,640]{2,1,0:T(8,128)(2,1)}, bf16[2,256,640]{2,1,0:T(8,128)(2,1)}, u32[]{:S(2)}, u32[]{:S(2)}) collective-permute-start(bf16[2,256,640]{2,1,0:T(8,128)(2,1)} %collective-permute-done.6.refs_2_.refs_4_), channel_id=1, source_target_pairs={{0,1},{1,0},{2,3},{3,2},{4,5},{5,4},{6,7},{7,6},{8,9},{9,8},{10,11... | collective-permute-start | bytes 1966088 | tf_op jit(solution)/shard_map/ppermute | solution.py:626
  138.8 15.8 %collective-permute-start.9 = (bf16[2,512,384]{2,1,0:T(8,128)(2,1)S(1)}, bf16[2,512,384]{2,1,0:T(8,128)(2,1)S(1)}, u32[]{:S(2)}, u32[]{:S(2)}) collective-permute-start(bf16[2,512,384]{2,1,0:T(8,128)(2,1)S(1)} %pad_maximum_fusion), channel_id=1, source_target_pairs={{0,1},{1,0},{2,3},{3,2},{4,5},{5,4},{6,7},{7,6},{8,9},{9,8},{10,11... | collective-permute-start | bytes 2359304 | tf_op jit(solution)/shard_map/ppermute | solution.py:626
  140.0 20.9 %collective-permute-start.13 = (bf16[512,640]{1,0:T(8,128)(2,1)S(1)}, bf16[512,640]{1,0:T(8,128)(2,1)}, u32[]{:S(2)}, u32[]{:S(2)}) collective-permute-start(bf16[512,640]{1,0:T(8,128)(2,1)S(1)} %bitcast.126), channel_id=1, source_target_pairs={{0,1},{1,0},{2,3},{3,2},{4,5},{5,4},{6,7},{7,6},{8,9},{9,8},{10,11... | collective-permute-start | bytes 1966088 | tf_op jit(solution)/shard_map/ppermute | solution.py:626
  143.0 11.6 %collective-permute-start.11 = (bf16[160,640]{1,0:T(8,128)(2,1)S(1)}, bf16[160,640]{1,0:T(8,128)(2,1)S(1)}, u32[]{:S(2)}, u32[]{:S(2)}) collective-permute-start(bf16[160,640]{1,0:T(8,128)(2,1)S(1)} %copy-done.27), channel_id=1, source_target_pairs={{0,64},{32,96},{64,0},{96,32},{1,65},{33,97},{65,1},{97,33},{2,66}... | collective-permute-start | bytes 614408 | tf_op jit(solution)/shard_map/ppermute | solution.py:617
  267.7 59.7 %collective-permute-start.16 = (bf16[5,2,256,640]{3,2,1,0:T(8,128)(2,1)}, bf16[5,2,256,640]{3,2,1,0:T(8,128)(2,1)}, u32[]{:S(2)}, u32[]{:S(2)}) collective-permute-start(bf16[5,2,256,640]{3,2,1,0:T(8,128)(2,1)} %get-tuple-element.107), channel_id=1, source_target_pairs={{0,1},{1,0},{2,3},{3,2},{4,5},{5,4},{6,7},{7,6},{8,9},{9,8},{10,11... | collective-permute-start | bytes 9830408 | tf_op jit(solution)/shard_map/ppermute | solution.py:626
  304.0 49.6 %all-to-all-start = ((bf16[64,40,384]{2,1,0:T(8,128)(2,1)}), bf16[64,40,384]{2,1,0:T(8,128)(2,1)S(1)}, u32[]{:S(2)}, u32[]{:S(2)}) async-start(bf16[64,40,384]{2,1,0:T(8,128)(2,1)} %copy-done.5), calls=%async_computation.1 | async-start | bytes 3932160 | tf_op jit(solution)/shard_map/all_to_all | solution.py:714
  326.2 64.3 %all-gather.8.cloned.1.call-start = ((), (), s32[]{:S(2)}) async-start(), calls=%async_computation.5 | async-start | bytes 1740800 | tf_op jit(solution)/shard_map/all_gather | solution.py:715
  357.4 15.9 %collective-permute-start.23 = (bf16[2,256,640]{2,1,0:T(8,128)(2,1)}, bf16[2,256,640]{2,1,0:T(8,128)(2,1)S(1)}, u32[]{:S(2)}, u32[]{:S(2)}) collective-permute-start(bf16[2,256,640]{2,1,0:T(8,128)(2,1)} %get-tuple-element.112), channel_id=1, source_target_pairs={{0,2},{2,4},{4,6},{6,8},{8,10},{10,12},{12,14},{14,16},{16,18},{18... | collective-permute-start | bytes 1966088 | tf_op jit(solution)/shard_map/ppermute | solution.py:622
  359.2 20.7 %collective-permute-start.24 = (bf16[2,256,640]{2,1,0:T(8,128)(2,1)S(1)}, bf16[2,256,640]{2,1,0:T(8,128)(2,1)S(1)}, u32[]{:S(2)}, u32[]{:S(2)}) collective-permute-start(bf16[2,256,640]{2,1,0:T(8,128)(2,1)S(1)} %get-tuple-element.113), channel_id=1, source_target_pairs={{2,0},{4,2},{6,4},{8,6},{10,8},{12,10},{14,12},{16,14},{18,16},{20... | collective-permute-start | bytes 1966088 | tf_op jit(solution)/shard_map/ppermute | solution.py:622
  384.2 12.1 %collective-permute-start.26 = (bf16[160,384]{1,0:T(8,128)(2,1)S(1)}, bf16[160,384]{1,0:T(8,128)(2,1)S(1)}, u32[]{:S(2)}, u32[]{:S(2)}) collective-permute-start(bf16[160,384]{1,0:T(8,128)(2,1)S(1)} %bitcast.132), channel_id=1, source_target_pairs={{0,24},{8,0},{16,8},{24,16},{1,25},{9,1},{17,9},{25,17},{2,26},{10... | collective-permute-start | bytes 368648 | tf_op jit(solution)/shard_map/ppermute | solution.py:617
  388.8 12.5 %collective-permute-start.29 = (bf16[2,256,640]{2,1,0:T(8,128)(2,1)S(1)}, bf16[2,256,640]{2,1,0:T(8,128)(2,1)}, u32[]{:S(2)}, u32[]{:S(2)}) collective-permute-start(bf16[2,256,640]{2,1,0:T(8,128)(2,1)S(1)} %get-tuple-element.116), channel_id=1, source_target_pairs={{2,0},{4,2},{6,4},{8,6},{10,8},{12,10},{14,12},{16,14},{18,16},{20... | collective-permute-start | bytes 1966088 | tf_op jit(solution)/shard_map/ppermute | solution.py:622
  390.5 26.8 %collective-permute-start.31 = (bf16[16,80,640]{2,1,0:T(8,128)(2,1)}, bf16[16,80,640]{2,1,0:T(8,128)(2,1)S(1)}, u32[]{:S(2)}, u32[]{:S(2)}) collective-permute-start(bf16[16,80,640]{2,1,0:T(8,128)(2,1)} %bitcast.124), channel_id=1, source_target_pairs={{0,1},{1,0},{2,3},{3,2},{4,5},{5,4},{6,7},{7,6},{8,9},{9,8},{10,11... | collective-permute-start | bytes 4915208 | tf_op jit(solution)/shard_map/ppermute | solution.py:626
  401.3 13.9 %collective-permute-start.30 = (bf16[16,40,384]{2,1,0:T(8,128)(2,1)S(1)}, bf16[16,40,384]{2,1,0:T(8,128)(2,1)S(1)}, u32[]{:S(2)}, u32[]{:S(2)}) collective-permute-start(bf16[16,40,384]{2,1,0:T(8,128)(2,1)S(1)} %bitcast.122), channel_id=1, source_target_pairs={{0,1},{1,0},{2,3},{3,2},{4,5},{5,4},{6,7},{7,6},{8,9},{9,8},{10,11... | collective-permute-start | bytes 1474568 | tf_op jit(solution)/shard_map/ppermute | solution.py:626
  (54 other events, 311.8 us)
Sparse Core Ops, SparseCore 0:
  12.1 30.2 all-gather.3
  46.7 67.7 all-gather.5
  196.1 96.5 reduce-scatter.1
  329.7 53.9 all-gather.7

commit v4 on v3

--- a/solution.py
+++ b/solution.py
@@ -115,7 +115,7 @@
             scratch_shapes=[pltpu.VMEM((256, 2 * TILE), bf16)],
         ),
         compiler_params=pltpu.CompilerParams(vmem_limit_bytes=28 << 20),
-        cost_estimate=pl.CostEstimate(flops=20 * 10**9, bytes_accessed=6 << 20, transcendentals=5 * 10**6),
+        cost_estimate=pl.CostEstimate(flops=int(20 * 10**9 * 0.02), bytes_accessed=0, transcendentals=0),
         name="attend",
     )(info, qT, k, vT, kaug, qaugT)
 
@@ -223,7 +223,7 @@
                             pltpu.VMEM((win, 128), f32), pltpu.VMEM((win, 128), f32)],
         ),
         compiler_params=pltpu.CompilerParams(vmem_limit_bytes=32 << 20),
-        cost_estimate=pl.CostEstimate(flops=40 * 10**9, bytes_accessed=12 << 20, transcendentals=5 * 10**6),
+        cost_estimate=pl.CostEstimate(flops=int(40 * 10**9 * 0.02), bytes_accessed=0, transcendentals=0),
         name="attend_back",
     )(info, qT, q, k, kT, v, doT, do, oT, lse, kaug, qaugT)
 
@@ -243,7 +243,7 @@
     return pl.pallas_call(
         kernel, out_shape=out_shape, name=name,
         compiler_params=pltpu.CompilerParams(vmem_limit_bytes=limit << 20),
-        cost_estimate=pl.CostEstimate(flops=flops, bytes_accessed=8 << 20, transcendentals=0), **spec)
+        cost_estimate=pl.CostEstimate(flops=int(flops * 0.02), bytes_accessed=0, transcendentals=0), **spec)
 
 
 def shape(*dims, dtype=bf16):
@@ -628,14 +628,6 @@
 
 def pick(array, index):
     return lax.dynamic_index_in_dim(array, index, 0, keepdims=False)
-
-
-def summed_share(array, axis):
-    me, devices = lax.axis_index(axis), lax.axis_size(axis)
-    total = pick(array, me).astype(f32)
-    for by in (1, devices - 1, 2):
-        total = total + shifted(pick(array, (me + by) % devices), axis, by).astype(f32)
-    return total.astype(bf16)
 
 
 def gathered(array, axis):
@@ -681,51 +673,59 @@
     together = lambda *arrays: lax.optimization_barrier(arrays)
 
     vectors = jnp.pad(jnp.stack([gain_one, bias_one, gain_two, bias_two], axis=1), ((0, 0), (0, 124)))
+    before, after, tok_other = passed_along(tok, 1), passed_along(tok, -1), swapped(tok)
     heads = lax.all_gather(pack_heads(core_arg, w_qkv, vectors), "batch", axis=0, tiled=True)
-    before, after, tok_other = passed_along(tok, 1), passed_along(tok, -1), swapped(tok)
-    own = (passed_along(before, 1), before, tok, after, passed_along(after, -1))
-    other = (swapped(own[0]), swapped(before), tok_other, swapped(after), swapped(own[4]))
-    heads, w_up, w_down = together(heads, w_up, w_down)
+    heads, before, after, tok_other, w_up, w_down = together(heads, before, after, tok_other, w_up, w_down)
     feed_weights = lax.all_gather(pack_feed(core_arg, w_up, w_down), "batch", axis=0, tiled=True)
     vec = vector_rows(heads)
-
     windows = [window_info(lengths[m, 0], chip, core, 2560) for m in range(2)]
     place = jnp.stack([core] + windows[0][3] + windows[1][3] + [lax.axis_index("batch")]).astype(jnp.int32)
+    own, other = [None, before, tok, after, None], [None, swapped(before), tok_other, swapped(after), None]
+    before, after, place, own[1:4], other[1:4] = together(before, after, place, own[1:4], other[1:4])
+    own[0], own[4] = passed_along(before, 1), passed_along(after, -1)
     *near_parts, q, qT = project((1, 2, 3), place, own, other, vec, heads)
+    own[0], own[4], near_parts = together(own[0], own[4], near_parts)
+    other[0], other[4] = swapped(own[0]), swapped(own[4])
     k, v, kT, vT = project((0, 4), place, own, other, vec, heads, near_parts)
-    (oT0, low0, lse0), (oT1, low1, lse1) = (
-        attend(m, info, qT, k, vT, key_rows, query_rows) for m, (info, key_rows, query_rows, _) in enumerate(windows))
+    w_out_parts = [shifted(w_out, "batch", by) for by in (1, 2, 3)]
+    info, key_rows, query_rows, _ = windows[0]
+    oT0, low0, lse0 = attend(0, info, qT, k, vT, key_rows, query_rows)
+    w_out_parts, qT_next, low0 = together(w_out_parts, qT, low0)
+    w_out_parts = [w_out] + w_out_parts
+    info, key_rows, query_rows, _ = windows[1]
+    oT1, low1, lse1 = attend(1, info, qT_next, k, vT, key_rows, query_rows)
 
     theirs = swapped(jnp.stack([low0, low1]))
-    w_out_parts = [w_out] + [shifted(w_out, "batch", by) for by in (1, 2, 3)]
     middle, hidden_two, hidden_other, w_out_all = middle_step(place, low0, low1, theirs, tok, tok_other, vec, *w_out_parts)
     mine, partial, feed_grads = feed_forward(hidden_two, hidden_other, cot, swapped(cot), feed_weights)
-    feed_grads = lax.psum_scatter(feed_grads.reshape(5120, 640), ("z", "x"), scatter_dimension=0, tiled=True).reshape(4, 80, 640)
+    feed_grads = lax.psum_scatter(feed_grads.reshape(5120, 640), ("z", "x"), scatter_dimension=0, tiled=True)
     block_out, grad_middle, branch, g_two = after_feed(middle, mine, swapped(partial), cot, vec)
 
     do, doT, g_out = branch_step(core_arg, branch, swapped(branch), w_out_all, low0, low1, theirs)
     dq, dk, dv = zip(*(
         attend_back(m, info, qT, q, k, kT, v, doT, do, oT, lse, key_rows, query_rows)
         for m, ((info, key_rows, query_rows, _), oT, lse) in enumerate(zip(windows, (oT0, oT1), (lse0, lse1)))))
+    dq, feed_grads = together(dq, feed_grads)
+    feed = lax.psum_scatter(feed_grads, "batch", scatter_dimension=0, tiled=True).reshape(80, 640)
     mine, theirs, tail = project_back(place, own, other, vec, heads, dq, dk, dv, g_out, g_two)
 
-    feed = summed_share(feed_grads, "batch")
-    tail, feed = together(tail, feed)
+    feed, mine, theirs, tail = together(feed, mine, theirs, tail)
+
     tail = lax.all_to_all(tail, ("batch", "z", "x"), 0, 0, tiled=True)
     feed = lax.all_gather(feed, ("z", "x"), axis=0, tiled=True).reshape(16, 80, 640)
     theirs = swapped(theirs)
     sums = [mine[j].astype(f32) + theirs[j].astype(f32) for j in range(5)]
-    tail, right, left = together(tail, sums[4].astype(bf16), sums[0].astype(bf16))
+    right, left = passed_along(sums[4].astype(bf16), 1), passed_along(sums[0].astype(bf16), -1)
+    tail, right, left = together(tail, right, left)
+    right = passed_along((right.astype(f32) + sums[3]).astype(bf16), 1)
+    left = passed_along((left.astype(f32) + sums[1]).astype(bf16), -1)
     tail = gathered(jnp.sum(tail.astype(f32), axis=0).astype(bf16), "x").reshape(160, 384)
-    right = (passed_along(right, 1).astype(f32) + sums[3]).astype(bf16)
-    left = (passed_along(left, -1).astype(f32) + sums[1]).astype(bf16)
     tail, right, left = together(tail, right, left)
     tail = gathered(tail, "z").reshape(16, 40, 384)
-    right, left = passed_along(right, 1), passed_along(left, -1)
-    tail, right, left = together(tail, right, left)
     d_one = (sums[2] + right.astype(f32) + left.astype(f32)).reshape(512, 640)
     n_one, r_one = moments(tok.reshape(512, 640).astype(f32))
     grad_tokens = (grad_middle + norm_back(d_one, n_one, r_one, vec[0:1])).astype(bf16)
+    tail, grad_tokens = together(tail, grad_tokens)
     grad_qkv, grad_out, spare = final_heads(core_arg, tail, swapped(tail))
     grad_up, grad_down = final_feed(core_arg, feed, swapped(feed))
     return (

time: 431 us -> 423 us (0.981)
  the two profiles are of different devices: /device:TPU:1 before, /device:TPU:7 now
where the time goes in v4:
time: 423 us; the launch traced here: 414 us
  Pallas kernels  159 us (38%)
  waiting for transfers between devices  130 us (31%)
  starting transfers between devices  53.6 us (13%)
  local copies, waits for them, and re-layouts  36.2 us (9%)
  between operations  20.3 us (5%)
  other arithmetic  15.2 us (4%)
    all_gather x1, waiting for transfers between devices, body(): lax.all_gather(feed, ('z', 'x'), axis=0, tiled=True).reshape(16, 80, 640)  53.7 us
    pallas_call x2, Pallas kernels, attend_back(): pl.pallas_call(attend_back_kernel, out_shape=(far(nq, 384), far(win, 384)...  42.5 us
    ppermute x8, waiting for transfers between devices, passed_along(): lax.ppermute(array, ('z', 'x'), [(i, i + by) for i in range(devices) if 0...  36.3 us
    unnamed x114, local copies, waits for them, and re-layouts  31.7 us
    pallas_call x1, Pallas kernels, feed_forward(): call(feed_kernel, (shape(2, 512, 640), shape(2, 512, 640), shape(16, 4, 8...  31.5 us
    pallas_call x2, Pallas kernels, attend(): pl.pallas_call(attend_kernel, out_shape=(jax.ShapeDtypeStruct((384, nq),...  28.5 us
    reduce_scatter x1, waiting for transfers between devices, body(): lax.psum_scatter(feed_grads.reshape(5120, 640), ('z', 'x'), scatter_dimen...  27.3 us
    pallas_call x1, Pallas kernels, project_back(): call(project_back_kernel, (shape(5, 2, 256, 640), shape(5, 2, 256, 640),...  22 us
  transfers between devices with their start and end apart: 35, of which 13 were waited for; matrix products, arithmetic and copies ran while one was open for 4% of the time, Pallas kernels for 30%

profile of v4, /device:TPU:7, one launch (start us, length us, event | category | flops | bytes accessed | tf_op | source)
XLA Modules:
  0.0 414.2 jit_solution(2513450361003797314)
XLA Ops:
  12.1 3.5 collective-permute-start
  18.7 11.0 %collective-permute-done.refs_1_ = bf16[2,256,640]{2,1,0:T(8,128)(2,1)S(1)} collective-permute-done((bf16[2,256,640]{2,1,0:T(8,128)(2,1)S(1)}, bf16[2,256,640]{2,1,0:T(8,128)(2,1)S(1)}, u32[]{:S(2)}, u32[]{:S(2)}) %collective-permute-start) | collective-permute-done | bytes 655392 | tf_op jit(solution)/shard_map/ppermute | solution.py:622
  29.7 5.2 %collective-permute-done.1.refs_3_ = bf16[2,256,640]{2,1,0:T(8,128)(2,1)S(1)} collective-permute-done((bf16[2,256,640]{2,1,0:T(8,128)(2,1)S(1)}, bf16[2,256,640]{2,1,0:T(8,128)(2,1)S(1)}, u32[]{:S(2)}, u32[]{:S(2)}) %collective-permute-start.1) | collective-permute-done | bytes 655392 | tf_op jit(solution)/shard_map/ppermute | solution.py:622
  35.6 5.9 %all-gather.4.cloned.1.call-done.vec_ref.refs_8_.refs_6_.refs_11_ = bf16[640,1280]{1,0:T(8,128)(2,1)} async-done(((bf16[160,1280]{1,0:T(8,128)(2,1)}), bf16[640,1280]{1,0:T(8,128)(2,1)}) %all-gather.4.cloned.1.call-update) | async-done | bytes 1638416 | tf_op jit(solution)/shard_map/all_gather | solution.py:677
  57.9 3.2 collective-permute-start.8
  64.6 13.0 %project.2 = (bf16[2,2560,384]{2,1,0:T(8,128)(2,1)}, bf16[2,2560,384]{2,1,0:T(8,128)(2,1)}, bf16[2,384,2560]{2,1,0:T(8,128)(2,1)}, bf16[2,384,2560]{2,1,0:T(8,12...) custom-call(s32[6]{0:T(128)S(1)} %stack.85.refs_0_.place_ref.core_ref, ...), custom_call_target="tpu_custom_call" | custom-call | flops 100000000 | tf_op jit(solution)/shard_map/project/pallas_call | solution.py:366
  77.6 3.3 collective-permute-done.9.refs_2_.refs_4_
  85.6 7.7 %project.3 = (bf16[2,2560,384]{2,1,0:T(8,128)(2,1)}, bf16[2,2560,384]{2,1,0:T(8,128)(2,1)}, bf16[2,384,2560]{2,1,0:T(8,128)(2,1)}, bf16[2,384,2560]{2,1,0:T(8,128)(2,1)}) custom-call(s32[6]{0:T(128)S(1)} %stack.85.refs_0_.place_ref.core_ref, ...), custom_call_target="tpu_custom_call", output_to_operand_aliasing={{0}: (7, {}), {1}: (8, {}), {2}: (9, {}), {3}: (10, {})} | custom-call | flops 100000000 | tf_op jit(solution)/shard_map/project/pallas_call | solution.py:366
  93.3 14.3 %attend.2 = (f32[384,512]{1,0:T(8,128)S(1)}, bf16[512,384]{1,0:T(8,128)(2,1)S(1)}, f32[5,8,512]{2,1,0:T(8,128)S(1)}) custom-call(s32[5]{0:T(128)S(1)} %stack.90.info_ref, bf16[2,384,512]{2,1,0:T(8,128)(2,1)} %get-tuple-element.123.qT_ref, bf16[2,2560,384]{2,1,0:T(8,128)(2,1)} %get-tuple-element.119.k_ref, bf16[2,384,2560]{2,1,0:T(8,128)(2,1)} %get-tuple-element.120.vT_ref, ...), custom_call_target="tpu_custom_call" | custom-call | flops 400000000 | tf_op jit(solution)/shard_map/attend/pallas_call | solution.py:98
  109.2 14.2 %attend.3 = (f32[384,512]{1,0:T(8,128)S(1)}, bf16[512,384]{1,0:T(8,128)(2,1)S(1)}, f32[5,8,512]{2,1,0:T(8,128)S(1)}) custom-call(s32[5]{0:T(128)S(1)} %stack.95.info_ref, bf16[2,384,512]{2,1,0:T(8,128)(2,1)} %get-tuple-element.123.qT_ref, bf16[2,2560,384]{2,1,0:T(8,128)(2,1)} %get-tuple-element.119.k_ref, bf16[2,384,2560]{2,1,0:T(8,128)(2,1)} %get-tuple-element.120.vT_ref, ...), custom_call_target="tpu_custom_call" | custom-call | flops 400000000 | tf_op jit(solution)/shard_map/attend/pallas_call | solution.py:98
  125.9 3.8 middle.1
  136.7 31.5 %feed_forward.1 = (bf16[2,512,640]{2,1,0:T(8,128)(2,1)}, bf16[2,512,640]{2,1,0:T(8,128)(2,1)}, bf16[16,4,80,640]{3,2,1,0:T(8,128)(2,1)}) custom-call(bf16[512,640]{1,0:T(8,128)(2,1)S(1)} %copy-done.43, bf16[512,640]{1,0:T(8,128)(2,1)S(1)} %copy-done.45, bf16[512,640]{1,0:T(8,128)(2,1)S(1)} %bitcast.113, bf16[512,640]{1,0:T(8,128)(2,1)} %collective-permute-done.13.cot2_ref, ...), custom_call_target="tpu_custom_call" | custom-call | flops 600000000 | tf_op jit(solution)/shard_map/feed_forward/pallas_call | solution.py:442
  182.3 21.3 %attend_back.3 = (bf16[512,384]{1,0:T(8,128)(2,1)}, bf16[2560,384]{1,0:T(8,128)(2,1)}, bf16[2560,384]{1,0:T(8,128)(2,1)}) custom-call(s32[5]{0:T(128)S(1)} %stack.95.info_ref, bf16[2,384,512]{2,1,0:T(8,128)(2,1)} %get-tuple-element.123.qT_ref, bf16[2,512,384]{2,1,0:T(8,128)(2,1)} %get-tuple-element.136.q_ref, ...), custom_call_target="tpu_custom_call" | custom-call | flops 800000000 | tf_op jit(solution)/shard_map/attend_back/pallas_call | solution.py:211
  203.6 21.2 %attend_back.2 = (bf16[512,384]{1,0:T(8,128)(2,1)}, bf16[2560,384]{1,0:T(8,128)(2,1)}, bf16[2560,384]{1,0:T(8,128)(2,1)}) custom-call(s32[5]{0:T(128)S(1)} %stack.90.info_ref, bf16[2,384,512]{2,1,0:T(8,128)(2,1)} %get-tuple-element.123.qT_ref, bf16[2,512,384]{2,1,0:T(8,128)(2,1)} %get-tuple-element.136.q_ref, ...), custom_call_target="tpu_custom_call" | custom-call | flops 800000000 | tf_op jit(solution)/shard_map/attend_back/pallas_call | solution.py:211
  224.8 27.3 %reduce-scatter.3.cloned.1.call-done = bf16[320,640]{1,0:T(8,128)(2,1)} async-done(((bf16[5120,640]{1,0:T(8,128)(2,1)}), bf16[320,640]{1,0:T(8,128)(2,1)}) %reduce-scatter.3.cloned.1.call-update) | async-done | bytes 409616 | tf_op jit(solution)/shard_map/reduce_scatter | solution.py:701
  257.8 22.0 %project_back.1 = (bf16[5,2,256,640]{3,2,1,0:T(8,128)(2,1)S(1)}, bf16[5,2,256,640]{3,2,1,0:T(8,128)(2,1)S(1)}, bf16[64,40,384]{2,1,0:T(8,128)(2,1)S(1)}) custom-call(s32[6]{0:T(128)S(1)} %stack.85.refs_0_.place_ref.core_ref, bf16[2,256,640]{2,1,0:T(8,128)(2,1)} %collective-permute-done.8.refs_1_.refs_0_, bf16[2,256,640]{2,1,0:T(8,128)(2,1)S(1)} %copy-done.14, ...), custom_call_target="tpu_custom_call" | custom-call | flops 200000000 | tf_op jit(solution)/shard_map/project_back/pallas_call | solution.py:564
  286.3 7.7 %all-to-all-start = ((bf16[64,40,384]{2,1,0:T(8,128)(2,1)}), bf16[64,40,384]{2,1,0:T(8,128)(2,1)}, u32[]{:S(2)}, u32[]{:S(2)}) async-start(bf16[64,40,384]{2,1,0:T(8,128)(2,1)} %copy-done.21), calls=%async_computation.2 | async-start | bytes 3932160 | tf_op jit(solution)/shard_map/all_to_all | solution.py:714
  294.3 3.1 fusion.11
  303.1 53.7 %all-gather.8.cloned.1.call-done = bf16[1280,640]{1,0:T(8,128)(2,1)} async-done(((bf16[80,640]{1,0:T(8,128)(2,1)}), bf16[1280,640]{1,0:T(8,128)(2,1)}) %all-gather.8.cloned.1.call-update) | async-done | bytes 1638416 | tf_op jit(solution)/shard_map/all_gather | solution.py:715
  365.3 3.1 collective-permute-start.22
  370.7 11.9 %collective-permute-done.22 = bf16[2,256,640]{2,1,0:T(8,128)(2,1)S(1)} collective-permute-done((bf16[2,256,640]{2,1,0:T(8,128)(2,1)S(1)}, bf16[2,256,640]{2,1,0:T(8,128)(2,1)S(1)}, u32[]{:S(2)}, u32[]{:S(2)}) %collective-permute-start.22) | collective-permute-done | bytes 655392 | tf_op jit(solution)/shard_map/ppermute | solution.py:622
  382.6 5.0 %collective-permute-done.23 = bf16[2,256,640]{2,1,0:T(8,128)(2,1)S(1)} collective-permute-done((bf16[2,256,640]{2,1,0:T(8,128)(2,1)S(1)}, bf16[2,256,640]{2,1,0:T(8,128)(2,1)S(1)}, u32[]{:S(2)}, u32[]{:S(2)}) %collective-permute-start.23) | collective-permute-done | bytes 655392 | tf_op jit(solution)/shard_map/ppermute | solution.py:622
  395.9 3.6 collective-permute-start.27
  402.2 3.1 final_feed.1
  (231 shorter events, 94.5 us)
Async XLA Ops:
  7.2 34.4 %all-gather.4.cloned.1.call-start = ((), (), s32[]{:S(2)}) async-start(), calls=%async_computation.3 | async-start | bytes 2048000 | tf_op jit(solution)/shard_map/all_gather | solution.py:677
  12.0 121.5 %all-gather.6.cloned.1.call-start = ((), (), s32[]{:S(2)}) async-start(), calls=%async_computation.4 | async-start | bytes 8192000 | tf_op jit(solution)/shard_map/all_gather | solution.py:679
  12.1 17.6 %collective-permute-start = (bf16[2,256,640]{2,1,0:T(8,128)(2,1)S(1)}, bf16[2,256,640]{2,1,0:T(8,128)(2,1)S(1)}, u32[]{:S(2)}, u32[]{:S(2)}) collective-permute-start(bf16[2,256,640]{2,1,0:T(8,128)(2,1)S(1)} %bitcast.104), channel_id=1, source_target_pairs={{0,2},{2,4},{4,6},{6,8},{8,10},{10,12},{12,14},{14,16},{16,18},{18... | collective-permute-start | bytes 1966088 | tf_op jit(solution)/shard_map/ppermute | solution.py:622
  15.5 19.3 %collective-permute-start.1 = (bf16[2,256,640]{2,1,0:T(8,128)(2,1)S(1)}, bf16[2,256,640]{2,1,0:T(8,128)(2,1)S(1)}, u32[]{:S(2)}, u32[]{:S(2)}) collective-permute-start(bf16[2,256,640]{2,1,0:T(8,128)(2,1)S(1)} %bitcast.105), channel_id=1, source_target_pairs={{2,0},{4,2},{6,4},{8,6},{10,8},{12,10},{14,12},{16,14},{18,16},{20... | collective-permute-start | bytes 1966088 | tf_op jit(solution)/shard_map/ppermute | solution.py:622
  17.5 17.4 %collective-permute-start.2 = (bf16[2,256,640]{2,1,0:T(8,128)(2,1)S(1)}, bf16[2,256,640]{2,1,0:T(8,128)(2,1)S(1)}, u32[]{:S(2)}, u32[]{:S(2)}) collective-permute-start(bf16[2,256,640]{2,1,0:T(8,128)(2,1)S(1)} %bitcast.106), channel_id=1, source_target_pairs={{0,1},{1,0},{2,3},{3,2},{4,5},{5,4},{6,7},{7,6},{8,9},{9,8},{10,11... | collective-permute-start | bytes 1966088 | tf_op jit(solution)/shard_map/ppermute | solution.py:626
  45.7 206.3 %reduce-scatter.3.cloned.1.call-start = ((), (), s32[]{:S(2)}) async-start(), calls=%async_computation.5 | async-start | bytes 6963200 | tf_op jit(solution)/shard_map/reduce_scatter | solution.py:701
  45.8 63.3 %collective-permute-start.5 = (bf16[160,640]{1,0:T(8,128)(2,1)}, bf16[160,640]{1,0:T(8,128)(2,1)}, u32[]{:S(2)}, u32[]{:S(2)}) collective-permute-start(bf16[160,640]{1,0:T(8,128)(2,1)} %w0_ref.1), channel_id=1, source_target_pairs={{0,32},{32,64},{64,96},{96,0},{1,33},{33,65},{65,97},{97,1},{2,34}... | collective-permute-start | bytes 614408 | tf_op jit(solution)/shard_map/ppermute | solution.py:617
  46.0 63.1 %collective-permute-start.6 = (bf16[160,640]{1,0:T(8,128)(2,1)}, bf16[160,640]{1,0:T(8,128)(2,1)}, u32[]{:S(2)}, u32[]{:S(2)}) collective-permute-start(bf16[160,640]{1,0:T(8,128)(2,1)} %w0_ref.1), channel_id=1, source_target_pairs={{0,64},{32,96},{64,0},{96,32},{1,65},{33,97},{65,1},{97,33},{2,66}... | collective-permute-start | bytes 614408 | tf_op jit(solution)/shard_map/ppermute | solution.py:617
  47.9 61.2 %collective-permute-start.7 = (bf16[160,640]{1,0:T(8,128)(2,1)}, bf16[160,640]{1,0:T(8,128)(2,1)}, u32[]{:S(2)}, u32[]{:S(2)}) collective-permute-start(bf16[160,640]{1,0:T(8,128)(2,1)} %w0_ref.1), channel_id=1, source_target_pairs={{0,96},{32,0},{64,32},{96,64},{1,97},{33,1},{65,33},{97,65},{2,98}... | collective-permute-start | bytes 614408 | tf_op jit(solution)/shard_map/ppermute | solution.py:617
  49.1 8.8 %collective-permute-start.3 = (bf16[2,256,640]{2,1,0:T(8,128)(2,1)}, bf16[2,256,640]{2,1,0:T(8,128)(2,1)}, u32[]{:S(2)}, u32[]{:S(2)}) collective-permute-start(bf16[2,256,640]{2,1,0:T(8,128)(2,1)} %copy-done.12), channel_id=1, source_target_pairs={{0,1},{1,0},{2,3},{3,2},{4,5},{5,4},{6,7},{7,6},{8,9},{9,8},{10,11... | collective-permute-start | bytes 1966088 | tf_op jit(solution)/shard_map/ppermute | solution.py:626
  57.9 19.7 %collective-permute-start.8 = (bf16[2,256,640]{2,1,0:T(8,128)(2,1)}, bf16[2,256,640]{2,1,0:T(8,128)(2,1)}, u32[]{:S(2)}, u32[]{:S(2)}) collective-permute-start(bf16[2,256,640]{2,1,0:T(8,128)(2,1)} %copy-done.12), channel_id=1, source_target_pairs={{0,2},{2,4},{4,6},{6,8},{8,10},{10,12},{12,14},{14,16},{16,18},{18... | collective-permute-start | bytes 1966088 | tf_op jit(solution)/shard_map/ppermute | solution.py:622
  61.1 19.8 %collective-permute-start.9 = (bf16[2,256,640]{2,1,0:T(8,128)(2,1)}, bf16[2,256,640]{2,1,0:T(8,128)(2,1)}, u32[]{:S(2)}, u32[]{:S(2)}) collective-permute-start(bf16[2,256,640]{2,1,0:T(8,128)(2,1)} %copy-done.15), channel_id=1, source_target_pairs={{2,0},{4,2},{6,4},{8,6},{10,8},{12,10},{14,12},{16,14},{18,16},{20... | collective-permute-start | bytes 1966088 | tf_op jit(solution)/shard_map/ppermute | solution.py:622
  168.2 116.3 %reduce-scatter.5.cloned.1.call-start = ((), (), s32[]{:S(2)}) async-start(), calls=%async_computation.6 | async-start | bytes 512000 | tf_op jit(solution)/shard_map/reduce_scatter | solution.py:709
  252.1 104.6 %all-gather.8.cloned.1.call-start = ((), (), s32[]{:S(2)}) async-start(), calls=%async_computation.7 | async-start | bytes 1740800 | tf_op jit(solution)/shard_map/all_gather | solution.py:715
  284.5 9.8 %collective-permute-start.16 = (bf16[5,2,256,640]{3,2,1,0:T(8,128)(2,1)}, bf16[5,2,256,640]{3,2,1,0:T(8,128)(2,1)}, u32[]{:S(2)}, u32[]{:S(2)}) collective-permute-start(bf16[5,2,256,640]{3,2,1,0:T(8,128)(2,1)} %copy-done.53), channel_id=1, source_target_pairs={{0,1},{1,0},{2,3},{3,2},{4,5},{5,4},{6,7},{7,6},{8,9},{9,8},{10,11... | collective-permute-start | bytes 9830408 | tf_op jit(solution)/shard_map/ppermute | solution.py:626
  286.3 72.1 %all-to-all-start = ((bf16[64,40,384]{2,1,0:T(8,128)(2,1)}), bf16[64,40,384]{2,1,0:T(8,128)(2,1)}, u32[]{:S(2)}, u32[]{:S(2)}) async-start(bf16[64,40,384]{2,1,0:T(8,128)(2,1)} %copy-done.21), calls=%async_computation.2 | async-start | bytes 3932160 | tf_op jit(solution)/shard_map/all_to_all | solution.py:714
  297.4 61.0 %collective-permute-start.17 = (bf16[2,256,640]{2,1,0:T(8,128)(2,1)}, bf16[2,256,640]{2,1,0:T(8,128)(2,1)S(1)}, u32[]{:S(2)}, u32[]{:S(2)}) collective-permute-start(bf16[2,256,640]{2,1,0:T(8,128)(2,1)} %get-tuple-element.230), channel_id=1, source_target_pairs={{0,2},{2,4},{4,6},{6,8},{8,10},{10,12},{12,14},{14,16},{16,18},{18... | collective-permute-start | bytes 1966088 | tf_op jit(solution)/shard_map/ppermute | solution.py:622
  300.5 57.9 %collective-permute-start.18 = (bf16[2,256,640]{2,1,0:T(8,128)(2,1)}, bf16[2,256,640]{2,1,0:T(8,128)(2,1)}, u32[]{:S(2)}, u32[]{:S(2)}) collective-permute-start(bf16[2,256,640]{2,1,0:T(8,128)(2,1)} %get-tuple-element.229), channel_id=1, source_target_pairs={{2,0},{4,2},{6,4},{8,6},{10,8},{12,10},{14,12},{16,14},{18,16},{20... | collective-permute-start | bytes 1966088 | tf_op jit(solution)/shard_map/ppermute | solution.py:622
  356.8 42.8 %collective-permute-start.28 = (bf16[16,80,640]{2,1,0:T(8,128)(2,1)}, bf16[16,80,640]{2,1,0:T(8,128)(2,1)S(1)}, u32[]{:S(2)}, u32[]{:S(2)}) collective-permute-start(bf16[16,80,640]{2,1,0:T(8,128)(2,1)} %bitcast.117), channel_id=1, source_target_pairs={{0,1},{1,0},{2,3},{3,2},{4,5},{5,4},{6,7},{7,6},{8,9},{9,8},{10,11... | collective-permute-start | bytes 4915208 | tf_op jit(solution)/shard_map/ppermute | solution.py:626
  361.1 9.6 %collective-permute-start.20 = (bf16[40,384]{1,0:T(8,128)(2,1)S(1)}, bf16[40,384]{1,0:T(8,128)(2,1)S(1)}, u32[]{:S(2)}, u32[]{:S(2)}) collective-permute-start(bf16[40,384]{1,0:T(8,128)(2,1)S(1)} %reduce_sum.48), channel_id=1, source_target_pairs={{0,6},{2,0},{4,2},{6,4},{1,7},{3,1},{5,3},{7,5},{8,14},{10,8},{12,... | collective-permute-start | bytes 92168 | tf_op jit(solution)/shard_map/ppermute | solution.py:617
  361.8 8.9 %collective-permute-start.21 = (bf16[40,384]{1,0:T(8,128)(2,1)S(1)}, bf16[40,384]{1,0:T(8,128)(2,1)S(1)}, u32[]{:S(2)}, u32[]{:S(2)}) collective-permute-start(bf16[40,384]{1,0:T(8,128)(2,1)S(1)} %reduce_sum.48), channel_id=1, source_target_pairs={{0,4},{2,6},{4,0},{6,2},{1,5},{3,7},{5,1},{7,3},{8,12},{10,14},{12... | collective-permute-start | bytes 92168 | tf_op jit(solution)/shard_map/ppermute | solution.py:617
  365.3 17.3 %collective-permute-start.22 = (bf16[2,256,640]{2,1,0:T(8,128)(2,1)S(1)}, bf16[2,256,640]{2,1,0:T(8,128)(2,1)S(1)}, u32[]{:S(2)}, u32[]{:S(2)}) collective-permute-start(bf16[2,256,640]{2,1,0:T(8,128)(2,1)S(1)} %get-tuple-element.228), channel_id=1, source_target_pairs={{0,2},{2,4},{4,6},{6,8},{8,10},{10,12},{12,14},{14,16},{16,18},{18... | collective-permute-start | bytes 1966088 | tf_op jit(solution)/shard_map/ppermute | solution.py:622
  368.5 19.1 %collective-permute-start.23 = (bf16[2,256,640]{2,1,0:T(8,128)(2,1)S(1)}, bf16[2,256,640]{2,1,0:T(8,128)(2,1)S(1)}, u32[]{:S(2)}, u32[]{:S(2)}) collective-permute-start(bf16[2,256,640]{2,1,0:T(8,128)(2,1)S(1)} %get-tuple-element.227), channel_id=1, source_target_pairs={{2,0},{4,2},{6,4},{8,6},{10,8},{12,10},{14,12},{16,14},{18,16},{20... | collective-permute-start | bytes 1966088 | tf_op jit(solution)/shard_map/ppermute | solution.py:622
  395.9 9.3 %collective-permute-start.27 = (bf16[16,40,384]{2,1,0:T(8,128)(2,1)S(1)}, bf16[16,40,384]{2,1,0:T(8,128)(2,1)S(1)}, u32[]{:S(2)}, u32[]{:S(2)}) collective-permute-start(bf16[16,40,384]{2,1,0:T(8,128)(2,1)S(1)} %bitcast.115), channel_id=1, source_target_pairs={{0,1},{1,0},{2,3},{3,2},{4,5},{5,4},{6,7},{7,6},{8,9},{9,8},{10,11... | collective-permute-start | bytes 1474568 | tf_op jit(solution)/shard_map/ppermute | solution.py:626
  (66 other events, 348.7 us)
Sparse Core Ops, SparseCore 0:
  12.1 29.3 all-gather.3
  45.9 67.7 all-gather.5
  168.4 83.6 reduce-scatter.2
  254.5 19.4 reduce-scatter.4
  286.4 70.2 all-gather.7

commit v5 on v4

--- a/solution.py
+++ b/solution.py
@@ -201,7 +201,7 @@
 
 def attend_back(m, info, qT, q, k, kT, v, doT, do, oT, lse, kaug, qaugT):
     win, nq = k.shape[1], qT.shape[2]
-    qT, q, k, kT, v = stay(qT, q, k, kT, v)
+    qT, q, k, kT, v, doT, do = stay(qT, q, k, kT, v, doT, do)
     wide = pl.BlockSpec((128, nq), lambda p, *_: (p // 2, 0))
     tall = pl.BlockSpec((nq, 128), lambda p, *_: (0, p // 2))
     keys = pl.BlockSpec((win, 128), lambda p, *_: (0, p // 2))
@@ -250,8 +250,8 @@
     return jax.ShapeDtypeStruct(dims, dtype)
 
 
-def far(*dims):
-    return pltpu.MemorySpace.HBM(dims, bf16)
+def far(*dims, dtype=bf16):
+    return pltpu.MemorySpace.HBM(dims, dtype)
 
 
 def stay(*arrays):
@@ -289,16 +289,17 @@
                 in_specs=[pl.BlockSpec((640, 128), lambda i: (0, 9))], out_specs=full(16, 640))(heads)
 
 
-def pack_feed_kernel(core_ref, up_ref, down_ref, feed_ref):
+def pack_feed_kernel(core_ref, out_ref, up_ref, down_ref, feed_ref):
     core = core_ref[0]
+    feed_ref[:, 5120:5760] = out_ref[...]
     for f in range(4):
         feed_ref[:, 640 * f:640 * (f + 1)] = up_ref[:, pl.ds(pl.multiple_of(1280 * f + 640 * core, 128), 640)]
         feed_ref[:, 2560 + 640 * f:2560 + 640 * (f + 1)] = down_ref[pl.ds(pl.multiple_of(640 * core + 160 * f, 32), 160), :]
 
 
-def pack_feed(core, w_up, w_down):
-    return call(pack_feed_kernel, shape(160, 5120), "pack_feed", 10**6, 16, **scalar_first(
-        (1,), [full(160, 5120), full(1280, 640)], full(160, 5120)))(core, w_up, w_down)
+def pack_feed(core, w_out, w_up, w_down):
+    return call(pack_feed_kernel, far(160, 5760), "pack_feed", 10**6, 16, **scalar_first(
+        (1,), [full(160, 640), full(160, 5120), full(1280, 640)], full(160, 5760)))(core, *stay(w_out, w_up, w_down))
 
 
 def rows_in_order(core, mine, theirs, x_ref):
@@ -367,7 +368,7 @@
         lambda *refs: project_kernel(chips, *refs), shapes, "project", 5 * 10**9, 28,
         input_output_aliases={2 * n + 3 + i: i for i in range(len(earlier))}, **scalar_first(
             (2, n), [full(2, 256, 640)] * (2 * n) + [full(16, 640), full(640, 1152)] + [pl.BlockSpec(memory_space=pl.ANY)] * len(earlier),
-            specs, [pltpu.VMEM((512, 640), f32), pltpu.VMEM((512, 640), bf16)]))(place, *own, *other, vec, w, *earlier)
+            specs, [pltpu.VMEM((512, 640), f32), pltpu.VMEM((512, 640), bf16)]))(place, *own, *other, vec, *stay(w), *earlier)
 
 
 def heads_joined(core, mine, theirs):
@@ -375,11 +376,8 @@
     return jnp.concatenate([first[:, :256], second[:, :256], first[:, 256:] + second[:, 256:]], axis=1)
 
 
-def middle_kernel(place_ref, low0_ref, low1_ref, theirs_ref, tok_ref, tok2_ref, vec_ref, w0_ref, w1_ref, w2_ref, w3_ref,
-                  mid_ref, hid_ref, hid2_ref, w_ref):
-    core = place_ref[0]
-    for by, part in enumerate((w0_ref, w1_ref, w2_ref, w3_ref)):
-        w_ref[pl.ds(pl.multiple_of(lax.rem(place_ref[5] + 4 - by, 4) * 160, 32), 160), :] = part[...]
+def middle_kernel(core_ref, w_ref, low0_ref, low1_ref, theirs_ref, tok_ref, tok2_ref, vec_ref, mid_ref, hid_ref, hid2_ref):
+    core = core_ref[0]
     for m, low_ref in enumerate((low0_ref, low1_ref)):
         attended = heads_joined(core, low_ref[...].astype(f32), theirs_ref[m].astype(f32)).astype(bf16)
         branch = jnp.dot(attended, w_ref[...], preferred_element_type=f32)
@@ -391,9 +389,12 @@
         hid2_ref[part, :] = (moments(theirs)[0] * vec_ref[2:3, :] + vec_ref[3:4, :]).astype(bf16)
 
 
-def middle_step(place, *args):
-    return call(middle_kernel, (shape(512, 640, dtype=f32), shape(512, 640), shape(512, 640), shape(640, 640)), "middle", 10**9, 20, **scalar_first(
-        (1,), [full(*a.shape) for a in args], [full(512, 640)] * 3 + [full(640, 640)]))(place, *args)
+W_OUT = pl.BlockSpec((640, 640), lambda *_: (0, 8))
+
+
+def middle_step(core, weights, *args):
+    return call(middle_kernel, (far(512, 640, dtype=f32), far(512, 640), far(512, 640)), "middle", 10**9, 20, **scalar_first(
+        (1,), [W_OUT] + [full(*a.shape) for a in args], [full(512, 640)] * 3))(core, *stay(weights), *args)
 
 
 def feed_kernel(h_ref, h2_ref, cot_ref, cot2_ref, up_ref, down_ref, mine_ref, theirs_ref, g_ref, h, cot, hT, cT, out, dh):
@@ -441,32 +442,36 @@
 def feed_forward(h, h2, cot, cot2, weights):
     return call(
         feed_kernel,
-        (shape(2, 512, 640), shape(2, 512, 640), shape(16, 4, 80, 640)),
+        (far(2, 512, 640), far(2, 512, 640), far(16, 4, 80, 640)),
         "feed_forward", 30 * 10**9, 52, grid=(2,),
         in_specs=[full(512, 640)] * 4 + [pl.BlockSpec((640, 1280), lambda f: (0, f)), pl.BlockSpec((320, 2560), lambda f: (f, 1))],
         out_specs=[full(2, 512, 640), full(2, 512, 640), full(16, 4, 80, 640)],
         scratch_shapes=[pltpu.VMEM((1024, 640), bf16), pltpu.VMEM((1024, 640), bf16), pltpu.VMEM((640, 1024), bf16), pltpu.VMEM((640, 1024), bf16),
                         pltpu.VMEM((1024, 640), f32), pltpu.VMEM((1024, 640), f32)],
-    )(h, h2, cot, cot2, weights, weights)
+    )(*stay(h, h2, cot), cot2, *stay(weights, weights))
 
 
 def after_kernel(mid_ref, mine_ref, theirs_ref, cot_ref, vec_ref, block_ref, grad_ref, branch_ref, g_ref):
+    @pl.when(pl.program_id(0) == 0)
+    def _():
+        g_ref[...] = jnp.zeros_like(g_ref)
+
     middle = mid_ref[...]
     block_ref[...] = (middle + mine_ref[0].astype(f32) + theirs_ref[0].astype(f32)).astype(bf16)
     d_hidden = mine_ref[1].astype(f32) + theirs_ref[1].astype(f32)
     n, r = moments(middle)
-    g_ref[...] = jnp.zeros_like(g_ref)
-    g_ref[0:1, :] = jnp.sum(d_hidden * n, axis=0, keepdims=True)
-    g_ref[1:2, :] = jnp.sum(d_hidden, axis=0, keepdims=True)
+    g_ref[0:1, :] += jnp.sum(d_hidden * n, axis=0, keepdims=True)
+    g_ref[1:2, :] += jnp.sum(d_hidden, axis=0, keepdims=True)
     grad = cot_ref[...].astype(f32) + norm_back(d_hidden, n, r, vec_ref[2:3, :])
     grad_ref[...] = grad
     branch_ref[...] = grad.astype(bf16)
 
 
 def after_feed(*args):
+    rows, pair = pl.BlockSpec((128, 640), lambda i: (i, 0)), pl.BlockSpec((2, 128, 640), lambda i: (0, i, 0))
     return call(
-        after_kernel, (shape(512, 640), shape(512, 640, dtype=f32), shape(512, 640), shape(8, 640, dtype=f32)), "after_feed", 10**9, 24,
-        in_specs=[pl.BlockSpec(memory_space=pltpu.VMEM)] * 5, out_specs=[pl.BlockSpec(memory_space=pltpu.VMEM)] * 4)(*args)
+        after_kernel, (far(512, 640), far(512, 640, dtype=f32), shape(512, 640), shape(8, 640, dtype=f32)), "after_feed", 10**9, 16,
+        grid=(4,), in_specs=[rows, pair, pair, rows, full(16, 640)], out_specs=[rows, rows, rows, full(8, 640)])(*stay(args[0], args[1]), args[2], *stay(args[3]), args[4])
 
 
 def branch_kernel(core_ref, own_ref, their_ref, w_ref, low0_ref, low1_ref, theirs_ref, do_ref, doT_ref, g_ref):
@@ -488,11 +493,11 @@
     g_ref[...] = g
 
 
-def branch_step(core, *args):
-    specs = [full(*a.shape) for a in args]
+def branch_step(core, own, their, weights, *args):
     return call(
-        branch_kernel, (shape(1024, 384), shape(384, 1024), shape(640, 384, dtype=f32)), "branch", 10**9, 24, **scalar_first(
-            (1,), specs, [full(1024, 384), full(384, 1024), full(640, 384)]))(core, *args)
+        branch_kernel, (far(1024, 384), far(384, 1024), far(640, 384, dtype=f32)), "branch", 10**9, 24, **scalar_first(
+            (1,), [full(512, 640)] * 2 + [W_OUT] + [full(*a.shape) for a in args], [full(1024, 384), full(384, 1024), full(640, 384)]))(
+                core, own, their, *stay(weights), *args)
 
 
 def project_back_kernel(core_ref, *refs):
@@ -558,7 +563,7 @@
 
 
 def project_back(core, own, other, vec, w, dq, dk, dv, g_out, g_two):
-    dk, dv = stay(*dk), stay(*dv)
+    dq, dk, dv, (g_out,) = stay(*dq), stay(*dk), stay(*dv), stay(g_out)
     first = pl.BlockSpec((512, 384), lambda b, *_: (jnp.minimum(b, 4), 0))
     second = pl.BlockSpec((512, 384), lambda b, *_: (jnp.maximum(b - 5, 0), 0))
     return call(
@@ -567,7 +572,7 @@
                                                full(640, 384), full(8, 640)],
             [pl.BlockSpec((1, 1, 256, 640), lambda b, *_: (lax.rem(b, 5), b // 5, 0, 0))] * 2 + [full(64, 40, 384)],
             [pltpu.VMEM((512, 640), f32), pltpu.VMEM((512, 768), bf16), pltpu.VMEM((512, 384), bf16),
-             pltpu.VMEM((512, 640), f32), pltpu.VMEM((640, 1152), f32), pltpu.VMEM((8, 640), f32)]))(core, *own, *other, vec, w, *dq, *dk, *dv, g_out, g_two)
+             pltpu.VMEM((512, 640), f32), pltpu.VMEM((640, 1152), f32), pltpu.VMEM((8, 640), f32)]))(core, *own, *other, vec, *stay(w), *dq, *dk, *dv, g_out, g_two)
 
 
 def in_core_order(core_ref, mine, theirs):
@@ -675,33 +680,29 @@
     vectors = jnp.pad(jnp.stack([gain_one, bias_one, gain_two, bias_two], axis=1), ((0, 0), (0, 124)))
     before, after, tok_other = passed_along(tok, 1), passed_along(tok, -1), swapped(tok)
     heads = lax.all_gather(pack_heads(core_arg, w_qkv, vectors), "batch", axis=0, tiled=True)
-    heads, before, after, tok_other, w_up, w_down = together(heads, before, after, tok_other, w_up, w_down)
-    feed_weights = lax.all_gather(pack_feed(core_arg, w_up, w_down), "batch", axis=0, tiled=True)
+    windows = [window_info(lengths[m, 0], chip, core, 2560) for m in range(2)]
+    place = jnp.stack([core] + windows[0][3] + windows[1][3]).astype(jnp.int32)
+    feed_pack = pack_feed(core_arg, w_out, w_up, w_down)
+    before, after, tok_other, feed_pack, place, windows = together(before, after, tok_other, feed_pack, place, windows)
+    own = [passed_along(before, 1), before, tok, after, passed_along(after, -1)]
+    other = [None, swapped(before), tok_other, swapped(after), None]
+    heads, feed_pack = together(heads, feed_pack)
+    feed_weights = lax.all_gather(feed_pack, "batch", axis=0, tiled=True)
     vec = vector_rows(heads)
-    windows = [window_info(lengths[m, 0], chip, core, 2560) for m in range(2)]
-    place = jnp.stack([core] + windows[0][3] + windows[1][3] + [lax.axis_index("batch")]).astype(jnp.int32)
-    own, other = [None, before, tok, after, None], [None, swapped(before), tok_other, swapped(after), None]
-    before, after, place, own[1:4], other[1:4] = together(before, after, place, own[1:4], other[1:4])
-    own[0], own[4] = passed_along(before, 1), passed_along(after, -1)
     *near_parts, q, qT = project((1, 2, 3), place, own, other, vec, heads)
     own[0], own[4], near_parts = together(own[0], own[4], near_parts)
     other[0], other[4] = swapped(own[0]), swapped(own[4])
     k, v, kT, vT = project((0, 4), place, own, other, vec, heads, near_parts)
-    w_out_parts = [shifted(w_out, "batch", by) for by in (1, 2, 3)]
-    info, key_rows, query_rows, _ = windows[0]
-    oT0, low0, lse0 = attend(0, info, qT, k, vT, key_rows, query_rows)
-    w_out_parts, qT_next, low0 = together(w_out_parts, qT, low0)
-    w_out_parts = [w_out] + w_out_parts
-    info, key_rows, query_rows, _ = windows[1]
-    oT1, low1, lse1 = attend(1, info, qT_next, k, vT, key_rows, query_rows)
+    (oT0, low0, lse0), (oT1, low1, lse1) = (
+        attend(m, info, qT, k, vT, key_rows, query_rows) for m, (info, key_rows, query_rows, _) in enumerate(windows))
 
     theirs = swapped(jnp.stack([low0, low1]))
-    middle, hidden_two, hidden_other, w_out_all = middle_step(place, low0, low1, theirs, tok, tok_other, vec, *w_out_parts)
+    middle, hidden_two, hidden_other = middle_step(core_arg, feed_weights, low0, low1, theirs, tok, tok_other, vec)
     mine, partial, feed_grads = feed_forward(hidden_two, hidden_other, cot, swapped(cot), feed_weights)
     feed_grads = lax.psum_scatter(feed_grads.reshape(5120, 640), ("z", "x"), scatter_dimension=0, tiled=True)
     block_out, grad_middle, branch, g_two = after_feed(middle, mine, swapped(partial), cot, vec)
 
-    do, doT, g_out = branch_step(core_arg, branch, swapped(branch), w_out_all, low0, low1, theirs)
+    do, doT, g_out = branch_step(core_arg, branch, swapped(branch), feed_weights, low0, low1, theirs)
     dq, dk, dv = zip(*(
         attend_back(m, info, qT, q, k, kT, v, doT, do, oT, lse, key_rows, query_rows)
         for m, ((info, key_rows, query_rows, _), oT, lse) in enumerate(zip(windows, (oT0, oT1), (lse0, lse1)))))
@@ -725,7 +726,7 @@
     d_one = (sums[2] + right.astype(f32) + left.astype(f32)).reshape(512, 640)
     n_one, r_one = moments(tok.reshape(512, 640).astype(f32))
     grad_tokens = (grad_middle + norm_back(d_one, n_one, r_one, vec[0:1])).astype(bf16)
-    tail, grad_tokens = together(tail, grad_tokens)
+    tail, grad_tokens, feed = together(tail, grad_tokens, feed)
     grad_qkv, grad_out, spare = final_heads(core_arg, tail, swapped(tail))
     grad_up, grad_down = final_feed(core_arg, feed, swapped(feed))
     return (

time: 423 us -> 397 us (0.939)
  the two profiles are of different devices: /device:TPU:7 before, /device:TPU:1 now
where the time goes in v5:
time: 397 us; the launch traced here: 391 us
  Pallas kernels  156 us (39%)
  waiting for transfers between devices  128 us (32%)
  starting transfers between devices  51.3 us (13%)
  local copies, waits for them, and re-layouts  21.9 us (6%)
  between operations  20.3 us (5%)
  other arithmetic  13.3 us (3%)
    pallas_call x2, Pallas kernels, attend_back(): pl.pallas_call(attend_back_kernel, out_shape=(far(nq, 384), far(win, 384)...  39 us
    ppermute x8, waiting for transfers between devices, passed_along(): lax.ppermute(array, ('z', 'x'), [(i, i + by) for i in range(devices) if 0...  34.2 us
    pallas_call x1, Pallas kernels, feed_forward(): call(feed_kernel, (far(2, 512, 640), far(2, 512, 640), far(16, 4, 80, 640...  32.1 us
    reduce_scatter x1, waiting for transfers between devices, body(): lax.psum_scatter(feed_grads.reshape(5120, 640), ('z', 'x'), scatter_dimen...  28.2 us
    pallas_call x2, Pallas kernels, attend(): pl.pallas_call(attend_kernel, out_shape=(jax.ShapeDtypeStruct((384, nq),...  25.8 us
    all_to_all x1, waiting for transfers between devices, body(): tail = lax.all_to_all(tail, ('batch', 'z', 'x'), 0, 0, tiled=True)  20.4 us
    pallas_call x1, Pallas kernels, project_back(): call(project_back_kernel, (shape(5, 2, 256, 640), shape(5, 2, 256, 640),...  18.8 us
    pallas_call x2, Pallas kernels, project(): call(lambda *refs: project_kernel(chips, *refs), shapes, 'project', 5 * 1...  18.4 us
  transfers between devices with their start and end apart: 32, of which 16 were waited for; matrix products, arithmetic and copies ran while one was open for 5% of the time, Pallas kernels for 31%

profile of v5, /device:TPU:1, one launch (start us, length us, event | category | flops | bytes accessed | tf_op | source)
XLA Modules:
  0.0 390.6 jit_solution(1997990959091714991)
XLA Ops:
  7.2 4.0 %collective-permute-start = (bf16[2,256,640]{2,1,0:T(8,128)(2,1)}, bf16[2,256,640]{2,1,0:T(8,128)(2,1)S(1)}, u32[]{:S(2)}, u32[]{:S(2)}) collective-permute-start(bf16[2,256,640]{2,1,0:T(8,128)(2,1)} %bitcast.103), channel_id=1, source_target_pairs={{0,2},{2,4},{4,6},{6,8},{8,10},{10,12},{12,14},{14,16},{16,18},{18... | collective-permute-start | bytes 1966088 | tf_op jit(solution)/shard_map/ppermute | solution.py:627
  18.3 3.4 pack_feed.1
  31.3 17.7 %all-gather.4.cloned.1.call-done.vec_ref.refs_8_.refs_6_.refs_11_ = bf16[640,1280]{1,0:T(8,128)(2,1)} async-done(((bf16[160,1280]{1,0:T(8,128)(2,1)}), bf16[640,1280]{1,0:T(8,128)(2,1)}) %all-gather.4.cloned.1.call-update) | async-done | bytes 1638416 | tf_op jit(solution)/shard_map/all_gather | solution.py:682
  49.9 3.1 collective-permute-start.5
  55.9 12.0 %project.2 = (bf16[2,2560,384]{2,1,0:T(8,128)(2,1)}, bf16[2,2560,384]{2,1,0:T(8,128)(2,1)}, bf16[2,384,2560]{2,1,0:T(8,128)(2,1)}, bf16[2,384,2560]{2,1,0:T(8,12...) custom-call(s32[5]{0:T(128)S(1)} %stack.81.refs_0_.core_ref, ...), custom_call_target="tpu_custom_call" | custom-call | flops 100000000 | tf_op jit(solution)/shard_map/project/pallas_call | solution.py:367
  75.0 6.4 %project.3 = (bf16[2,2560,384]{2,1,0:T(8,128)(2,1)}, bf16[2,2560,384]{2,1,0:T(8,128)(2,1)}, bf16[2,384,2560]{2,1,0:T(8,128)(2,1)}, bf16[2,384,2560]{2,1,0:T(8,128)(2,1)}) custom-call(s32[5]{0:T(128)S(1)} %stack.81.refs_0_.core_ref, ...), custom_call_target="tpu_custom_call", output_to_operand_aliasing={{0}: (7, {}), {1}: (8, {}), {2}: (9, {}), {3}: (10, {})} | custom-call | flops 100000000 | tf_op jit(solution)/shard_map/project/pallas_call | solution.py:367
  81.4 14.1 %attend.3 = (f32[384,512]{1,0:T(8,128)S(1)}, bf16[512,384]{1,0:T(8,128)(2,1)S(1)}, f32[5,8,512]{2,1,0:T(8,128)S(1)}) custom-call(s32[5]{0:T(128)S(1)} %stack.91.info_ref, bf16[2,384,512]{2,1,0:T(8,128)(2,1)} %get-tuple-element.96.qT_ref, bf16[2,2560,384]{2,1,0:T(8,128)(2,1)} %get-tuple-element.107.k_ref, bf16[2,384,2560]{2,1,0:T(8,128)(2,1)} %get-tuple-element.108.vT_ref, ...), custom_call_target="tpu_custom_call" | custom-call | flops 400000000 | tf_op jit(solution)/shard_map/attend/pallas_call | solution.py:98
  96.4 11.7 %attend.2 = (f32[384,512]{1,0:T(8,128)S(1)}, bf16[512,384]{1,0:T(8,128)(2,1)S(1)}, f32[5,8,512]{2,1,0:T(8,128)S(1)}) custom-call(s32[5]{0:T(128)S(1)} %stack.86.info_ref, bf16[2,384,512]{2,1,0:T(8,128)(2,1)} %get-tuple-element.96.qT_ref, bf16[2,2560,384]{2,1,0:T(8,128)(2,1)} %get-tuple-element.107.k_ref, bf16[2,384,2560]{2,1,0:T(8,128)(2,1)} %get-tuple-element.108.vT_ref, ...), custom_call_target="tpu_custom_call" | custom-call | flops 400000000 | tf_op jit(solution)/shard_map/attend/pallas_call | solution.py:98
  111.5 14.3 %all-gather.6.cloned.1.call-done.w_ref.up_ref.down_ref = bf16[640,5760]{1,0:T(8,128)(2,1)} async-done(((bf16[160,5760]{1,0:T(8,128)(2,1)}), bf16[640,5760]{1,0:T(8,128)(2,1)}) %all-gather.6.cloned.1.call-update) | async-done | bytes 7372816 | tf_op jit(solution)/shard_map/all_gather | solution.py:690
  127.0 4.4 %middle.1 = (f32[512,640]{1,0:T(8,128)}, bf16[512,640]{1,0:T(8,128)(2,1)}, bf16[512,640]{1,0:T(8,128)(2,1)}) custom-call(s32[1]{0:T(128)} %bitcast.core_ref, bf16[640,5760]{1,0:T(8,128)(2,1)} %all-gather.6.cloned.1.call-done.w_ref.up_ref.down_ref, bf16[512,384]{1,0:T(8,128)(2,1)S(1)} %get-tuple-element.111.low0_ref, ...), custom_call_target="tpu_custom_call" | custom-call | flops 20000000 | tf_op jit(solution)/shard_map/middle/pallas_call | solution.py:396
  131.4 32.1 %feed_forward.1 = (bf16[2,512,640]{2,1,0:T(8,128)(2,1)}, bf16[2,512,640]{2,1,0:T(8,128)(2,1)}, bf16[16,4,80,640]{3,2,1,0:T(8,128)(2,1)}) custom-call(bf16[512,640]{1,0:T(8,128)(2,1)} %get-tuple-element.117.h_ref, bf16[512,640]{1,0:T(8,128)(2,1)} %get-tuple-element.118.h2_ref, bf16[512,640]{1,0:T(8,128)(2,1)} %bitcast.20.cot_ref, ...), custom_call_target="tpu_custom_call" | custom-call | flops 600000000 | tf_op jit(solution)/shard_map/feed_forward/pallas_call | solution.py:443
  167.2 4.7 %after_feed.1 = (bf16[512,640]{1,0:T(8,128)(2,1)}, f32[512,640]{1,0:T(8,128)}, bf16[512,640]{1,0:T(8,128)(2,1)S(1)}, f32[8,640]{1,0:T(8,128)S(1)}) custom-call(f32[512,640]{1,0:T(8,128)} %get-tuple-element.116.mid_ref, bf16[2,512,640]{2,1,0:T(8,128)(2,1)} %get-tuple-element.119.mine_ref, bf16[2,512,640]{2,1,0:T(8,128)(2,1)S(1)} %collective-permute-done.11.theirs_ref, ...), custom_call_target="tpu_custom_call" | custom-call | flops 20000000 | tf_op jit(solution)/shard_map/after_feed/pallas_call | solution.py:472
  174.1 4.1 %branch.1 = (bf16[1024,384]{1,0:T(8,128)(2,1)}, bf16[384,1024]{1,0:T(8,128)(2,1)}, f32[640,384]{1,0:T(8,128)}) custom-call(s32[1]{0:T(128)} %bitcast.core_ref, bf16[512,640]{1,0:T(8,128)(2,1)S(1)} %get-tuple-element.125.own_ref, bf16[512,640]{1,0:T(8,128)(2,1)S(1)} %collective-permute-done.12.their_ref, ...), custom_call_target="tpu_custom_call" | custom-call | flops 20000000 | tf_op jit(solution)/shard_map/branch/pallas_call | solution.py:497
  178.2 22.1 %attend_back.3 = (bf16[512,384]{1,0:T(8,128)(2,1)}, bf16[2560,384]{1,0:T(8,128)(2,1)}, bf16[2560,384]{1,0:T(8,128)(2,1)}) custom-call(s32[5]{0:T(128)S(1)} %copy-done.36, bf16[2,384,512]{2,1,0:T(8,128)(2,1)} %get-tuple-element.96.qT_ref, bf16[2,512,384]{2,1,0:T(8,128)(2,1)} %get-tuple-element.122.q_ref, bf16[2,2560,384]{2,1,0:T(8,128)(2,1)} %get-tuple-element.107.k_ref, ...), custom_call_target="tpu_custom_call" | custom-call | flops 800000000 | tf_op jit(solution)/shard_map/attend_back/pallas_call | solution.py:211
  200.3 16.9 %attend_back.2 = (bf16[512,384]{1,0:T(8,128)(2,1)}, bf16[2560,384]{1,0:T(8,128)(2,1)}, bf16[2560,384]{1,0:T(8,128)(2,1)}) custom-call(s32[5]{0:T(128)S(1)} %copy-done.34, bf16[2,384,512]{2,1,0:T(8,128)(2,1)} %get-tuple-element.96.qT_ref, bf16[2,512,384]{2,1,0:T(8,128)(2,1)} %get-tuple-element.122.q_ref, bf16[2,2560,384]{2,1,0:T(8,128)(2,1)} %get-tuple-element.107.k_ref, ...), custom_call_target="tpu_custom_call" | custom-call | flops 800000000 | tf_op jit(solution)/shard_map/attend_back/pallas_call | solution.py:211
  217.2 28.2 %reduce-scatter.3.cloned.1.call-done = bf16[320,640]{1,0:T(8,128)(2,1)} async-done(((bf16[5120,640]{1,0:T(8,128)(2,1)}), bf16[320,640]{1,0:T(8,128)(2,1)}) %reduce-scatter.3.cloned.1.call-update) | async-done | bytes 409616 | tf_op jit(solution)/shard_map/reduce_scatter | solution.py:702
  250.8 18.8 %project_back.1 = (bf16[5,2,256,640]{3,2,1,0:T(8,128)(2,1)S(1)}, bf16[5,2,256,640]{3,2,1,0:T(8,128)(2,1)S(1)}, bf16[64,40,384]{2,1,0:T(8,128)(2,1)S(1)}) custom-call(s32[5]{0:T(128)S(1)} %stack.81.refs_0_.core_ref, bf16[2,256,640]{2,1,0:T(8,128)(2,1)S(1)} %copy-done.13, bf16[2,256,640]{2,1,0:T(8,128)(2,1)S(1)} %copy-done.7, ...), custom_call_target="tpu_custom_call" | custom-call | flops 200000000 | tf_op jit(solution)/shard_map/project_back/pallas_call | solution.py:569
  276.1 13.1 %all-to-all-start = ((bf16[64,40,384]{2,1,0:T(8,128)(2,1)}), bf16[64,40,384]{2,1,0:T(8,128)(2,1)S(1)}, u32[]{:S(2)}, u32[]{:S(2)}) async-start(bf16[64,40,384]{2,1,0:T(8,128)(2,1)} %copy-done.20), calls=%async_computation.2 | async-start | bytes 3932160 | tf_op jit(solution)/shard_map/all_to_all | solution.py:715
  297.3 20.4 %all-to-all-done = bf16[64,40,384]{2,1,0:T(8,128)(2,1)S(1)} async-done(((bf16[64,40,384]{2,1,0:T(8,128)(2,1)}), bf16[64,40,384]{2,1,0:T(8,128)(2,1)S(1)}, u32[]{:S(2)}, u32[]{:S(2)}) %all-to-all-start) | async-done | bytes 1966112 | tf_op jit(solution)/shard_map/all_to_all | solution.py:715
  317.6 8.1 %collective-permute-done.14 = bf16[2,256,640]{2,1,0:T(8,128)(2,1)S(1)} collective-permute-done((bf16[2,256,640]{2,1,0:T(8,128)(2,1)}, bf16[2,256,640]{2,1,0:T(8,128)(2,1)S(1)}, u32[]{:S(2)}, u32[]{:S(2)}) %collective-permute-start.14) | collective-permute-done | bytes 655392 | tf_op jit(solution)/shard_map/ppermute | solution.py:627
  338.6 15.6 %collective-permute-done.19 = bf16[2,256,640]{2,1,0:T(8,128)(2,1)S(1)} collective-permute-done((bf16[2,256,640]{2,1,0:T(8,128)(2,1)S(1)}, bf16[2,256,640]{2,1,0:T(8,128)(2,1)S(1)}, u32[]{:S(2)}, u32[]{:S(2)}) %collective-permute-start.19) | collective-permute-done | bytes 655392 | tf_op jit(solution)/shard_map/ppermute | solution.py:627
  354.2 5.9 %collective-permute-done.20 = bf16[2,256,640]{2,1,0:T(8,128)(2,1)S(1)} collective-permute-done((bf16[2,256,640]{2,1,0:T(8,128)(2,1)S(1)}, bf16[2,256,640]{2,1,0:T(8,128)(2,1)S(1)}, u32[]{:S(2)}, u32[]{:S(2)}) %collective-permute-start.20) | collective-permute-done | bytes 655392 | tf_op jit(solution)/shard_map/ppermute | solution.py:627
  373.6 3.6 collective-permute-done.24.theirs_ref
  380.8 3.1 final_feed.1
  (195 shorter events, 82.8 us)
Async XLA Ops:
  7.2 41.8 %all-gather.4.cloned.1.call-start = ((), (), s32[]{:S(2)}) async-start(), calls=%async_computation.3 | async-start | bytes 2048000 | tf_op jit(solution)/shard_map/all_gather | solution.py:682
  7.2 24.0 %collective-permute-start = (bf16[2,256,640]{2,1,0:T(8,128)(2,1)}, bf16[2,256,640]{2,1,0:T(8,128)(2,1)S(1)}, u32[]{:S(2)}, u32[]{:S(2)}) collective-permute-start(bf16[2,256,640]{2,1,0:T(8,128)(2,1)} %bitcast.103), channel_id=1, source_target_pairs={{0,2},{2,4},{4,6},{6,8},{8,10},{10,12},{12,14},{14,16},{16,18},{18... | collective-permute-start | bytes 1966088 | tf_op jit(solution)/shard_map/ppermute | solution.py:627
  11.2 20.0 %collective-permute-start.1 = (bf16[2,256,640]{2,1,0:T(8,128)(2,1)}, bf16[2,256,640]{2,1,0:T(8,128)(2,1)}, u32[]{:S(2)}, u32[]{:S(2)}) collective-permute-start(bf16[2,256,640]{2,1,0:T(8,128)(2,1)} %bitcast.104), channel_id=1, source_target_pairs={{2,0},{4,2},{6,4},{8,6},{10,8},{12,10},{14,12},{16,14},{18,16},{20... | collective-permute-start | bytes 1966088 | tf_op jit(solution)/shard_map/ppermute | solution.py:627
  12.5 18.8 %collective-permute-start.2 = (bf16[2,256,640]{2,1,0:T(8,128)(2,1)}, bf16[2,256,640]{2,1,0:T(8,128)(2,1)S(1)}, u32[]{:S(2)}, u32[]{:S(2)}) collective-permute-start(bf16[2,256,640]{2,1,0:T(8,128)(2,1)} %bitcast.105), channel_id=1, source_target_pairs={{0,1},{1,0},{2,3},{3,2},{4,5},{5,4},{6,7},{7,6},{8,9},{9,8},{10,11... | collective-permute-start | bytes 1966088 | tf_op jit(solution)/shard_map/ppermute | solution.py:631
  18.3 107.6 %all-gather.6.cloned.1.call-start = ((), (), s32[]{:S(2)}) async-start(), calls=%async_computation.4 | async-start | bytes 9216000 | tf_op jit(solution)/shard_map/all_gather | solution.py:690
  49.0 196.3 %reduce-scatter.3.cloned.1.call-start = ((), (), s32[]{:S(2)}) async-start(), calls=%async_computation.5 | async-start | bytes 6963200 | tf_op jit(solution)/shard_map/reduce_scatter | solution.py:702
  49.1 6.8 %collective-permute-start.3 = (bf16[2,256,640]{2,1,0:T(8,128)(2,1)S(1)}, bf16[2,256,640]{2,1,0:T(8,128)(2,1)S(1)}, u32[]{:S(2)}, u32[]{:S(2)}) collective-permute-start(bf16[2,256,640]{2,1,0:T(8,128)(2,1)S(1)} %collective-permute-done.refs_1_), channel_id=1, source_target_pairs={{0,1},{1,0},{2,3},{3,2},{4,5},{5,4},{6,7},{7,6},{8,9},{9,8},{10,11... | collective-permute-start | bytes 1966088 | tf_op jit(solution)/shard_map/ppermute | solution.py:631
  49.9 18.1 %collective-permute-start.5 = (bf16[2,256,640]{2,1,0:T(8,128)(2,1)S(1)}, bf16[2,256,640]{2,1,0:T(8,128)(2,1)S(1)}, u32[]{:S(2)}, u32[]{:S(2)}) collective-permute-start(bf16[2,256,640]{2,1,0:T(8,128)(2,1)S(1)} %collective-permute-done.refs_1_), channel_id=1, source_target_pairs={{0,2},{2,4},{4,6},{6,8},{8,10},{10,12},{12,14},{14,16},{16,18},{18... | collective-permute-start | bytes 1966088 | tf_op jit(solution)/shard_map/ppermute | solution.py:627
  53.0 17.8 %collective-permute-start.6 = (bf16[2,256,640]{2,1,0:T(8,128)(2,1)}, bf16[2,256,640]{2,1,0:T(8,128)(2,1)S(1)}, u32[]{:S(2)}, u32[]{:S(2)}) collective-permute-start(bf16[2,256,640]{2,1,0:T(8,128)(2,1)} %collective-permute-done.1.refs_3_), channel_id=1, source_target_pairs={{2,0},{4,2},{6,4},{8,6},{10,8},{12,10},{14,12},{16,14},{18,16},{20... | collective-permute-start | bytes 1966088 | tf_op jit(solution)/shard_map/ppermute | solution.py:627
  109.0 22.4 %collective-permute-start.10 = (bf16[512,640]{1,0:T(8,128)(2,1)}, bf16[512,640]{1,0:T(8,128)(2,1)}, u32[]{:S(2)}, u32[]{:S(2)}) collective-permute-start(bf16[512,640]{1,0:T(8,128)(2,1)} %bitcast.20.cot_ref), channel_id=1, source_target_pairs={{0,1},{1,0},{2,3},{3,2},{4,5},{5,4},{6,7},{7,6},{8,9},{9,8},{10,11... | collective-permute-start | bytes 1966088 | tf_op jit(solution)/shard_map/ppermute | solution.py:631
  163.5 110.8 %reduce-scatter.5.cloned.1.call-start = ((), (), s32[]{:S(2)}) async-start(), calls=%async_computation.6 | async-start | bytes 512000 | tf_op jit(solution)/shard_map/reduce_scatter | solution.py:710
  274.3 15.2 %collective-permute-start.13 = (bf16[5,2,256,640]{3,2,1,0:T(8,128)(2,1)}, bf16[5,2,256,640]{3,2,1,0:T(8,128)(2,1)}, u32[]{:S(2)}, u32[]{:S(2)}) collective-permute-start(bf16[5,2,256,640]{3,2,1,0:T(8,128)(2,1)} %copy-done.37), channel_id=1, source_target_pairs={{0,1},{1,0},{2,3},{3,2},{4,5},{5,4},{6,7},{7,6},{8,9},{9,8},{10,11... | collective-permute-start | bytes 9830408 | tf_op jit(solution)/shard_map/ppermute | solution.py:631
  276.1 41.5 %all-to-all-start = ((bf16[64,40,384]{2,1,0:T(8,128)(2,1)}), bf16[64,40,384]{2,1,0:T(8,128)(2,1)S(1)}, u32[]{:S(2)}, u32[]{:S(2)}) async-start(bf16[64,40,384]{2,1,0:T(8,128)(2,1)} %copy-done.20), calls=%async_computation.2 | async-start | bytes 3932160 | tf_op jit(solution)/shard_map/all_to_all | solution.py:715
  289.2 82.2 %all-gather.8.cloned.1.call-start = ((), (), s32[]{:S(2)}) async-start(), calls=%async_computation.7 | async-start | bytes 1740800 | tf_op jit(solution)/shard_map/all_gather | solution.py:716
  292.5 33.2 %collective-permute-start.14 = (bf16[2,256,640]{2,1,0:T(8,128)(2,1)}, bf16[2,256,640]{2,1,0:T(8,128)(2,1)S(1)}, u32[]{:S(2)}, u32[]{:S(2)}) collective-permute-start(bf16[2,256,640]{2,1,0:T(8,128)(2,1)} %get-tuple-element.216), channel_id=1, source_target_pairs={{0,2},{2,4},{4,6},{6,8},{8,10},{10,12},{12,14},{14,16},{16,18},{18... | collective-permute-start | bytes 1966088 | tf_op jit(solution)/shard_map/ppermute | solution.py:627
  295.5 32.0 %collective-permute-start.15 = (bf16[2,256,640]{2,1,0:T(8,128)(2,1)}, bf16[2,256,640]{2,1,0:T(8,128)(2,1)}, u32[]{:S(2)}, u32[]{:S(2)}) collective-permute-start(bf16[2,256,640]{2,1,0:T(8,128)(2,1)} %get-tuple-element.215), channel_id=1, source_target_pairs={{2,0},{4,2},{6,4},{8,6},{10,8},{12,10},{14,12},{16,14},{18,16},{20... | collective-permute-start | bytes 1966088 | tf_op jit(solution)/shard_map/ppermute | solution.py:627
  327.7 10.8 %collective-permute-start.16 = (bf16[40,384]{1,0:T(8,128)(2,1)S(1)}, bf16[40,384]{1,0:T(8,128)(2,1)S(1)}, u32[]{:S(2)}, u32[]{:S(2)}) collective-permute-start(bf16[40,384]{1,0:T(8,128)(2,1)S(1)} %reduce_sum.48), channel_id=1, source_target_pairs={{0,2},{2,4},{4,6},{6,0},{1,3},{3,5},{5,7},{7,1},{8,10},{10,12},{12... | collective-permute-start | bytes 92168 | tf_op jit(solution)/shard_map/ppermute | solution.py:622
  329.0 9.6 %collective-permute-start.17 = (bf16[40,384]{1,0:T(8,128)(2,1)S(1)}, bf16[40,384]{1,0:T(8,128)(2,1)S(1)}, u32[]{:S(2)}, u32[]{:S(2)}) collective-permute-start(bf16[40,384]{1,0:T(8,128)(2,1)S(1)} %reduce_sum.48), channel_id=1, source_target_pairs={{0,6},{2,0},{4,2},{6,4},{1,7},{3,1},{5,3},{7,5},{8,14},{10,8},{12,... | collective-permute-start | bytes 92168 | tf_op jit(solution)/shard_map/ppermute | solution.py:622
  330.9 7.7 %collective-permute-start.18 = (bf16[40,384]{1,0:T(8,128)(2,1)S(1)}, bf16[40,384]{1,0:T(8,128)(2,1)S(1)}, u32[]{:S(2)}, u32[]{:S(2)}) collective-permute-start(bf16[40,384]{1,0:T(8,128)(2,1)S(1)} %reduce_sum.48), channel_id=1, source_target_pairs={{0,4},{2,6},{4,0},{6,2},{1,5},{3,7},{5,1},{7,3},{8,12},{10,14},{12... | collective-permute-start | bytes 92168 | tf_op jit(solution)/shard_map/ppermute | solution.py:622
  334.4 19.9 %collective-permute-start.19 = (bf16[2,256,640]{2,1,0:T(8,128)(2,1)S(1)}, bf16[2,256,640]{2,1,0:T(8,128)(2,1)S(1)}, u32[]{:S(2)}, u32[]{:S(2)}) collective-permute-start(bf16[2,256,640]{2,1,0:T(8,128)(2,1)S(1)} %get-tuple-element.214), channel_id=1, source_target_pairs={{0,2},{2,4},{4,6},{6,8},{8,10},{10,12},{12,14},{14,16},{16,18},{18... | collective-permute-start | bytes 1966088 | tf_op jit(solution)/shard_map/ppermute | solution.py:627
  337.2 22.9 %collective-permute-start.20 = (bf16[2,256,640]{2,1,0:T(8,128)(2,1)S(1)}, bf16[2,256,640]{2,1,0:T(8,128)(2,1)S(1)}, u32[]{:S(2)}, u32[]{:S(2)}) collective-permute-start(bf16[2,256,640]{2,1,0:T(8,128)(2,1)S(1)} %get-tuple-element.213), channel_id=1, source_target_pairs={{2,0},{4,2},{6,4},{8,6},{10,8},{12,10},{14,12},{16,14},{18,16},{20... | collective-permute-start | bytes 1966088 | tf_op jit(solution)/shard_map/ppermute | solution.py:627
  360.1 9.5 %collective-permute-start.21 = (bf16[160,384]{1,0:T(8,128)(2,1)S(1)}, bf16[160,384]{1,0:T(8,128)(2,1)S(1)}, u32[]{:S(2)}, u32[]{:S(2)}) collective-permute-start(bf16[160,384]{1,0:T(8,128)(2,1)S(1)} %bitcast.117), channel_id=1, source_target_pairs={{0,8},{8,16},{16,24},{24,0},{1,9},{9,17},{17,25},{25,1},{2,10},{10... | collective-permute-start | bytes 368648 | tf_op jit(solution)/shard_map/ppermute | solution.py:622
  364.6 6.7 %collective-permute-start.23 = (bf16[160,384]{1,0:T(8,128)(2,1)S(1)}, bf16[160,384]{1,0:T(8,128)(2,1)S(1)}, u32[]{:S(2)}, u32[]{:S(2)}) collective-permute-start(bf16[160,384]{1,0:T(8,128)(2,1)S(1)} %bitcast.119), channel_id=1, source_target_pairs={{0,16},{8,24},{16,0},{24,8},{1,17},{9,25},{17,1},{25,9},{2,18},{10... | collective-permute-start | bytes 368648 | tf_op jit(solution)/shard_map/ppermute | solution.py:622
  371.4 8.0 %collective-permute-start.25 = (bf16[16,80,640]{2,1,0:T(8,128)(2,1)}, bf16[16,80,640]{2,1,0:T(8,128)(2,1)S(1)}, u32[]{:S(2)}, u32[]{:S(2)}) collective-permute-start(bf16[16,80,640]{2,1,0:T(8,128)(2,1)} %bitcast.113), channel_id=1, source_target_pairs={{0,1},{1,0},{2,3},{3,2},{4,5},{5,4},{6,7},{7,6},{8,9},{9,8},{10,11... | collective-permute-start | bytes 4915208 | tf_op jit(solution)/shard_map/ppermute | solution.py:631
  (48 other events, 551.2 us)
Sparse Core Ops, SparseCore 0:
  18.4 30.5 all-gather.3
  51.2 74.5 all-gather.5
  163.6 81.6 reduce-scatter.2
  247.7 19.1 reduce-scatter.4
  297.4 62.6 all-gather.7

commit v6 on v5

--- a/solution.py
+++ b/solution.py
@@ -503,9 +503,30 @@
 def project_back_kernel(core_ref, *refs):
     own_refs, other_refs = refs[:5], refs[5:10]
     (vec_ref, w_ref, dq0_ref, dq1_ref, dk0_ref, dk1_ref, dv0_ref, dv1_ref, g_out_ref, g_two_ref,
-     mine_ref, theirs_ref, tail_ref, x_ref, d_kv, d_q, d_hid, g_ref, g_vec) = refs[10:]
+     mine_ref, theirs_ref, tail_ref, x_ref, d_kv, d_q, d_hid, g_ref, g_vec, slots, arrived) = refs[10:]
     step, core = pl.program_id(0), core_ref[0]
     block = lax.rem(step, 5)
+
+    def copies(at, j, m, slot):
+        for i, refs_of in enumerate((own_refs, other_refs)):
+            getattr(pltpu.make_async_copy(refs_of[j].at[m], slots.at[slot, i], arrived.at[slot, i]), at)()
+
+    def fetch(number):
+        for j in range(5):
+            for m in range(2):
+                @pl.when(number == 5 * m + j)
+                def _():
+                    copies("start", j, m, lax.rem(number, 2))
+
+    @pl.when(step == 0)
+    def _():
+        fetch(step)
+
+    copies("wait", 0, 0, lax.rem(step, 2))
+
+    @pl.when(step < 9)
+    def _():
+        fetch(step + 1)
 
     @pl.when(step == 0)
     def _():
@@ -524,7 +545,7 @@
     for m, (dq, dk, dv) in enumerate(((dq0_ref, dk0_ref, dv0_ref), (dq1_ref, dk1_ref, dv1_ref))):
         @pl.when(needed & (second == m))
         def _():
-            window_rows(core, own_refs, other_refs, m, block, x_ref)
+            rows_in_order(core, slots[lax.rem(step, 2), 0], slots[lax.rem(step, 2), 1], x_ref)
             d_kv[:, :384], d_kv[:, 384:] = dk[...], dv[...]
             d_q[...] = dq[...]
 
@@ -568,11 +589,12 @@
     second = pl.BlockSpec((512, 384), lambda b, *_: (jnp.maximum(b - 5, 0), 0))
     return call(
         project_back_kernel, (shape(5, 2, 256, 640), shape(5, 2, 256, 640), shape(64, 40, 384)), "project_back", 10**10, 36, **scalar_first(
-            (10,), [full(2, 256, 640)] * 10 + [full(16, 640), full(640, 1152), full(512, 384), full(512, 384), first, second, first, second,
+            (10,), [pl.BlockSpec(memory_space=pl.ANY)] * 10 + [full(16, 640), full(640, 1152), full(512, 384), full(512, 384), first, second, first, second,
                                                full(640, 384), full(8, 640)],
             [pl.BlockSpec((1, 1, 256, 640), lambda b, *_: (lax.rem(b, 5), b // 5, 0, 0))] * 2 + [full(64, 40, 384)],
             [pltpu.VMEM((512, 640), f32), pltpu.VMEM((512, 768), bf16), pltpu.VMEM((512, 384), bf16),
-             pltpu.VMEM((512, 640), f32), pltpu.VMEM((640, 1152), f32), pltpu.VMEM((8, 640), f32)]))(core, *own, *other, vec, *stay(w), *dq, *dk, *dv, g_out, g_two)
+             pltpu.VMEM((512, 640), f32), pltpu.VMEM((640, 1152), f32), pltpu.VMEM((8, 640), f32),
+             pltpu.VMEM((2, 2, 256, 640), bf16), pltpu.SemaphoreType.DMA((2, 2))]))(core, *stay(*own, *other), vec, *stay(w), *dq, *dk, *dv, g_out, g_two)
 
 
 def in_core_order(core_ref, mine, theirs):
@@ -678,8 +700,9 @@
     together = lambda *arrays: lax.optimization_barrier(arrays)
 
     vectors = jnp.pad(jnp.stack([gain_one, bias_one, gain_two, bias_two], axis=1), ((0, 0), (0, 124)))
+    heads, tok = together(pack_heads(core_arg, w_qkv, vectors), tok)
+    heads = lax.all_gather(heads, "batch", axis=0, tiled=True)
     before, after, tok_other = passed_along(tok, 1), passed_along(tok, -1), swapped(tok)
-    heads = lax.all_gather(pack_heads(core_arg, w_qkv, vectors), "batch", axis=0, tiled=True)
     windows = [window_info(lengths[m, 0], chip, core, 2560) for m in range(2)]
     place = jnp.stack([core] + windows[0][3] + windows[1][3]).astype(jnp.int32)
     feed_pack = pack_feed(core_arg, w_out, w_up, w_down)
@@ -706,24 +729,21 @@
     dq, dk, dv = zip(*(
         attend_back(m, info, qT, q, k, kT, v, doT, do, oT, lse, key_rows, query_rows)
         for m, ((info, key_rows, query_rows, _), oT, lse) in enumerate(zip(windows, (oT0, oT1), (lse0, lse1)))))
-    dq, feed_grads = together(dq, feed_grads)
+    mine, theirs, tail = project_back(place, own, other, vec, heads, dq, dk, dv, g_out, g_two)
+    feed_grads, mine, theirs, tail = together(feed_grads, mine, theirs, tail)
+
     feed = lax.psum_scatter(feed_grads, "batch", scatter_dimension=0, tiled=True).reshape(80, 640)
-    mine, theirs, tail = project_back(place, own, other, vec, heads, dq, dk, dv, g_out, g_two)
-
-    feed, mine, theirs, tail = together(feed, mine, theirs, tail)
-
     tail = lax.all_to_all(tail, ("batch", "z", "x"), 0, 0, tiled=True)
     feed = lax.all_gather(feed, ("z", "x"), axis=0, tiled=True).reshape(16, 80, 640)
     theirs = swapped(theirs)
     sums = [mine[j].astype(f32) + theirs[j].astype(f32) for j in range(5)]
-    right, left = passed_along(sums[4].astype(bf16), 1), passed_along(sums[0].astype(bf16), -1)
-    tail, right, left = together(tail, right, left)
-    right = passed_along((right.astype(f32) + sums[3]).astype(bf16), 1)
-    left = passed_along((left.astype(f32) + sums[1]).astype(bf16), -1)
+    returned = [passed_along(sums[2 + by].astype(bf16), by) for by in (1, -1, 2, -2)]
+    tail, sums[2] = together(tail, sums[2])
     tail = gathered(jnp.sum(tail.astype(f32), axis=0).astype(bf16), "x").reshape(160, 384)
-    tail, right, left = together(tail, right, left)
+    tail, returned[0], returned[1] = together(tail, returned[0], returned[1])
     tail = gathered(tail, "z").reshape(16, 40, 384)
-    d_one = (sums[2] + right.astype(f32) + left.astype(f32)).reshape(512, 640)
+    tail, returned = together(tail, returned)
+    d_one = sum((part.astype(f32) for part in returned), sums[2]).reshape(512, 640)
     n_one, r_one = moments(tok.reshape(512, 640).astype(f32))
     grad_tokens = (grad_middle + norm_back(d_one, n_one, r_one, vec[0:1])).astype(bf16)
     tail, grad_tokens, feed = together(tail, grad_tokens, feed)

time: 397 us -> 400 us (level)
  starting transfers between devices: 51.3 us -> 63.4 us
  waiting for transfers between devices: 128 us -> 116 us
  Pallas kernels: 156 us -> 167 us
  local copies, waits for them, and re-layouts: 21.9 us -> 16.2 us
    reduce_scatter x1, waiting for transfers between devices: 0.01 us -> 31.6 us  [body(): lax.psum_scatter(feed_grads, 'batch', scatter_dimension=0, tiled=True)]
    reduce_scatter x1, waiting for transfers between devices: 28.2 us -> 0.01 us  [body(): lax.psum_scatter(feed_grads.reshape(5120, 640), ('z', 'x'), scatter_dimen...]
    all_to_all x1, waiting for transfers between devices: 20.4 us -> 0.01 us  [body(): tail = lax.all_to_all(tail, ('batch', 'z', 'x'), 0, 0, tiled=True)]
    ppermute x6, waiting for transfers between devices: 1.63 us -> 13.2 us  [shifted(): lax.ppermute(array, axis, [(i, (i + by) % devices) for i in range(devices)])]
    ppermute x8, waiting for transfers between devices: 34.2 us -> 25 us  [passed_along(): lax.ppermute(array, ('z', 'x'), [(i, i + by) for i in range(devices) if 0...]
    all_gather x1, waiting for transfers between devices: 0.02 us -> 7.32 us  [body(): lax.all_gather(feed, ('z', 'x'), axis=0, tiled=True).reshape(16, 80, 640)]
    all_to_all x1, starting transfers between devices: 13.1 us -> 20.3 us  [body(): tail = lax.all_to_all(tail, ('batch', 'z', 'x'), 0, 0, tiled=True)]
    unnamed x84 -> x66, local copies, waits for them, and re-layouts: 17.4 us -> 11.7 us
  transfers between devices with their start and end apart: 32 -> 32, of which waited for: 16 -> 17; matrix products, arithmetic and copies ran while one was open for 5% -> 3% of each run, Pallas kernels for 31% -> 33%
where the time goes in v6:
time: 400 us; the launch traced here: 394 us
  Pallas kernels  167 us (42%)
  waiting for transfers between devices  116 us (29%)
  starting transfers between devices  63.4 us (16%)
  between operations  20.1 us (5%)
  local copies, waits for them, and re-layouts  16.2 us (4%)
  other arithmetic  11.7 us (3%)
    pallas_call x2, Pallas kernels, attend_back(): pl.pallas_call(attend_back_kernel, out_shape=(far(nq, 384), far(win, 384)...  42.5 us
    pallas_call x1, Pallas kernels, feed_forward(): call(feed_kernel, (far(2, 512, 640), far(2, 512, 640), far(16, 4, 80, 640...  32.1 us
    reduce_scatter x1, waiting for transfers between devices, body(): lax.psum_scatter(feed_grads, 'batch', scatter_dimension=0, tiled=True)  31.6 us
    pallas_call x2, Pallas kernels, attend(): pl.pallas_call(attend_kernel, out_shape=(jax.ShapeDtypeStruct((384, nq),...  28.6 us
    ppermute x8, waiting for transfers between devices, passed_along(): lax.ppermute(array, ('z', 'x'), [(i, i + by) for i in range(devices) if 0...  25 us
    pallas_call x1, Pallas kernels, project_back(): call(project_back_kernel, (shape(5, 2, 256, 640), shape(5, 2, 256, 640),...  23.5 us
    ppermute x8, starting transfers between devices, passed_along(): lax.ppermute(array, ('z', 'x'), [(i, i + by) for i in range(devices) if 0...  20.9 us
    all_to_all x1, starting transfers between devices, body(): tail = lax.all_to_all(tail, ('batch', 'z', 'x'), 0, 0, tiled=True)  20.3 us
  transfers between devices with their start and end apart: 32, of which 17 were waited for; matrix products, arithmetic and copies ran while one was open for 3% of the time, Pallas kernels for 33%

profile of v6, /device:TPU:1, one launch (start us, length us, event | category | flops | bytes accessed | tf_op | source)
XLA Modules:
  0.0 394.4 jit_solution(5255595331804612391)
XLA Ops:
  11.9 4.0 %collective-permute-start = (bf16[2,256,640]{2,1,0:T(8,128)(2,1)}, bf16[2,256,640]{2,1,0:T(8,128)(2,1)S(1)}, u32[]{:S(2)}, u32[]{:S(2)}) collective-permute-start(bf16[2,256,640]{2,1,0:T(8,128)(2,1)} %bitcast.95), channel_id=1, source_target_pairs={{0,2},{2,4},{4,6},{6,8},{8,10},{10,12},{12,14},{14,16},{16,18},{18... | collective-permute-start | bytes 1966088 | tf_op jit(solution)/shard_map/ppermute | solution.py:649
  33.4 15.6 %all-gather.4.cloned.1.call-done.vec_ref.refs_8_.refs_6_.refs_11_ = bf16[640,1280]{1,0:T(8,128)(2,1)} async-done(((bf16[160,1280]{1,0:T(8,128)(2,1)}), bf16[640,1280]{1,0:T(8,128)(2,1)}) %all-gather.4.cloned.1.call-update) | async-done | bytes 1638416 | tf_op jit(solution)/shard_map/all_gather | solution.py:704
  55.9 12.0 %project.2 = (bf16[2,2560,384]{2,1,0:T(8,128)(2,1)}, bf16[2,2560,384]{2,1,0:T(8,128)(2,1)}, bf16[2,384,2560]{2,1,0:T(8,128)(2,1)}, bf16[2,384,2560]{2,1,0:T(8,12...) custom-call(s32[5]{0:T(128)S(1)} %stack.81.refs_0_.core_ref, ...), custom_call_target="tpu_custom_call" | custom-call | flops 100000000 | tf_op jit(solution)/shard_map/project/pallas_call | solution.py:367
  74.9 6.4 %project.3 = (bf16[2,2560,384]{2,1,0:T(8,128)(2,1)}, bf16[2,2560,384]{2,1,0:T(8,128)(2,1)}, bf16[2,384,2560]{2,1,0:T(8,128)(2,1)}, bf16[2,384,2560]{2,1,0:T(8,128)(2,1)}) custom-call(s32[5]{0:T(128)S(1)} %stack.81.refs_0_.core_ref, ...), custom_call_target="tpu_custom_call", output_to_operand_aliasing={{0}: (7, {}), {1}: (8, {}), {2}: (9, {}), {3}: (10, {})} | custom-call | flops 100000000 | tf_op jit(solution)/shard_map/project/pallas_call | solution.py:367
  81.4 16.9 %attend.3 = (f32[384,512]{1,0:T(8,128)S(1)}, bf16[512,384]{1,0:T(8,128)(2,1)S(1)}, f32[5,8,512]{2,1,0:T(8,128)S(1)}) custom-call(s32[5]{0:T(128)S(1)} %stack.91.info_ref, bf16[2,384,512]{2,1,0:T(8,128)(2,1)} %get-tuple-element.101.qT_ref, bf16[2,2560,384]{2,1,0:T(8,128)(2,1)} %get-tuple-element.112.k_ref, bf16[2,384,2560]{2,1,0:T(8,128)(2,1)} %get-tuple-element.113.vT_ref, ...), custom_call_target="tpu_custom_call" | custom-call | flops 400000000 | tf_op jit(solution)/shard_map/attend/pallas_call | solution.py:98
  99.8 11.7 %attend.2 = (f32[384,512]{1,0:T(8,128)S(1)}, bf16[512,384]{1,0:T(8,128)(2,1)S(1)}, f32[5,8,512]{2,1,0:T(8,128)S(1)}) custom-call(s32[5]{0:T(128)S(1)} %stack.86.info_ref, bf16[2,384,512]{2,1,0:T(8,128)(2,1)} %get-tuple-element.101.qT_ref, bf16[2,2560,384]{2,1,0:T(8,128)(2,1)} %get-tuple-element.112.k_ref, bf16[2,384,2560]{2,1,0:T(8,128)(2,1)} %get-tuple-element.113.vT_ref, ...), custom_call_target="tpu_custom_call" | custom-call | flops 400000000 | tf_op jit(solution)/shard_map/attend/pallas_call | solution.py:98
  114.8 11.0 %all-gather.6.cloned.1.call-done.w_ref.up_ref.down_ref = bf16[640,5760]{1,0:T(8,128)(2,1)} async-done(((bf16[160,5760]{1,0:T(8,128)(2,1)}), bf16[640,5760]{1,0:T(8,128)(2,1)}) %all-gather.6.cloned.1.call-update) | async-done | bytes 7372816 | tf_op jit(solution)/shard_map/all_gather | solution.py:713
  127.0 4.4 %middle.1 = (f32[512,640]{1,0:T(8,128)}, bf16[512,640]{1,0:T(8,128)(2,1)}, bf16[512,640]{1,0:T(8,128)(2,1)}) custom-call(s32[1]{0:T(128)} %bitcast.core_ref, bf16[640,5760]{1,0:T(8,128)(2,1)} %all-gather.6.cloned.1.call-done.w_ref.up_ref.down_ref, bf16[512,384]{1,0:T(8,128)(2,1)S(1)} %get-tuple-element.116.low0_ref, ...), custom_call_target="tpu_custom_call" | custom-call | flops 20000000 | tf_op jit(solution)/shard_map/middle/pallas_call | solution.py:396
  131.4 32.1 %feed_forward.1 = (bf16[2,512,640]{2,1,0:T(8,128)(2,1)}, bf16[2,512,640]{2,1,0:T(8,128)(2,1)}, bf16[16,4,80,640]{3,2,1,0:T(8,128)(2,1)}) custom-call(bf16[512,640]{1,0:T(8,128)(2,1)} %get-tuple-element.122.h_ref, bf16[512,640]{1,0:T(8,128)(2,1)} %get-tuple-element.123.h2_ref, bf16[512,640]{1,0:T(8,128)(2,1)} %bitcast.20.cot_ref, ...), custom_call_target="tpu_custom_call" | custom-call | flops 600000000 | tf_op jit(solution)/shard_map/feed_forward/pallas_call | solution.py:443
  167.2 4.8 %after_feed.1 = (bf16[512,640]{1,0:T(8,128)(2,1)}, f32[512,640]{1,0:T(8,128)}, bf16[512,640]{1,0:T(8,128)(2,1)S(1)}, f32[8,640]{1,0:T(8,128)S(1)}) custom-call(f32[512,640]{1,0:T(8,128)} %get-tuple-element.121.mid_ref, bf16[2,512,640]{2,1,0:T(8,128)(2,1)} %get-tuple-element.124.mine_ref, bf16[2,512,640]{2,1,0:T(8,128)(2,1)S(1)} %collective-permute-done.11.theirs_ref, ...), custom_call_target="tpu_custom_call" | custom-call | flops 20000000 | tf_op jit(solution)/shard_map/after_feed/pallas_call | solution.py:472
  174.2 4.1 %branch.1 = (bf16[1024,384]{1,0:T(8,128)(2,1)}, bf16[384,1024]{1,0:T(8,128)(2,1)}, f32[640,384]{1,0:T(8,128)}) custom-call(s32[1]{0:T(128)} %bitcast.core_ref, bf16[512,640]{1,0:T(8,128)(2,1)S(1)} %get-tuple-element.131.own_ref, bf16[512,640]{1,0:T(8,128)(2,1)S(1)} %collective-permute-done.12.their_ref, ...), custom_call_target="tpu_custom_call" | custom-call | flops 20000000 | tf_op jit(solution)/shard_map/branch/pallas_call | solution.py:497
  178.3 25.5 %attend_back.3 = (bf16[512,384]{1,0:T(8,128)(2,1)}, bf16[2560,384]{1,0:T(8,128)(2,1)}, bf16[2560,384]{1,0:T(8,128)(2,1)}) custom-call(s32[5]{0:T(128)S(1)} %stack.91.info_ref, bf16[2,384,512]{2,1,0:T(8,128)(2,1)} %get-tuple-element.101.qT_ref, bf16[2,512,384]{2,1,0:T(8,128)(2,1)} %get-tuple-element.128.q_ref, ...), custom_call_target="tpu_custom_call" | custom-call | flops 800000000 | tf_op jit(solution)/shard_map/attend_back/pallas_call | solution.py:211
  203.8 17.0 %attend_back.2 = (bf16[512,384]{1,0:T(8,128)(2,1)}, bf16[2560,384]{1,0:T(8,128)(2,1)}, bf16[2560,384]{1,0:T(8,128)(2,1)}) custom-call(s32[5]{0:T(128)S(1)} %stack.86.info_ref, bf16[2,384,512]{2,1,0:T(8,128)(2,1)} %get-tuple-element.101.qT_ref, bf16[2,512,384]{2,1,0:T(8,128)(2,1)} %get-tuple-element.128.q_ref, ...), custom_call_target="tpu_custom_call" | custom-call | flops 800000000 | tf_op jit(solution)/shard_map/attend_back/pallas_call | solution.py:211
  220.8 23.5 %project_back.1 = (bf16[5,2,256,640]{3,2,1,0:T(8,128)(2,1)S(1)}, bf16[5,2,256,640]{3,2,1,0:T(8,128)(2,1)S(1)}, bf16[64,40,384]{2,1,0:T(8,128)(2,1)}) custom-call(s32[5]{0:T(128)S(1)} %stack.81.refs_0_.core_ref, bf16[2,256,640]{2,1,0:T(8,128)(2,1)} %copy-done.11, bf16[2,256,640]{2,1,0:T(8,128)(2,1)} %copy-done.8, bf16[2,256,640]{2,1,0:T(8,128)(2,1)} %bitcast.98, ...), custom_call_target="tpu_custom_call" | custom-call | flops 200000000 | tf_op jit(solution)/shard_map/project_back/pallas_call | solution.py:590
  248.1 20.3 %all-to-all-start = ((bf16[64,40,384]{2,1,0:T(8,128)(2,1)}), bf16[64,40,384]{2,1,0:T(8,128)(2,1)S(1)}, u32[]{:S(2)}, u32[]{:S(2)}) async-start(bf16[64,40,384]{2,1,0:T(8,128)(2,1)} %get-tuple-element.149), calls=%async_computation.1 | async-start | bytes 3932160 | tf_op jit(solution)/shard_map/all_to_all | solution.py:736
  269.7 31.6 %reduce-scatter.5.cloned.1.call-done = bf16[80,640]{1,0:T(8,128)(2,1)} async-done(((bf16[320,640]{1,0:T(8,128)(2,1)}), bf16[80,640]{1,0:T(8,128)(2,1)}) %reduce-scatter.5.cloned.1.call-update) | async-done | bytes 102416 | tf_op jit(solution)/shard_map/reduce_scatter | solution.py:735
  301.3 5.1 %fusion.10 = (bf16[2,256,640]{2,1,0:T(8,128)(2,1)S(1)}, bf16[2,256,640]{2,1,0:T(8,128)(2,1)}, bf16[2,256,640]{2,1,0:T(8,128)(2,1)}, bf16[2,256,640]{2,1,0:T(8,128)(2,1)}, f32[2,256,640]{2,1,0:T(8,128)}) fusion(bf16[5,2,256,640]{3,2,1,0:T(8,128)(2,1)} %collective-permute-done.13, bf16[5,2,256,640]{3,2,1,0:T(8,128)(2,1)} %copy-done.4), kind=kLoop, calls=%fused_computation.25 | loop fusion | flops 6225920 | bytes 10485760 | tf_op jit(solution)/shard_map/convert_element_type | solution.py:740
  313.4 6.4 %collective-permute-start.22 = (bf16[2,256,640]{2,1,0:T(8,128)(2,1)}, bf16[2,256,640]{2,1,0:T(8,128)(2,1)S(1)}, u32[]{:S(2)}, u32[]{:S(2)}) collective-permute-start(bf16[2,256,640]{2,1,0:T(8,128)(2,1)} %get-tuple-element.220), channel_id=1, source_target_pairs={{0,4},{2,6},{4,8},{6,10},{8,12},{10,14},{12,16},{14,18},{16,20},{1... | collective-permute-start | bytes 1966088 | tf_op jit(solution)/shard_map/ppermute | solution.py:649
  321.1 5.2 %collective-permute-done.17 = bf16[2,256,640]{2,1,0:T(8,128)(2,1)S(1)} collective-permute-done((bf16[2,256,640]{2,1,0:T(8,128)(2,1)}, bf16[2,256,640]{2,1,0:T(8,128)(2,1)S(1)}, u32[]{:S(2)}, u32[]{:S(2)}) %collective-permute-start.17) | collective-permute-done | bytes 655392 | tf_op jit(solution)/shard_map/ppermute | solution.py:649
  336.0 9.1 %collective-permute-done.19 = bf16[160,384]{1,0:T(8,128)(2,1)S(1)} collective-permute-done((bf16[160,384]{1,0:T(8,128)(2,1)S(1)}, bf16[160,384]{1,0:T(8,128)(2,1)S(1)}, u32[]{:S(2)}, u32[]{:S(2)}) %collective-permute-start.19) | collective-permute-done | bytes 122912 | tf_op jit(solution)/shard_map/ppermute | solution.py:644
  345.3 4.0 %collective-permute-done.21 = bf16[160,384]{1,0:T(8,128)(2,1)S(1)} collective-permute-done((bf16[160,384]{1,0:T(8,128)(2,1)S(1)}, bf16[160,384]{1,0:T(8,128)(2,1)S(1)}, u32[]{:S(2)}, u32[]{:S(2)}) %collective-permute-start.21) | collective-permute-done | bytes 122912 | tf_op jit(solution)/shard_map/ppermute | solution.py:644
  349.3 11.6 %collective-permute-done.23 = bf16[2,256,640]{2,1,0:T(8,128)(2,1)S(1)} collective-permute-done((bf16[2,256,640]{2,1,0:T(8,128)(2,1)S(1)}, bf16[2,256,640]{2,1,0:T(8,128)(2,1)S(1)}, u32[]{:S(2)}, u32[]{:S(2)}) %collective-permute-start.23) | collective-permute-done | bytes 655392 | tf_op jit(solution)/shard_map/ppermute | solution.py:649
  363.6 7.3 %all-gather.8.cloned.1.call-done = bf16[1280,640]{1,0:T(8,128)(2,1)} async-done(((bf16[80,640]{1,0:T(8,128)(2,1)}), bf16[1280,640]{1,0:T(8,128)(2,1)}) %all-gather.8.cloned.1.call-update) | async-done | bytes 1638416 | tf_op jit(solution)/shard_map/all_gather | solution.py:737
  370.9 6.3 %collective-permute-start.25 = (bf16[16,80,640]{2,1,0:T(8,128)(2,1)}, bf16[16,80,640]{2,1,0:T(8,128)(2,1)S(1)}, u32[]{:S(2)}, u32[]{:S(2)}) collective-permute-start(bf16[16,80,640]{2,1,0:T(8,128)(2,1)} %bitcast.109), channel_id=1, source_target_pairs={{0,1},{1,0},{2,3},{3,2},{4,5},{5,4},{6,7},{7,6},{8,9},{9,8},{10,11... | collective-permute-start | bytes 4915208 | tf_op jit(solution)/shard_map/ppermute | solution.py:653
  (176 shorter events, 78.3 us)
Async XLA Ops:
  7.2 41.8 %all-gather.4.cloned.1.call-start = ((), (), s32[]{:S(2)}) async-start(), calls=%async_computation.3 | async-start | bytes 2048000 | tf_op jit(solution)/shard_map/all_gather | solution.py:704
  11.9 19.3 %collective-permute-start = (bf16[2,256,640]{2,1,0:T(8,128)(2,1)}, bf16[2,256,640]{2,1,0:T(8,128)(2,1)S(1)}, u32[]{:S(2)}, u32[]{:S(2)}) collective-permute-start(bf16[2,256,640]{2,1,0:T(8,128)(2,1)} %bitcast.95), channel_id=1, source_target_pairs={{0,2},{2,4},{4,6},{6,8},{8,10},{10,12},{12,14},{14,16},{16,18},{18... | collective-permute-start | bytes 1966088 | tf_op jit(solution)/shard_map/ppermute | solution.py:649
  15.9 17.5 %collective-permute-start.1 = (bf16[2,256,640]{2,1,0:T(8,128)(2,1)}, bf16[2,256,640]{2,1,0:T(8,128)(2,1)}, u32[]{:S(2)}, u32[]{:S(2)}) collective-permute-start(bf16[2,256,640]{2,1,0:T(8,128)(2,1)} %bitcast.96), channel_id=1, source_target_pairs={{2,0},{4,2},{6,4},{8,6},{10,8},{12,10},{14,12},{16,14},{18,16},{20... | collective-permute-start | bytes 1966088 | tf_op jit(solution)/shard_map/ppermute | solution.py:649
  17.2 16.2 %collective-permute-start.2 = (bf16[2,256,640]{2,1,0:T(8,128)(2,1)}, bf16[2,256,640]{2,1,0:T(8,128)(2,1)S(1)}, u32[]{:S(2)}, u32[]{:S(2)}) collective-permute-start(bf16[2,256,640]{2,1,0:T(8,128)(2,1)} %bitcast.97), channel_id=1, source_target_pairs={{0,1},{1,0},{2,3},{3,2},{4,5},{5,4},{6,7},{7,6},{8,9},{9,8},{10,11... | collective-permute-start | bytes 1966088 | tf_op jit(solution)/shard_map/ppermute | solution.py:653
  18.3 107.6 %all-gather.6.cloned.1.call-start = ((), (), s32[]{:S(2)}) async-start(), calls=%async_computation.4 | async-start | bytes 9216000 | tf_op jit(solution)/shard_map/all_gather | solution.py:713
  49.0 198.7 %reduce-scatter.3.cloned.1.call-start = ((), (), s32[]{:S(2)}) async-start(), calls=%async_computation.5 | async-start | bytes 6963200 | tf_op jit(solution)/shard_map/reduce_scatter | solution.py:725
  49.0 6.8 %collective-permute-start.3 = (bf16[2,256,640]{2,1,0:T(8,128)(2,1)S(1)}, bf16[2,256,640]{2,1,0:T(8,128)(2,1)S(1)}, u32[]{:S(2)}, u32[]{:S(2)}) collective-permute-start(bf16[2,256,640]{2,1,0:T(8,128)(2,1)S(1)} %collective-permute-done.refs_1_), channel_id=1, source_target_pairs={{0,1},{1,0},{2,3},{3,2},{4,5},{5,4},{6,7},{7,6},{8,9},{9,8},{10,11... | collective-permute-start | bytes 1966088 | tf_op jit(solution)/shard_map/ppermute | solution.py:653
  49.9 18.1 %collective-permute-start.5 = (bf16[2,256,640]{2,1,0:T(8,128)(2,1)S(1)}, bf16[2,256,640]{2,1,0:T(8,128)(2,1)S(1)}, u32[]{:S(2)}, u32[]{:S(2)}) collective-permute-start(bf16[2,256,640]{2,1,0:T(8,128)(2,1)S(1)} %collective-permute-done.refs_1_), channel_id=1, source_target_pairs={{0,2},{2,4},{4,6},{6,8},{8,10},{10,12},{12,14},{14,16},{16,18},{18... | collective-permute-start | bytes 1966088 | tf_op jit(solution)/shard_map/ppermute | solution.py:649
  53.0 17.8 %collective-permute-start.6 = (bf16[2,256,640]{2,1,0:T(8,128)(2,1)}, bf16[2,256,640]{2,1,0:T(8,128)(2,1)S(1)}, u32[]{:S(2)}, u32[]{:S(2)}) collective-permute-start(bf16[2,256,640]{2,1,0:T(8,128)(2,1)} %collective-permute-done.1.refs_3_), channel_id=1, source_target_pairs={{2,0},{4,2},{6,4},{8,6},{10,8},{12,10},{14,12},{16,14},{18,16},{20... | collective-permute-start | bytes 1966088 | tf_op jit(solution)/shard_map/ppermute | solution.py:649
  112.4 19.1 %collective-permute-start.10 = (bf16[512,640]{1,0:T(8,128)(2,1)}, bf16[512,640]{1,0:T(8,128)(2,1)}, u32[]{:S(2)}, u32[]{:S(2)}) collective-permute-start(bf16[512,640]{1,0:T(8,128)(2,1)} %bitcast.20.cot_ref), channel_id=1, source_target_pairs={{0,1},{1,0},{2,3},{3,2},{4,5},{5,4},{6,7},{7,6},{8,9},{9,8},{10,11... | collective-permute-start | bytes 1966088 | tf_op jit(solution)/shard_map/ppermute | solution.py:653
  247.7 53.6 %collective-permute-start.13 = (bf16[5,2,256,640]{3,2,1,0:T(8,128)(2,1)}, bf16[5,2,256,640]{3,2,1,0:T(8,128)(2,1)}, u32[]{:S(2)}, u32[]{:S(2)}) collective-permute-start(bf16[5,2,256,640]{3,2,1,0:T(8,128)(2,1)} %copy-done.27), channel_id=1, source_target_pairs={{0,1},{1,0},{2,3},{3,2},{4,5},{5,4},{6,7},{7,6},{8,9},{9,8},{10,11... | collective-permute-start | bytes 9830408 | tf_op jit(solution)/shard_map/ppermute | solution.py:653
  248.1 58.3 %all-to-all-start = ((bf16[64,40,384]{2,1,0:T(8,128)(2,1)}), bf16[64,40,384]{2,1,0:T(8,128)(2,1)S(1)}, u32[]{:S(2)}, u32[]{:S(2)}) async-start(bf16[64,40,384]{2,1,0:T(8,128)(2,1)} %get-tuple-element.149), calls=%async_computation.1 | async-start | bytes 3932160 | tf_op jit(solution)/shard_map/all_to_all | solution.py:736
  268.4 32.9 %reduce-scatter.5.cloned.1.call-start = ((), (), s32[]{:S(2)}) async-start(), calls=%async_computation.6 | async-start | bytes 512000 | tf_op jit(solution)/shard_map/reduce_scatter | solution.py:735
  269.0 101.9 %all-gather.8.cloned.1.call-start = ((), (), s32[]{:S(2)}) async-start(), calls=%async_computation.7 | async-start | bytes 1740800 | tf_op jit(solution)/shard_map/all_gather | solution.py:737
  307.1 12.6 %collective-permute-start.15 = (bf16[40,384]{1,0:T(8,128)(2,1)S(1)}, bf16[40,384]{1,0:T(8,128)(2,1)S(1)}, u32[]{:S(2)}, u32[]{:S(2)}) collective-permute-start(bf16[40,384]{1,0:T(8,128)(2,1)S(1)} %reduce_sum.48), channel_id=1, source_target_pairs={{0,6},{2,0},{4,2},{6,4},{1,7},{3,1},{5,3},{7,5},{8,14},{10,8},{12,... | collective-permute-start | bytes 92168 | tf_op jit(solution)/shard_map/ppermute | solution.py:644
  309.5 11.6 %collective-permute-start.16 = (bf16[40,384]{1,0:T(8,128)(2,1)S(1)}, bf16[40,384]{1,0:T(8,128)(2,1)S(1)}, u32[]{:S(2)}, u32[]{:S(2)}) collective-permute-start(bf16[40,384]{1,0:T(8,128)(2,1)S(1)} %reduce_sum.48), channel_id=1, source_target_pairs={{0,4},{2,6},{4,0},{6,2},{1,5},{3,7},{5,1},{7,3},{8,12},{10,14},{12... | collective-permute-start | bytes 92168 | tf_op jit(solution)/shard_map/ppermute | solution.py:644
  309.8 16.6 %collective-permute-start.17 = (bf16[2,256,640]{2,1,0:T(8,128)(2,1)}, bf16[2,256,640]{2,1,0:T(8,128)(2,1)S(1)}, u32[]{:S(2)}, u32[]{:S(2)}) collective-permute-start(bf16[2,256,640]{2,1,0:T(8,128)(2,1)} %get-tuple-element.222), channel_id=1, source_target_pairs={{0,2},{2,4},{4,6},{6,8},{8,10},{10,12},{12,14},{14,16},{16,18},{18... | collective-permute-start | bytes 1966088 | tf_op jit(solution)/shard_map/ppermute | solution.py:649
  312.0 17.6 %collective-permute-start.18 = (bf16[2,256,640]{2,1,0:T(8,128)(2,1)}, bf16[2,256,640]{2,1,0:T(8,128)(2,1)S(1)}, u32[]{:S(2)}, u32[]{:S(2)}) collective-permute-start(bf16[2,256,640]{2,1,0:T(8,128)(2,1)} %get-tuple-element.221), channel_id=1, source_target_pairs={{2,0},{4,2},{6,4},{8,6},{10,8},{12,10},{14,12},{16,14},{18,16},{20... | collective-permute-start | bytes 1966088 | tf_op jit(solution)/shard_map/ppermute | solution.py:649
  313.4 35.9 %collective-permute-start.22 = (bf16[2,256,640]{2,1,0:T(8,128)(2,1)}, bf16[2,256,640]{2,1,0:T(8,128)(2,1)S(1)}, u32[]{:S(2)}, u32[]{:S(2)}) collective-permute-start(bf16[2,256,640]{2,1,0:T(8,128)(2,1)} %get-tuple-element.220), channel_id=1, source_target_pairs={{0,4},{2,6},{4,8},{6,10},{8,12},{10,14},{12,16},{14,18},{16,20},{1... | collective-permute-start | bytes 1966088 | tf_op jit(solution)/shard_map/ppermute | solution.py:649
  319.8 41.1 %collective-permute-start.23 = (bf16[2,256,640]{2,1,0:T(8,128)(2,1)S(1)}, bf16[2,256,640]{2,1,0:T(8,128)(2,1)S(1)}, u32[]{:S(2)}, u32[]{:S(2)}) collective-permute-start(bf16[2,256,640]{2,1,0:T(8,128)(2,1)S(1)} %get-tuple-element.219), channel_id=1, source_target_pairs={{4,0},{6,2},{8,4},{10,6},{12,8},{14,10},{16,12},{18,14},{20,16},{2... | collective-permute-start | bytes 1966088 | tf_op jit(solution)/shard_map/ppermute | solution.py:649
  329.6 15.6 %collective-permute-start.19 = (bf16[160,384]{1,0:T(8,128)(2,1)S(1)}, bf16[160,384]{1,0:T(8,128)(2,1)S(1)}, u32[]{:S(2)}, u32[]{:S(2)}) collective-permute-start(bf16[160,384]{1,0:T(8,128)(2,1)S(1)} %bitcast.113), channel_id=1, source_target_pairs={{0,8},{8,16},{16,24},{24,0},{1,9},{9,17},{17,25},{25,1},{2,10},{10... | collective-permute-start | bytes 368648 | tf_op jit(solution)/shard_map/ppermute | solution.py:644
  331.5 13.7 %collective-permute-start.20 = (bf16[160,384]{1,0:T(8,128)(2,1)S(1)}, bf16[160,384]{1,0:T(8,128)(2,1)S(1)}, u32[]{:S(2)}, u32[]{:S(2)}) collective-permute-start(bf16[160,384]{1,0:T(8,128)(2,1)S(1)} %bitcast.114), channel_id=1, source_target_pairs={{0,24},{8,0},{16,8},{24,16},{1,25},{9,1},{17,9},{25,17},{2,26},{10... | collective-permute-start | bytes 368648 | tf_op jit(solution)/shard_map/ppermute | solution.py:644
  334.8 14.5 %collective-permute-start.21 = (bf16[160,384]{1,0:T(8,128)(2,1)S(1)}, bf16[160,384]{1,0:T(8,128)(2,1)S(1)}, u32[]{:S(2)}, u32[]{:S(2)}) collective-permute-start(bf16[160,384]{1,0:T(8,128)(2,1)S(1)} %bitcast.115), channel_id=1, source_target_pairs={{0,16},{8,24},{16,0},{24,8},{1,17},{9,25},{17,1},{25,9},{2,18},{10... | collective-permute-start | bytes 368648 | tf_op jit(solution)/shard_map/ppermute | solution.py:644
  370.9 12.3 %collective-permute-start.25 = (bf16[16,80,640]{2,1,0:T(8,128)(2,1)}, bf16[16,80,640]{2,1,0:T(8,128)(2,1)S(1)}, u32[]{:S(2)}, u32[]{:S(2)}) collective-permute-start(bf16[16,80,640]{2,1,0:T(8,128)(2,1)} %bitcast.109), channel_id=1, source_target_pairs={{0,1},{1,0},{2,3},{3,2},{4,5},{5,4},{6,7},{7,6},{8,9},{9,8},{10,11... | collective-permute-start | bytes 4915208 | tf_op jit(solution)/shard_map/ppermute | solution.py:653
  (39 other events, 470.7 us)
Sparse Core Ops, SparseCore 0:
  18.4 30.5 all-gather.3
  51.2 74.5 all-gather.5
  163.6 81.7 reduce-scatter.2
  271.5 29.7 reduce-scatter.4
  303.3 67.5 all-gather.7

commit v7 on v6

--- a/solution.py
+++ b/solution.py
@@ -429,9 +429,9 @@
     for f in range(2):
         for y in range(4):
             for i in range(2):
-                g_ref[4 * chunk + 2 * f + i, y] = g_up[160 * y + 80 * i:160 * y + 80 * (i + 1), 640 * f:640 * (f + 1)]
+                g_ref[y, 4 * chunk + 2 * f + i] = g_up[160 * y + 80 * i:160 * y + 80 * (i + 1), 640 * f:640 * (f + 1)]
         for i in range(8):
-            g_ref[8 + i, 2 * chunk + f] = g_down[640 * f + 80 * i:640 * f + 80 * (i + 1)]
+            g_ref[2 * chunk + f, 8 + i] = g_down[640 * f + 80 * i:640 * f + 80 * (i + 1)]
 
     @pl.when(chunk == 1)
     def _():
@@ -442,10 +442,10 @@
 def feed_forward(h, h2, cot, cot2, weights):
     return call(
         feed_kernel,
-        (far(2, 512, 640), far(2, 512, 640), far(16, 4, 80, 640)),
+        (far(2, 512, 640), far(2, 512, 640), far(4, 16, 80, 640)),
         "feed_forward", 30 * 10**9, 52, grid=(2,),
         in_specs=[full(512, 640)] * 4 + [pl.BlockSpec((640, 1280), lambda f: (0, f)), pl.BlockSpec((320, 2560), lambda f: (f, 1))],
-        out_specs=[full(2, 512, 640), full(2, 512, 640), full(16, 4, 80, 640)],
+        out_specs=[full(2, 512, 640), full(2, 512, 640), full(4, 16, 80, 640)],
         scratch_shapes=[pltpu.VMEM((1024, 640), bf16), pltpu.VMEM((1024, 640), bf16), pltpu.VMEM((640, 1024), bf16), pltpu.VMEM((640, 1024), bf16),
                         pltpu.VMEM((1024, 640), f32), pltpu.VMEM((1024, 640), f32)],
     )(*stay(h, h2, cot), cot2, *stay(weights, weights))
@@ -588,7 +588,7 @@
     first = pl.BlockSpec((512, 384), lambda b, *_: (jnp.minimum(b, 4), 0))
     second = pl.BlockSpec((512, 384), lambda b, *_: (jnp.maximum(b - 5, 0), 0))
     return call(
-        project_back_kernel, (shape(5, 2, 256, 640), shape(5, 2, 256, 640), shape(64, 40, 384)), "project_back", 10**10, 36, **scalar_first(
+        project_back_kernel, (far(5, 2, 256, 640), far(5, 2, 256, 640), far(64, 40, 384)), "project_back", 10**10, 36, **scalar_first(
             (10,), [pl.BlockSpec(memory_space=pl.ANY)] * 10 + [full(16, 640), full(640, 1152), full(512, 384), full(512, 384), first, second, first, second,
                                                full(640, 384), full(8, 640)],
             [pl.BlockSpec((1, 1, 256, 640), lambda b, *_: (lax.rem(b, 5), b // 5, 0, 0))] * 2 + [full(64, 40, 384)],
@@ -700,16 +700,16 @@
     together = lambda *arrays: lax.optimization_barrier(arrays)
 
     vectors = jnp.pad(jnp.stack([gain_one, bias_one, gain_two, bias_two], axis=1), ((0, 0), (0, 124)))
-    heads, tok = together(pack_heads(core_arg, w_qkv, vectors), tok)
+    heads, tok_sent = together(pack_heads(core_arg, w_qkv, vectors), tok)
     heads = lax.all_gather(heads, "batch", axis=0, tiled=True)
-    before, after, tok_other = passed_along(tok, 1), passed_along(tok, -1), swapped(tok)
+    before, after, tok_other = passed_along(tok_sent, 1), passed_along(tok_sent, -1), swapped(tok_sent)
     windows = [window_info(lengths[m, 0], chip, core, 2560) for m in range(2)]
     place = jnp.stack([core] + windows[0][3] + windows[1][3]).astype(jnp.int32)
     feed_pack = pack_feed(core_arg, w_out, w_up, w_down)
     before, after, tok_other, feed_pack, place, windows = together(before, after, tok_other, feed_pack, place, windows)
     own = [passed_along(before, 1), before, tok, after, passed_along(after, -1)]
     other = [None, swapped(before), tok_other, swapped(after), None]
-    heads, feed_pack = together(heads, feed_pack)
+    heads, feed_pack, own[0], own[4] = together(heads, feed_pack, own[0], own[4])
     feed_weights = lax.all_gather(feed_pack, "batch", axis=0, tiled=True)
     vec = vector_rows(heads)
     *near_parts, q, qT = project((1, 2, 3), place, own, other, vec, heads)
@@ -722,7 +722,7 @@
     theirs = swapped(jnp.stack([low0, low1]))
     middle, hidden_two, hidden_other = middle_step(core_arg, feed_weights, low0, low1, theirs, tok, tok_other, vec)
     mine, partial, feed_grads = feed_forward(hidden_two, hidden_other, cot, swapped(cot), feed_weights)
-    feed_grads = lax.psum_scatter(feed_grads.reshape(5120, 640), ("z", "x"), scatter_dimension=0, tiled=True)
+    feed_grads = lax.all_to_all(feed_grads.reshape(64, 80, 640), ("batch", "z", "x"), 0, 0, tiled=True)
     block_out, grad_middle, branch, g_two = after_feed(middle, mine, swapped(partial), cot, vec)
 
     do, doT, g_out = branch_step(core_arg, branch, swapped(branch), feed_weights, low0, low1, theirs)
@@ -732,7 +732,7 @@
     mine, theirs, tail = project_back(place, own, other, vec, heads, dq, dk, dv, g_out, g_two)
     feed_grads, mine, theirs, tail = together(feed_grads, mine, theirs, tail)
 
-    feed = lax.psum_scatter(feed_grads, "batch", scatter_dimension=0, tiled=True).reshape(80, 640)
+    feed = jnp.sum(feed_grads.astype(f32), axis=0).astype(bf16)
     tail = lax.all_to_all(tail, ("batch", "z", "x"), 0, 0, tiled=True)
     feed = lax.all_gather(feed, ("z", "x"), axis=0, tiled=True).reshape(16, 80, 640)
     theirs = swapped(theirs)

time: 400 us -> 411 us (1.028)
  starting transfers between devices: 63.4 us -> 81.6 us
  Pallas kernels: 167 us -> 154 us
  other arithmetic: 11.7 us -> 16.2 us
    reduce_scatter x2 -> x0, waiting for transfers between devices: 31.6 us -> none  [the longest x1 31.6 us: body(): lax.psum_scatter(feed_grads, 'batch', scatter_dimension=0, tiled=True)]
    all_to_all x1, waiting for transfers between devices: 0.01 us -> 18.5 us  [body(): tail = lax.all_to_all(tail, ('batch', 'z', 'x'), 0, 0, tiled=True)]
    all_gather x1, waiting for transfers between devices: 11 us -> 26.7 us  [body(): feed_weights = lax.all_gather(feed_pack, 'batch', axis=0, tiled=True)]
    all_gather x1, waiting for transfers between devices: 15.6 us -> 0.01 us  [body(): heads = lax.all_gather(heads, 'batch', axis=0, tiled=True)]
    ppermute x8, waiting for transfers between devices: 25 us -> 39.6 us  [passed_along(): lax.ppermute(array, ('z', 'x'), [(i, i + by) for i in range(devices) if 0...]
    all_to_all x0 -> x1, starting transfers between devices: none -> 9.81 us  [body(): lax.all_to_all(feed_grads.reshape(64, 80, 640), ('batch', 'z', 'x'), 0, 0...]
    ppermute x12, starting transfers between devices: 12.6 us -> 22.2 us  [swapped(): return lax.ppermute(array, 'core', [(0, 1), (1, 0)])]
    all_to_all x0 -> x1, waiting for transfers between devices: none -> 8.01 us  [body(): lax.all_to_all(feed_grads.reshape(64, 80, 640), ('batch', 'z', 'x'), 0, 0...]
  transfers between devices with their start and end apart: 32 -> 31, of which waited for: 17 -> 19; matrix products, arithmetic and copies ran while one was open for 3% -> 4% of each run, Pallas kernels for 33% -> 29%
where the time goes in v7:
time: 411 us; the launch traced here: 405 us
  Pallas kernels  154 us (37%)
  waiting for transfers between devices  119 us (29%)
  starting transfers between devices  81.6 us (20%)
  between operations  20.1 us (5%)
  other arithmetic  16.2 us (4%)
  local copies, waits for them, and re-layouts  13.7 us (3%)
    ppermute x8, waiting for transfers between devices, passed_along(): lax.ppermute(array, ('z', 'x'), [(i, i + by) for i in range(devices) if 0...  39.6 us
    pallas_call x2, Pallas kernels, attend_back(): pl.pallas_call(attend_back_kernel, out_shape=(far(nq, 384), far(win, 384)...  34.7 us
    pallas_call x1, Pallas kernels, feed_forward(): call(feed_kernel, (far(2, 512, 640), far(2, 512, 640), far(4, 16, 80, 640...  32 us
    all_gather x1, waiting for transfers between devices, body(): feed_weights = lax.all_gather(feed_pack, 'batch', axis=0, tiled=True)  26.7 us
    pallas_call x1, Pallas kernels, project_back(): call(project_back_kernel, (far(5, 2, 256, 640), far(5, 2, 256, 640), far(...  24.1 us
    pallas_call x2, Pallas kernels, attend(): pl.pallas_call(attend_kernel, out_shape=(jax.ShapeDtypeStruct((384, nq),...  23.2 us
    ppermute x12, starting transfers between devices, swapped(): return lax.ppermute(array, 'core', [(0, 1), (1, 0)])  22.2 us
    ppermute x8, starting transfers between devices, passed_along(): lax.ppermute(array, ('z', 'x'), [(i, i + by) for i in range(devices) if 0...  21.2 us
  transfers between devices with their start and end apart: 31, of which 19 were waited for; matrix products, arithmetic and copies ran while one was open for 4% of the time, Pallas kernels for 29%

profile of v7, /device:TPU:1, one launch (start us, length us, event | category | flops | bytes accessed | tf_op | source)
XLA Modules:
  0.0 404.7 jit_solution(10994898037849821550)
XLA Ops:
  38.0 10.8 %collective-permute-done.3.refs_1_.refs_0_ = bf16[2,256,640]{2,1,0:T(8,128)(2,1)S(1)} collective-permute-done((bf16[2,256,640]{2,1,0:T(8,128)(2,1)S(1)}, bf16[2,256,640]{2,1,0:T(8,128)(2,1)S(1)}, u32[]{:S(2)}, u32[]{:S(2)}) %collective-permute-start.3) | collective-permute-done | bytes 655392 | tf_op jit(solution)/shard_map/ppermute | solution.py:649
  59.0 11.9 %project.2 = (bf16[2,2560,384]{2,1,0:T(8,128)(2,1)}, bf16[2,2560,384]{2,1,0:T(8,128)(2,1)}, bf16[2,384,2560]{2,1,0:T(8,128)(2,1)}, bf16[2,384,2560]{2,1,0:T(8,12...) custom-call(s32[5]{0:T(128)S(1)} %stack.81.refs_0_.core_ref, ...), custom_call_target="tpu_custom_call" | custom-call | flops 100000000 | tf_op jit(solution)/shard_map/project/pallas_call | solution.py:367
  74.3 6.3 %project.3 = (bf16[2,2560,384]{2,1,0:T(8,128)(2,1)}, bf16[2,2560,384]{2,1,0:T(8,128)(2,1)}, bf16[2,384,2560]{2,1,0:T(8,128)(2,1)}, bf16[2,384,2560]{2,1,0:T(8,128)(2,1)}) custom-call(s32[5]{0:T(128)S(1)} %stack.81.refs_0_.core_ref, bf16[2,256,640]{2,1,0:T(8,128)(2,1)S(1)} %copy-done.11, ...), custom_call_target="tpu_custom_call", output_to_operand_aliasing={{0}: (7, {}), {1}: (8, {}), {2}: (9, {}), {3}: (10, {})} | custom-call | flops 100000000 | tf_op jit(solution)/shard_map/project/pallas_call | solution.py:367
  80.6 11.7 %attend.3 = (f32[384,512]{1,0:T(8,128)S(1)}, bf16[512,384]{1,0:T(8,128)(2,1)S(1)}, f32[5,8,512]{2,1,0:T(8,128)S(1)}) custom-call(s32[5]{0:T(128)S(1)} %stack.91.info_ref, bf16[2,384,512]{2,1,0:T(8,128)(2,1)} %get-tuple-element.103.qT_ref, bf16[2,2560,384]{2,1,0:T(8,128)(2,1)} %get-tuple-element.116.k_ref, bf16[2,384,2560]{2,1,0:T(8,128)(2,1)} %get-tuple-element.117.vT_ref, ...), custom_call_target="tpu_custom_call" | custom-call | flops 400000000 | tf_op jit(solution)/shard_map/attend/pallas_call | solution.py:98
  93.9 11.5 %attend.2 = (f32[384,512]{1,0:T(8,128)S(1)}, bf16[512,384]{1,0:T(8,128)(2,1)S(1)}, f32[5,8,512]{2,1,0:T(8,128)S(1)}) custom-call(s32[5]{0:T(128)S(1)} %stack.86.info_ref, bf16[2,384,512]{2,1,0:T(8,128)(2,1)} %get-tuple-element.103.qT_ref, bf16[2,2560,384]{2,1,0:T(8,128)(2,1)} %get-tuple-element.116.k_ref, bf16[2,384,2560]{2,1,0:T(8,128)(2,1)} %get-tuple-element.117.vT_ref, ...), custom_call_target="tpu_custom_call" | custom-call | flops 400000000 | tf_op jit(solution)/shard_map/attend/pallas_call | solution.py:98
  108.8 26.7 %all-gather.6.cloned.1.call-done.w_ref.up_ref.down_ref = bf16[640,5760]{1,0:T(8,128)(2,1)} async-done(((bf16[160,5760]{1,0:T(8,128)(2,1)}), bf16[640,5760]{1,0:T(8,128)(2,1)}) %all-gather.6.cloned.1.call-update) | async-done | bytes 7372816 | tf_op jit(solution)/shard_map/all_gather | solution.py:713
  136.6 4.5 %middle.1 = (f32[512,640]{1,0:T(8,128)}, bf16[512,640]{1,0:T(8,128)(2,1)}, bf16[512,640]{1,0:T(8,128)(2,1)}) custom-call(s32[1]{0:T(128)} %bitcast.core_ref, bf16[640,5760]{1,0:T(8,128)(2,1)} %all-gather.6.cloned.1.call-done.w_ref.up_ref.down_ref, bf16[512,384]{1,0:T(8,128)(2,1)S(1)} %get-tuple-element.120.low0_ref, ...), custom_call_target="tpu_custom_call" | custom-call | flops 20000000 | tf_op jit(solution)/shard_map/middle/pallas_call | solution.py:396
  141.1 32.0 %feed_forward.1 = (bf16[2,512,640]{2,1,0:T(8,128)(2,1)}, bf16[2,512,640]{2,1,0:T(8,128)(2,1)}, bf16[4,16,80,640]{3,2,1,0:T(8,128)(2,1)}) custom-call(bf16[512,640]{1,0:T(8,128)(2,1)} %get-tuple-element.126.h_ref, bf16[512,640]{1,0:T(8,128)(2,1)} %get-tuple-element.127.h2_ref, bf16[512,640]{1,0:T(8,128)(2,1)} %bitcast.20.cot_ref, ...), custom_call_target="tpu_custom_call" | custom-call | flops 600000000 | tf_op jit(solution)/shard_map/feed_forward/pallas_call | solution.py:443
  173.1 9.8 %all-to-all-start = ((bf16[64,80,640]{2,1,0:T(8,128)(2,1)}), bf16[64,80,640]{2,1,0:T(8,128)(2,1)}, u32[]{:S(2)}, u32[]{:S(2)}) async-start(bf16[64,80,640]{2,1,0:T(8,128)(2,1)} %bitcast.108), calls=%async_computation | async-start | bytes 13107200 | tf_op jit(solution)/shard_map/all_to_all | solution.py:725
  186.8 4.5 %after_feed.1 = (bf16[512,640]{1,0:T(8,128)(2,1)}, f32[512,640]{1,0:T(8,128)}, bf16[512,640]{1,0:T(8,128)(2,1)S(1)}, f32[8,640]{1,0:T(8,128)S(1)}) custom-call(f32[512,640]{1,0:T(8,128)} %get-tuple-element.125.mid_ref, bf16[2,512,640]{2,1,0:T(8,128)(2,1)} %get-tuple-element.128.mine_ref, bf16[2,512,640]{2,1,0:T(8,128)(2,1)S(1)} %collective-permute-done.11.theirs_ref, ...), custom_call_target="tpu_custom_call" | custom-call | flops 20000000 | tf_op jit(solution)/shard_map/after_feed/pallas_call | solution.py:472
  197.6 17.0 %attend_back.3 = (bf16[512,384]{1,0:T(8,128)(2,1)}, bf16[2560,384]{1,0:T(8,128)(2,1)}, bf16[2560,384]{1,0:T(8,128)(2,1)}) custom-call(s32[5]{0:T(128)S(1)} %stack.91.info_ref, bf16[2,384,512]{2,1,0:T(8,128)(2,1)} %get-tuple-element.103.qT_ref, bf16[2,512,384]{2,1,0:T(8,128)(2,1)} %get-tuple-element.132.q_ref, ...), custom_call_target="tpu_custom_call" | custom-call | flops 800000000 | tf_op jit(solution)/shard_map/attend_back/pallas_call | solution.py:211
  214.6 17.7 %attend_back.2 = (bf16[512,384]{1,0:T(8,128)(2,1)}, bf16[2560,384]{1,0:T(8,128)(2,1)}, bf16[2560,384]{1,0:T(8,128)(2,1)}) custom-call(s32[5]{0:T(128)S(1)} %stack.86.info_ref, bf16[2,384,512]{2,1,0:T(8,128)(2,1)} %get-tuple-element.103.qT_ref, bf16[2,512,384]{2,1,0:T(8,128)(2,1)} %get-tuple-element.132.q_ref, ...), custom_call_target="tpu_custom_call" | custom-call | flops 800000000 | tf_op jit(solution)/shard_map/attend_back/pallas_call | solution.py:211
  232.3 24.1 %project_back.1 = (bf16[5,2,256,640]{3,2,1,0:T(8,128)(2,1)}, bf16[5,2,256,640]{3,2,1,0:T(8,128)(2,1)}, bf16[64,40,384]{2,1,0:T(8,128)(2,1)}) custom-call(s32[5]{0:T(128)S(1)} %stack.81.refs_0_.core_ref, bf16[2,256,640]{2,1,0:T(8,128)(2,1)} %copy-done.10, bf16[2,256,640]{2,1,0:T(8,128)(2,1)} %copy-done.7, bf16[2,256,640]{2,1,0:T(8,128)(2,1)} %bitcast.99, ...), custom_call_target="tpu_custom_call" | custom-call | flops 200000000 | tf_op jit(solution)/shard_map/project_back/pallas_call | solution.py:590
  256.4 8.0 %all-to-all-done = bf16[64,80,640]{2,1,0:T(8,128)(2,1)} async-done(((bf16[64,80,640]{2,1,0:T(8,128)(2,1)}), bf16[64,80,640]{2,1,0:T(8,128)(2,1)}, u32[]{:S(2)}, u32[]{:S(2)}) %all-to-all-start) | async-done | bytes 6553632 | tf_op jit(solution)/shard_map/all_to_all | solution.py:725
  267.5 21.1 %all-to-all-start.1 = ((bf16[64,40,384]{2,1,0:T(8,128)(2,1)}), bf16[64,40,384]{2,1,0:T(8,128)(2,1)S(1)}, u32[]{:S(2)}, u32[]{:S(2)}) async-start(bf16[64,40,384]{2,1,0:T(8,128)(2,1)} %get-tuple-element.153), calls=%async_computation.1 | async-start | bytes 3932160 | tf_op jit(solution)/shard_map/all_to_all | solution.py:736
  289.3 4.5 %reduce_sum.65 = bf16[80,640]{1,0:T(8,128)(2,1)} reduce(bf16[64,80,640]{2,1,0:T(8,128)(2,1)} %all-to-all-done, bf16[]{:T(256)} %constant.193.clone.1), dimensions={0}, to_apply=%region_15.16 | reduce | flops 3225600 | bytes 6656002 | tf_op jit(solution)/shard_map/reduce_sum | solution.py:735
  293.8 5.1 %fusion.10 = (bf16[2,256,640]{2,1,0:T(8,128)(2,1)S(1)}, bf16[2,256,640]{2,1,0:T(8,128)(2,1)}, bf16[2,256,640]{2,1,0:T(8,128)(2,1)}, bf16[2,256,640]{2,1,0:T(8,128)(2,1)}, f32[2,256,640]{2,1,0:T(8,128)}) fusion(bf16[5,2,256,640]{3,2,1,0:T(8,128)(2,1)} %collective-permute-done.13, bf16[5,2,256,640]{3,2,1,0:T(8,128)(2,1)} %get-tuple-element.154), kind=kLoop, calls=%fused_computation.24 | loop fusion | flops 6225920 | bytes 10485760 | tf_op jit(solution)/shard_map/convert_element_type | solution.py:740
  298.9 18.5 %all-to-all-done.1 = bf16[64,40,384]{2,1,0:T(8,128)(2,1)S(1)} async-done(((bf16[64,40,384]{2,1,0:T(8,128)(2,1)}), bf16[64,40,384]{2,1,0:T(8,128)(2,1)S(1)}, u32[]{:S(2)}, u32[]{:S(2)}) %all-to-all-start.1) | async-done | bytes 1966112 | tf_op jit(solution)/shard_map/all_to_all | solution.py:736
  324.3 6.4 %collective-permute-start.22 = (bf16[2,256,640]{2,1,0:T(8,128)(2,1)}, bf16[2,256,640]{2,1,0:T(8,128)(2,1)S(1)}, u32[]{:S(2)}, u32[]{:S(2)}) collective-permute-start(bf16[2,256,640]{2,1,0:T(8,128)(2,1)} %get-tuple-element.224), channel_id=1, source_target_pairs={{0,4},{2,6},{4,8},{6,10},{8,12},{10,14},{12,16},{14,18},{16,20},{1... | collective-permute-start | bytes 1966088 | tf_op jit(solution)/shard_map/ppermute | solution.py:649
  332.1 7.4 %collective-permute-done.17 = bf16[2,256,640]{2,1,0:T(8,128)(2,1)S(1)} collective-permute-done((bf16[2,256,640]{2,1,0:T(8,128)(2,1)}, bf16[2,256,640]{2,1,0:T(8,128)(2,1)S(1)}, u32[]{:S(2)}, u32[]{:S(2)}) %collective-permute-start.17) | collective-permute-done | bytes 655392 | tf_op jit(solution)/shard_map/ppermute | solution.py:649
  339.5 6.2 %collective-permute-done.18 = bf16[2,256,640]{2,1,0:T(8,128)(2,1)S(1)} collective-permute-done((bf16[2,256,640]{2,1,0:T(8,128)(2,1)}, bf16[2,256,640]{2,1,0:T(8,128)(2,1)S(1)}, u32[]{:S(2)}, u32[]{:S(2)}) %collective-permute-start.18) | collective-permute-done | bytes 655392 | tf_op jit(solution)/shard_map/ppermute | solution.py:649
  350.1 9.9 %collective-permute-done.19 = bf16[160,384]{1,0:T(8,128)(2,1)S(1)} collective-permute-done((bf16[160,384]{1,0:T(8,128)(2,1)S(1)}, bf16[160,384]{1,0:T(8,128)(2,1)S(1)}, u32[]{:S(2)}, u32[]{:S(2)}) %collective-permute-start.19) | collective-permute-done | bytes 122912 | tf_op jit(solution)/shard_map/ppermute | solution.py:644
  363.5 9.7 %collective-permute-done.23 = bf16[2,256,640]{2,1,0:T(8,128)(2,1)S(1)} collective-permute-done((bf16[2,256,640]{2,1,0:T(8,128)(2,1)S(1)}, bf16[2,256,640]{2,1,0:T(8,128)(2,1)S(1)}, u32[]{:S(2)}, u32[]{:S(2)}) %collective-permute-start.23) | collective-permute-done | bytes 655392 | tf_op jit(solution)/shard_map/ppermute | solution.py:649
  375.9 11.6 %collective-permute-start.25 = (bf16[16,80,640]{2,1,0:T(8,128)(2,1)}, bf16[16,80,640]{2,1,0:T(8,128)(2,1)S(1)}, u32[]{:S(2)}, u32[]{:S(2)}) collective-permute-start(bf16[16,80,640]{2,1,0:T(8,128)(2,1)} %bitcast.106), channel_id=1, source_target_pairs={{0,1},{1,0},{2,3},{3,2},{4,5},{5,4},{6,7},{7,6},{8,9},{9,8},{10,11... | collective-permute-start | bytes 4915208 | tf_op jit(solution)/shard_map/ppermute | solution.py:653
  (169 shorter events, 87.7 us)
Async XLA Ops:
  7.2 45.8 %all-gather.4.cloned.1.call-start = ((), (), s32[]{:S(2)}) async-start(), calls=%async_computation.2 | async-start | bytes 2048000 | tf_op jit(solution)/shard_map/all_gather | solution.py:704
  11.9 19.3 %collective-permute-start = (bf16[2,256,640]{2,1,0:T(8,128)(2,1)}, bf16[2,256,640]{2,1,0:T(8,128)(2,1)S(1)}, u32[]{:S(2)}, u32[]{:S(2)}) collective-permute-start(bf16[2,256,640]{2,1,0:T(8,128)(2,1)} %bitcast.96), channel_id=1, source_target_pairs={{0,2},{2,4},{4,6},{6,8},{8,10},{10,12},{12,14},{14,16},{16,18},{18... | collective-permute-start | bytes 1966088 | tf_op jit(solution)/shard_map/ppermute | solution.py:649
  15.9 17.5 %collective-permute-start.1 = (bf16[2,256,640]{2,1,0:T(8,128)(2,1)}, bf16[2,256,640]{2,1,0:T(8,128)(2,1)}, u32[]{:S(2)}, u32[]{:S(2)}) collective-permute-start(bf16[2,256,640]{2,1,0:T(8,128)(2,1)} %bitcast.97), channel_id=1, source_target_pairs={{2,0},{4,2},{6,4},{8,6},{10,8},{12,10},{14,12},{16,14},{18,16},{20... | collective-permute-start | bytes 1966088 | tf_op jit(solution)/shard_map/ppermute | solution.py:649
  17.2 16.2 %collective-permute-start.2 = (bf16[2,256,640]{2,1,0:T(8,128)(2,1)}, bf16[2,256,640]{2,1,0:T(8,128)(2,1)S(1)}, u32[]{:S(2)}, u32[]{:S(2)}) collective-permute-start(bf16[2,256,640]{2,1,0:T(8,128)(2,1)} %bitcast.98), channel_id=1, source_target_pairs={{0,1},{1,0},{2,3},{3,2},{4,5},{5,4},{6,7},{7,6},{8,9},{9,8},{10,11... | collective-permute-start | bytes 1966088 | tf_op jit(solution)/shard_map/ppermute | solution.py:653
  18.3 117.2 %all-gather.6.cloned.1.call-start = ((), (), s32[]{:S(2)}) async-start(), calls=%async_computation.3 | async-start | bytes 9216000 | tf_op jit(solution)/shard_map/all_gather | solution.py:713
  33.4 15.4 %collective-permute-start.3 = (bf16[2,256,640]{2,1,0:T(8,128)(2,1)S(1)}, bf16[2,256,640]{2,1,0:T(8,128)(2,1)S(1)}, u32[]{:S(2)}, u32[]{:S(2)}) collective-permute-start(bf16[2,256,640]{2,1,0:T(8,128)(2,1)S(1)} %collective-permute-done.refs_1_), channel_id=1, source_target_pairs={{0,2},{2,4},{4,6},{6,8},{8,10},{10,12},{12,14},{14,16},{16,18},{18... | collective-permute-start | bytes 1966088 | tf_op jit(solution)/shard_map/ppermute | solution.py:649
  36.7 16.3 %collective-permute-start.4 = (bf16[2,256,640]{2,1,0:T(8,128)(2,1)}, bf16[2,256,640]{2,1,0:T(8,128)(2,1)}, u32[]{:S(2)}, u32[]{:S(2)}) collective-permute-start(bf16[2,256,640]{2,1,0:T(8,128)(2,1)} %collective-permute-done.1.refs_3_), channel_id=1, source_target_pairs={{2,0},{4,2},{6,4},{8,6},{10,8},{12,10},{14,12},{16,14},{18,16},{20... | collective-permute-start | bytes 1966088 | tf_op jit(solution)/shard_map/ppermute | solution.py:649
  53.0 4.9 %collective-permute-start.5 = (bf16[2,256,640]{2,1,0:T(8,128)(2,1)S(1)}, bf16[2,256,640]{2,1,0:T(8,128)(2,1)S(1)}, u32[]{:S(2)}, u32[]{:S(2)}) collective-permute-start(bf16[2,256,640]{2,1,0:T(8,128)(2,1)S(1)} %collective-permute-done.refs_1_), channel_id=1, source_target_pairs={{0,1},{1,0},{2,3},{3,2},{4,5},{5,4},{6,7},{7,6},{8,9},{9,8},{10,11... | collective-permute-start | bytes 1966088 | tf_op jit(solution)/shard_map/ppermute | solution.py:653
  106.3 34.7 %collective-permute-start.10 = (bf16[512,640]{1,0:T(8,128)(2,1)}, bf16[512,640]{1,0:T(8,128)(2,1)}, u32[]{:S(2)}, u32[]{:S(2)}) collective-permute-start(bf16[512,640]{1,0:T(8,128)(2,1)} %bitcast.20.cot_ref), channel_id=1, source_target_pairs={{0,1},{1,0},{2,3},{3,2},{4,5},{5,4},{6,7},{7,6},{8,9},{9,8},{10,11... | collective-permute-start | bytes 1966088 | tf_op jit(solution)/shard_map/ppermute | solution.py:653
  173.1 91.4 %all-to-all-start = ((bf16[64,80,640]{2,1,0:T(8,128)(2,1)}), bf16[64,80,640]{2,1,0:T(8,128)(2,1)}, u32[]{:S(2)}, u32[]{:S(2)}) async-start(bf16[64,80,640]{2,1,0:T(8,128)(2,1)} %bitcast.108), calls=%async_computation | async-start | bytes 13107200 | tf_op jit(solution)/shard_map/all_to_all | solution.py:725
  264.5 29.4 %collective-permute-start.13 = (bf16[5,2,256,640]{3,2,1,0:T(8,128)(2,1)}, bf16[5,2,256,640]{3,2,1,0:T(8,128)(2,1)}, u32[]{:S(2)}, u32[]{:S(2)}) collective-permute-start(bf16[5,2,256,640]{3,2,1,0:T(8,128)(2,1)} %get-tuple-element.155), channel_id=1, source_target_pairs={{0,1},{1,0},{2,3},{3,2},{4,5},{5,4},{6,7},{7,6},{8,9},{9,8},{10,11... | collective-permute-start | bytes 9830408 | tf_op jit(solution)/shard_map/ppermute | solution.py:653
  267.5 49.9 %all-to-all-start.1 = ((bf16[64,40,384]{2,1,0:T(8,128)(2,1)}), bf16[64,40,384]{2,1,0:T(8,128)(2,1)S(1)}, u32[]{:S(2)}, u32[]{:S(2)}) async-start(bf16[64,40,384]{2,1,0:T(8,128)(2,1)} %get-tuple-element.153), calls=%async_computation.1 | async-start | bytes 3932160 | tf_op jit(solution)/shard_map/all_to_all | solution.py:736
  288.6 87.3 %all-gather.8.cloned.1.call-start = ((), (), s32[]{:S(2)}) async-start(), calls=%async_computation.4 | async-start | bytes 1740800 | tf_op jit(solution)/shard_map/all_gather | solution.py:737
  317.7 6.6 %collective-permute-start.14 = (bf16[40,384]{1,0:T(8,128)(2,1)S(1)}, bf16[40,384]{1,0:T(8,128)(2,1)S(1)}, u32[]{:S(2)}, u32[]{:S(2)}) collective-permute-start(bf16[40,384]{1,0:T(8,128)(2,1)S(1)} %reduce_sum.60), channel_id=1, source_target_pairs={{0,2},{2,4},{4,6},{6,0},{1,3},{3,5},{5,7},{7,1},{8,10},{10,12},{12... | collective-permute-start | bytes 92168 | tf_op jit(solution)/shard_map/ppermute | solution.py:644
  317.8 12.9 %collective-permute-start.15 = (bf16[40,384]{1,0:T(8,128)(2,1)S(1)}, bf16[40,384]{1,0:T(8,128)(2,1)S(1)}, u32[]{:S(2)}, u32[]{:S(2)}) collective-permute-start(bf16[40,384]{1,0:T(8,128)(2,1)S(1)} %reduce_sum.60), channel_id=1, source_target_pairs={{0,6},{2,0},{4,2},{6,4},{1,7},{3,1},{5,3},{7,5},{8,14},{10,8},{12,... | collective-permute-start | bytes 92168 | tf_op jit(solution)/shard_map/ppermute | solution.py:644
  320.5 11.6 %collective-permute-start.16 = (bf16[40,384]{1,0:T(8,128)(2,1)S(1)}, bf16[40,384]{1,0:T(8,128)(2,1)S(1)}, u32[]{:S(2)}, u32[]{:S(2)}) collective-permute-start(bf16[40,384]{1,0:T(8,128)(2,1)S(1)} %reduce_sum.60), channel_id=1, source_target_pairs={{0,4},{2,6},{4,0},{6,2},{1,5},{3,7},{5,1},{7,3},{8,12},{10,14},{12... | collective-permute-start | bytes 92168 | tf_op jit(solution)/shard_map/ppermute | solution.py:644
  320.6 18.9 %collective-permute-start.17 = (bf16[2,256,640]{2,1,0:T(8,128)(2,1)}, bf16[2,256,640]{2,1,0:T(8,128)(2,1)S(1)}, u32[]{:S(2)}, u32[]{:S(2)}) collective-permute-start(bf16[2,256,640]{2,1,0:T(8,128)(2,1)} %get-tuple-element.226), channel_id=1, source_target_pairs={{0,2},{2,4},{4,6},{6,8},{8,10},{10,12},{12,14},{14,16},{16,18},{18... | collective-permute-start | bytes 1966088 | tf_op jit(solution)/shard_map/ppermute | solution.py:649
  323.0 22.7 %collective-permute-start.18 = (bf16[2,256,640]{2,1,0:T(8,128)(2,1)}, bf16[2,256,640]{2,1,0:T(8,128)(2,1)S(1)}, u32[]{:S(2)}, u32[]{:S(2)}) collective-permute-start(bf16[2,256,640]{2,1,0:T(8,128)(2,1)} %get-tuple-element.225), channel_id=1, source_target_pairs={{2,0},{4,2},{6,4},{8,6},{10,8},{12,10},{14,12},{16,14},{18,16},{20... | collective-permute-start | bytes 1966088 | tf_op jit(solution)/shard_map/ppermute | solution.py:649
  324.3 39.1 %collective-permute-start.22 = (bf16[2,256,640]{2,1,0:T(8,128)(2,1)}, bf16[2,256,640]{2,1,0:T(8,128)(2,1)S(1)}, u32[]{:S(2)}, u32[]{:S(2)}) collective-permute-start(bf16[2,256,640]{2,1,0:T(8,128)(2,1)} %get-tuple-element.224), channel_id=1, source_target_pairs={{0,4},{2,6},{4,8},{6,10},{8,12},{10,14},{12,16},{14,18},{16,20},{1... | collective-permute-start | bytes 1966088 | tf_op jit(solution)/shard_map/ppermute | solution.py:649
  330.8 42.4 %collective-permute-start.23 = (bf16[2,256,640]{2,1,0:T(8,128)(2,1)S(1)}, bf16[2,256,640]{2,1,0:T(8,128)(2,1)S(1)}, u32[]{:S(2)}, u32[]{:S(2)}) collective-permute-start(bf16[2,256,640]{2,1,0:T(8,128)(2,1)S(1)} %get-tuple-element.223), channel_id=1, source_target_pairs={{4,0},{6,2},{8,4},{10,6},{12,8},{14,10},{16,12},{18,14},{20,16},{2... | collective-permute-start | bytes 1966088 | tf_op jit(solution)/shard_map/ppermute | solution.py:649
  345.7 14.4 %collective-permute-start.19 = (bf16[160,384]{1,0:T(8,128)(2,1)S(1)}, bf16[160,384]{1,0:T(8,128)(2,1)S(1)}, u32[]{:S(2)}, u32[]{:S(2)}) collective-permute-start(bf16[160,384]{1,0:T(8,128)(2,1)S(1)} %bitcast.110), channel_id=1, source_target_pairs={{0,8},{8,16},{16,24},{24,0},{1,9},{9,17},{17,25},{25,1},{2,10},{10... | collective-permute-start | bytes 368648 | tf_op jit(solution)/shard_map/ppermute | solution.py:644
  348.3 11.8 %collective-permute-start.20 = (bf16[160,384]{1,0:T(8,128)(2,1)S(1)}, bf16[160,384]{1,0:T(8,128)(2,1)S(1)}, u32[]{:S(2)}, u32[]{:S(2)}) collective-permute-start(bf16[160,384]{1,0:T(8,128)(2,1)S(1)} %bitcast.111), channel_id=1, source_target_pairs={{0,24},{8,0},{16,8},{24,16},{1,25},{9,1},{17,9},{25,17},{2,26},{10... | collective-permute-start | bytes 368648 | tf_op jit(solution)/shard_map/ppermute | solution.py:644
  348.4 15.0 %collective-permute-start.21 = (bf16[160,384]{1,0:T(8,128)(2,1)S(1)}, bf16[160,384]{1,0:T(8,128)(2,1)S(1)}, u32[]{:S(2)}, u32[]{:S(2)}) collective-permute-start(bf16[160,384]{1,0:T(8,128)(2,1)S(1)} %bitcast.112), channel_id=1, source_target_pairs={{0,16},{8,24},{16,0},{24,8},{1,17},{9,25},{17,1},{25,9},{2,18},{10... | collective-permute-start | bytes 368648 | tf_op jit(solution)/shard_map/ppermute | solution.py:644
  375.9 17.5 %collective-permute-start.25 = (bf16[16,80,640]{2,1,0:T(8,128)(2,1)}, bf16[16,80,640]{2,1,0:T(8,128)(2,1)S(1)}, u32[]{:S(2)}, u32[]{:S(2)}) collective-permute-start(bf16[16,80,640]{2,1,0:T(8,128)(2,1)} %bitcast.106), channel_id=1, source_target_pairs={{0,1},{1,0},{2,3},{3,2},{4,5},{5,4},{6,7},{7,6},{8,9},{9,8},{10,11... | collective-permute-start | bytes 4915208 | tf_op jit(solution)/shard_map/ppermute | solution.py:653
  (36 other events, 452.6 us)
Sparse Core Ops, SparseCore 0:
  18.4 30.5 all-gather.3
  53.1 82.3 all-gather.5
  293.9 54.0 all-gather.7

commit v8 on v7

--- a/solution.py
+++ b/solution.py
@@ -286,7 +286,7 @@
 
 def vector_rows(heads):
     return call(turn_kernel, shape(16, 640, dtype=f32), "vector_rows", 10**6, 8, grid=(1,),
-                in_specs=[pl.BlockSpec((640, 128), lambda i: (0, 9))], out_specs=full(16, 640))(heads)
+                in_specs=[pl.BlockSpec((640, 128), lambda i: (0, 9))], out_specs=full(16, 640))(*stay(heads))
 
 
 def pack_feed_kernel(core_ref, out_ref, up_ref, down_ref, feed_ref):
@@ -706,10 +706,9 @@
     windows = [window_info(lengths[m, 0], chip, core, 2560) for m in range(2)]
     place = jnp.stack([core] + windows[0][3] + windows[1][3]).astype(jnp.int32)
     feed_pack = pack_feed(core_arg, w_out, w_up, w_down)
-    before, after, tok_other, feed_pack, place, windows = together(before, after, tok_other, feed_pack, place, windows)
+    heads, before, after, tok_other, feed_pack, place, windows = together(heads, before, after, tok_other, feed_pack, place, windows)
     own = [passed_along(before, 1), before, tok, after, passed_along(after, -1)]
     other = [None, swapped(before), tok_other, swapped(after), None]
-    heads, feed_pack, own[0], own[4] = together(heads, feed_pack, own[0], own[4])
     feed_weights = lax.all_gather(feed_pack, "batch", axis=0, tiled=True)
     vec = vector_rows(heads)
     *near_parts, q, qT = project((1, 2, 3), place, own, other, vec, heads)
@@ -737,13 +736,14 @@
     feed = lax.all_gather(feed, ("z", "x"), axis=0, tiled=True).reshape(16, 80, 640)
     theirs = swapped(theirs)
     sums = [mine[j].astype(f32) + theirs[j].astype(f32) for j in range(5)]
-    returned = [passed_along(sums[2 + by].astype(bf16), by) for by in (1, -1, 2, -2)]
-    tail, sums[2] = together(tail, sums[2])
+    right, left = passed_along(sums[4].astype(bf16), 1), passed_along(sums[0].astype(bf16), -1)
+    tail, right, left = together(tail, right, left)
+    right = passed_along((right.astype(f32) + sums[3]).astype(bf16), 1)
+    left = passed_along((left.astype(f32) + sums[1]).astype(bf16), -1)
     tail = gathered(jnp.sum(tail.astype(f32), axis=0).astype(bf16), "x").reshape(160, 384)
-    tail, returned[0], returned[1] = together(tail, returned[0], returned[1])
     tail = gathered(tail, "z").reshape(16, 40, 384)
-    tail, returned = together(tail, returned)
-    d_one = sum((part.astype(f32) for part in returned), sums[2]).reshape(512, 640)
+    tail, right, left = together(tail, right, left)
+    d_one = (sums[2] + right.astype(f32) + left.astype(f32)).reshape(512, 640)
     n_one, r_one = moments(tok.reshape(512, 640).astype(f32))
     grad_tokens = (grad_middle + norm_back(d_one, n_one, r_one, vec[0:1])).astype(bf16)
     tail, grad_tokens, feed = together(tail, grad_tokens, feed)

time: 411 us -> 387 us (0.942)
  waiting for transfers between devices: 119 us -> 105 us
  starting transfers between devices: 81.6 us -> 73 us
    ppermute x8, waiting for transfers between devices: 39.6 us -> 15.3 us  [passed_along(): lax.ppermute(array, ('z', 'x'), [(i, i + by) for i in range(devices) if 0...]
    all_gather x1, waiting for transfers between devices: 0.01 us -> 15.6 us  [body(): heads = lax.all_gather(heads, 'batch', axis=0, tiled=True)]
    ppermute x12, starting transfers between devices: 22.2 us -> 9.85 us  [swapped(): return lax.ppermute(array, 'core', [(0, 1), (1, 0)])]
    all_gather x1, waiting for transfers between devices: 26.7 us -> 17.6 us  [body(): feed_weights = lax.all_gather(feed_pack, 'batch', axis=0, tiled=True)]
    ppermute x6, starting transfers between devices: 7.2 us -> 14.8 us  [shifted(): lax.ppermute(array, axis, [(i, (i + by) % devices) for i in range(devices)])]
    ppermute x6, waiting for transfers between devices: 13.2 us -> 19.7 us  [shifted(): lax.ppermute(array, axis, [(i, (i + by) % devices) for i in range(devices)])]
    ppermute x8, starting transfers between devices: 21.2 us -> 16.5 us  [passed_along(): lax.ppermute(array, ('z', 'x'), [(i, i + by) for i in range(devices) if 0...]
    unnamed x62 -> x58, local copies, waits for them, and re-layouts: 9.26 us -> 6.43 us
  transfers between devices with their start and end apart: 31 -> 31, of which waited for: 19 -> 18; matrix products, arithmetic and copies ran while one was open for 4% -> 5% of each run, Pallas kernels for 29% -> 31%
where the time goes in v8:
time: 387 us; the launch traced here: 379 us
  Pallas kernels  152 us (39%)
  waiting for transfers between devices  105 us (27%)
  starting transfers between devices  73 us (19%)
  between operations  20.1 us (5%)
  other arithmetic  17.9 us (5%)
  local copies, waits for them, and re-layouts  10.9 us (3%)
    pallas_call x2, Pallas kernels, attend_back(): pl.pallas_call(attend_back_kernel, out_shape=(far(nq, 384), far(win, 384)...  34 us
    pallas_call x1, Pallas kernels, feed_forward(): call(feed_kernel, (far(2, 512, 640), far(2, 512, 640), far(4, 16, 80, 640...  32 us
    pallas_call x1, Pallas kernels, project_back(): call(project_back_kernel, (far(5, 2, 256, 640), far(5, 2, 256, 640), far(...  23.5 us
    pallas_call x2, Pallas kernels, attend(): pl.pallas_call(attend_kernel, out_shape=(jax.ShapeDtypeStruct((384, nq),...  23.3 us
    all_to_all x1, starting transfers between devices, body(): tail = lax.all_to_all(tail, ('batch', 'z', 'x'), 0, 0, tiled=True)  21.9 us
    ppermute x6, waiting for transfers between devices, shifted(): lax.ppermute(array, axis, [(i, (i + by) % devices) for i in range(devices)])  19.7 us
    all_gather x1, waiting for transfers between devices, body(): feed_weights = lax.all_gather(feed_pack, 'batch', axis=0, tiled=True)  17.6 us
    pallas_call x2, Pallas kernels, project(): call(lambda *refs: project_kernel(chips, *refs), shapes, 'project', 5 * 1...  17 us
  transfers between devices with their start and end apart: 31, of which 18 were waited for; matrix products, arithmetic and copies ran while one was open for 5% of the time, Pallas kernels for 31%

profile of v8, /device:TPU:1, one launch (start us, length us, event | category | flops | bytes accessed | tf_op | source)
XLA Modules:
  0.0 379.0 jit_solution(4740735918228103193)
XLA Ops:
  11.9 4.0 %collective-permute-start = (bf16[2,256,640]{2,1,0:T(8,128)(2,1)}, bf16[2,256,640]{2,1,0:T(8,128)(2,1)S(1)}, u32[]{:S(2)}, u32[]{:S(2)}) collective-permute-start(bf16[2,256,640]{2,1,0:T(8,128)(2,1)} %bitcast.104), channel_id=1, source_target_pairs={{0,2},{2,4},{4,6},{6,8},{8,10},{10,12},{12,14},{14,16},{16,18},{18... | collective-permute-start | bytes 1966088 | tf_op jit(solution)/shard_map/ppermute | solution.py:649
  33.4 15.6 %all-gather.4.cloned.1.call-done.vec_ref.refs_8_.refs_6_.refs_11_ = bf16[640,1280]{1,0:T(8,128)(2,1)} async-done(((bf16[160,1280]{1,0:T(8,128)(2,1)}), bf16[640,1280]{1,0:T(8,128)(2,1)}) %all-gather.4.cloned.1.call-update) | async-done | bytes 1638416 | tf_op jit(solution)/shard_map/all_gather | solution.py:704
  55.3 11.9 %project.2 = (bf16[2,2560,384]{2,1,0:T(8,128)(2,1)}, bf16[2,2560,384]{2,1,0:T(8,128)(2,1)}, bf16[2,384,2560]{2,1,0:T(8,128)(2,1)}, bf16[2,384,2560]{2,1,0:T(8,12...) custom-call(s32[5]{0:T(128)S(1)} %stack.81.refs_0_.core_ref, ...), custom_call_target="tpu_custom_call" | custom-call | flops 100000000 | tf_op jit(solution)/shard_map/project/pallas_call | solution.py:367
  67.3 3.5 collective-permute-done.6.refs_2_.refs_4_
  74.9 5.1 %project.3 = (bf16[2,2560,384]{2,1,0:T(8,128)(2,1)}, bf16[2,2560,384]{2,1,0:T(8,128)(2,1)}, bf16[2,384,2560]{2,1,0:T(8,128)(2,1)}, bf16[2,384,2560]{2,1,0:T(8,128)(2,1)}) custom-call(s32[5]{0:T(128)S(1)} %stack.81.refs_0_.core_ref, ...), custom_call_target="tpu_custom_call", output_to_operand_aliasing={{0}: (7, {}), {1}: (8, {}), {2}: (9, {}), {3}: (10, {})} | custom-call | flops 100000000 | tf_op jit(solution)/shard_map/project/pallas_call | solution.py:367
  80.0 11.7 %attend.3 = (f32[384,512]{1,0:T(8,128)S(1)}, bf16[512,384]{1,0:T(8,128)(2,1)S(1)}, f32[5,8,512]{2,1,0:T(8,128)S(1)}) custom-call(s32[5]{0:T(128)S(1)} %stack.91.info_ref, bf16[2,384,512]{2,1,0:T(8,128)(2,1)} %get-tuple-element.95.qT_ref, bf16[2,2560,384]{2,1,0:T(8,128)(2,1)} %get-tuple-element.106.k_ref, bf16[2,384,2560]{2,1,0:T(8,128)(2,1)} %get-tuple-element.107.vT_ref, ...), custom_call_target="tpu_custom_call" | custom-call | flops 400000000 | tf_op jit(solution)/shard_map/attend/pallas_call | solution.py:98
  93.2 11.7 %attend.2 = (f32[384,512]{1,0:T(8,128)S(1)}, bf16[512,384]{1,0:T(8,128)(2,1)S(1)}, f32[5,8,512]{2,1,0:T(8,128)S(1)}) custom-call(s32[5]{0:T(128)S(1)} %stack.86.info_ref, bf16[2,384,512]{2,1,0:T(8,128)(2,1)} %get-tuple-element.95.qT_ref, bf16[2,2560,384]{2,1,0:T(8,128)(2,1)} %get-tuple-element.106.k_ref, bf16[2,384,2560]{2,1,0:T(8,128)(2,1)} %get-tuple-element.107.vT_ref, ...), custom_call_target="tpu_custom_call" | custom-call | flops 400000000 | tf_op jit(solution)/shard_map/attend/pallas_call | solution.py:98
  108.3 17.6 %all-gather.6.cloned.1.call-done.w_ref.up_ref.down_ref = bf16[640,5760]{1,0:T(8,128)(2,1)} async-done(((bf16[160,5760]{1,0:T(8,128)(2,1)}), bf16[640,5760]{1,0:T(8,128)(2,1)}) %all-gather.6.cloned.1.call-update) | async-done | bytes 7372816 | tf_op jit(solution)/shard_map/all_gather | solution.py:712
  127.0 4.4 %middle.1 = (f32[512,640]{1,0:T(8,128)}, bf16[512,640]{1,0:T(8,128)(2,1)}, bf16[512,640]{1,0:T(8,128)(2,1)}) custom-call(s32[1]{0:T(128)} %bitcast.core_ref, bf16[640,5760]{1,0:T(8,128)(2,1)} %all-gather.6.cloned.1.call-done.w_ref.up_ref.down_ref, bf16[512,384]{1,0:T(8,128)(2,1)S(1)} %get-tuple-element.110.low0_ref, ...), custom_call_target="tpu_custom_call" | custom-call | flops 20000000 | tf_op jit(solution)/shard_map/middle/pallas_call | solution.py:396
  131.4 32.0 %feed_forward.1 = (bf16[2,512,640]{2,1,0:T(8,128)(2,1)}, bf16[2,512,640]{2,1,0:T(8,128)(2,1)}, bf16[4,16,80,640]{3,2,1,0:T(8,128)(2,1)}) custom-call(bf16[512,640]{1,0:T(8,128)(2,1)} %get-tuple-element.116.h_ref, bf16[512,640]{1,0:T(8,128)(2,1)} %get-tuple-element.117.h2_ref, bf16[512,640]{1,0:T(8,128)(2,1)} %bitcast.20.cot_ref, ...), custom_call_target="tpu_custom_call" | custom-call | flops 600000000 | tf_op jit(solution)/shard_map/feed_forward/pallas_call | solution.py:443
  163.4 9.8 %all-to-all-start = ((bf16[64,80,640]{2,1,0:T(8,128)(2,1)}), bf16[64,80,640]{2,1,0:T(8,128)(2,1)}, u32[]{:S(2)}, u32[]{:S(2)}) async-start(bf16[64,80,640]{2,1,0:T(8,128)(2,1)} %bitcast.116), calls=%async_computation | async-start | bytes 13107200 | tf_op jit(solution)/shard_map/all_to_all | solution.py:724
  177.1 4.5 %after_feed.1 = (bf16[512,640]{1,0:T(8,128)(2,1)}, f32[512,640]{1,0:T(8,128)}, bf16[512,640]{1,0:T(8,128)(2,1)S(1)}, f32[8,640]{1,0:T(8,128)S(1)}) custom-call(f32[512,640]{1,0:T(8,128)} %get-tuple-element.115.mid_ref, bf16[2,512,640]{2,1,0:T(8,128)(2,1)} %get-tuple-element.118.mine_ref, bf16[2,512,640]{2,1,0:T(8,128)(2,1)S(1)} %collective-permute-done.11.theirs_ref, ...), custom_call_target="tpu_custom_call" | custom-call | flops 20000000 | tf_op jit(solution)/shard_map/after_feed/pallas_call | solution.py:472
  183.8 4.1 %branch.1 = (bf16[1024,384]{1,0:T(8,128)(2,1)}, bf16[384,1024]{1,0:T(8,128)(2,1)}, f32[640,384]{1,0:T(8,128)}) custom-call(s32[1]{0:T(128)} %bitcast.core_ref, bf16[512,640]{1,0:T(8,128)(2,1)S(1)} %get-tuple-element.125.own_ref, bf16[512,640]{1,0:T(8,128)(2,1)S(1)} %collective-permute-done.12.their_ref, ...), custom_call_target="tpu_custom_call" | custom-call | flops 20000000 | tf_op jit(solution)/shard_map/branch/pallas_call | solution.py:497
  187.9 17.0 %attend_back.3 = (bf16[512,384]{1,0:T(8,128)(2,1)}, bf16[2560,384]{1,0:T(8,128)(2,1)}, bf16[2560,384]{1,0:T(8,128)(2,1)}) custom-call(s32[5]{0:T(128)S(1)} %stack.91.info_ref, bf16[2,384,512]{2,1,0:T(8,128)(2,1)} %get-tuple-element.95.qT_ref, bf16[2,512,384]{2,1,0:T(8,128)(2,1)} %get-tuple-element.122.q_ref, bf16[2,2560,384]{2,1,0:T(8,128)(2,1)} %get-tuple-element.106.k_ref, ...), custom_call_target="tpu_custom_call" | custom-call | flops 800000000 | tf_op jit(solution)/shard_map/attend_back/pallas_call | solution.py:211
  204.9 17.0 %attend_back.2 = (bf16[512,384]{1,0:T(8,128)(2,1)}, bf16[2560,384]{1,0:T(8,128)(2,1)}, bf16[2560,384]{1,0:T(8,128)(2,1)}) custom-call(s32[5]{0:T(128)S(1)} %stack.86.info_ref, bf16[2,384,512]{2,1,0:T(8,128)(2,1)} %get-tuple-element.95.qT_ref, bf16[2,512,384]{2,1,0:T(8,128)(2,1)} %get-tuple-element.122.q_ref, bf16[2,2560,384]{2,1,0:T(8,128)(2,1)} %get-tuple-element.106.k_ref, ...), custom_call_target="tpu_custom_call" | custom-call | flops 800000000 | tf_op jit(solution)/shard_map/attend_back/pallas_call | solution.py:211
  221.9 23.5 %project_back.1 = (bf16[5,2,256,640]{3,2,1,0:T(8,128)(2,1)}, bf16[5,2,256,640]{3,2,1,0:T(8,128)(2,1)}, bf16[64,40,384]{2,1,0:T(8,128)(2,1)}) custom-call(s32[5]{0:T(128)S(1)} %stack.81.refs_0_.core_ref, bf16[2,256,640]{2,1,0:T(8,128)(2,1)} %copy-done.9, bf16[2,256,640]{2,1,0:T(8,128)(2,1)} %copy-done.6, bf16[2,256,640]{2,1,0:T(8,128)(2,1)} %bitcast.107, ...), custom_call_target="tpu_custom_call" | custom-call | flops 200000000 | tf_op jit(solution)/shard_map/project_back/pallas_call | solution.py:590
  245.4 9.0 %all-to-all-done = bf16[64,80,640]{2,1,0:T(8,128)(2,1)} async-done(((bf16[64,80,640]{2,1,0:T(8,128)(2,1)}), bf16[64,80,640]{2,1,0:T(8,128)(2,1)}, u32[]{:S(2)}, u32[]{:S(2)}) %all-to-all-start) | async-done | bytes 6553632 | tf_op jit(solution)/shard_map/all_to_all | solution.py:724
  256.7 21.9 %all-to-all-start.1 = ((bf16[64,40,384]{2,1,0:T(8,128)(2,1)}), bf16[64,40,384]{2,1,0:T(8,128)(2,1)S(1)}, u32[]{:S(2)}, u32[]{:S(2)}) async-start(bf16[64,40,384]{2,1,0:T(8,128)(2,1)} %get-tuple-element.143), calls=%async_computation.1 | async-start | bytes 3932160 | tf_op jit(solution)/shard_map/all_to_all | solution.py:735
  286.7 4.5 %reduce_sum.65 = bf16[80,640]{1,0:T(8,128)(2,1)} reduce(bf16[64,80,640]{2,1,0:T(8,128)(2,1)} %all-to-all-done, bf16[]{:T(256)} %constant.193.clone.1), dimensions={0}, to_apply=%region_15.16 | reduce | flops 3225600 | bytes 6656002 | tf_op jit(solution)/shard_map/reduce_sum | solution.py:734
  291.2 15.8 %all-to-all-done.1 = bf16[64,40,384]{2,1,0:T(8,128)(2,1)S(1)} async-done(((bf16[64,40,384]{2,1,0:T(8,128)(2,1)}), bf16[64,40,384]{2,1,0:T(8,128)(2,1)S(1)}, u32[]{:S(2)}, u32[]{:S(2)}) %all-to-all-start.1) | async-done | bytes 1966112 | tf_op jit(solution)/shard_map/all_to_all | solution.py:735
  307.0 7.8 %collective-permute-done.14 = bf16[2,256,640]{2,1,0:T(8,128)(2,1)S(1)} collective-permute-done((bf16[2,256,640]{2,1,0:T(8,128)(2,1)}, bf16[2,256,640]{2,1,0:T(8,128)(2,1)S(1)}, u32[]{:S(2)}, u32[]{:S(2)}) %collective-permute-start.14) | collective-permute-done | bytes 655392 | tf_op jit(solution)/shard_map/ppermute | solution.py:649
  332.5 6.4 %collective-permute-start.20 = (bf16[160,384]{1,0:T(8,128)(2,1)S(1)}, bf16[160,384]{1,0:T(8,128)(2,1)S(1)}, u32[]{:S(2)}, u32[]{:S(2)}) collective-permute-start(bf16[160,384]{1,0:T(8,128)(2,1)S(1)} %bitcast.119), channel_id=1, source_target_pairs={{0,24},{8,0},{16,8},{24,16},{1,25},{9,1},{17,9},{25,17},{2,26},{10... | collective-permute-start | bytes 368648 | tf_op jit(solution)/shard_map/ppermute | solution.py:644
  342.4 14.5 %collective-permute-done.21 = bf16[160,384]{1,0:T(8,128)(2,1)S(1)} collective-permute-done((bf16[160,384]{1,0:T(8,128)(2,1)S(1)}, bf16[160,384]{1,0:T(8,128)(2,1)S(1)}, u32[]{:S(2)}, u32[]{:S(2)}) %collective-permute-start.21) | collective-permute-done | bytes 122912 | tf_op jit(solution)/shard_map/ppermute | solution.py:644
  361.8 3.7 collective-permute-done.24.theirs_ref
  (166 shorter events, 82.1 us)
Async XLA Ops:
  7.2 41.8 %all-gather.4.cloned.1.call-start = ((), (), s32[]{:S(2)}) async-start(), calls=%async_computation.2 | async-start | bytes 2048000 | tf_op jit(solution)/shard_map/all_gather | solution.py:704
  11.9 19.3 %collective-permute-start = (bf16[2,256,640]{2,1,0:T(8,128)(2,1)}, bf16[2,256,640]{2,1,0:T(8,128)(2,1)S(1)}, u32[]{:S(2)}, u32[]{:S(2)}) collective-permute-start(bf16[2,256,640]{2,1,0:T(8,128)(2,1)} %bitcast.104), channel_id=1, source_target_pairs={{0,2},{2,4},{4,6},{6,8},{8,10},{10,12},{12,14},{14,16},{16,18},{18... | collective-permute-start | bytes 1966088 | tf_op jit(solution)/shard_map/ppermute | solution.py:649
  15.9 17.5 %collective-permute-start.1 = (bf16[2,256,640]{2,1,0:T(8,128)(2,1)}, bf16[2,256,640]{2,1,0:T(8,128)(2,1)}, u32[]{:S(2)}, u32[]{:S(2)}) collective-permute-start(bf16[2,256,640]{2,1,0:T(8,128)(2,1)} %bitcast.105), channel_id=1, source_target_pairs={{2,0},{4,2},{6,4},{8,6},{10,8},{12,10},{14,12},{16,14},{18,16},{20... | collective-permute-start | bytes 1966088 | tf_op jit(solution)/shard_map/ppermute | solution.py:649
  17.2 16.2 %collective-permute-start.2 = (bf16[2,256,640]{2,1,0:T(8,128)(2,1)}, bf16[2,256,640]{2,1,0:T(8,128)(2,1)S(1)}, u32[]{:S(2)}, u32[]{:S(2)}) collective-permute-start(bf16[2,256,640]{2,1,0:T(8,128)(2,1)} %bitcast.106), channel_id=1, source_target_pairs={{0,1},{1,0},{2,3},{3,2},{4,5},{5,4},{6,7},{7,6},{8,9},{9,8},{10,11... | collective-permute-start | bytes 1966088 | tf_op jit(solution)/shard_map/ppermute | solution.py:653
  18.3 107.6 %all-gather.6.cloned.1.call-start = ((), (), s32[]{:S(2)}) async-start(), calls=%async_computation.3 | async-start | bytes 9216000 | tf_op jit(solution)/shard_map/all_gather | solution.py:712
  49.0 6.3 %collective-permute-start.3 = (bf16[2,256,640]{2,1,0:T(8,128)(2,1)S(1)}, bf16[2,256,640]{2,1,0:T(8,128)(2,1)S(1)}, u32[]{:S(2)}, u32[]{:S(2)}) collective-permute-start(bf16[2,256,640]{2,1,0:T(8,128)(2,1)S(1)} %collective-permute-done.refs_1_), channel_id=1, source_target_pairs={{0,1},{1,0},{2,3},{3,2},{4,5},{5,4},{6,7},{7,6},{8,9},{9,8},{10,11... | collective-permute-start | bytes 1966088 | tf_op jit(solution)/shard_map/ppermute | solution.py:653
  49.7 5.5 %collective-permute-start.4 = (bf16[2,256,640]{2,1,0:T(8,128)(2,1)}, bf16[2,256,640]{2,1,0:T(8,128)(2,1)S(1)}, u32[]{:S(2)}, u32[]{:S(2)}) collective-permute-start(bf16[2,256,640]{2,1,0:T(8,128)(2,1)} %collective-permute-done.1.refs_3_), channel_id=1, source_target_pairs={{0,1},{1,0},{2,3},{3,2},{4,5},{5,4},{6,7},{7,6},{8,9},{9,8},{10,11... | collective-permute-start | bytes 1966088 | tf_op jit(solution)/shard_map/ppermute | solution.py:653
  49.8 17.4 %collective-permute-start.5 = (bf16[2,256,640]{2,1,0:T(8,128)(2,1)S(1)}, bf16[2,256,640]{2,1,0:T(8,128)(2,1)S(1)}, u32[]{:S(2)}, u32[]{:S(2)}) collective-permute-start(bf16[2,256,640]{2,1,0:T(8,128)(2,1)S(1)} %collective-permute-done.refs_1_), channel_id=1, source_target_pairs={{0,2},{2,4},{4,6},{6,8},{8,10},{10,12},{12,14},{14,16},{16,18},{18... | collective-permute-start | bytes 1966088 | tf_op jit(solution)/shard_map/ppermute | solution.py:649
  53.0 17.8 %collective-permute-start.6 = (bf16[2,256,640]{2,1,0:T(8,128)(2,1)}, bf16[2,256,640]{2,1,0:T(8,128)(2,1)S(1)}, u32[]{:S(2)}, u32[]{:S(2)}) collective-permute-start(bf16[2,256,640]{2,1,0:T(8,128)(2,1)} %collective-permute-done.1.refs_3_), channel_id=1, source_target_pairs={{2,0},{4,2},{6,4},{8,6},{10,8},{12,10},{14,12},{16,14},{18,16},{20... | collective-permute-start | bytes 1966088 | tf_op jit(solution)/shard_map/ppermute | solution.py:649
  105.8 25.6 %collective-permute-start.10 = (bf16[512,640]{1,0:T(8,128)(2,1)}, bf16[512,640]{1,0:T(8,128)(2,1)}, u32[]{:S(2)}, u32[]{:S(2)}) collective-permute-start(bf16[512,640]{1,0:T(8,128)(2,1)} %bitcast.20.cot_ref), channel_id=1, source_target_pairs={{0,1},{1,0},{2,3},{3,2},{4,5},{5,4},{6,7},{7,6},{8,9},{9,8},{10,11... | collective-permute-start | bytes 1966088 | tf_op jit(solution)/shard_map/ppermute | solution.py:653
  163.4 91.0 %all-to-all-start = ((bf16[64,80,640]{2,1,0:T(8,128)(2,1)}), bf16[64,80,640]{2,1,0:T(8,128)(2,1)}, u32[]{:S(2)}, u32[]{:S(2)}) async-start(bf16[64,80,640]{2,1,0:T(8,128)(2,1)} %bitcast.116), calls=%async_computation | async-start | bytes 13107200 | tf_op jit(solution)/shard_map/all_to_all | solution.py:724
  254.4 24.5 %collective-permute-start.13 = (bf16[5,2,256,640]{3,2,1,0:T(8,128)(2,1)}, bf16[5,2,256,640]{3,2,1,0:T(8,128)(2,1)}, u32[]{:S(2)}, u32[]{:S(2)}) collective-permute-start(bf16[5,2,256,640]{3,2,1,0:T(8,128)(2,1)} %get-tuple-element.145), channel_id=1, source_target_pairs={{0,1},{1,0},{2,3},{3,2},{4,5},{5,4},{6,7},{7,6},{8,9},{9,8},{10,11... | collective-permute-start | bytes 9830408 | tf_op jit(solution)/shard_map/ppermute | solution.py:653
  256.7 50.2 %all-to-all-start.1 = ((bf16[64,40,384]{2,1,0:T(8,128)(2,1)}), bf16[64,40,384]{2,1,0:T(8,128)(2,1)S(1)}, u32[]{:S(2)}, u32[]{:S(2)}) async-start(bf16[64,40,384]{2,1,0:T(8,128)(2,1)} %get-tuple-element.143), calls=%async_computation.1 | async-start | bytes 3932160 | tf_op jit(solution)/shard_map/all_to_all | solution.py:735
  278.7 81.9 %all-gather.8.cloned.1.call-start = ((), (), s32[]{:S(2)}) async-start(), calls=%async_computation.4 | async-start | bytes 1740800 | tf_op jit(solution)/shard_map/all_gather | solution.py:736
  282.0 32.8 %collective-permute-start.14 = (bf16[2,256,640]{2,1,0:T(8,128)(2,1)}, bf16[2,256,640]{2,1,0:T(8,128)(2,1)S(1)}, u32[]{:S(2)}, u32[]{:S(2)}) collective-permute-start(bf16[2,256,640]{2,1,0:T(8,128)(2,1)} %get-tuple-element.212), channel_id=1, source_target_pairs={{0,2},{2,4},{4,6},{6,8},{8,10},{10,12},{12,14},{14,16},{16,18},{18... | collective-permute-start | bytes 1966088 | tf_op jit(solution)/shard_map/ppermute | solution.py:649
  285.0 31.7 %collective-permute-start.15 = (bf16[2,256,640]{2,1,0:T(8,128)(2,1)}, bf16[2,256,640]{2,1,0:T(8,128)(2,1)}, u32[]{:S(2)}, u32[]{:S(2)}) collective-permute-start(bf16[2,256,640]{2,1,0:T(8,128)(2,1)} %get-tuple-element.211), channel_id=1, source_target_pairs={{2,0},{4,2},{6,4},{8,6},{10,8},{12,10},{14,12},{16,14},{18,16},{20... | collective-permute-start | bytes 1966088 | tf_op jit(solution)/shard_map/ppermute | solution.py:649
  317.0 4.7 %collective-permute-start.16 = (bf16[40,384]{1,0:T(8,128)(2,1)S(1)}, bf16[40,384]{1,0:T(8,128)(2,1)S(1)}, u32[]{:S(2)}, u32[]{:S(2)}) collective-permute-start(bf16[40,384]{1,0:T(8,128)(2,1)S(1)} %reduce_sum.60), channel_id=1, source_target_pairs={{0,2},{2,4},{4,6},{6,0},{1,3},{3,5},{5,7},{7,1},{8,10},{10,12},{12... | collective-permute-start | bytes 92168 | tf_op jit(solution)/shard_map/ppermute | solution.py:644
  320.4 4.5 %collective-permute-start.18 = (bf16[40,384]{1,0:T(8,128)(2,1)S(1)}, bf16[40,384]{1,0:T(8,128)(2,1)S(1)}, u32[]{:S(2)}, u32[]{:S(2)}) collective-permute-start(bf16[40,384]{1,0:T(8,128)(2,1)S(1)} %reduce_sum.60), channel_id=1, source_target_pairs={{0,4},{2,6},{4,0},{6,2},{1,5},{3,7},{5,1},{7,3},{8,12},{10,14},{12... | collective-permute-start | bytes 92168 | tf_op jit(solution)/shard_map/ppermute | solution.py:644
  324.9 15.5 %collective-permute-start.19 = (bf16[160,384]{1,0:T(8,128)(2,1)S(1)}, bf16[160,384]{1,0:T(8,128)(2,1)S(1)}, u32[]{:S(2)}, u32[]{:S(2)}) collective-permute-start(bf16[160,384]{1,0:T(8,128)(2,1)S(1)} %bitcast.118), channel_id=1, source_target_pairs={{0,8},{8,16},{16,24},{24,0},{1,9},{9,17},{17,25},{25,1},{2,10},{10... | collective-permute-start | bytes 368648 | tf_op jit(solution)/shard_map/ppermute | solution.py:644
  329.9 27.0 %collective-permute-start.22 = (bf16[2,256,640]{2,1,0:T(8,128)(2,1)S(1)}, bf16[2,256,640]{2,1,0:T(8,128)(2,1)S(1)}, u32[]{:S(2)}, u32[]{:S(2)}) collective-permute-start(bf16[2,256,640]{2,1,0:T(8,128)(2,1)S(1)} %get-tuple-element.210), channel_id=1, source_target_pairs={{0,2},{2,4},{4,6},{6,8},{8,10},{10,12},{12,14},{14,16},{16,18},{18... | collective-permute-start | bytes 1966088 | tf_op jit(solution)/shard_map/ppermute | solution.py:649
  331.2 25.7 %collective-permute-start.23 = (bf16[2,256,640]{2,1,0:T(8,128)(2,1)S(1)}, bf16[2,256,640]{2,1,0:T(8,128)(2,1)S(1)}, u32[]{:S(2)}, u32[]{:S(2)}) collective-permute-start(bf16[2,256,640]{2,1,0:T(8,128)(2,1)S(1)} %get-tuple-element.209), channel_id=1, source_target_pairs={{2,0},{4,2},{6,4},{8,6},{10,8},{12,10},{14,12},{16,14},{18,16},{20... | collective-permute-start | bytes 1966088 | tf_op jit(solution)/shard_map/ppermute | solution.py:649
  332.5 9.8 %collective-permute-start.20 = (bf16[160,384]{1,0:T(8,128)(2,1)S(1)}, bf16[160,384]{1,0:T(8,128)(2,1)S(1)}, u32[]{:S(2)}, u32[]{:S(2)}) collective-permute-start(bf16[160,384]{1,0:T(8,128)(2,1)S(1)} %bitcast.119), channel_id=1, source_target_pairs={{0,24},{8,0},{16,8},{24,16},{1,25},{9,1},{17,9},{25,17},{2,26},{10... | collective-permute-start | bytes 368648 | tf_op jit(solution)/shard_map/ppermute | solution.py:644
  338.9 18.0 %collective-permute-start.21 = (bf16[160,384]{1,0:T(8,128)(2,1)S(1)}, bf16[160,384]{1,0:T(8,128)(2,1)S(1)}, u32[]{:S(2)}, u32[]{:S(2)}) collective-permute-start(bf16[160,384]{1,0:T(8,128)(2,1)S(1)} %bitcast.120), channel_id=1, source_target_pairs={{0,16},{8,24},{16,0},{24,8},{1,17},{9,25},{17,1},{25,9},{2,18},{10... | collective-permute-start | bytes 368648 | tf_op jit(solution)/shard_map/ppermute | solution.py:644
  360.5 7.2 %collective-permute-start.25 = (bf16[16,80,640]{2,1,0:T(8,128)(2,1)}, bf16[16,80,640]{2,1,0:T(8,128)(2,1)S(1)}, u32[]{:S(2)}, u32[]{:S(2)}) collective-permute-start(bf16[16,80,640]{2,1,0:T(8,128)(2,1)} %bitcast.114), channel_id=1, source_target_pairs={{0,1},{1,0},{2,3},{3,2},{4,5},{5,4},{6,7},{7,6},{8,9},{9,8},{10,11... | collective-permute-start | bytes 4915208 | tf_op jit(solution)/shard_map/ppermute | solution.py:653
  (34 other events, 361.0 us)
Sparse Core Ops, SparseCore 0:
  18.4 30.5 all-gather.3
  51.2 74.5 all-gather.5
  291.3 53.6 all-gather.7

commit v9 on v8

--- a/solution.py
+++ b/solution.py
@@ -210,7 +210,7 @@
     keys_m = pl.BlockSpec((None, win, 128), lambda p, *_: (m, 0, p // 2))
     return pl.pallas_call(
         attend_back_kernel,
-        out_shape=(far(nq, 384), far(win, 384), far(win, 384)),
+        out_shape=tuple(pltpu.MemorySpace.VMEM(d, bf16) for d in ((nq, 384), (win, 384), (win, 384))),
         grid_spec=pltpu.PrefetchScalarGridSpec(
             num_scalar_prefetch=1, grid=(PAIRS,),
             in_specs=[wide_m, tall_m, keys_m, pl.BlockSpec((None, 128, win), lambda p, *_: (m, p // 2, 0)), keys_m,
@@ -285,7 +285,7 @@
 
 
 def vector_rows(heads):
-    return call(turn_kernel, shape(16, 640, dtype=f32), "vector_rows", 10**6, 8, grid=(1,),
+    return call(turn_kernel, shape(16, 640, dtype=f32), "vector_rows", 10**12, 8, grid=(1,),
                 in_specs=[pl.BlockSpec((640, 128), lambda i: (0, 9))], out_specs=full(16, 640))(*stay(heads))
 
 
@@ -302,17 +302,20 @@
         (1,), [full(160, 640), full(160, 5120), full(1280, 640)], full(160, 5760)))(core, *stay(w_out, w_up, w_down))
 
 
-def rows_in_order(core, mine, theirs, x_ref):
-    mine, theirs = mine.astype(f32), theirs.astype(f32)
-    x_ref[0:256, :] = jnp.where(core == 0, mine, theirs)
-    x_ref[256:512, :] = jnp.where(core == 0, theirs, mine)
-
-
-def window_rows(core, own_refs, other_refs, m, block, x_ref):
-    for j in range(len(own_refs)):
-        @pl.when(block == j)
+def rows_in_order(core, mine_ref, theirs_ref, x_ref):
+    for c, (first, second) in enumerate(((mine_ref, theirs_ref), (theirs_ref, mine_ref))):
+        @pl.when(core == c)
         def _():
-            rows_in_order(core, own_refs[j][m], other_refs[j][m], x_ref)
+            x_ref[0:256, :], x_ref[256:512, :] = first[...], second[...]
+
+
+def normal_kernel(tok_ref, n_ref):
+    for m in range(2):
+        n_ref[m] = moments(tok_ref[m].astype(f32))[0].astype(bf16)
+
+
+def normal_rows(tok):
+    return call(normal_kernel, shape(2, 256, 640), "normal_rows", 10**6, 8, grid=(1,), in_specs=[full(2, 256, 640)], out_specs=full(2, 256, 640))(tok)
 
 
 def project_kernel(chips, place_ref, *refs):
@@ -332,8 +335,12 @@
 
     @pl.when(needed)
     def _():
-        window_rows(place_ref[0], own_refs, other_refs, m, step, x_ref)
-        hidden = (moments(x_ref[...])[0] * vec_ref[0:1, :] + vec_ref[1:2, :]).astype(bf16)
+        for j in range(n):
+            @pl.when(step == j)
+            def _():
+                rows_in_order(place_ref[0], own_refs[j].at[m], other_refs[j].at[m], x_ref)
+
+        hidden = (x_ref[...].astype(f32) * vec_ref[0:1, :] + vec_ref[1:2, :]).astype(bf16)
         hid_ref[...] = hidden
         kv = jnp.dot(hidden, w_ref[:, 384:], preferred_element_type=f32)
         low = kv.astype(bf16)
@@ -368,7 +375,7 @@
         lambda *refs: project_kernel(chips, *refs), shapes, "project", 5 * 10**9, 28,
         input_output_aliases={2 * n + 3 + i: i for i in range(len(earlier))}, **scalar_first(
             (2, n), [full(2, 256, 640)] * (2 * n) + [full(16, 640), full(640, 1152)] + [pl.BlockSpec(memory_space=pl.ANY)] * len(earlier),
-            specs, [pltpu.VMEM((512, 640), f32), pltpu.VMEM((512, 640), bf16)]))(place, *own, *other, vec, *stay(w), *earlier)
+            specs, [pltpu.VMEM((512, 640), bf16), pltpu.VMEM((512, 640), bf16)]))(place, *own, *other, vec, *stay(w), *earlier)
 
 
 def heads_joined(core, mine, theirs):
@@ -490,70 +497,67 @@
         doT_ref[:, rows] = do.T.astype(bf16)
         attended = heads_joined(core, (low0_ref, low1_ref)[m][...].astype(f32), theirs_ref[m].astype(f32))
         g = g + jnp.dot(attended.T.astype(bf16), kept, preferred_element_type=f32)
-    g_ref[...] = g
+    g_ref[...] = g.astype(bf16)
 
 
 def branch_step(core, own, their, weights, *args):
     return call(
-        branch_kernel, (far(1024, 384), far(384, 1024), far(640, 384, dtype=f32)), "branch", 10**9, 24, **scalar_first(
+        branch_kernel, (far(1024, 384), far(384, 1024), shape(640, 384)), "branch", 10**9, 24, **scalar_first(
             (1,), [full(512, 640)] * 2 + [W_OUT] + [full(*a.shape) for a in args], [full(1024, 384), full(384, 1024), full(640, 384)]))(
                 core, own, their, *stay(weights), *args)
 
 
-def project_back_kernel(core_ref, *refs):
+def near_by(*arrays):
+    return [pltpu.with_memory_space_constraint(a, pltpu.MemorySpace.VMEM) for a in arrays]
+
+
+def project_back_kernel(place_ref, *refs):
     own_refs, other_refs = refs[:5], refs[5:10]
     (vec_ref, w_ref, dq0_ref, dq1_ref, dk0_ref, dk1_ref, dv0_ref, dv1_ref, g_out_ref, g_two_ref,
-     mine_ref, theirs_ref, tail_ref, x_ref, d_kv, d_q, d_hid, g_ref, g_vec, slots, arrived) = refs[10:]
-    step, core = pl.program_id(0), core_ref[0]
-    block = lax.rem(step, 5)
-
-    def copies(at, j, m, slot):
-        for i, refs_of in enumerate((own_refs, other_refs)):
-            getattr(pltpu.make_async_copy(refs_of[j].at[m], slots.at[slot, i], arrived.at[slot, i]), at)()
-
-    def fetch(number):
-        for j in range(5):
-            for m in range(2):
-                @pl.when(number == 5 * m + j)
+     mine_ref, theirs_ref, tail_ref, n_ref, d_kv, d_q, d_hid, g_ref, g_vec, slots, arrived) = refs[10:]
+    step, core = pl.program_id(0), place_ref[0]
+    block, second = lax.rem(step, 5), lax.div(step, 5)
+    inside = lambda j, m: (j >= place_ref[1 + 2 * m]) & (j < place_ref[2 + 2 * m])
+    needed = inside(block, second)
+
+    def copies(j, m, slot):
+        return [pltpu.make_async_copy(refs_of[j].at[m], slots.at[slot, i], arrived.at[slot, i]) for i, refs_of in enumerate((own_refs, other_refs))]
+
+    @pl.when(step == 0)
+    def _():
+        for m in range(2):
+            for j in range(5):
+                @pl.when(inside(j, m))
                 def _():
-                    copies("start", j, m, lax.rem(number, 2))
-
-    @pl.when(step == 0)
-    def _():
-        fetch(step)
-
-    copies("wait", 0, 0, lax.rem(step, 2))
-
-    @pl.when(step < 9)
-    def _():
-        fetch(step + 1)
-
-    @pl.when(step == 0)
-    def _():
+                    for copy in copies(j, m, 5 * m + j):
+                        copy.start()
         g_ref[...] = jnp.zeros_like(g_ref)
         g_vec[...] = jnp.zeros_like(g_vec)
         g_vec[2:4, :] = g_two_ref[0:2, :]
 
-    second = lax.div(step, 5)
-    needed = (block >= core_ref[1 + 2 * second]) & (block < core_ref[2 + 2 * second])
-
     @pl.when(jnp.logical_not(needed))
     def _():
         mine_ref[...] = jnp.zeros_like(mine_ref)
         theirs_ref[...] = jnp.zeros_like(theirs_ref)
+
+    @pl.when(needed)
+    def _():
+        for copy in copies(0, 0, step):
+            copy.wait()
+        rows_in_order(core, slots.at[step, 0], slots.at[step, 1], n_ref)
 
     for m, (dq, dk, dv) in enumerate(((dq0_ref, dk0_ref, dv0_ref), (dq1_ref, dk1_ref, dv1_ref))):
         @pl.when(needed & (second == m))
         def _():
-            rows_in_order(core, slots[lax.rem(step, 2), 0], slots[lax.rem(step, 2), 1], x_ref)
-            d_kv[:, :384], d_kv[:, 384:] = dk[...], dv[...]
+            rows = pl.ds(pl.multiple_of(block * 512, 512), 512)
+            d_kv[:, :384], d_kv[:, 384:] = dk[rows, :], dv[rows, :]
             d_q[...] = dq[...]
 
     @pl.when(needed)
     def _():
-        n = moments(x_ref[...])[0]
+        n = n_ref[...].astype(f32)
         hiddenT = (n * vec_ref[0:1, :] + vec_ref[1:2, :]).T.astype(bf16)
-        d_hid[...] = lax.dot_general(d_kv[...], w_ref[:, 384:], NT, preferred_element_type=f32)
+        d_hid[...] = lax.dot_general(d_kv[...], w_ref[:, 384:1152], NT, preferred_element_type=f32)
         g_ref[:, 384:] += jnp.dot(hiddenT, d_kv[...], preferred_element_type=f32)
 
         @pl.when(block == 2)
@@ -562,8 +566,11 @@
             d_hid[...] += lax.dot_general(d_q[...], w_ref[:, :384], NT, preferred_element_type=f32)
 
         dh = d_hid[...]
-        mine_ref[0, 0] = jnp.where(core == 0, dh[:256], dh[256:]).astype(bf16)
-        theirs_ref[0, 0] = jnp.where(core == 0, dh[256:], dh[:256]).astype(bf16)
+        low = dh.astype(bf16)
+        for c, (first, other) in enumerate(((mine_ref, theirs_ref), (theirs_ref, mine_ref))):
+            @pl.when(core == c)
+            def _():
+                first[0, 0], other[0, 0] = low[:256], low[256:]
         g_vec[0:1, :] += jnp.sum(dh * n, axis=0, keepdims=True)
         g_vec[1:2, :] += jnp.sum(dh, axis=0, keepdims=True)
 
@@ -583,18 +590,16 @@
                 tail_ref[16 * y + 4 * z + 3] = g_out_ref[rows, :].astype(bf16)
 
 
-def project_back(core, own, other, vec, w, dq, dk, dv, g_out, g_two):
-    dq, dk, dv, (g_out,) = stay(*dq), stay(*dk), stay(*dv), stay(g_out)
-    first = pl.BlockSpec((512, 384), lambda b, *_: (jnp.minimum(b, 4), 0))
-    second = pl.BlockSpec((512, 384), lambda b, *_: (jnp.maximum(b - 5, 0), 0))
+def project_back(place, own, other, vec, w, dq, dk, dv, g_out, g_two):
+    here = pl.BlockSpec(memory_space=pltpu.VMEM)
+    part = pl.BlockSpec((1, 1, 256, 640), lambda b, *_: (lax.rem(b, 5), b // 5, 0, 0))
     return call(
-        project_back_kernel, (far(5, 2, 256, 640), far(5, 2, 256, 640), far(64, 40, 384)), "project_back", 10**10, 36, **scalar_first(
-            (10,), [pl.BlockSpec(memory_space=pl.ANY)] * 10 + [full(16, 640), full(640, 1152), full(512, 384), full(512, 384), first, second, first, second,
-                                               full(640, 384), full(8, 640)],
-            [pl.BlockSpec((1, 1, 256, 640), lambda b, *_: (lax.rem(b, 5), b // 5, 0, 0))] * 2 + [full(64, 40, 384)],
-            [pltpu.VMEM((512, 640), f32), pltpu.VMEM((512, 768), bf16), pltpu.VMEM((512, 384), bf16),
+        project_back_kernel, (far(5, 2, 256, 640), far(5, 2, 256, 640), far(64, 40, 384)), "project_back", 10**10, 30, **scalar_first(
+            (10,), [pl.BlockSpec(memory_space=pl.ANY)] * 10 + [here] * 10, [part, part, full(64, 40, 384)],
+            [pltpu.VMEM((512, 640), bf16), pltpu.VMEM((512, 768), bf16), pltpu.VMEM((512, 384), bf16),
              pltpu.VMEM((512, 640), f32), pltpu.VMEM((640, 1152), f32), pltpu.VMEM((8, 640), f32),
-             pltpu.VMEM((2, 2, 256, 640), bf16), pltpu.SemaphoreType.DMA((2, 2))]))(core, *stay(*own, *other), vec, *stay(w), *dq, *dk, *dv, g_out, g_two)
+             pltpu.VMEM((10, 2, 256, 640), bf16), pltpu.SemaphoreType.DMA((10, 2))]))(
+                 place, *stay(*own, *other), *near_by(vec, w, *dq, *dk, *dv, g_out, g_two))
 
 
 def in_core_order(core_ref, mine, theirs):
@@ -702,15 +707,17 @@
     vectors = jnp.pad(jnp.stack([gain_one, bias_one, gain_two, bias_two], axis=1), ((0, 0), (0, 124)))
     heads, tok_sent = together(pack_heads(core_arg, w_qkv, vectors), tok)
     heads = lax.all_gather(heads, "batch", axis=0, tiled=True)
-    before, after, tok_other = passed_along(tok_sent, 1), passed_along(tok_sent, -1), swapped(tok_sent)
+    vec = vector_rows(heads)
+    normal = normal_rows(tok_sent)
+    before, after, normal_other, tok_other = passed_along(normal, 1), passed_along(normal, -1), swapped(normal), swapped(tok)
     windows = [window_info(lengths[m, 0], chip, core, 2560) for m in range(2)]
     place = jnp.stack([core] + windows[0][3] + windows[1][3]).astype(jnp.int32)
     feed_pack = pack_feed(core_arg, w_out, w_up, w_down)
-    heads, before, after, tok_other, feed_pack, place, windows = together(heads, before, after, tok_other, feed_pack, place, windows)
-    own = [passed_along(before, 1), before, tok, after, passed_along(after, -1)]
-    other = [None, swapped(before), tok_other, swapped(after), None]
+    heads, vec, before, after, normal_other, tok_other, feed_pack, place, windows = together(
+        heads, vec, before, after, normal_other, tok_other, feed_pack, place, windows)
+    own = [passed_along(before, 1), before, normal, after, passed_along(after, -1)]
+    other = [None, swapped(before), normal_other, swapped(after), None]
     feed_weights = lax.all_gather(feed_pack, "batch", axis=0, tiled=True)
-    vec = vector_rows(heads)
     *near_parts, q, qT = project((1, 2, 3), place, own, other, vec, heads)
     own[0], own[4], near_parts = together(own[0], own[4], near_parts)
     other[0], other[4] = swapped(own[0]), swapped(own[4])
@@ -738,9 +745,10 @@
     sums = [mine[j].astype(f32) + theirs[j].astype(f32) for j in range(5)]
     right, left = passed_along(sums[4].astype(bf16), 1), passed_along(sums[0].astype(bf16), -1)
     tail, right, left = together(tail, right, left)
-    right = passed_along((right.astype(f32) + sums[3]).astype(bf16), 1)
-    left = passed_along((left.astype(f32) + sums[1]).astype(bf16), -1)
-    tail = gathered(jnp.sum(tail.astype(f32), axis=0).astype(bf16), "x").reshape(160, 384)
+    right, left = (right.astype(f32) + sums[3]).astype(bf16), (left.astype(f32) + sums[1]).astype(bf16)
+    tail, right, left = together(jnp.sum(tail.astype(f32), axis=0).astype(bf16), right, left)
+    right, left = passed_along(right, 1), passed_along(left, -1)
+    tail = gathered(tail, "x").reshape(160, 384)
     tail = gathered(tail, "z").reshape(16, 40, 384)
     tail, right, left = together(tail, right, left)
     d_one = (sums[2] + right.astype(f32) + left.astype(f32)).reshape(512, 640)

time: 387 us -> 379 us (0.979)
  starting transfers between devices: 73 us -> 63.6 us
  Pallas kernels: 152 us -> 157 us
  waiting for transfers between devices: 105 us -> 101 us
    all_to_all x1, starting transfers between devices: 21.9 us -> 12.9 us  [body(): tail = lax.all_to_all(tail, ('batch', 'z', 'x'), 0, 0, tiled=True)]
    pallas_call x4 -> x5, Pallas kernels: 39.1 us -> 46.7 us  [the longest x2 41.6 us: attend_back(): pl.pallas_call(attend_back_kernel, out_shape=tuple((pltpu.MemorySpace.VME...]
    pallas_call x1, Pallas kernels: 23.5 us -> 16.6 us  [project_back(): call(project_back_kernel, (far(5, 2, 256, 640), far(5, 2, 256, 640), far(...]
    all_gather x1, waiting for transfers between devices: 17.6 us -> 11.1 us  [body(): feed_weights = lax.all_gather(feed_pack, 'batch', axis=0, tiled=True)]
    pallas_call x2, Pallas kernels: 23.3 us -> 28.5 us  [attend(): pl.pallas_call(attend_kernel, out_shape=(jax.ShapeDtypeStruct((384, nq),...]
    ppermute x12 -> x13, starting transfers between devices: 9.85 us -> 9.5 us  [swapped(): return lax.ppermute(array, 'core', [(0, 1), (1, 0)])]
    ppermute x12 -> x13, waiting for transfers between devices: 11.7 us -> 11.7 us  [swapped(): return lax.ppermute(array, 'core', [(0, 1), (1, 0)])]
  transfers between devices with their start and end apart: 31 -> 32, of which waited for: 18 -> 18; matrix products, arithmetic and copies ran while one was open for 5% -> 5% of each run, Pallas kernels for 31% -> 33%
where the time goes in v9:
time: 379 us; the launch traced here: 373 us
  Pallas kernels  157 us (41%)
  waiting for transfers between devices  101 us (27%)
  starting transfers between devices  63.6 us (17%)
  between operations  20.2 us (5%)
  other arithmetic  18.2 us (5%)
  local copies, waits for them, and re-layouts  12 us (3%)
    pallas_call x2, Pallas kernels, attend_back(): pl.pallas_call(attend_back_kernel, out_shape=tuple((pltpu.MemorySpace.VME...  41.6 us
    pallas_call x1, Pallas kernels, feed_forward(): call(feed_kernel, (far(2, 512, 640), far(2, 512, 640), far(4, 16, 80, 640...  31.9 us
    pallas_call x2, Pallas kernels, attend(): pl.pallas_call(attend_kernel, out_shape=(jax.ShapeDtypeStruct((384, nq),...  28.5 us
    ppermute x6, waiting for transfers between devices, shifted(): lax.ppermute(array, axis, [(i, (i + by) % devices) for i in range(devices)])  21 us
    all_gather x1, waiting for transfers between devices, body(): heads = lax.all_gather(heads, 'batch', axis=0, tiled=True)  18.6 us
    pallas_call x1, Pallas kernels, project_back(): call(project_back_kernel, (far(5, 2, 256, 640), far(5, 2, 256, 640), far(...  16.6 us
    ppermute x8, starting transfers between devices, passed_along(): lax.ppermute(array, ('z', 'x'), [(i, i + by) for i in range(devices) if 0...  16.5 us
    pallas_call x2, Pallas kernels, project(): call(lambda *refs: project_kernel(chips, *refs), shapes, 'project', 5 * 1...  16 us
  transfers between devices with their start and end apart: 32, of which 18 were waited for; matrix products, arithmetic and copies ran while one was open for 5% of the time, Pallas kernels for 33%

profile of v9, /device:TPU:1, one launch (start us, length us, event | category | flops | bytes accessed | tf_op | source)
XLA Modules:
  0.0 372.6 jit_solution(17902851015977544792)
XLA Ops:
  12.4 4.0 %collective-permute-start = (bf16[2,256,640]{2,1,0:T(8,128)(2,1)S(1)}, bf16[2,256,640]{2,1,0:T(8,128)(2,1)S(1)}, u32[]{:S(2)}, u32[]{:S(2)}) collective-permute-start(bf16[2,256,640]{2,1,0:T(8,128)(2,1)S(1)} %normal_rows.1.refs_2_), channel_id=1, source_target_pairs={{0,2},{2,4},{4,6},{6,8},{8,10},{10,12},{12,14},{14,16},{16,18},{18... | collective-permute-start | bytes 1966088 | tf_op jit(solution)/shard_map/ppermute | solution.py:654
  31.2 18.6 %all-gather.4.cloned.1.call-done.vec_ref.refs_8_.refs_6_.refs_11_ = bf16[640,1280]{1,0:T(8,128)(2,1)} async-done(((bf16[160,1280]{1,0:T(8,128)(2,1)}), bf16[640,1280]{1,0:T(8,128)(2,1)}) %all-gather.4.cloned.1.call-update) | async-done | bytes 1638416 | tf_op jit(solution)/shard_map/all_gather | solution.py:709
  57.6 10.5 %project.2 = (bf16[2,2560,384]{2,1,0:T(8,128)(2,1)}, bf16[2,2560,384]{2,1,0:T(8,128)(2,1)}, bf16[2,384,2560]{2,1,0:T(8,128)(2,1)}, bf16[2,384,2560]{2,1,0:T(8,12...) custom-call(s32[5]{0:T(128)S(1)} %stack.81.refs_0_.place_ref, ...), custom_call_target="tpu_custom_call" | custom-call | flops 100000000 | tf_op jit(solution)/shard_map/project/pallas_call | solution.py:374
  69.1 4.1 %collective-permute-done.7.refs_2_.refs_4_ = bf16[2,256,640]{2,1,0:T(8,128)(2,1)S(1)} collective-permute-done((bf16[2,256,640]{2,1,0:T(8,128)(2,1)}, bf16[2,256,640]{2,1,0:T(8,128)(2,1)S(1)}, u32[]{:S(2)}, u32[]{:S(2)}) %collective-permute-start.7) | collective-permute-done | bytes 655392 | tf_op jit(solution)/shard_map/ppermute | solution.py:654
  77.4 5.5 %project.3 = (bf16[2,2560,384]{2,1,0:T(8,128)(2,1)}, bf16[2,2560,384]{2,1,0:T(8,128)(2,1)}, bf16[2,384,2560]{2,1,0:T(8,128)(2,1)}, bf16[2,384,2560]{2,1,0:T(8,128)(2,1)}) custom-call(s32[5]{0:T(128)S(1)} %stack.81.refs_0_.place_ref, ...), custom_call_target="tpu_custom_call", output_to_operand_aliasing={{0}: (7, {}), {1}: (8, {}), {2}: (9, {}), {3}: (10, {})} | custom-call | flops 100000000 | tf_op jit(solution)/shard_map/project/pallas_call | solution.py:374
  82.9 14.5 %attend.3 = (f32[384,512]{1,0:T(8,128)S(1)}, bf16[512,384]{1,0:T(8,128)(2,1)S(1)}, f32[5,8,512]{2,1,0:T(8,128)S(1)}) custom-call(s32[5]{0:T(128)S(1)} %stack.91.info_ref, bf16[2,384,512]{2,1,0:T(8,128)(2,1)} %get-tuple-element.101.qT_ref, bf16[2,2560,384]{2,1,0:T(8,128)(2,1)} %get-tuple-element.112.k_ref, bf16[2,384,2560]{2,1,0:T(8,128)(2,1)} %get-tuple-element.113.vT_ref, ...), custom_call_target="tpu_custom_call" | custom-call | flops 400000000 | tf_op jit(solution)/shard_map/attend/pallas_call | solution.py:98
  98.4 14.0 %attend.2 = (f32[384,512]{1,0:T(8,128)S(1)}, bf16[512,384]{1,0:T(8,128)(2,1)S(1)}, f32[5,8,512]{2,1,0:T(8,128)S(1)}) custom-call(s32[5]{0:T(128)S(1)} %stack.86.info_ref, bf16[2,384,512]{2,1,0:T(8,128)(2,1)} %get-tuple-element.101.qT_ref, bf16[2,2560,384]{2,1,0:T(8,128)(2,1)} %get-tuple-element.112.k_ref, bf16[2,384,2560]{2,1,0:T(8,128)(2,1)} %get-tuple-element.113.vT_ref, ...), custom_call_target="tpu_custom_call" | custom-call | flops 400000000 | tf_op jit(solution)/shard_map/attend/pallas_call | solution.py:98
  115.5 11.1 %all-gather.6.cloned.1.call-done.w_ref.up_ref.down_ref = bf16[640,5760]{1,0:T(8,128)(2,1)} async-done(((bf16[160,5760]{1,0:T(8,128)(2,1)}), bf16[640,5760]{1,0:T(8,128)(2,1)}) %all-gather.6.cloned.1.call-update) | async-done | bytes 7372816 | tf_op jit(solution)/shard_map/all_gather | solution.py:720
  127.4 4.6 %middle.1 = (f32[512,640]{1,0:T(8,128)}, bf16[512,640]{1,0:T(8,128)(2,1)}, bf16[512,640]{1,0:T(8,128)(2,1)}) custom-call(s32[1]{0:T(128)} %bitcast.core_ref, bf16[640,5760]{1,0:T(8,128)(2,1)} %all-gather.6.cloned.1.call-done.w_ref.up_ref.down_ref, bf16[512,384]{1,0:T(8,128)(2,1)S(1)} %get-tuple-element.116.low0_ref, ...), custom_call_target="tpu_custom_call" | custom-call | flops 20000000 | tf_op jit(solution)/shard_map/middle/pallas_call | solution.py:403
  132.1 31.9 %feed_forward.1 = (bf16[2,512,640]{2,1,0:T(8,128)(2,1)}, bf16[2,512,640]{2,1,0:T(8,128)(2,1)}, bf16[4,16,80,640]{3,2,1,0:T(8,128)(2,1)}) custom-call(bf16[512,640]{1,0:T(8,128)(2,1)} %get-tuple-element.123.h_ref, bf16[512,640]{1,0:T(8,128)(2,1)} %get-tuple-element.124.h2_ref, bf16[512,640]{1,0:T(8,128)(2,1)} %bitcast.20.cot_ref, ...), custom_call_target="tpu_custom_call" | custom-call | flops 600000000 | tf_op jit(solution)/shard_map/feed_forward/pallas_call | solution.py:450
  164.0 9.8 %all-to-all-start = ((bf16[64,80,640]{2,1,0:T(8,128)(2,1)}), bf16[64,80,640]{2,1,0:T(8,128)(2,1)}, u32[]{:S(2)}, u32[]{:S(2)}) async-start(bf16[64,80,640]{2,1,0:T(8,128)(2,1)} %bitcast.113), calls=%async_computation | async-start | bytes 13107200 | tf_op jit(solution)/shard_map/all_to_all | solution.py:731
  178.5 4.4 %after_feed.1 = (bf16[512,640]{1,0:T(8,128)(2,1)}, f32[512,640]{1,0:T(8,128)}, bf16[512,640]{1,0:T(8,128)(2,1)S(1)}, f32[8,640]{1,0:T(8,128)S(1)}) custom-call(f32[512,640]{1,0:T(8,128)} %get-tuple-element.122.mid_ref, bf16[2,512,640]{2,1,0:T(8,128)(2,1)} %get-tuple-element.125.mine_ref, bf16[2,512,640]{2,1,0:T(8,128)(2,1)S(1)} %collective-permute-done.12.theirs_ref, ...), custom_call_target="tpu_custom_call" | custom-call | flops 20000000 | tf_op jit(solution)/shard_map/after_feed/pallas_call | solution.py:479
  185.1 3.7 %branch.1 = (bf16[1024,384]{1,0:T(8,128)(2,1)}, bf16[384,1024]{1,0:T(8,128)(2,1)}, bf16[640,384]{1,0:T(8,128)(2,1)S(1)}) custom-call(s32[1]{0:T(128)} %bitcast.core_ref, bf16[512,640]{1,0:T(8,128)(2,1)S(1)} %get-tuple-element.132.own_ref, bf16[512,640]{1,0:T(8,128)(2,1)S(1)} %collective-permute-done.13.their_ref, ...), custom_call_target="tpu_custom_call" | custom-call | flops 20000000 | tf_op jit(solution)/shard_map/branch/pallas_call | solution.py:504
  188.9 20.0 %attend_back.3 = (bf16[512,384]{1,0:T(8,128)(2,1)S(1)}, bf16[2560,384]{1,0:T(8,128)(2,1)S(1)}, bf16[2560,384]{1,0:T(8,128)(2,1)S(1)}) custom-call(s32[5]{0:T(128)S(1)} %stack.91.info_ref, bf16[2,384,512]{2,1,0:T(8,128)(2,1)} %get-tuple-element.101.qT_ref, bf16[2,512,384]{2,1,0:T(8,128)(2,1)} %get-tuple-element.129.q_ref, ...), custom_call_target="tpu_custom_call" | custom-call | flops 800000000 | tf_op jit(solution)/shard_map/attend_back/pallas_call | solution.py:211
  209.0 21.6 %attend_back.2 = (bf16[512,384]{1,0:T(8,128)(2,1)S(1)}, bf16[2560,384]{1,0:T(8,128)(2,1)S(1)}, bf16[2560,384]{1,0:T(8,128)(2,1)S(1)}) custom-call(s32[5]{0:T(128)S(1)} %stack.86.info_ref, bf16[2,384,512]{2,1,0:T(8,128)(2,1)} %get-tuple-element.101.qT_ref, bf16[2,512,384]{2,1,0:T(8,128)(2,1)} %get-tuple-element.129.q_ref, ...), custom_call_target="tpu_custom_call" | custom-call | flops 800000000 | tf_op jit(solution)/shard_map/attend_back/pallas_call | solution.py:211
  230.6 16.6 %project_back.1 = (bf16[5,2,256,640]{3,2,1,0:T(8,128)(2,1)}, bf16[5,2,256,640]{3,2,1,0:T(8,128)(2,1)}, bf16[64,40,384]{2,1,0:T(8,128)(2,1)}) custom-call(s32[5]{0:T(128)S(1)} %stack.81.refs_0_.place_ref, bf16[2,256,640]{2,1,0:T(8,128)(2,1)} %copy-done.6, bf16[2,256,640]{2,1,0:T(8,128)(2,1)} %copy-done.3, bf16[2,256,640]{2,1,0:T(8,128)(2,1)} %copy-done.2, ...), custom_call_target="tpu_custom_call" | custom-call | flops 200000000 | tf_op jit(solution)/shard_map/project_back/pallas_call | solution.py:596
  247.2 8.1 %all-to-all-done = bf16[64,80,640]{2,1,0:T(8,128)(2,1)} async-done(((bf16[64,80,640]{2,1,0:T(8,128)(2,1)}), bf16[64,80,640]{2,1,0:T(8,128)(2,1)}, u32[]{:S(2)}, u32[]{:S(2)}) %all-to-all-start) | async-done | bytes 6553632 | tf_op jit(solution)/shard_map/all_to_all | solution.py:731
  257.9 12.9 %all-to-all-start.1 = ((bf16[64,40,384]{2,1,0:T(8,128)(2,1)}), bf16[64,40,384]{2,1,0:T(8,128)(2,1)S(1)}, u32[]{:S(2)}, u32[]{:S(2)}) async-start(bf16[64,40,384]{2,1,0:T(8,128)(2,1)} %get-tuple-element.150), calls=%async_computation.1 | async-start | bytes 3932160 | tf_op jit(solution)/shard_map/all_to_all | solution.py:742
  278.8 4.5 %reduce_sum.65 = bf16[80,640]{1,0:T(8,128)(2,1)} reduce(bf16[64,80,640]{2,1,0:T(8,128)(2,1)} %all-to-all-done, bf16[]{:T(256)} %constant.193.clone.1), dimensions={0}, to_apply=%region_15.16 | reduce | flops 3225600 | bytes 6656002 | tf_op jit(solution)/shard_map/reduce_sum | solution.py:741
  283.3 15.8 %all-to-all-done.1 = bf16[64,40,384]{2,1,0:T(8,128)(2,1)S(1)} async-done(((bf16[64,40,384]{2,1,0:T(8,128)(2,1)}), bf16[64,40,384]{2,1,0:T(8,128)(2,1)S(1)}, u32[]{:S(2)}, u32[]{:S(2)}) %all-to-all-start.1) | async-done | bytes 1966112 | tf_op jit(solution)/shard_map/all_to_all | solution.py:742
  299.1 7.8 %collective-permute-done.15 = bf16[2,256,640]{2,1,0:T(8,128)(2,1)S(1)} collective-permute-done((bf16[2,256,640]{2,1,0:T(8,128)(2,1)}, bf16[2,256,640]{2,1,0:T(8,128)(2,1)S(1)}, u32[]{:S(2)}, u32[]{:S(2)}) %collective-permute-start.15) | collective-permute-done | bytes 655392 | tf_op jit(solution)/shard_map/ppermute | solution.py:654
  325.6 6.5 %collective-permute-start.21 = (bf16[160,384]{1,0:T(8,128)(2,1)S(1)}, bf16[160,384]{1,0:T(8,128)(2,1)S(1)}, u32[]{:S(2)}, u32[]{:S(2)}) collective-permute-start(bf16[160,384]{1,0:T(8,128)(2,1)S(1)} %bitcast.116), channel_id=1, source_target_pairs={{0,24},{8,0},{16,8},{24,16},{1,25},{9,1},{17,9},{25,17},{2,26},{10... | collective-permute-start | bytes 368648 | tf_op jit(solution)/shard_map/ppermute | solution.py:649
  336.1 15.0 %collective-permute-done.22 = bf16[160,384]{1,0:T(8,128)(2,1)S(1)} collective-permute-done((bf16[160,384]{1,0:T(8,128)(2,1)S(1)}, bf16[160,384]{1,0:T(8,128)(2,1)S(1)}, u32[]{:S(2)}, u32[]{:S(2)}) %collective-permute-start.22) | collective-permute-done | bytes 122912 | tf_op jit(solution)/shard_map/ppermute | solution.py:649
  355.5 3.7 collective-permute-done.25.theirs_ref
  (179 shorter events, 83.0 us)
Async XLA Ops:
  7.2 42.6 %all-gather.4.cloned.1.call-start = ((), (), s32[]{:S(2)}) async-start(), calls=%async_computation.2 | async-start | bytes 2048000 | tf_op jit(solution)/shard_map/all_gather | solution.py:709
  12.4 39.0 %collective-permute-start = (bf16[2,256,640]{2,1,0:T(8,128)(2,1)S(1)}, bf16[2,256,640]{2,1,0:T(8,128)(2,1)S(1)}, u32[]{:S(2)}, u32[]{:S(2)}) collective-permute-start(bf16[2,256,640]{2,1,0:T(8,128)(2,1)S(1)} %normal_rows.1.refs_2_), channel_id=1, source_target_pairs={{0,2},{2,4},{4,6},{6,8},{8,10},{10,12},{12,14},{14,16},{16,18},{18... | collective-permute-start | bytes 1966088 | tf_op jit(solution)/shard_map/ppermute | solution.py:654
  16.4 35.1 %collective-permute-start.1 = (bf16[2,256,640]{2,1,0:T(8,128)(2,1)S(1)}, bf16[2,256,640]{2,1,0:T(8,128)(2,1)}, u32[]{:S(2)}, u32[]{:S(2)}) collective-permute-start(bf16[2,256,640]{2,1,0:T(8,128)(2,1)S(1)} %normal_rows.1.refs_2_), channel_id=1, source_target_pairs={{2,0},{4,2},{6,4},{8,6},{10,8},{12,10},{14,12},{16,14},{18,16},{20... | collective-permute-start | bytes 1966088 | tf_op jit(solution)/shard_map/ppermute | solution.py:654
  17.7 33.8 %collective-permute-start.2 = (bf16[2,256,640]{2,1,0:T(8,128)(2,1)S(1)}, bf16[2,256,640]{2,1,0:T(8,128)(2,1)}, u32[]{:S(2)}, u32[]{:S(2)}) collective-permute-start(bf16[2,256,640]{2,1,0:T(8,128)(2,1)S(1)} %normal_rows.1.refs_2_), channel_id=1, source_target_pairs={{0,1},{1,0},{2,3},{3,2},{4,5},{5,4},{6,7},{7,6},{8,9},{9,8},{10,11... | collective-permute-start | bytes 1966088 | tf_op jit(solution)/shard_map/ppermute | solution.py:658
  18.7 32.7 %collective-permute-start.3 = (bf16[2,256,640]{2,1,0:T(8,128)(2,1)S(1)}, bf16[2,256,640]{2,1,0:T(8,128)(2,1)}, u32[]{:S(2)}, u32[]{:S(2)}) collective-permute-start(bf16[2,256,640]{2,1,0:T(8,128)(2,1)S(1)} %bitcast.105), channel_id=1, source_target_pairs={{0,1},{1,0},{2,3},{3,2},{4,5},{5,4},{6,7},{7,6},{8,9},{9,8},{10,11... | collective-permute-start | bytes 1966088 | tf_op jit(solution)/shard_map/ppermute | solution.py:658
  18.8 107.8 %all-gather.6.cloned.1.call-start = ((), (), s32[]{:S(2)}) async-start(), calls=%async_computation.3 | async-start | bytes 9216000 | tf_op jit(solution)/shard_map/all_gather | solution.py:720
  51.5 5.3 %collective-permute-start.4 = (bf16[2,256,640]{2,1,0:T(8,128)(2,1)S(1)}, bf16[2,256,640]{2,1,0:T(8,128)(2,1)S(1)}, u32[]{:S(2)}, u32[]{:S(2)}) collective-permute-start(bf16[2,256,640]{2,1,0:T(8,128)(2,1)S(1)} %collective-permute-done.refs_1_), channel_id=1, source_target_pairs={{0,1},{1,0},{2,3},{3,2},{4,5},{5,4},{6,7},{7,6},{8,9},{9,8},{10,11... | collective-permute-start | bytes 1966088 | tf_op jit(solution)/shard_map/ppermute | solution.py:658
  52.3 16.8 %collective-permute-start.6 = (bf16[2,256,640]{2,1,0:T(8,128)(2,1)S(1)}, bf16[2,256,640]{2,1,0:T(8,128)(2,1)S(1)}, u32[]{:S(2)}, u32[]{:S(2)}) collective-permute-start(bf16[2,256,640]{2,1,0:T(8,128)(2,1)S(1)} %collective-permute-done.refs_1_), channel_id=1, source_target_pairs={{0,2},{2,4},{4,6},{6,8},{8,10},{10,12},{12,14},{14,16},{16,18},{18... | collective-permute-start | bytes 1966088 | tf_op jit(solution)/shard_map/ppermute | solution.py:654
  55.5 17.8 %collective-permute-start.7 = (bf16[2,256,640]{2,1,0:T(8,128)(2,1)}, bf16[2,256,640]{2,1,0:T(8,128)(2,1)S(1)}, u32[]{:S(2)}, u32[]{:S(2)}) collective-permute-start(bf16[2,256,640]{2,1,0:T(8,128)(2,1)} %collective-permute-done.1.refs_3_), channel_id=1, source_target_pairs={{2,0},{4,2},{6,4},{8,6},{10,8},{12,10},{14,12},{16,14},{18,16},{20... | collective-permute-start | bytes 1966088 | tf_op jit(solution)/shard_map/ppermute | solution.py:654
  113.9 18.1 %collective-permute-start.11 = (bf16[512,640]{1,0:T(8,128)(2,1)}, bf16[512,640]{1,0:T(8,128)(2,1)}, u32[]{:S(2)}, u32[]{:S(2)}) collective-permute-start(bf16[512,640]{1,0:T(8,128)(2,1)} %bitcast.20.cot_ref), channel_id=1, source_target_pairs={{0,1},{1,0},{2,3},{3,2},{4,5},{5,4},{6,7},{7,6},{8,9},{9,8},{10,11... | collective-permute-start | bytes 1966088 | tf_op jit(solution)/shard_map/ppermute | solution.py:658
  164.0 91.3 %all-to-all-start = ((bf16[64,80,640]{2,1,0:T(8,128)(2,1)}), bf16[64,80,640]{2,1,0:T(8,128)(2,1)}, u32[]{:S(2)}, u32[]{:S(2)}) async-start(bf16[64,80,640]{2,1,0:T(8,128)(2,1)} %bitcast.113), calls=%async_computation | async-start | bytes 13107200 | tf_op jit(solution)/shard_map/all_to_all | solution.py:731
  255.3 15.6 %collective-permute-start.14 = (bf16[5,2,256,640]{3,2,1,0:T(8,128)(2,1)}, bf16[5,2,256,640]{3,2,1,0:T(8,128)(2,1)}, u32[]{:S(2)}, u32[]{:S(2)}) collective-permute-start(bf16[5,2,256,640]{3,2,1,0:T(8,128)(2,1)} %get-tuple-element.152), channel_id=1, source_target_pairs={{0,1},{1,0},{2,3},{3,2},{4,5},{5,4},{6,7},{7,6},{8,9},{9,8},{10,11... | collective-permute-start | bytes 9830408 | tf_op jit(solution)/shard_map/ppermute | solution.py:658
  257.9 41.2 %all-to-all-start.1 = ((bf16[64,40,384]{2,1,0:T(8,128)(2,1)}), bf16[64,40,384]{2,1,0:T(8,128)(2,1)S(1)}, u32[]{:S(2)}, u32[]{:S(2)}) async-start(bf16[64,40,384]{2,1,0:T(8,128)(2,1)} %get-tuple-element.150), calls=%async_computation.1 | async-start | bytes 3932160 | tf_op jit(solution)/shard_map/all_to_all | solution.py:742
  270.8 84.0 %all-gather.8.cloned.1.call-start = ((), (), s32[]{:S(2)}) async-start(), calls=%async_computation.4 | async-start | bytes 1740800 | tf_op jit(solution)/shard_map/all_gather | solution.py:743
  273.9 33.0 %collective-permute-start.15 = (bf16[2,256,640]{2,1,0:T(8,128)(2,1)}, bf16[2,256,640]{2,1,0:T(8,128)(2,1)S(1)}, u32[]{:S(2)}, u32[]{:S(2)}) collective-permute-start(bf16[2,256,640]{2,1,0:T(8,128)(2,1)} %get-tuple-element.222), channel_id=1, source_target_pairs={{0,2},{2,4},{4,6},{6,8},{8,10},{10,12},{12,14},{14,16},{16,18},{18... | collective-permute-start | bytes 1966088 | tf_op jit(solution)/shard_map/ppermute | solution.py:654
  276.9 32.0 %collective-permute-start.16 = (bf16[2,256,640]{2,1,0:T(8,128)(2,1)}, bf16[2,256,640]{2,1,0:T(8,128)(2,1)}, u32[]{:S(2)}, u32[]{:S(2)}) collective-permute-start(bf16[2,256,640]{2,1,0:T(8,128)(2,1)} %get-tuple-element.221), channel_id=1, source_target_pairs={{2,0},{4,2},{6,4},{8,6},{10,8},{12,10},{14,12},{16,14},{18,16},{20... | collective-permute-start | bytes 1966088 | tf_op jit(solution)/shard_map/ppermute | solution.py:654
  312.5 4.7 %collective-permute-start.17 = (bf16[40,384]{1,0:T(8,128)(2,1)S(1)}, bf16[40,384]{1,0:T(8,128)(2,1)S(1)}, u32[]{:S(2)}, u32[]{:S(2)}) collective-permute-start(bf16[40,384]{1,0:T(8,128)(2,1)S(1)} %reduce_sum.60), channel_id=1, source_target_pairs={{0,2},{2,4},{4,6},{6,0},{1,3},{3,5},{5,7},{7,1},{8,10},{10,12},{12... | collective-permute-start | bytes 92168 | tf_op jit(solution)/shard_map/ppermute | solution.py:649
  316.0 4.5 %collective-permute-start.19 = (bf16[40,384]{1,0:T(8,128)(2,1)S(1)}, bf16[40,384]{1,0:T(8,128)(2,1)S(1)}, u32[]{:S(2)}, u32[]{:S(2)}) collective-permute-start(bf16[40,384]{1,0:T(8,128)(2,1)S(1)} %reduce_sum.60), channel_id=1, source_target_pairs={{0,4},{2,6},{4,0},{6,2},{1,5},{3,7},{5,1},{7,3},{8,12},{10,14},{12... | collective-permute-start | bytes 92168 | tf_op jit(solution)/shard_map/ppermute | solution.py:649
  320.5 12.9 %collective-permute-start.20 = (bf16[160,384]{1,0:T(8,128)(2,1)S(1)}, bf16[160,384]{1,0:T(8,128)(2,1)S(1)}, u32[]{:S(2)}, u32[]{:S(2)}) collective-permute-start(bf16[160,384]{1,0:T(8,128)(2,1)S(1)} %bitcast.115), channel_id=1, source_target_pairs={{0,8},{8,16},{16,24},{24,0},{1,9},{9,17},{17,25},{25,1},{2,10},{10... | collective-permute-start | bytes 368648 | tf_op jit(solution)/shard_map/ppermute | solution.py:649
  322.9 28.2 %collective-permute-start.23 = (bf16[2,256,640]{2,1,0:T(8,128)(2,1)}, bf16[2,256,640]{2,1,0:T(8,128)(2,1)S(1)}, u32[]{:S(2)}, u32[]{:S(2)}) collective-permute-start(bf16[2,256,640]{2,1,0:T(8,128)(2,1)} %get-tuple-element.157), channel_id=1, source_target_pairs={{0,2},{2,4},{4,6},{6,8},{8,10},{10,12},{12,14},{14,16},{16,18},{18... | collective-permute-start | bytes 1966088 | tf_op jit(solution)/shard_map/ppermute | solution.py:654
  324.3 26.9 %collective-permute-start.24 = (bf16[2,256,640]{2,1,0:T(8,128)(2,1)}, bf16[2,256,640]{2,1,0:T(8,128)(2,1)S(1)}, u32[]{:S(2)}, u32[]{:S(2)}) collective-permute-start(bf16[2,256,640]{2,1,0:T(8,128)(2,1)} %get-tuple-element.158), channel_id=1, source_target_pairs={{2,0},{4,2},{6,4},{8,6},{10,8},{12,10},{14,12},{16,14},{18,16},{20... | collective-permute-start | bytes 1966088 | tf_op jit(solution)/shard_map/ppermute | solution.py:654
  325.6 10.5 %collective-permute-start.21 = (bf16[160,384]{1,0:T(8,128)(2,1)S(1)}, bf16[160,384]{1,0:T(8,128)(2,1)S(1)}, u32[]{:S(2)}, u32[]{:S(2)}) collective-permute-start(bf16[160,384]{1,0:T(8,128)(2,1)S(1)} %bitcast.116), channel_id=1, source_target_pairs={{0,24},{8,0},{16,8},{24,16},{1,25},{9,1},{17,9},{25,17},{2,26},{10... | collective-permute-start | bytes 368648 | tf_op jit(solution)/shard_map/ppermute | solution.py:649
  332.1 19.1 %collective-permute-start.22 = (bf16[160,384]{1,0:T(8,128)(2,1)S(1)}, bf16[160,384]{1,0:T(8,128)(2,1)S(1)}, u32[]{:S(2)}, u32[]{:S(2)}) collective-permute-start(bf16[160,384]{1,0:T(8,128)(2,1)S(1)} %bitcast.117), channel_id=1, source_target_pairs={{0,16},{8,24},{16,0},{24,8},{1,17},{9,25},{17,1},{25,9},{2,18},{10... | collective-permute-start | bytes 368648 | tf_op jit(solution)/shard_map/ppermute | solution.py:649
  354.8 6.6 %collective-permute-start.26 = (bf16[16,80,640]{2,1,0:T(8,128)(2,1)}, bf16[16,80,640]{2,1,0:T(8,128)(2,1)S(1)}, u32[]{:S(2)}, u32[]{:S(2)}) collective-permute-start(bf16[16,80,640]{2,1,0:T(8,128)(2,1)} %bitcast.111), channel_id=1, source_target_pairs={{0,1},{1,0},{2,3},{3,2},{4,5},{5,4},{6,7},{7,6},{8,9},{9,8},{10,11... | collective-permute-start | bytes 4915208 | tf_op jit(solution)/shard_map/ppermute | solution.py:658
  (40 other events, 439.0 us)
Sparse Core Ops, SparseCore 0:
  18.9 30.7 all-gather.3
  52.0 74.5 all-gather.5
  283.4 53.4 all-gather.7

commit v10 on v9

--- a/solution.py
+++ b/solution.py
@@ -436,9 +436,9 @@
     for f in range(2):
         for y in range(4):
             for i in range(2):
-                g_ref[y, 4 * chunk + 2 * f + i] = g_up[160 * y + 80 * i:160 * y + 80 * (i + 1), 640 * f:640 * (f + 1)]
+                g_ref[4 * chunk + 2 * f + i, y] = g_up[160 * y + 80 * i:160 * y + 80 * (i + 1), 640 * f:640 * (f + 1)]
         for i in range(8):
-            g_ref[2 * chunk + f, 8 + i] = g_down[640 * f + 80 * i:640 * f + 80 * (i + 1)]
+            g_ref[8 + i, 2 * chunk + f] = g_down[640 * f + 80 * i:640 * f + 80 * (i + 1)]
 
     @pl.when(chunk == 1)
     def _():
@@ -449,10 +449,10 @@
 def feed_forward(h, h2, cot, cot2, weights):
     return call(
         feed_kernel,
-        (far(2, 512, 640), far(2, 512, 640), far(4, 16, 80, 640)),
+        (far(2, 512, 640), far(2, 512, 640), far(16, 4, 80, 640)),
         "feed_forward", 30 * 10**9, 52, grid=(2,),
         in_specs=[full(512, 640)] * 4 + [pl.BlockSpec((640, 1280), lambda f: (0, f)), pl.BlockSpec((320, 2560), lambda f: (f, 1))],
-        out_specs=[full(2, 512, 640), full(2, 512, 640), full(4, 16, 80, 640)],
+        out_specs=[full(2, 512, 640), full(2, 512, 640), full(16, 4, 80, 640)],
         scratch_shapes=[pltpu.VMEM((1024, 640), bf16), pltpu.VMEM((1024, 640), bf16), pltpu.VMEM((640, 1024), bf16), pltpu.VMEM((640, 1024), bf16),
                         pltpu.VMEM((1024, 640), f32), pltpu.VMEM((1024, 640), f32)],
     )(*stay(h, h2, cot), cot2, *stay(weights, weights))
@@ -660,6 +660,14 @@
 
 def pick(array, index):
     return lax.dynamic_index_in_dim(array, index, 0, keepdims=False)
+
+
+def summed_share(array, axis):
+    me, devices = lax.axis_index(axis), lax.axis_size(axis)
+    total = pick(array, me).astype(f32)
+    for by in (1, devices - 1, 2):
+        total = total + shifted(pick(array, (me + by) % devices), axis, by).astype(f32)
+    return total.astype(bf16)
 
 
 def gathered(array, axis):
@@ -728,7 +736,7 @@
     theirs = swapped(jnp.stack([low0, low1]))
     middle, hidden_two, hidden_other = middle_step(core_arg, feed_weights, low0, low1, theirs, tok, tok_other, vec)
     mine, partial, feed_grads = feed_forward(hidden_two, hidden_other, cot, swapped(cot), feed_weights)
-    feed_grads = lax.all_to_all(feed_grads.reshape(64, 80, 640), ("batch", "z", "x"), 0, 0, tiled=True)
+    feed_grads = lax.psum_scatter(feed_grads.reshape(5120, 640), ("z", "x"), scatter_dimension=0, tiled=True)
     block_out, grad_middle, branch, g_two = after_feed(middle, mine, swapped(partial), cot, vec)
 
     do, doT, g_out = branch_step(core_arg, branch, swapped(branch), feed_weights, low0, low1, theirs)
@@ -738,10 +746,10 @@
     mine, theirs, tail = project_back(place, own, other, vec, heads, dq, dk, dv, g_out, g_two)
     feed_grads, mine, theirs, tail = together(feed_grads, mine, theirs, tail)
 
-    feed = jnp.sum(feed_grads.astype(f32), axis=0).astype(bf16)
+    feed = summed_share(feed_grads.reshape(4, 80, 640), "batch")
     tail = lax.all_to_all(tail, ("batch", "z", "x"), 0, 0, tiled=True)
+    theirs, mine, feed = together(swapped(theirs), mine, feed)
     feed = lax.all_gather(feed, ("z", "x"), axis=0, tiled=True).reshape(16, 80, 640)
-    theirs = swapped(theirs)
     sums = [mine[j].astype(f32) + theirs[j].astype(f32) for j in range(5)]
     right, left = passed_along(sums[4].astype(bf16), 1), passed_along(sums[0].astype(bf16), -1)
     tail, right, left = together(tail, right, left)

time: 379 us -> 385 us (1.016)
  waiting for transfers between devices: 101 us -> 131 us
  Pallas kernels: 157 us -> 143 us
  starting transfers between devices: 63.6 us -> 58.1 us
    ppermute x6 -> x9, waiting for transfers between devices: 21 us -> 45.3 us  [shifted(): lax.ppermute(array, axis, [(i, (i + by) % devices) for i in range(devices)])]
    reduce_scatter x0 -> x1, waiting for transfers between devices: none -> 17.8 us  [body(): lax.psum_scatter(feed_grads.reshape(5120, 640), ('z', 'x'), scatter_dimen...]
    all_to_all x1, waiting for transfers between devices: 15.8 us -> 0.01 us  [body(): tail = lax.all_to_all(tail, ('batch', 'z', 'x'), 0, 0, tiled=True)]
    all_to_all x1 -> x0, starting transfers between devices: 9.82 us -> none  [body(): lax.all_to_all(feed_grads.reshape(64, 80, 640), ('batch', 'z', 'x'), 0, 0...]
    pallas_call x2, Pallas kernels: 41.6 us -> 33.4 us  [attend_back(): pl.pallas_call(attend_back_kernel, out_shape=tuple((pltpu.MemorySpace.VME...]
    all_to_all x1 -> x0, waiting for transfers between devices: 8.13 us -> none  [body(): lax.all_to_all(feed_grads.reshape(64, 80, 640), ('batch', 'z', 'x'), 0, 0...]
    ppermute x8, waiting for transfers between devices: 14.8 us -> 20.9 us  [passed_along(): lax.ppermute(array, ('z', 'x'), [(i, i + by) for i in range(devices) if 0...]
    all_gather x1, waiting for transfers between devices: 11.1 us -> 16.6 us  [body(): feed_weights = lax.all_gather(feed_pack, 'batch', axis=0, tiled=True)]
  transfers between devices with their start and end apart: 32 -> 35, of which waited for: 18 -> 20; matrix products, arithmetic and copies ran while one was open for 5% -> 5% of each run, Pallas kernels for 33% -> 28%
where the time goes in v10:
time: 385 us; the launch traced here: 380 us
  Pallas kernels  143 us (37%)
  waiting for transfers between devices  131 us (34%)
  starting transfers between devices  58.1 us (15%)
  between operations  20.3 us (5%)
  other arithmetic  15.4 us (4%)
  local copies, waits for them, and re-layouts  12.7 us (3%)
    ppermute x9, waiting for transfers between devices, shifted(): lax.ppermute(array, axis, [(i, (i + by) % devices) for i in range(devices)])  45.3 us
    pallas_call x2, Pallas kernels, attend_back(): pl.pallas_call(attend_back_kernel, out_shape=tuple((pltpu.MemorySpace.VME...  33.4 us
    pallas_call x1, Pallas kernels, feed_forward(): call(feed_kernel, (far(2, 512, 640), far(2, 512, 640), far(16, 4, 80, 640...  32.1 us
    pallas_call x2, Pallas kernels, attend(): pl.pallas_call(attend_kernel, out_shape=(jax.ShapeDtypeStruct((384, nq),...  23.4 us
    ppermute x8, waiting for transfers between devices, passed_along(): lax.ppermute(array, ('z', 'x'), [(i, i + by) for i in range(devices) if 0...  20.9 us
    all_gather x1, waiting for transfers between devices, body(): heads = lax.all_gather(heads, 'batch', axis=0, tiled=True)  18.6 us
    reduce_scatter x1, waiting for transfers between devices, body(): lax.psum_scatter(feed_grads.reshape(5120, 640), ('z', 'x'), scatter_dimen...  17.8 us
    ppermute x9, starting transfers between devices, shifted(): lax.ppermute(array, axis, [(i, (i + by) % devices) for i in range(devices)])  17.6 us
  transfers between devices with their start and end apart: 35, of which 20 were waited for; matrix products, arithmetic and copies ran while one was open for 5% of the time, Pallas kernels for 28%

profile of v10, /device:TPU:1, one launch (start us, length us, event | category | flops | bytes accessed | tf_op | source)
XLA Modules:
  0.0 380.5 jit_solution(2093445986724480777)
XLA Ops:
  12.4 4.0 %collective-permute-start = (bf16[2,256,640]{2,1,0:T(8,128)(2,1)S(1)}, bf16[2,256,640]{2,1,0:T(8,128)(2,1)S(1)}, u32[]{:S(2)}, u32[]{:S(2)}) collective-permute-start(bf16[2,256,640]{2,1,0:T(8,128)(2,1)S(1)} %normal_rows.1.refs_2_), channel_id=1, source_target_pairs={{0,2},{2,4},{4,6},{6,8},{8,10},{10,12},{12,14},{14,16},{16,18},{18... | collective-permute-start | bytes 1966088 | tf_op jit(solution)/shard_map/ppermute | solution.py:654
  31.2 18.6 %all-gather.4.cloned.1.call-done.vec_ref.refs_8_.refs_6_.refs_11_ = bf16[640,1280]{1,0:T(8,128)(2,1)} async-done(((bf16[160,1280]{1,0:T(8,128)(2,1)}), bf16[640,1280]{1,0:T(8,128)(2,1)}) %all-gather.4.cloned.1.call-update) | async-done | bytes 1638416 | tf_op jit(solution)/shard_map/all_gather | solution.py:717
  57.7 10.5 %project.2 = (bf16[2,2560,384]{2,1,0:T(8,128)(2,1)}, bf16[2,2560,384]{2,1,0:T(8,128)(2,1)}, bf16[2,384,2560]{2,1,0:T(8,128)(2,1)}, bf16[2,384,2560]{2,1,0:T(8,12...) custom-call(s32[5]{0:T(128)S(1)} %stack.81.refs_0_.place_ref, ...), custom_call_target="tpu_custom_call" | custom-call | flops 100000000 | tf_op jit(solution)/shard_map/project/pallas_call | solution.py:374
  69.2 4.1 %collective-permute-done.7.refs_2_.refs_4_ = bf16[2,256,640]{2,1,0:T(8,128)(2,1)S(1)} collective-permute-done((bf16[2,256,640]{2,1,0:T(8,128)(2,1)}, bf16[2,256,640]{2,1,0:T(8,128)(2,1)S(1)}, u32[]{:S(2)}, u32[]{:S(2)}) %collective-permute-start.7) | collective-permute-done | bytes 655392 | tf_op jit(solution)/shard_map/ppermute | solution.py:654
  77.4 5.1 %project.3 = (bf16[2,2560,384]{2,1,0:T(8,128)(2,1)}, bf16[2,2560,384]{2,1,0:T(8,128)(2,1)}, bf16[2,384,2560]{2,1,0:T(8,128)(2,1)}, bf16[2,384,2560]{2,1,0:T(8,128)(2,1)}) custom-call(s32[5]{0:T(128)S(1)} %stack.81.refs_0_.place_ref, ...), custom_call_target="tpu_custom_call", output_to_operand_aliasing={{0}: (7, {}), {1}: (8, {}), {2}: (9, {}), {3}: (10, {})} | custom-call | flops 100000000 | tf_op jit(solution)/shard_map/project/pallas_call | solution.py:374
  82.6 11.7 %attend.3 = (f32[384,512]{1,0:T(8,128)S(1)}, bf16[512,384]{1,0:T(8,128)(2,1)S(1)}, f32[5,8,512]{2,1,0:T(8,128)S(1)}) custom-call(s32[5]{0:T(128)S(1)} %stack.91.info_ref, bf16[2,384,512]{2,1,0:T(8,128)(2,1)} %get-tuple-element.104.qT_ref, bf16[2,2560,384]{2,1,0:T(8,128)(2,1)} %get-tuple-element.115.k_ref, bf16[2,384,2560]{2,1,0:T(8,128)(2,1)} %get-tuple-element.116.vT_ref, ...), custom_call_target="tpu_custom_call" | custom-call | flops 400000000 | tf_op jit(solution)/shard_map/attend/pallas_call | solution.py:98
  95.3 11.7 %attend.2 = (f32[384,512]{1,0:T(8,128)S(1)}, bf16[512,384]{1,0:T(8,128)(2,1)S(1)}, f32[5,8,512]{2,1,0:T(8,128)S(1)}) custom-call(s32[5]{0:T(128)S(1)} %stack.86.info_ref, bf16[2,384,512]{2,1,0:T(8,128)(2,1)} %get-tuple-element.104.qT_ref, bf16[2,2560,384]{2,1,0:T(8,128)(2,1)} %get-tuple-element.115.k_ref, bf16[2,384,2560]{2,1,0:T(8,128)(2,1)} %get-tuple-element.116.vT_ref, ...), custom_call_target="tpu_custom_call" | custom-call | flops 400000000 | tf_op jit(solution)/shard_map/attend/pallas_call | solution.py:98
  110.1 16.6 %all-gather.6.cloned.1.call-done.w_ref.up_ref.down_ref = bf16[640,5760]{1,0:T(8,128)(2,1)} async-done(((bf16[160,5760]{1,0:T(8,128)(2,1)}), bf16[640,5760]{1,0:T(8,128)(2,1)}) %all-gather.6.cloned.1.call-update) | async-done | bytes 7372816 | tf_op jit(solution)/shard_map/all_gather | solution.py:728
  127.4 4.6 %middle.1 = (f32[512,640]{1,0:T(8,128)}, bf16[512,640]{1,0:T(8,128)(2,1)}, bf16[512,640]{1,0:T(8,128)(2,1)}) custom-call(s32[1]{0:T(128)} %bitcast.core_ref, bf16[640,5760]{1,0:T(8,128)(2,1)} %all-gather.6.cloned.1.call-done.w_ref.up_ref.down_ref, bf16[512,384]{1,0:T(8,128)(2,1)S(1)} %get-tuple-element.119.low0_ref, ...), custom_call_target="tpu_custom_call" | custom-call | flops 20000000 | tf_op jit(solution)/shard_map/middle/pallas_call | solution.py:403
  132.0 32.1 %feed_forward.1 = (bf16[2,512,640]{2,1,0:T(8,128)(2,1)}, bf16[2,512,640]{2,1,0:T(8,128)(2,1)}, bf16[16,4,80,640]{3,2,1,0:T(8,128)(2,1)}) custom-call(bf16[512,640]{1,0:T(8,128)(2,1)} %get-tuple-element.126.h_ref, bf16[512,640]{1,0:T(8,128)(2,1)} %get-tuple-element.127.h2_ref, bf16[512,640]{1,0:T(8,128)(2,1)} %bitcast.20.cot_ref, ...), custom_call_target="tpu_custom_call" | custom-call | flops 600000000 | tf_op jit(solution)/shard_map/feed_forward/pallas_call | solution.py:450
  168.6 4.8 %after_feed.1 = (bf16[512,640]{1,0:T(8,128)(2,1)}, f32[512,640]{1,0:T(8,128)}, bf16[512,640]{1,0:T(8,128)(2,1)S(1)}, f32[8,640]{1,0:T(8,128)S(1)}) custom-call(f32[512,640]{1,0:T(8,128)} %get-tuple-element.125.mid_ref, bf16[2,512,640]{2,1,0:T(8,128)(2,1)} %get-tuple-element.128.mine_ref, bf16[2,512,640]{2,1,0:T(8,128)(2,1)S(1)} %collective-permute-done.12.theirs_ref, ...), custom_call_target="tpu_custom_call" | custom-call | flops 20000000 | tf_op jit(solution)/shard_map/after_feed/pallas_call | solution.py:479
  175.6 3.7 branch.1
  179.4 16.6 %attend_back.3 = (bf16[512,384]{1,0:T(8,128)(2,1)S(1)}, bf16[2560,384]{1,0:T(8,128)(2,1)S(1)}, bf16[2560,384]{1,0:T(8,128)(2,1)S(1)}) custom-call(s32[5]{0:T(128)S(1)} %stack.91.info_ref, bf16[2,384,512]{2,1,0:T(8,128)(2,1)} %get-tuple-element.104.qT_ref, bf16[2,512,384]{2,1,0:T(8,128)(2,1)} %get-tuple-element.132.q_ref, ...), custom_call_target="tpu_custom_call" | custom-call | flops 800000000 | tf_op jit(solution)/shard_map/attend_back/pallas_call | solution.py:211
  196.0 16.8 %attend_back.2 = (bf16[512,384]{1,0:T(8,128)(2,1)S(1)}, bf16[2560,384]{1,0:T(8,128)(2,1)S(1)}, bf16[2560,384]{1,0:T(8,128)(2,1)S(1)}) custom-call(s32[5]{0:T(128)S(1)} %stack.86.info_ref, bf16[2,384,512]{2,1,0:T(8,128)(2,1)} %get-tuple-element.104.qT_ref, bf16[2,512,384]{2,1,0:T(8,128)(2,1)} %get-tuple-element.132.q_ref, ...), custom_call_target="tpu_custom_call" | custom-call | flops 800000000 | tf_op jit(solution)/shard_map/attend_back/pallas_call | solution.py:211
  212.8 15.4 %project_back.1 = (bf16[5,2,256,640]{3,2,1,0:T(8,128)(2,1)}, bf16[5,2,256,640]{3,2,1,0:T(8,128)(2,1)}, bf16[64,40,384]{2,1,0:T(8,128)(2,1)}) custom-call(s32[5]{0:T(128)S(1)} %stack.81.refs_0_.place_ref, bf16[2,256,640]{2,1,0:T(8,128)(2,1)} %copy-done.6, bf16[2,256,640]{2,1,0:T(8,128)(2,1)} %copy-done.3, bf16[2,256,640]{2,1,0:T(8,128)(2,1)} %copy-done.2, ...), custom_call_target="tpu_custom_call" | custom-call | flops 200000000 | tf_op jit(solution)/shard_map/project_back/pallas_call | solution.py:596
  228.2 17.8 %reduce-scatter.2.cloned.1.call-done = bf16[320,640]{1,0:T(8,128)(2,1)} async-done(((bf16[5120,640]{1,0:T(8,128)(2,1)}), bf16[320,640]{1,0:T(8,128)(2,1)}) %reduce-scatter.2.cloned.1.call-update) | async-done | bytes 409616 | tf_op jit(solution)/shard_map/reduce_scatter | solution.py:739
  247.8 12.9 %all-to-all-start = ((bf16[64,40,384]{2,1,0:T(8,128)(2,1)}), bf16[64,40,384]{2,1,0:T(8,128)(2,1)S(1)}, u32[]{:S(2)}, u32[]{:S(2)}) async-start(bf16[64,40,384]{2,1,0:T(8,128)(2,1)} %get-tuple-element.153), calls=%async_computation.1 | async-start | bytes 3932160 | tf_op jit(solution)/shard_map/all_to_all | solution.py:750
  265.6 16.0 %collective-permute-done.15 = bf16[80,640]{1,0:T(8,128)(2,1)S(1)} collective-permute-done((bf16[80,640]{1,0:T(8,128)(2,1)}, bf16[80,640]{1,0:T(8,128)(2,1)S(1)}, u32[]{:S(2)}, u32[]{:S(2)}) %collective-permute-start.15) | collective-permute-done | bytes 102432 | tf_op jit(solution)/shard_map/ppermute | solution.py:649
  285.0 4.1 %collective-permute-done.17 = bf16[80,640]{1,0:T(8,128)(2,1)} collective-permute-done((bf16[80,640]{1,0:T(8,128)(2,1)S(1)}, bf16[80,640]{1,0:T(8,128)(2,1)}, u32[]{:S(2)}, u32[]{:S(2)}) %collective-permute-start.17) | collective-permute-done | bytes 102432 | tf_op jit(solution)/shard_map/ppermute | solution.py:649
  299.4 11.6 %collective-permute-done.18 = bf16[2,256,640]{2,1,0:T(8,128)(2,1)S(1)} collective-permute-done((bf16[2,256,640]{2,1,0:T(8,128)(2,1)}, bf16[2,256,640]{2,1,0:T(8,128)(2,1)S(1)}, u32[]{:S(2)}, u32[]{:S(2)}) %collective-permute-start.18) | collective-permute-done | bytes 655392 | tf_op jit(solution)/shard_map/ppermute | solution.py:654
  311.0 4.3 %collective-permute-done.19 = bf16[2,256,640]{2,1,0:T(8,128)(2,1)} collective-permute-done((bf16[2,256,640]{2,1,0:T(8,128)(2,1)}, bf16[2,256,640]{2,1,0:T(8,128)(2,1)}, u32[]{:S(2)}, u32[]{:S(2)}) %collective-permute-start.19) | collective-permute-done | bytes 655392 | tf_op jit(solution)/shard_map/ppermute | solution.py:654
  331.0 6.2 %collective-permute-start.24 = (bf16[160,384]{1,0:T(8,128)(2,1)S(1)}, bf16[160,384]{1,0:T(8,128)(2,1)S(1)}, u32[]{:S(2)}, u32[]{:S(2)}) collective-permute-start(bf16[160,384]{1,0:T(8,128)(2,1)S(1)} %bitcast.126), channel_id=1, source_target_pairs={{0,24},{8,0},{16,8},{24,16},{1,25},{9,1},{17,9},{25,17},{2,26},{10... | collective-permute-start | bytes 368648 | tf_op jit(solution)/shard_map/ppermute | solution.py:649
  338.6 3.8 collective-permute-done.24
  342.4 14.8 %collective-permute-done.25 = bf16[160,384]{1,0:T(8,128)(2,1)S(1)} collective-permute-done((bf16[160,384]{1,0:T(8,128)(2,1)S(1)}, bf16[160,384]{1,0:T(8,128)(2,1)S(1)}, u32[]{:S(2)}, u32[]{:S(2)}) %collective-permute-start.25) | collective-permute-done | bytes 122912 | tf_op jit(solution)/shard_map/ppermute | solution.py:649
  (189 shorter events, 92.3 us)
Async XLA Ops:
  7.2 42.6 %all-gather.4.cloned.1.call-start = ((), (), s32[]{:S(2)}) async-start(), calls=%async_computation.2 | async-start | bytes 2048000 | tf_op jit(solution)/shard_map/all_gather | solution.py:717
  12.4 39.1 %collective-permute-start = (bf16[2,256,640]{2,1,0:T(8,128)(2,1)S(1)}, bf16[2,256,640]{2,1,0:T(8,128)(2,1)S(1)}, u32[]{:S(2)}, u32[]{:S(2)}) collective-permute-start(bf16[2,256,640]{2,1,0:T(8,128)(2,1)S(1)} %normal_rows.1.refs_2_), channel_id=1, source_target_pairs={{0,2},{2,4},{4,6},{6,8},{8,10},{10,12},{12,14},{14,16},{16,18},{18... | collective-permute-start | bytes 1966088 | tf_op jit(solution)/shard_map/ppermute | solution.py:654
  16.4 35.1 %collective-permute-start.1 = (bf16[2,256,640]{2,1,0:T(8,128)(2,1)S(1)}, bf16[2,256,640]{2,1,0:T(8,128)(2,1)}, u32[]{:S(2)}, u32[]{:S(2)}) collective-permute-start(bf16[2,256,640]{2,1,0:T(8,128)(2,1)S(1)} %normal_rows.1.refs_2_), channel_id=1, source_target_pairs={{2,0},{4,2},{6,4},{8,6},{10,8},{12,10},{14,12},{16,14},{18,16},{20... | collective-permute-start | bytes 1966088 | tf_op jit(solution)/shard_map/ppermute | solution.py:654
  17.7 33.8 %collective-permute-start.2 = (bf16[2,256,640]{2,1,0:T(8,128)(2,1)S(1)}, bf16[2,256,640]{2,1,0:T(8,128)(2,1)}, u32[]{:S(2)}, u32[]{:S(2)}) collective-permute-start(bf16[2,256,640]{2,1,0:T(8,128)(2,1)S(1)} %normal_rows.1.refs_2_), channel_id=1, source_target_pairs={{0,1},{1,0},{2,3},{3,2},{4,5},{5,4},{6,7},{7,6},{8,9},{9,8},{10,11... | collective-permute-start | bytes 1966088 | tf_op jit(solution)/shard_map/ppermute | solution.py:658
  18.7 32.7 %collective-permute-start.3 = (bf16[2,256,640]{2,1,0:T(8,128)(2,1)S(1)}, bf16[2,256,640]{2,1,0:T(8,128)(2,1)}, u32[]{:S(2)}, u32[]{:S(2)}) collective-permute-start(bf16[2,256,640]{2,1,0:T(8,128)(2,1)S(1)} %bitcast.115), channel_id=1, source_target_pairs={{0,1},{1,0},{2,3},{3,2},{4,5},{5,4},{6,7},{7,6},{8,9},{9,8},{10,11... | collective-permute-start | bytes 1966088 | tf_op jit(solution)/shard_map/ppermute | solution.py:658
  18.8 107.8 %all-gather.6.cloned.1.call-start = ((), (), s32[]{:S(2)}) async-start(), calls=%async_computation.3 | async-start | bytes 9216000 | tf_op jit(solution)/shard_map/all_gather | solution.py:728
  51.5 194.6 %reduce-scatter.2.cloned.1.call-start = ((), (), s32[]{:S(2)}) async-start(), calls=%async_computation.4 | async-start | bytes 6963200 | tf_op jit(solution)/shard_map/reduce_scatter | solution.py:739
  52.4 16.8 %collective-permute-start.6 = (bf16[2,256,640]{2,1,0:T(8,128)(2,1)S(1)}, bf16[2,256,640]{2,1,0:T(8,128)(2,1)S(1)}, u32[]{:S(2)}, u32[]{:S(2)}) collective-permute-start(bf16[2,256,640]{2,1,0:T(8,128)(2,1)S(1)} %collective-permute-done.refs_1_), channel_id=1, source_target_pairs={{0,2},{2,4},{4,6},{6,8},{8,10},{10,12},{12,14},{14,16},{16,18},{18... | collective-permute-start | bytes 1966088 | tf_op jit(solution)/shard_map/ppermute | solution.py:654
  55.5 17.8 %collective-permute-start.7 = (bf16[2,256,640]{2,1,0:T(8,128)(2,1)}, bf16[2,256,640]{2,1,0:T(8,128)(2,1)S(1)}, u32[]{:S(2)}, u32[]{:S(2)}) collective-permute-start(bf16[2,256,640]{2,1,0:T(8,128)(2,1)} %collective-permute-done.1.refs_3_), channel_id=1, source_target_pairs={{2,0},{4,2},{6,4},{8,6},{10,8},{12,10},{14,12},{16,14},{18,16},{20... | collective-permute-start | bytes 1966088 | tf_op jit(solution)/shard_map/ppermute | solution.py:654
  108.5 23.5 %collective-permute-start.11 = (bf16[512,640]{1,0:T(8,128)(2,1)}, bf16[512,640]{1,0:T(8,128)(2,1)}, u32[]{:S(2)}, u32[]{:S(2)}) collective-permute-start(bf16[512,640]{1,0:T(8,128)(2,1)} %bitcast.20.cot_ref), channel_id=1, source_target_pairs={{0,1},{1,0},{2,3},{3,2},{4,5},{5,4},{6,7},{7,6},{8,9},{9,8},{10,11... | collective-permute-start | bytes 1966088 | tf_op jit(solution)/shard_map/ppermute | solution.py:658
  246.1 44.6 %collective-permute-start.14 = (bf16[5,2,256,640]{3,2,1,0:T(8,128)(2,1)}, bf16[5,2,256,640]{3,2,1,0:T(8,128)(2,1)}, u32[]{:S(2)}, u32[]{:S(2)}) collective-permute-start(bf16[5,2,256,640]{3,2,1,0:T(8,128)(2,1)} %get-tuple-element.154), channel_id=1, source_target_pairs={{0,1},{1,0},{2,3},{3,2},{4,5},{5,4},{6,7},{7,6},{8,9},{9,8},{10,11... | collective-permute-start | bytes 9830408 | tf_op jit(solution)/shard_map/ppermute | solution.py:658
  247.8 51.6 %all-to-all-start = ((bf16[64,40,384]{2,1,0:T(8,128)(2,1)}), bf16[64,40,384]{2,1,0:T(8,128)(2,1)S(1)}, u32[]{:S(2)}, u32[]{:S(2)}) async-start(bf16[64,40,384]{2,1,0:T(8,128)(2,1)} %get-tuple-element.153), calls=%async_computation.1 | async-start | bytes 3932160 | tf_op jit(solution)/shard_map/all_to_all | solution.py:750
  260.7 100.2 %all-gather.8.cloned.1.call-start = ((), (), s32[]{:S(2)}) async-start(), calls=%async_computation.5 | async-start | bytes 1740800 | tf_op jit(solution)/shard_map/all_gather | solution.py:752
  261.5 20.1 %collective-permute-start.15 = (bf16[80,640]{1,0:T(8,128)(2,1)}, bf16[80,640]{1,0:T(8,128)(2,1)S(1)}, u32[]{:S(2)}, u32[]{:S(2)}) collective-permute-start(bf16[80,640]{1,0:T(8,128)(2,1)} %get-tuple-element.229), channel_id=1, source_target_pairs={{0,32},{32,64},{64,96},{96,0},{1,33},{33,65},{65,97},{97,1},{2,34}... | collective-permute-start | bytes 307208 | tf_op jit(solution)/shard_map/ppermute | solution.py:649
  262.5 22.5 %collective-permute-start.16 = (bf16[80,640]{1,0:T(8,128)(2,1)S(1)}, bf16[80,640]{1,0:T(8,128)(2,1)S(1)}, u32[]{:S(2)}, u32[]{:S(2)}) collective-permute-start(bf16[80,640]{1,0:T(8,128)(2,1)S(1)} %get-tuple-element.231), channel_id=1, source_target_pairs={{0,96},{32,0},{64,32},{96,64},{1,97},{33,1},{65,33},{97,65},{2,98}... | collective-permute-start | bytes 307208 | tf_op jit(solution)/shard_map/ppermute | solution.py:649
  264.2 24.9 %collective-permute-start.17 = (bf16[80,640]{1,0:T(8,128)(2,1)S(1)}, bf16[80,640]{1,0:T(8,128)(2,1)}, u32[]{:S(2)}, u32[]{:S(2)}) collective-permute-start(bf16[80,640]{1,0:T(8,128)(2,1)S(1)} %get-tuple-element.230), channel_id=1, source_target_pairs={{0,64},{32,96},{64,0},{96,32},{1,65},{33,97},{65,1},{97,33},{2,66}... | collective-permute-start | bytes 307208 | tf_op jit(solution)/shard_map/ppermute | solution.py:649
  293.7 17.3 %collective-permute-start.18 = (bf16[2,256,640]{2,1,0:T(8,128)(2,1)}, bf16[2,256,640]{2,1,0:T(8,128)(2,1)S(1)}, u32[]{:S(2)}, u32[]{:S(2)}) collective-permute-start(bf16[2,256,640]{2,1,0:T(8,128)(2,1)} %get-tuple-element.228), channel_id=1, source_target_pairs={{0,2},{2,4},{4,6},{6,8},{8,10},{10,12},{12,14},{14,16},{16,18},{18... | collective-permute-start | bytes 1966088 | tf_op jit(solution)/shard_map/ppermute | solution.py:654
  297.4 17.9 %collective-permute-start.19 = (bf16[2,256,640]{2,1,0:T(8,128)(2,1)}, bf16[2,256,640]{2,1,0:T(8,128)(2,1)}, u32[]{:S(2)}, u32[]{:S(2)}) collective-permute-start(bf16[2,256,640]{2,1,0:T(8,128)(2,1)} %get-tuple-element.227), channel_id=1, source_target_pairs={{2,0},{4,2},{6,4},{8,6},{10,8},{12,10},{14,12},{16,14},{18,16},{20... | collective-permute-start | bytes 1966088 | tf_op jit(solution)/shard_map/ppermute | solution.py:654
  327.0 11.6 %collective-permute-start.23 = (bf16[160,384]{1,0:T(8,128)(2,1)S(1)}, bf16[160,384]{1,0:T(8,128)(2,1)S(1)}, u32[]{:S(2)}, u32[]{:S(2)}) collective-permute-start(bf16[160,384]{1,0:T(8,128)(2,1)S(1)} %bitcast.125), channel_id=1, source_target_pairs={{0,8},{8,16},{16,24},{24,0},{1,9},{9,17},{17,25},{25,1},{2,10},{10... | collective-permute-start | bytes 368648 | tf_op jit(solution)/shard_map/ppermute | solution.py:649
  328.3 29.0 %collective-permute-start.26 = (bf16[2,256,640]{2,1,0:T(8,128)(2,1)}, bf16[2,256,640]{2,1,0:T(8,128)(2,1)S(1)}, u32[]{:S(2)}, u32[]{:S(2)}) collective-permute-start(bf16[2,256,640]{2,1,0:T(8,128)(2,1)} %get-tuple-element.163), channel_id=1, source_target_pairs={{0,2},{2,4},{4,6},{6,8},{8,10},{10,12},{12,14},{14,16},{16,18},{18... | collective-permute-start | bytes 1966088 | tf_op jit(solution)/shard_map/ppermute | solution.py:654
  329.7 27.6 %collective-permute-start.27 = (bf16[2,256,640]{2,1,0:T(8,128)(2,1)}, bf16[2,256,640]{2,1,0:T(8,128)(2,1)S(1)}, u32[]{:S(2)}, u32[]{:S(2)}) collective-permute-start(bf16[2,256,640]{2,1,0:T(8,128)(2,1)} %get-tuple-element.164), channel_id=1, source_target_pairs={{2,0},{4,2},{6,4},{8,6},{10,8},{12,10},{14,12},{16,14},{18,16},{20... | collective-permute-start | bytes 1966088 | tf_op jit(solution)/shard_map/ppermute | solution.py:654
  331.0 11.4 %collective-permute-start.24 = (bf16[160,384]{1,0:T(8,128)(2,1)S(1)}, bf16[160,384]{1,0:T(8,128)(2,1)S(1)}, u32[]{:S(2)}, u32[]{:S(2)}) collective-permute-start(bf16[160,384]{1,0:T(8,128)(2,1)S(1)} %bitcast.126), channel_id=1, source_target_pairs={{0,24},{8,0},{16,8},{24,16},{1,25},{9,1},{17,9},{25,17},{2,26},{10... | collective-permute-start | bytes 368648 | tf_op jit(solution)/shard_map/ppermute | solution.py:649
  337.2 20.0 %collective-permute-start.25 = (bf16[160,384]{1,0:T(8,128)(2,1)S(1)}, bf16[160,384]{1,0:T(8,128)(2,1)S(1)}, u32[]{:S(2)}, u32[]{:S(2)}) collective-permute-start(bf16[160,384]{1,0:T(8,128)(2,1)S(1)} %bitcast.127), channel_id=1, source_target_pairs={{0,16},{8,24},{16,0},{24,8},{1,17},{9,25},{17,1},{25,9},{2,18},{10... | collective-permute-start | bytes 368648 | tf_op jit(solution)/shard_map/ppermute | solution.py:649
  360.9 8.3 %collective-permute-start.29 = (bf16[16,80,640]{2,1,0:T(8,128)(2,1)}, bf16[16,80,640]{2,1,0:T(8,128)(2,1)S(1)}, u32[]{:S(2)}, u32[]{:S(2)}) collective-permute-start(bf16[16,80,640]{2,1,0:T(8,128)(2,1)} %bitcast.121), channel_id=1, source_target_pairs={{0,1},{1,0},{2,3},{3,2},{4,5},{5,4},{6,7},{7,6},{8,9},{9,8},{10,11... | collective-permute-start | bytes 4915208 | tf_op jit(solution)/shard_map/ppermute | solution.py:658
  (44 other events, 442.0 us)
Sparse Core Ops, SparseCore 0:
  18.9 30.8 all-gather.3
  52.0 74.5 all-gather.5
  164.3 81.7 reduce-scatter.1
  299.5 56.7 all-gather.7

commit v11 on v10

--- a/solution.py
+++ b/solution.py
@@ -747,9 +747,10 @@
     feed_grads, mine, theirs, tail = together(feed_grads, mine, theirs, tail)
 
     feed = summed_share(feed_grads.reshape(4, 80, 640), "batch")
+    tail, feed = together(tail, feed)
     tail = lax.all_to_all(tail, ("batch", "z", "x"), 0, 0, tiled=True)
-    theirs, mine, feed = together(swapped(theirs), mine, feed)
     feed = lax.all_gather(feed, ("z", "x"), axis=0, tiled=True).reshape(16, 80, 640)
+    theirs = swapped(theirs)
     sums = [mine[j].astype(f32) + theirs[j].astype(f32) for j in range(5)]
     right, left = passed_along(sums[4].astype(bf16), 1), passed_along(sums[0].astype(bf16), -1)
     tail, right, left = together(tail, right, left)

time: 385 us -> 378 us (0.982)
  waiting for transfers between devices: 131 us -> 119 us
  Pallas kernels: 143 us -> 149 us
    ppermute x9, waiting for transfers between devices: 45.3 us -> 26.1 us  [shifted(): lax.ppermute(array, axis, [(i, (i + by) % devices) for i in range(devices)])]
    all_to_all x1, waiting for transfers between devices: 0.01 us -> 18.8 us  [body(): tail = lax.all_to_all(tail, ('batch', 'z', 'x'), 0, 0, tiled=True)]
    ppermute x8, waiting for transfers between devices: 20.9 us -> 15.4 us  [passed_along(): lax.ppermute(array, ('z', 'x'), [(i, i + by) for i in range(devices) if 0...]
  transfers between devices with their start and end apart: 35 -> 35, of which waited for: 20 -> 20; matrix products, arithmetic and copies ran while one was open for 5% -> 5% of each run, Pallas kernels for 28% -> 30%
where the time goes in v11:
time: 378 us; the launch traced here: 374 us
  Pallas kernels  149 us (39%)
  waiting for transfers between devices  119 us (31%)
  starting transfers between devices  56.9 us (15%)
  between operations  20.2 us (5%)
  other arithmetic  15.4 us (4%)
  local copies, waits for them, and re-layouts  13 us (3%)
    pallas_call x2, Pallas kernels, attend_back(): pl.pallas_call(attend_back_kernel, out_shape=tuple((pltpu.MemorySpace.VME...  36.9 us
    pallas_call x1, Pallas kernels, feed_forward(): call(feed_kernel, (far(2, 512, 640), far(2, 512, 640), far(16, 4, 80, 640...  32.1 us
    pallas_call x2, Pallas kernels, attend(): pl.pallas_call(attend_kernel, out_shape=(jax.ShapeDtypeStruct((384, nq),...  26.2 us
    ppermute x9, waiting for transfers between devices, shifted(): lax.ppermute(array, axis, [(i, (i + by) % devices) for i in range(devices)])  26.1 us
    all_to_all x1, waiting for transfers between devices, body(): tail = lax.all_to_all(tail, ('batch', 'z', 'x'), 0, 0, tiled=True)  18.8 us
    all_gather x1, waiting for transfers between devices, body(): heads = lax.all_gather(heads, 'batch', axis=0, tiled=True)  18.6 us
    ppermute x9, starting transfers between devices, shifted(): lax.ppermute(array, axis, [(i, (i + by) % devices) for i in range(devices)])  18.6 us
    ppermute x8, starting transfers between devices, passed_along(): lax.ppermute(array, ('z', 'x'), [(i, i + by) for i in range(devices) if 0...  16.5 us
  transfers between devices with their start and end apart: 35, of which 20 were waited for; matrix products, arithmetic and copies ran while one was open for 5% of the time, Pallas kernels for 30%

profile of v11, /device:TPU:1, one launch (start us, length us, event | category | flops | bytes accessed | tf_op | source)
XLA Modules:
  0.0 373.6 jit_solution(1295823035115122308)
XLA Ops:
  12.4 4.0 %collective-permute-start = (bf16[2,256,640]{2,1,0:T(8,128)(2,1)S(1)}, bf16[2,256,640]{2,1,0:T(8,128)(2,1)S(1)}, u32[]{:S(2)}, u32[]{:S(2)}) collective-permute-start(bf16[2,256,640]{2,1,0:T(8,128)(2,1)S(1)} %normal_rows.1.refs_2_), channel_id=1, source_target_pairs={{0,2},{2,4},{4,6},{6,8},{8,10},{10,12},{12,14},{14,16},{16,18},{18... | collective-permute-start | bytes 1966088 | tf_op jit(solution)/shard_map/ppermute | solution.py:654
  18.9 3.4 pack_feed.1
  31.2 18.6 %all-gather.4.cloned.1.call-done.vec_ref.refs_8_.refs_6_.refs_11_ = bf16[640,1280]{1,0:T(8,128)(2,1)} async-done(((bf16[160,1280]{1,0:T(8,128)(2,1)}), bf16[640,1280]{1,0:T(8,128)(2,1)}) %all-gather.4.cloned.1.call-update) | async-done | bytes 1638416 | tf_op jit(solution)/shard_map/all_gather | solution.py:717
  57.7 10.5 %project.2 = (bf16[2,2560,384]{2,1,0:T(8,128)(2,1)}, bf16[2,2560,384]{2,1,0:T(8,128)(2,1)}, bf16[2,384,2560]{2,1,0:T(8,128)(2,1)}, bf16[2,384,2560]{2,1,0:T(8,12...) custom-call(s32[5]{0:T(128)S(1)} %stack.81.refs_0_.place_ref, ...), custom_call_target="tpu_custom_call" | custom-call | flops 100000000 | tf_op jit(solution)/shard_map/project/pallas_call | solution.py:374
  69.2 4.1 %collective-permute-done.7.refs_2_.refs_4_ = bf16[2,256,640]{2,1,0:T(8,128)(2,1)S(1)} collective-permute-done((bf16[2,256,640]{2,1,0:T(8,128)(2,1)}, bf16[2,256,640]{2,1,0:T(8,128)(2,1)S(1)}, u32[]{:S(2)}, u32[]{:S(2)}) %collective-permute-start.7) | collective-permute-done | bytes 655392 | tf_op jit(solution)/shard_map/ppermute | solution.py:654
  77.4 5.2 %project.3 = (bf16[2,2560,384]{2,1,0:T(8,128)(2,1)}, bf16[2,2560,384]{2,1,0:T(8,128)(2,1)}, bf16[2,384,2560]{2,1,0:T(8,128)(2,1)}, bf16[2,384,2560]{2,1,0:T(8,128)(2,1)}) custom-call(s32[5]{0:T(128)S(1)} %stack.81.refs_0_.place_ref, ...), custom_call_target="tpu_custom_call", output_to_operand_aliasing={{0}: (7, {}), {1}: (8, {}), {2}: (9, {}), {3}: (10, {})} | custom-call | flops 100000000 | tf_op jit(solution)/shard_map/project/pallas_call | solution.py:374
  82.6 11.7 %attend.3 = (f32[384,512]{1,0:T(8,128)S(1)}, bf16[512,384]{1,0:T(8,128)(2,1)S(1)}, f32[5,8,512]{2,1,0:T(8,128)S(1)}) custom-call(s32[5]{0:T(128)S(1)} %stack.91.info_ref, bf16[2,384,512]{2,1,0:T(8,128)(2,1)} %get-tuple-element.103.qT_ref, bf16[2,2560,384]{2,1,0:T(8,128)(2,1)} %get-tuple-element.114.k_ref, bf16[2,384,2560]{2,1,0:T(8,128)(2,1)} %get-tuple-element.115.vT_ref, ...), custom_call_target="tpu_custom_call" | custom-call | flops 400000000 | tf_op jit(solution)/shard_map/attend/pallas_call | solution.py:98
  95.3 14.5 %attend.2 = (f32[384,512]{1,0:T(8,128)S(1)}, bf16[512,384]{1,0:T(8,128)(2,1)S(1)}, f32[5,8,512]{2,1,0:T(8,128)S(1)}) custom-call(s32[5]{0:T(128)S(1)} %stack.86.info_ref, bf16[2,384,512]{2,1,0:T(8,128)(2,1)} %get-tuple-element.103.qT_ref, bf16[2,2560,384]{2,1,0:T(8,128)(2,1)} %get-tuple-element.114.k_ref, bf16[2,384,2560]{2,1,0:T(8,128)(2,1)} %get-tuple-element.115.vT_ref, ...), custom_call_target="tpu_custom_call" | custom-call | flops 400000000 | tf_op jit(solution)/shard_map/attend/pallas_call | solution.py:98
  112.9 13.7 %all-gather.6.cloned.1.call-done.w_ref.up_ref.down_ref = bf16[640,5760]{1,0:T(8,128)(2,1)} async-done(((bf16[160,5760]{1,0:T(8,128)(2,1)}), bf16[640,5760]{1,0:T(8,128)(2,1)}) %all-gather.6.cloned.1.call-update) | async-done | bytes 7372816 | tf_op jit(solution)/shard_map/all_gather | solution.py:728
  127.4 4.6 %middle.1 = (f32[512,640]{1,0:T(8,128)}, bf16[512,640]{1,0:T(8,128)(2,1)}, bf16[512,640]{1,0:T(8,128)(2,1)}) custom-call(s32[1]{0:T(128)} %bitcast.core_ref, bf16[640,5760]{1,0:T(8,128)(2,1)} %all-gather.6.cloned.1.call-done.w_ref.up_ref.down_ref, bf16[512,384]{1,0:T(8,128)(2,1)S(1)} %get-tuple-element.118.low0_ref, ...), custom_call_target="tpu_custom_call" | custom-call | flops 20000000 | tf_op jit(solution)/shard_map/middle/pallas_call | solution.py:403
  132.0 32.1 %feed_forward.1 = (bf16[2,512,640]{2,1,0:T(8,128)(2,1)}, bf16[2,512,640]{2,1,0:T(8,128)(2,1)}, bf16[16,4,80,640]{3,2,1,0:T(8,128)(2,1)}) custom-call(bf16[512,640]{1,0:T(8,128)(2,1)} %get-tuple-element.125.h_ref, bf16[512,640]{1,0:T(8,128)(2,1)} %get-tuple-element.126.h2_ref, bf16[512,640]{1,0:T(8,128)(2,1)} %bitcast.20.cot_ref, ...), custom_call_target="tpu_custom_call" | custom-call | flops 600000000 | tf_op jit(solution)/shard_map/feed_forward/pallas_call | solution.py:450
  168.6 4.8 %after_feed.1 = (bf16[512,640]{1,0:T(8,128)(2,1)}, f32[512,640]{1,0:T(8,128)}, bf16[512,640]{1,0:T(8,128)(2,1)S(1)}, f32[8,640]{1,0:T(8,128)S(1)}) custom-call(f32[512,640]{1,0:T(8,128)} %get-tuple-element.124.mid_ref, bf16[2,512,640]{2,1,0:T(8,128)(2,1)} %get-tuple-element.127.mine_ref, bf16[2,512,640]{2,1,0:T(8,128)(2,1)S(1)} %collective-permute-done.12.theirs_ref, ...), custom_call_target="tpu_custom_call" | custom-call | flops 20000000 | tf_op jit(solution)/shard_map/after_feed/pallas_call | solution.py:479
  175.6 3.7 branch.1
  179.3 16.6 %attend_back.3 = (bf16[512,384]{1,0:T(8,128)(2,1)S(1)}, bf16[2560,384]{1,0:T(8,128)(2,1)S(1)}, bf16[2560,384]{1,0:T(8,128)(2,1)S(1)}) custom-call(s32[5]{0:T(128)S(1)} %stack.91.info_ref, bf16[2,384,512]{2,1,0:T(8,128)(2,1)} %get-tuple-element.103.qT_ref, bf16[2,512,384]{2,1,0:T(8,128)(2,1)} %get-tuple-element.131.q_ref, ...), custom_call_target="tpu_custom_call" | custom-call | flops 800000000 | tf_op jit(solution)/shard_map/attend_back/pallas_call | solution.py:211
  196.0 20.3 %attend_back.2 = (bf16[512,384]{1,0:T(8,128)(2,1)S(1)}, bf16[2560,384]{1,0:T(8,128)(2,1)S(1)}, bf16[2560,384]{1,0:T(8,128)(2,1)S(1)}) custom-call(s32[5]{0:T(128)S(1)} %stack.86.info_ref, bf16[2,384,512]{2,1,0:T(8,128)(2,1)} %get-tuple-element.103.qT_ref, bf16[2,512,384]{2,1,0:T(8,128)(2,1)} %get-tuple-element.131.q_ref, ...), custom_call_target="tpu_custom_call" | custom-call | flops 800000000 | tf_op jit(solution)/shard_map/attend_back/pallas_call | solution.py:211
  216.3 15.4 %project_back.1 = (bf16[5,2,256,640]{3,2,1,0:T(8,128)(2,1)}, bf16[5,2,256,640]{3,2,1,0:T(8,128)(2,1)}, bf16[64,40,384]{2,1,0:T(8,128)(2,1)}) custom-call(s32[5]{0:T(128)S(1)} %stack.81.refs_0_.place_ref, bf16[2,256,640]{2,1,0:T(8,128)(2,1)} %copy-done.6, bf16[2,256,640]{2,1,0:T(8,128)(2,1)} %copy-done.3, bf16[2,256,640]{2,1,0:T(8,128)(2,1)} %copy-done.2, ...), custom_call_target="tpu_custom_call" | custom-call | flops 200000000 | tf_op jit(solution)/shard_map/project_back/pallas_call | solution.py:596
  231.7 14.4 %reduce-scatter.2.cloned.1.call-done = bf16[320,640]{1,0:T(8,128)(2,1)} async-done(((bf16[5120,640]{1,0:T(8,128)(2,1)}), bf16[320,640]{1,0:T(8,128)(2,1)}) %reduce-scatter.2.cloned.1.call-update) | async-done | bytes 409616 | tf_op jit(solution)/shard_map/reduce_scatter | solution.py:739
  258.9 12.7 %all-to-all-start = ((bf16[64,40,384]{2,1,0:T(8,128)(2,1)}), bf16[64,40,384]{2,1,0:T(8,128)(2,1)S(1)}, u32[]{:S(2)}, u32[]{:S(2)}) async-start(bf16[64,40,384]{2,1,0:T(8,128)(2,1)} %get-tuple-element.154), calls=%async_computation.1 | async-start | bytes 3932160 | tf_op jit(solution)/shard_map/all_to_all | solution.py:751
  279.6 18.8 %all-to-all-done = bf16[64,40,384]{2,1,0:T(8,128)(2,1)S(1)} async-done(((bf16[64,40,384]{2,1,0:T(8,128)(2,1)}), bf16[64,40,384]{2,1,0:T(8,128)(2,1)S(1)}, u32[]{:S(2)}, u32[]{:S(2)}) %all-to-all-start) | async-done | bytes 1966112 | tf_op jit(solution)/shard_map/all_to_all | solution.py:751
  298.4 8.5 %collective-permute-done.18 = bf16[2,256,640]{2,1,0:T(8,128)(2,1)S(1)} collective-permute-done((bf16[2,256,640]{2,1,0:T(8,128)(2,1)}, bf16[2,256,640]{2,1,0:T(8,128)(2,1)S(1)}, u32[]{:S(2)}, u32[]{:S(2)}) %collective-permute-start.18) | collective-permute-done | bytes 655392 | tf_op jit(solution)/shard_map/ppermute | solution.py:654
  308.8 3.4 fusion.8
  324.9 6.4 %collective-permute-start.24 = (bf16[160,384]{1,0:T(8,128)(2,1)S(1)}, bf16[160,384]{1,0:T(8,128)(2,1)S(1)}, u32[]{:S(2)}, u32[]{:S(2)}) collective-permute-start(bf16[160,384]{1,0:T(8,128)(2,1)S(1)} %bitcast.126), channel_id=1, source_target_pairs={{0,24},{8,0},{16,8},{24,16},{1,25},{9,1},{17,9},{25,17},{2,26},{10... | collective-permute-start | bytes 368648 | tf_op jit(solution)/shard_map/ppermute | solution.py:649
  336.0 15.7 %collective-permute-done.25 = bf16[160,384]{1,0:T(8,128)(2,1)S(1)} collective-permute-done((bf16[160,384]{1,0:T(8,128)(2,1)S(1)}, bf16[160,384]{1,0:T(8,128)(2,1)S(1)}, u32[]{:S(2)}, u32[]{:S(2)}) %collective-permute-start.25) | collective-permute-done | bytes 122912 | tf_op jit(solution)/shard_map/ppermute | solution.py:649
  356.5 3.7 collective-permute-done.28.theirs_ref
  (187 shorter events, 86.7 us)
Async XLA Ops:
  7.2 42.6 %all-gather.4.cloned.1.call-start = ((), (), s32[]{:S(2)}) async-start(), calls=%async_computation.2 | async-start | bytes 2048000 | tf_op jit(solution)/shard_map/all_gather | solution.py:717
  12.4 39.1 %collective-permute-start = (bf16[2,256,640]{2,1,0:T(8,128)(2,1)S(1)}, bf16[2,256,640]{2,1,0:T(8,128)(2,1)S(1)}, u32[]{:S(2)}, u32[]{:S(2)}) collective-permute-start(bf16[2,256,640]{2,1,0:T(8,128)(2,1)S(1)} %normal_rows.1.refs_2_), channel_id=1, source_target_pairs={{0,2},{2,4},{4,6},{6,8},{8,10},{10,12},{12,14},{14,16},{16,18},{18... | collective-permute-start | bytes 1966088 | tf_op jit(solution)/shard_map/ppermute | solution.py:654
  16.4 35.1 %collective-permute-start.1 = (bf16[2,256,640]{2,1,0:T(8,128)(2,1)S(1)}, bf16[2,256,640]{2,1,0:T(8,128)(2,1)}, u32[]{:S(2)}, u32[]{:S(2)}) collective-permute-start(bf16[2,256,640]{2,1,0:T(8,128)(2,1)S(1)} %normal_rows.1.refs_2_), channel_id=1, source_target_pairs={{2,0},{4,2},{6,4},{8,6},{10,8},{12,10},{14,12},{16,14},{18,16},{20... | collective-permute-start | bytes 1966088 | tf_op jit(solution)/shard_map/ppermute | solution.py:654
  17.7 33.8 %collective-permute-start.2 = (bf16[2,256,640]{2,1,0:T(8,128)(2,1)S(1)}, bf16[2,256,640]{2,1,0:T(8,128)(2,1)}, u32[]{:S(2)}, u32[]{:S(2)}) collective-permute-start(bf16[2,256,640]{2,1,0:T(8,128)(2,1)S(1)} %normal_rows.1.refs_2_), channel_id=1, source_target_pairs={{0,1},{1,0},{2,3},{3,2},{4,5},{5,4},{6,7},{7,6},{8,9},{9,8},{10,11... | collective-permute-start | bytes 1966088 | tf_op jit(solution)/shard_map/ppermute | solution.py:658
  18.7 32.7 %collective-permute-start.3 = (bf16[2,256,640]{2,1,0:T(8,128)(2,1)S(1)}, bf16[2,256,640]{2,1,0:T(8,128)(2,1)}, u32[]{:S(2)}, u32[]{:S(2)}) collective-permute-start(bf16[2,256,640]{2,1,0:T(8,128)(2,1)S(1)} %bitcast.115), channel_id=1, source_target_pairs={{0,1},{1,0},{2,3},{3,2},{4,5},{5,4},{6,7},{7,6},{8,9},{9,8},{10,11... | collective-permute-start | bytes 1966088 | tf_op jit(solution)/shard_map/ppermute | solution.py:658
  18.8 107.8 %all-gather.6.cloned.1.call-start = ((), (), s32[]{:S(2)}) async-start(), calls=%async_computation.3 | async-start | bytes 9216000 | tf_op jit(solution)/shard_map/all_gather | solution.py:728
  51.5 194.6 %reduce-scatter.2.cloned.1.call-start = ((), (), s32[]{:S(2)}) async-start(), calls=%async_computation.4 | async-start | bytes 6963200 | tf_op jit(solution)/shard_map/reduce_scatter | solution.py:739
  51.5 5.3 %collective-permute-start.4 = (bf16[2,256,640]{2,1,0:T(8,128)(2,1)S(1)}, bf16[2,256,640]{2,1,0:T(8,128)(2,1)S(1)}, u32[]{:S(2)}, u32[]{:S(2)}) collective-permute-start(bf16[2,256,640]{2,1,0:T(8,128)(2,1)S(1)} %collective-permute-done.refs_1_), channel_id=1, source_target_pairs={{0,1},{1,0},{2,3},{3,2},{4,5},{5,4},{6,7},{7,6},{8,9},{9,8},{10,11... | collective-permute-start | bytes 1966088 | tf_op jit(solution)/shard_map/ppermute | solution.py:658
  52.4 16.8 %collective-permute-start.6 = (bf16[2,256,640]{2,1,0:T(8,128)(2,1)S(1)}, bf16[2,256,640]{2,1,0:T(8,128)(2,1)S(1)}, u32[]{:S(2)}, u32[]{:S(2)}) collective-permute-start(bf16[2,256,640]{2,1,0:T(8,128)(2,1)S(1)} %collective-permute-done.refs_1_), channel_id=1, source_target_pairs={{0,2},{2,4},{4,6},{6,8},{8,10},{10,12},{12,14},{14,16},{16,18},{18... | collective-permute-start | bytes 1966088 | tf_op jit(solution)/shard_map/ppermute | solution.py:654
  55.5 17.8 %collective-permute-start.7 = (bf16[2,256,640]{2,1,0:T(8,128)(2,1)}, bf16[2,256,640]{2,1,0:T(8,128)(2,1)S(1)}, u32[]{:S(2)}, u32[]{:S(2)}) collective-permute-start(bf16[2,256,640]{2,1,0:T(8,128)(2,1)} %collective-permute-done.1.refs_3_), channel_id=1, source_target_pairs={{2,0},{4,2},{6,4},{8,6},{10,8},{12,10},{14,12},{16,14},{18,16},{20... | collective-permute-start | bytes 1966088 | tf_op jit(solution)/shard_map/ppermute | solution.py:654
  111.3 20.7 %collective-permute-start.11 = (bf16[512,640]{1,0:T(8,128)(2,1)}, bf16[512,640]{1,0:T(8,128)(2,1)}, u32[]{:S(2)}, u32[]{:S(2)}) collective-permute-start(bf16[512,640]{1,0:T(8,128)(2,1)} %bitcast.20.cot_ref), channel_id=1, source_target_pairs={{0,1},{1,0},{2,3},{3,2},{4,5},{5,4},{6,7},{7,6},{8,9},{9,8},{10,11... | collective-permute-start | bytes 1966088 | tf_op jit(solution)/shard_map/ppermute | solution.py:658
  246.1 25.6 %collective-permute-start.17 = (bf16[5,2,256,640]{3,2,1,0:T(8,128)(2,1)}, bf16[5,2,256,640]{3,2,1,0:T(8,128)(2,1)}, u32[]{:S(2)}, u32[]{:S(2)}) collective-permute-start(bf16[5,2,256,640]{3,2,1,0:T(8,128)(2,1)} %get-tuple-element.156), channel_id=1, source_target_pairs={{0,1},{1,0},{2,3},{3,2},{4,5},{5,4},{6,7},{7,6},{8,9},{9,8},{10,11... | collective-permute-start | bytes 9830408 | tf_op jit(solution)/shard_map/ppermute | solution.py:658
  248.9 5.8 %collective-permute-start.14 = (bf16[80,640]{1,0:T(8,128)(2,1)S(1)}, bf16[80,640]{1,0:T(8,128)(2,1)S(1)}, u32[]{:S(2)}, u32[]{:S(2)}) collective-permute-start(bf16[80,640]{1,0:T(8,128)(2,1)S(1)} %get-tuple-element.227), channel_id=1, source_target_pairs={{0,32},{32,64},{64,96},{96,0},{1,33},{33,65},{65,97},{97,1},{2,34}... | collective-permute-start | bytes 307208 | tf_op jit(solution)/shard_map/ppermute | solution.py:649
  251.6 5.7 %collective-permute-start.16 = (bf16[80,640]{1,0:T(8,128)(2,1)S(1)}, bf16[80,640]{1,0:T(8,128)(2,1)S(1)}, u32[]{:S(2)}, u32[]{:S(2)}) collective-permute-start(bf16[80,640]{1,0:T(8,128)(2,1)S(1)} %get-tuple-element.228), channel_id=1, source_target_pairs={{0,64},{32,96},{64,0},{96,32},{1,65},{33,97},{65,1},{97,33},{2,66}... | collective-permute-start | bytes 307208 | tf_op jit(solution)/shard_map/ppermute | solution.py:649
  258.9 39.5 %all-to-all-start = ((bf16[64,40,384]{2,1,0:T(8,128)(2,1)}), bf16[64,40,384]{2,1,0:T(8,128)(2,1)S(1)}, u32[]{:S(2)}, u32[]{:S(2)}) async-start(bf16[64,40,384]{2,1,0:T(8,128)(2,1)} %get-tuple-element.154), calls=%async_computation.1 | async-start | bytes 3932160 | tf_op jit(solution)/shard_map/all_to_all | solution.py:751
  271.6 83.7 %all-gather.8.cloned.1.call-start = ((), (), s32[]{:S(2)}) async-start(), calls=%async_computation.5 | async-start | bytes 1740800 | tf_op jit(solution)/shard_map/all_gather | solution.py:752
  274.7 32.2 %collective-permute-start.18 = (bf16[2,256,640]{2,1,0:T(8,128)(2,1)}, bf16[2,256,640]{2,1,0:T(8,128)(2,1)S(1)}, u32[]{:S(2)}, u32[]{:S(2)}) collective-permute-start(bf16[2,256,640]{2,1,0:T(8,128)(2,1)} %get-tuple-element.226), channel_id=1, source_target_pairs={{0,2},{2,4},{4,6},{6,8},{8,10},{10,12},{12,14},{14,16},{16,18},{18... | collective-permute-start | bytes 1966088 | tf_op jit(solution)/shard_map/ppermute | solution.py:654
  277.6 31.2 %collective-permute-start.19 = (bf16[2,256,640]{2,1,0:T(8,128)(2,1)}, bf16[2,256,640]{2,1,0:T(8,128)(2,1)}, u32[]{:S(2)}, u32[]{:S(2)}) collective-permute-start(bf16[2,256,640]{2,1,0:T(8,128)(2,1)} %get-tuple-element.225), channel_id=1, source_target_pairs={{2,0},{4,2},{6,4},{8,6},{10,8},{12,10},{14,12},{16,14},{18,16},{20... | collective-permute-start | bytes 1966088 | tf_op jit(solution)/shard_map/ppermute | solution.py:654
  319.8 12.8 %collective-permute-start.23 = (bf16[160,384]{1,0:T(8,128)(2,1)S(1)}, bf16[160,384]{1,0:T(8,128)(2,1)S(1)}, u32[]{:S(2)}, u32[]{:S(2)}) collective-permute-start(bf16[160,384]{1,0:T(8,128)(2,1)S(1)} %bitcast.125), channel_id=1, source_target_pairs={{0,8},{8,16},{16,24},{24,0},{1,9},{9,17},{17,25},{25,1},{2,10},{10... | collective-permute-start | bytes 368648 | tf_op jit(solution)/shard_map/ppermute | solution.py:649
  322.3 29.4 %collective-permute-start.26 = (bf16[2,256,640]{2,1,0:T(8,128)(2,1)}, bf16[2,256,640]{2,1,0:T(8,128)(2,1)S(1)}, u32[]{:S(2)}, u32[]{:S(2)}) collective-permute-start(bf16[2,256,640]{2,1,0:T(8,128)(2,1)} %get-tuple-element.161), channel_id=1, source_target_pairs={{0,2},{2,4},{4,6},{6,8},{8,10},{10,12},{12,14},{14,16},{16,18},{18... | collective-permute-start | bytes 1966088 | tf_op jit(solution)/shard_map/ppermute | solution.py:654
  323.6 28.0 %collective-permute-start.27 = (bf16[2,256,640]{2,1,0:T(8,128)(2,1)}, bf16[2,256,640]{2,1,0:T(8,128)(2,1)S(1)}, u32[]{:S(2)}, u32[]{:S(2)}) collective-permute-start(bf16[2,256,640]{2,1,0:T(8,128)(2,1)} %get-tuple-element.162), channel_id=1, source_target_pairs={{2,0},{4,2},{6,4},{8,6},{10,8},{12,10},{14,12},{16,14},{18,16},{20... | collective-permute-start | bytes 1966088 | tf_op jit(solution)/shard_map/ppermute | solution.py:654
  324.9 11.0 %collective-permute-start.24 = (bf16[160,384]{1,0:T(8,128)(2,1)S(1)}, bf16[160,384]{1,0:T(8,128)(2,1)S(1)}, u32[]{:S(2)}, u32[]{:S(2)}) collective-permute-start(bf16[160,384]{1,0:T(8,128)(2,1)S(1)} %bitcast.126), channel_id=1, source_target_pairs={{0,24},{8,0},{16,8},{24,16},{1,25},{9,1},{17,9},{25,17},{2,26},{10... | collective-permute-start | bytes 368648 | tf_op jit(solution)/shard_map/ppermute | solution.py:649
  331.3 20.3 %collective-permute-start.25 = (bf16[160,384]{1,0:T(8,128)(2,1)S(1)}, bf16[160,384]{1,0:T(8,128)(2,1)S(1)}, u32[]{:S(2)}, u32[]{:S(2)}) collective-permute-start(bf16[160,384]{1,0:T(8,128)(2,1)S(1)} %bitcast.127), channel_id=1, source_target_pairs={{0,16},{8,24},{16,0},{24,8},{1,17},{9,25},{17,1},{25,9},{2,18},{10... | collective-permute-start | bytes 368648 | tf_op jit(solution)/shard_map/ppermute | solution.py:649
  355.2 7.1 %collective-permute-start.29 = (bf16[16,80,640]{2,1,0:T(8,128)(2,1)}, bf16[16,80,640]{2,1,0:T(8,128)(2,1)S(1)}, u32[]{:S(2)}, u32[]{:S(2)}) collective-permute-start(bf16[16,80,640]{2,1,0:T(8,128)(2,1)} %bitcast.121), channel_id=1, source_target_pairs={{0,1},{1,0},{2,3},{3,2},{4,5},{5,4},{6,7},{7,6},{8,9},{9,8},{10,11... | collective-permute-start | bytes 4915208 | tf_op jit(solution)/shard_map/ppermute | solution.py:658
  (43 other events, 434.5 us)
Sparse Core Ops, SparseCore 0:
  18.9 30.7 all-gather.3
  52.0 74.5 all-gather.5
  164.3 81.7 reduce-scatter.1
  279.7 69.0 all-gather.7

commit v12 on v9

--- a/solution.py
+++ b/solution.py
@@ -375,7 +375,7 @@
         lambda *refs: project_kernel(chips, *refs), shapes, "project", 5 * 10**9, 28,
         input_output_aliases={2 * n + 3 + i: i for i in range(len(earlier))}, **scalar_first(
             (2, n), [full(2, 256, 640)] * (2 * n) + [full(16, 640), full(640, 1152)] + [pl.BlockSpec(memory_space=pl.ANY)] * len(earlier),
-            specs, [pltpu.VMEM((512, 640), bf16), pltpu.VMEM((512, 640), bf16)]))(place, *own, *other, vec, *stay(w), *earlier)
+            specs, [pltpu.VMEM((512, 640), bf16), pltpu.VMEM((512, 640), bf16)]))(place, *own, *other, *stay(vec, w), *earlier)
 
 
 def heads_joined(core, mine, theirs):
@@ -401,7 +401,7 @@
 
 def middle_step(core, weights, *args):
     return call(middle_kernel, (far(512, 640, dtype=f32), far(512, 640), far(512, 640)), "middle", 10**9, 20, **scalar_first(
-        (1,), [W_OUT] + [full(*a.shape) for a in args], [full(512, 640)] * 3))(core, *stay(weights), *args)
+        (1,), [W_OUT] + [full(*a.shape) for a in args], [full(512, 640)] * 3))(core, *stay(weights), *args[:-1], *stay(args[-1]))
 
 
 def feed_kernel(h_ref, h2_ref, cot_ref, cot2_ref, up_ref, down_ref, mine_ref, theirs_ref, g_ref, h, cot, hT, cT, out, dh):
@@ -478,7 +478,7 @@
     rows, pair = pl.BlockSpec((128, 640), lambda i: (i, 0)), pl.BlockSpec((2, 128, 640), lambda i: (0, i, 0))
     return call(
         after_kernel, (far(512, 640), far(512, 640, dtype=f32), shape(512, 640), shape(8, 640, dtype=f32)), "after_feed", 10**9, 16,
-        grid=(4,), in_specs=[rows, pair, pair, rows, full(16, 640)], out_specs=[rows, rows, rows, full(8, 640)])(*stay(args[0], args[1]), args[2], *stay(args[3]), args[4])
+        grid=(4,), in_specs=[rows, pair, pair, rows, full(16, 640)], out_specs=[rows, rows, rows, full(8, 640)])(*stay(args[0], args[1]), args[2], *stay(args[3], args[4]))
 
 
 def branch_kernel(core_ref, own_ref, their_ref, w_ref, low0_ref, low1_ref, theirs_ref, do_ref, doT_ref, g_ref):
@@ -739,18 +739,17 @@
     feed_grads, mine, theirs, tail = together(feed_grads, mine, theirs, tail)
 
     feed = jnp.sum(feed_grads.astype(f32), axis=0).astype(bf16)
-    tail = lax.all_to_all(tail, ("batch", "z", "x"), 0, 0, tiled=True)
-    feed = lax.all_gather(feed, ("z", "x"), axis=0, tiled=True).reshape(16, 80, 640)
     theirs = swapped(theirs)
     sums = [mine[j].astype(f32) + theirs[j].astype(f32) for j in range(5)]
     right, left = passed_along(sums[4].astype(bf16), 1), passed_along(sums[0].astype(bf16), -1)
+    tail, feed, right, left = together(tail, feed, right, left)
+    tail = lax.all_to_all(tail, ("batch", "z", "x"), 0, 0, tiled=True)
+    feed = lax.all_gather(feed, ("z", "x"), axis=0, tiled=True).reshape(16, 80, 640)
+    right = passed_along((right.astype(f32) + sums[3]).astype(bf16), 1)
+    left = passed_along((left.astype(f32) + sums[1]).astype(bf16), -1)
     tail, right, left = together(tail, right, left)
-    right, left = (right.astype(f32) + sums[3]).astype(bf16), (left.astype(f32) + sums[1]).astype(bf16)
-    tail, right, left = together(jnp.sum(tail.astype(f32), axis=0).astype(bf16), right, left)
-    right, left = passed_along(right, 1), passed_along(left, -1)
-    tail = gathered(tail, "x").reshape(160, 384)
+    tail = gathered(jnp.sum(tail.astype(f32), axis=0).astype(bf16), "x").reshape(160, 384)
     tail = gathered(tail, "z").reshape(16, 40, 384)
-    tail, right, left = together(tail, right, left)
     d_one = (sums[2] + right.astype(f32) + left.astype(f32)).reshape(512, 640)
     n_one, r_one = moments(tok.reshape(512, 640).astype(f32))
     grad_tokens = (grad_middle + norm_back(d_one, n_one, r_one, vec[0:1])).astype(bf16)

time: 379 us -> 391 us (1.032)
  waiting for transfers between devices: 101 us -> 125 us
  Pallas kernels: 157 us -> 149 us
    ppermute x8, waiting for transfers between devices: 14.8 us -> 46.1 us  [passed_along(): lax.ppermute(array, ('z', 'x'), [(i, i + by) for i in range(devices) if 0...]
    all_to_all x1, waiting for transfers between devices: 15.8 us -> 0.01 us  [body(): tail = lax.all_to_all(tail, ('batch', 'z', 'x'), 0, 0, tiled=True)]
    ppermute x6, waiting for transfers between devices: 21 us -> 7.61 us  [shifted(): lax.ppermute(array, axis, [(i, (i + by) % devices) for i in range(devices)])]
    all_gather x1, waiting for transfers between devices: 0.01 us -> 6.95 us  [body(): lax.all_gather(feed, ('z', 'x'), axis=0, tiled=True).reshape(16, 80, 640)]
    all_to_all x1, waiting for transfers between devices: 8.13 us -> 14.9 us  [body(): lax.all_to_all(feed_grads.reshape(64, 80, 640), ('batch', 'z', 'x'), 0, 0...]
    ppermute x13, waiting for transfers between devices: 11.7 us -> 17.4 us  [swapped(): return lax.ppermute(array, 'core', [(0, 1), (1, 0)])]
    pallas_call x2, Pallas kernels: 41.6 us -> 36.6 us  [attend_back(): pl.pallas_call(attend_back_kernel, out_shape=tuple((pltpu.MemorySpace.VME...]
    ppermute x6, starting transfers between devices: 14.7 us -> 9.69 us  [shifted(): lax.ppermute(array, axis, [(i, (i + by) % devices) for i in range(devices)])]
  transfers between devices with their start and end apart: 32 -> 32, of which waited for: 18 -> 20; matrix products, arithmetic and copies ran while one was open for 5% -> 4% of each run, Pallas kernels for 33% -> 29%
where the time goes in v12:
time: 391 us; the launch traced here: 385 us
  Pallas kernels  149 us (38%)
  waiting for transfers between devices  125 us (32%)
  starting transfers between devices  61.5 us (16%)
  between operations  20.2 us (5%)
  other arithmetic  17 us (4%)
  local copies, waits for them, and re-layouts  12.1 us (3%)
    ppermute x8, waiting for transfers between devices, passed_along(): lax.ppermute(array, ('z', 'x'), [(i, i + by) for i in range(devices) if 0...  46.1 us
    pallas_call x2, Pallas kernels, attend_back(): pl.pallas_call(attend_back_kernel, out_shape=tuple((pltpu.MemorySpace.VME...  36.6 us
    pallas_call x1, Pallas kernels, feed_forward(): call(feed_kernel, (far(2, 512, 640), far(2, 512, 640), far(4, 16, 80, 640...  32.1 us
    pallas_call x2, Pallas kernels, attend(): pl.pallas_call(attend_kernel, out_shape=(jax.ShapeDtypeStruct((384, nq),...  26.2 us
    ppermute x8, starting transfers between devices, passed_along(): lax.ppermute(array, ('z', 'x'), [(i, i + by) for i in range(devices) if 0...  19.2 us
    all_gather x1, waiting for transfers between devices, body(): heads = lax.all_gather(heads, 'batch', axis=0, tiled=True)  18.6 us
    ppermute x13, waiting for transfers between devices, swapped(): return lax.ppermute(array, 'core', [(0, 1), (1, 0)])  17.4 us
    pallas_call x2, Pallas kernels, project(): call(lambda *refs: project_kernel(chips, *refs), shapes, 'project', 5 * 1...  15.8 us
  transfers between devices with their start and end apart: 32, of which 20 were waited for; matrix products, arithmetic and copies ran while one was open for 4% of the time, Pallas kernels for 29%

profile of v12, /device:TPU:1, one launch (start us, length us, event | category | flops | bytes accessed | tf_op | source)
XLA Modules:
  0.0 384.7 jit_solution(4755060628711878636)
XLA Ops:
  12.4 4.0 %collective-permute-start = (bf16[2,256,640]{2,1,0:T(8,128)(2,1)S(1)}, bf16[2,256,640]{2,1,0:T(8,128)(2,1)S(1)}, u32[]{:S(2)}, u32[]{:S(2)}) collective-permute-start(bf16[2,256,640]{2,1,0:T(8,128)(2,1)S(1)} %normal_rows.1.refs_2_), channel_id=1, source_target_pairs={{0,2},{2,4},{4,6},{6,8},{8,10},{10,12},{12,14},{14,16},{16,18},{18... | collective-permute-start | bytes 1966088 | tf_op jit(solution)/shard_map/ppermute | solution.py:654
  31.2 18.6 %all-gather.4.cloned.1.call-done.vec_ref.refs_8_.refs_6_.refs_11_ = bf16[640,1280]{1,0:T(8,128)(2,1)} async-done(((bf16[160,1280]{1,0:T(8,128)(2,1)}), bf16[640,1280]{1,0:T(8,128)(2,1)}) %all-gather.4.cloned.1.call-update) | async-done | bytes 1638416 | tf_op jit(solution)/shard_map/all_gather | solution.py:709
  56.8 10.6 %project.2 = (bf16[2,2560,384]{2,1,0:T(8,128)(2,1)}, bf16[2,2560,384]{2,1,0:T(8,128)(2,1)}, bf16[2,384,2560]{2,1,0:T(8,128)(2,1)}, bf16[2,384,2560]{2,1,0:T(8,12...) custom-call(s32[5]{0:T(128)S(1)} %stack.81.refs_0_.place_ref, ...), custom_call_target="tpu_custom_call" | custom-call | flops 100000000 | tf_op jit(solution)/shard_map/project/pallas_call | solution.py:374
  69.1 4.1 %collective-permute-done.7.refs_2_.refs_4_ = bf16[2,256,640]{2,1,0:T(8,128)(2,1)S(1)} collective-permute-done((bf16[2,256,640]{2,1,0:T(8,128)(2,1)}, bf16[2,256,640]{2,1,0:T(8,128)(2,1)S(1)}, u32[]{:S(2)}, u32[]{:S(2)}) %collective-permute-start.7) | collective-permute-done | bytes 655392 | tf_op jit(solution)/shard_map/ppermute | solution.py:654
  77.4 5.2 %project.3 = (bf16[2,2560,384]{2,1,0:T(8,128)(2,1)}, bf16[2,2560,384]{2,1,0:T(8,128)(2,1)}, bf16[2,384,2560]{2,1,0:T(8,128)(2,1)}, bf16[2,384,2560]{2,1,0:T(8,128)(2,1)}) custom-call(s32[5]{0:T(128)S(1)} %stack.81.refs_0_.place_ref, ...), custom_call_target="tpu_custom_call", output_to_operand_aliasing={{0}: (7, {}), {1}: (8, {}), {2}: (9, {}), {3}: (10, {})} | custom-call | flops 100000000 | tf_op jit(solution)/shard_map/project/pallas_call | solution.py:374
  82.6 14.5 %attend.3 = (f32[384,512]{1,0:T(8,128)S(1)}, bf16[512,384]{1,0:T(8,128)(2,1)S(1)}, f32[5,8,512]{2,1,0:T(8,128)S(1)}) custom-call(s32[5]{0:T(128)S(1)} %stack.91.info_ref, bf16[2,384,512]{2,1,0:T(8,128)(2,1)} %get-tuple-element.99.qT_ref, bf16[2,2560,384]{2,1,0:T(8,128)(2,1)} %get-tuple-element.110.k_ref, bf16[2,384,2560]{2,1,0:T(8,128)(2,1)} %get-tuple-element.111.vT_ref, ...), custom_call_target="tpu_custom_call" | custom-call | flops 400000000 | tf_op jit(solution)/shard_map/attend/pallas_call | solution.py:98
  98.0 11.7 %attend.2 = (f32[384,512]{1,0:T(8,128)S(1)}, bf16[512,384]{1,0:T(8,128)(2,1)S(1)}, f32[5,8,512]{2,1,0:T(8,128)S(1)}) custom-call(s32[5]{0:T(128)S(1)} %stack.86.info_ref, bf16[2,384,512]{2,1,0:T(8,128)(2,1)} %get-tuple-element.99.qT_ref, bf16[2,2560,384]{2,1,0:T(8,128)(2,1)} %get-tuple-element.110.k_ref, bf16[2,384,2560]{2,1,0:T(8,128)(2,1)} %get-tuple-element.111.vT_ref, ...), custom_call_target="tpu_custom_call" | custom-call | flops 400000000 | tf_op jit(solution)/shard_map/attend/pallas_call | solution.py:98
  112.8 13.8 %all-gather.6.cloned.1.call-done.w_ref.up_ref.down_ref = bf16[640,5760]{1,0:T(8,128)(2,1)} async-done(((bf16[160,5760]{1,0:T(8,128)(2,1)}), bf16[640,5760]{1,0:T(8,128)(2,1)}) %all-gather.6.cloned.1.call-update) | async-done | bytes 7372816 | tf_op jit(solution)/shard_map/all_gather | solution.py:720
  126.6 4.5 %middle.1 = (f32[512,640]{1,0:T(8,128)}, bf16[512,640]{1,0:T(8,128)(2,1)}, bf16[512,640]{1,0:T(8,128)(2,1)}) custom-call(s32[1]{0:T(128)} %bitcast.core_ref, bf16[640,5760]{1,0:T(8,128)(2,1)} %all-gather.6.cloned.1.call-done.w_ref.up_ref.down_ref, bf16[512,384]{1,0:T(8,128)(2,1)S(1)} %get-tuple-element.114.low0_ref, ...), custom_call_target="tpu_custom_call" | custom-call | flops 20000000 | tf_op jit(solution)/shard_map/middle/pallas_call | solution.py:403
  131.1 32.1 %feed_forward.1 = (bf16[2,512,640]{2,1,0:T(8,128)(2,1)}, bf16[2,512,640]{2,1,0:T(8,128)(2,1)}, bf16[4,16,80,640]{3,2,1,0:T(8,128)(2,1)}) custom-call(bf16[512,640]{1,0:T(8,128)(2,1)} %get-tuple-element.121.h_ref, bf16[512,640]{1,0:T(8,128)(2,1)} %get-tuple-element.122.h2_ref, bf16[512,640]{1,0:T(8,128)(2,1)} %bitcast.20.cot_ref, ...), custom_call_target="tpu_custom_call" | custom-call | flops 600000000 | tf_op jit(solution)/shard_map/feed_forward/pallas_call | solution.py:450
  163.2 9.8 %all-to-all-start = ((bf16[64,80,640]{2,1,0:T(8,128)(2,1)}), bf16[64,80,640]{2,1,0:T(8,128)(2,1)}, u32[]{:S(2)}, u32[]{:S(2)}) async-start(bf16[64,80,640]{2,1,0:T(8,128)(2,1)} %bitcast.113), calls=%async_computation | async-start | bytes 13107200 | tf_op jit(solution)/shard_map/all_to_all | solution.py:731
  176.9 4.4 %after_feed.1 = (bf16[512,640]{1,0:T(8,128)(2,1)}, f32[512,640]{1,0:T(8,128)}, bf16[512,640]{1,0:T(8,128)(2,1)S(1)}, f32[8,640]{1,0:T(8,128)S(1)}) custom-call(f32[512,640]{1,0:T(8,128)} %get-tuple-element.120.mid_ref, bf16[2,512,640]{2,1,0:T(8,128)(2,1)} %get-tuple-element.123.mine_ref, bf16[2,512,640]{2,1,0:T(8,128)(2,1)S(1)} %collective-permute-done.12.theirs_ref, ...), custom_call_target="tpu_custom_call" | custom-call | flops 20000000 | tf_op jit(solution)/shard_map/after_feed/pallas_call | solution.py:479
  187.3 20.1 %attend_back.3 = (bf16[512,384]{1,0:T(8,128)(2,1)S(1)}, bf16[2560,384]{1,0:T(8,128)(2,1)S(1)}, bf16[2560,384]{1,0:T(8,128)(2,1)S(1)}) custom-call(s32[5]{0:T(128)S(1)} %stack.91.info_ref, bf16[2,384,512]{2,1,0:T(8,128)(2,1)} %get-tuple-element.99.qT_ref, bf16[2,512,384]{2,1,0:T(8,128)(2,1)} %get-tuple-element.127.q_ref, ...), custom_call_target="tpu_custom_call" | custom-call | flops 800000000 | tf_op jit(solution)/shard_map/attend_back/pallas_call | solution.py:211
  207.4 16.5 %attend_back.2 = (bf16[512,384]{1,0:T(8,128)(2,1)S(1)}, bf16[2560,384]{1,0:T(8,128)(2,1)S(1)}, bf16[2560,384]{1,0:T(8,128)(2,1)S(1)}) custom-call(s32[5]{0:T(128)S(1)} %stack.86.info_ref, bf16[2,384,512]{2,1,0:T(8,128)(2,1)} %get-tuple-element.99.qT_ref, bf16[2,512,384]{2,1,0:T(8,128)(2,1)} %get-tuple-element.127.q_ref, ...), custom_call_target="tpu_custom_call" | custom-call | flops 800000000 | tf_op jit(solution)/shard_map/attend_back/pallas_call | solution.py:211
  223.9 15.4 %project_back.1 = (bf16[5,2,256,640]{3,2,1,0:T(8,128)(2,1)}, bf16[5,2,256,640]{3,2,1,0:T(8,128)(2,1)}, bf16[64,40,384]{2,1,0:T(8,128)(2,1)}) custom-call(s32[5]{0:T(128)S(1)} %stack.81.refs_0_.place_ref, bf16[2,256,640]{2,1,0:T(8,128)(2,1)} %copy-done.6, bf16[2,256,640]{2,1,0:T(8,128)(2,1)} %copy-done.3, bf16[2,256,640]{2,1,0:T(8,128)(2,1)} %copy-done.2, ...), custom_call_target="tpu_custom_call" | custom-call | flops 200000000 | tf_op jit(solution)/shard_map/project_back/pallas_call | solution.py:596
  239.3 14.9 %all-to-all-done = bf16[64,80,640]{2,1,0:T(8,128)(2,1)} async-done(((bf16[64,80,640]{2,1,0:T(8,128)(2,1)}), bf16[64,80,640]{2,1,0:T(8,128)(2,1)}, u32[]{:S(2)}, u32[]{:S(2)}) %all-to-all-start) | async-done | bytes 6553632 | tf_op jit(solution)/shard_map/all_to_all | solution.py:731
  256.5 5.7 %collective-permute-done.14 = bf16[5,2,256,640]{3,2,1,0:T(8,128)(2,1)S(1)} collective-permute-done((bf16[5,2,256,640]{3,2,1,0:T(8,128)(2,1)}, bf16[5,2,256,640]{3,2,1,0:T(8,128)(2,1)S(1)}, u32[]{:S(2)}, u32[]{:S(2)}) %collective-permute-start.14) | collective-permute-done | bytes 3276832 | tf_op jit(solution)/shard_map/ppermute | solution.py:658
  265.5 3.9 %collective-permute-start.15 = (bf16[2,256,640]{2,1,0:T(8,128)(2,1)S(1)}, bf16[2,256,640]{2,1,0:T(8,128)(2,1)S(1)}, u32[]{:S(2)}, u32[]{:S(2)}) collective-permute-start(bf16[2,256,640]{2,1,0:T(8,128)(2,1)S(1)} %get-tuple-element.218), channel_id=1, source_target_pairs={{0,2},{2,4},{4,6},{6,8},{8,10},{10,12},{12,14},{14,16},{16,18},{18... | collective-permute-start | bytes 1966088 | tf_op jit(solution)/shard_map/ppermute | solution.py:654
  270.8 4.5 %reduce_sum.60 = bf16[80,640]{1,0:T(8,128)(2,1)} reduce(bf16[64,80,640]{2,1,0:T(8,128)(2,1)} %all-to-all-done, bf16[]{:T(256)} %constant.193.clone.1), dimensions={0}, to_apply=%region_10.11 | reduce | flops 3225600 | bytes 6656002 | tf_op jit(solution)/shard_map/reduce_sum | solution.py:741
  275.2 7.9 %collective-permute-done.15 = bf16[2,256,640]{2,1,0:T(8,128)(2,1)S(1)} collective-permute-done((bf16[2,256,640]{2,1,0:T(8,128)(2,1)S(1)}, bf16[2,256,640]{2,1,0:T(8,128)(2,1)S(1)}, u32[]{:S(2)}, u32[]{:S(2)}) %collective-permute-start.15) | collective-permute-done | bytes 655392 | tf_op jit(solution)/shard_map/ppermute | solution.py:654
  287.8 12.1 %all-to-all-start.1 = ((bf16[64,40,384]{2,1,0:T(8,128)(2,1)}), bf16[64,40,384]{2,1,0:T(8,128)(2,1)S(1)}, u32[]{:S(2)}, u32[]{:S(2)}) async-start(bf16[64,40,384]{2,1,0:T(8,128)(2,1)} %get-tuple-element.152), calls=%async_computation.1 | async-start | bytes 3932160 | tf_op jit(solution)/shard_map/all_to_all | solution.py:746
  308.3 26.5 %collective-permute-done.17 = bf16[2,256,640]{2,1,0:T(8,128)(2,1)S(1)} collective-permute-done((bf16[2,256,640]{2,1,0:T(8,128)(2,1)}, bf16[2,256,640]{2,1,0:T(8,128)(2,1)S(1)}, u32[]{:S(2)}, u32[]{:S(2)}) %collective-permute-start.17) | collective-permute-done | bytes 655392 | tf_op jit(solution)/shard_map/ppermute | solution.py:654
  354.6 3.9 %collective-permute-done.24 = bf16[160,384]{1,0:T(8,128)(2,1)S(1)} collective-permute-done((bf16[160,384]{1,0:T(8,128)(2,1)S(1)}, bf16[160,384]{1,0:T(8,128)(2,1)S(1)}, u32[]{:S(2)}, u32[]{:S(2)}) %collective-permute-start.24) | collective-permute-done | bytes 122912 | tf_op jit(solution)/shard_map/ppermute | solution.py:649
  358.5 7.0 %all-gather.8.cloned.1.call-done = bf16[1280,640]{1,0:T(8,128)(2,1)} async-done(((bf16[80,640]{1,0:T(8,128)(2,1)}), bf16[1280,640]{1,0:T(8,128)(2,1)}) %all-gather.8.cloned.1.call-update) | async-done | bytes 1638416 | tf_op jit(solution)/shard_map/all_gather | solution.py:747
  (175 shorter events, 93.0 us)
Async XLA Ops:
  7.2 42.6 %all-gather.4.cloned.1.call-start = ((), (), s32[]{:S(2)}) async-start(), calls=%async_computation.2 | async-start | bytes 2048000 | tf_op jit(solution)/shard_map/all_gather | solution.py:709
  12.4 39.0 %collective-permute-start = (bf16[2,256,640]{2,1,0:T(8,128)(2,1)S(1)}, bf16[2,256,640]{2,1,0:T(8,128)(2,1)S(1)}, u32[]{:S(2)}, u32[]{:S(2)}) collective-permute-start(bf16[2,256,640]{2,1,0:T(8,128)(2,1)S(1)} %normal_rows.1.refs_2_), channel_id=1, source_target_pairs={{0,2},{2,4},{4,6},{6,8},{8,10},{10,12},{12,14},{14,16},{16,18},{18... | collective-permute-start | bytes 1966088 | tf_op jit(solution)/shard_map/ppermute | solution.py:654
  16.4 35.1 %collective-permute-start.1 = (bf16[2,256,640]{2,1,0:T(8,128)(2,1)S(1)}, bf16[2,256,640]{2,1,0:T(8,128)(2,1)}, u32[]{:S(2)}, u32[]{:S(2)}) collective-permute-start(bf16[2,256,640]{2,1,0:T(8,128)(2,1)S(1)} %normal_rows.1.refs_2_), channel_id=1, source_target_pairs={{2,0},{4,2},{6,4},{8,6},{10,8},{12,10},{14,12},{16,14},{18,16},{20... | collective-permute-start | bytes 1966088 | tf_op jit(solution)/shard_map/ppermute | solution.py:654
  17.7 33.8 %collective-permute-start.2 = (bf16[2,256,640]{2,1,0:T(8,128)(2,1)S(1)}, bf16[2,256,640]{2,1,0:T(8,128)(2,1)}, u32[]{:S(2)}, u32[]{:S(2)}) collective-permute-start(bf16[2,256,640]{2,1,0:T(8,128)(2,1)S(1)} %normal_rows.1.refs_2_), channel_id=1, source_target_pairs={{0,1},{1,0},{2,3},{3,2},{4,5},{5,4},{6,7},{7,6},{8,9},{9,8},{10,11... | collective-permute-start | bytes 1966088 | tf_op jit(solution)/shard_map/ppermute | solution.py:658
  18.7 32.7 %collective-permute-start.3 = (bf16[2,256,640]{2,1,0:T(8,128)(2,1)S(1)}, bf16[2,256,640]{2,1,0:T(8,128)(2,1)}, u32[]{:S(2)}, u32[]{:S(2)}) collective-permute-start(bf16[2,256,640]{2,1,0:T(8,128)(2,1)S(1)} %bitcast.105), channel_id=1, source_target_pairs={{0,1},{1,0},{2,3},{3,2},{4,5},{5,4},{6,7},{7,6},{8,9},{9,8},{10,11... | collective-permute-start | bytes 1966088 | tf_op jit(solution)/shard_map/ppermute | solution.py:658
  18.8 107.8 %all-gather.6.cloned.1.call-start = ((), (), s32[]{:S(2)}) async-start(), calls=%async_computation.3 | async-start | bytes 9216000 | tf_op jit(solution)/shard_map/all_gather | solution.py:720
  51.5 5.3 %collective-permute-start.4 = (bf16[2,256,640]{2,1,0:T(8,128)(2,1)S(1)}, bf16[2,256,640]{2,1,0:T(8,128)(2,1)S(1)}, u32[]{:S(2)}, u32[]{:S(2)}) collective-permute-start(bf16[2,256,640]{2,1,0:T(8,128)(2,1)S(1)} %collective-permute-done.refs_1_), channel_id=1, source_target_pairs={{0,1},{1,0},{2,3},{3,2},{4,5},{5,4},{6,7},{7,6},{8,9},{9,8},{10,11... | collective-permute-start | bytes 1966088 | tf_op jit(solution)/shard_map/ppermute | solution.py:658
  52.3 16.8 %collective-permute-start.6 = (bf16[2,256,640]{2,1,0:T(8,128)(2,1)S(1)}, bf16[2,256,640]{2,1,0:T(8,128)(2,1)S(1)}, u32[]{:S(2)}, u32[]{:S(2)}) collective-permute-start(bf16[2,256,640]{2,1,0:T(8,128)(2,1)S(1)} %collective-permute-done.refs_1_), channel_id=1, source_target_pairs={{0,2},{2,4},{4,6},{6,8},{8,10},{10,12},{12,14},{14,16},{16,18},{18... | collective-permute-start | bytes 1966088 | tf_op jit(solution)/shard_map/ppermute | solution.py:654
  55.5 17.8 %collective-permute-start.7 = (bf16[2,256,640]{2,1,0:T(8,128)(2,1)}, bf16[2,256,640]{2,1,0:T(8,128)(2,1)S(1)}, u32[]{:S(2)}, u32[]{:S(2)}) collective-permute-start(bf16[2,256,640]{2,1,0:T(8,128)(2,1)} %collective-permute-done.1.refs_3_), channel_id=1, source_target_pairs={{2,0},{4,2},{6,4},{8,6},{10,8},{12,10},{14,12},{16,14},{18,16},{20... | collective-permute-start | bytes 1966088 | tf_op jit(solution)/shard_map/ppermute | solution.py:654
  111.2 19.8 %collective-permute-start.11 = (bf16[512,640]{1,0:T(8,128)(2,1)}, bf16[512,640]{1,0:T(8,128)(2,1)}, u32[]{:S(2)}, u32[]{:S(2)}) collective-permute-start(bf16[512,640]{1,0:T(8,128)(2,1)} %bitcast.20.cot_ref), channel_id=1, source_target_pairs={{0,1},{1,0},{2,3},{3,2},{4,5},{5,4},{6,7},{7,6},{8,9},{9,8},{10,11... | collective-permute-start | bytes 1966088 | tf_op jit(solution)/shard_map/ppermute | solution.py:658
  163.2 91.0 %all-to-all-start = ((bf16[64,80,640]{2,1,0:T(8,128)(2,1)}), bf16[64,80,640]{2,1,0:T(8,128)(2,1)}, u32[]{:S(2)}, u32[]{:S(2)}) async-start(bf16[64,80,640]{2,1,0:T(8,128)(2,1)} %bitcast.113), calls=%async_computation | async-start | bytes 13107200 | tf_op jit(solution)/shard_map/all_to_all | solution.py:731
  254.2 8.0 %collective-permute-start.14 = (bf16[5,2,256,640]{3,2,1,0:T(8,128)(2,1)}, bf16[5,2,256,640]{3,2,1,0:T(8,128)(2,1)S(1)}, u32[]{:S(2)}, u32[]{:S(2)}) collective-permute-start(bf16[5,2,256,640]{3,2,1,0:T(8,128)(2,1)} %get-tuple-element.151), channel_id=1, source_target_pairs={{0,1},{1,0},{2,3},{3,2},{4,5},{5,4},{6,7},{7,6},{8,9},{9,8},{10,11... | collective-permute-start | bytes 9830408 | tf_op jit(solution)/shard_map/ppermute | solution.py:658
  265.5 17.6 %collective-permute-start.15 = (bf16[2,256,640]{2,1,0:T(8,128)(2,1)S(1)}, bf16[2,256,640]{2,1,0:T(8,128)(2,1)S(1)}, u32[]{:S(2)}, u32[]{:S(2)}) collective-permute-start(bf16[2,256,640]{2,1,0:T(8,128)(2,1)S(1)} %get-tuple-element.218), channel_id=1, source_target_pairs={{0,2},{2,4},{4,6},{6,8},{8,10},{10,12},{12,14},{14,16},{16,18},{18... | collective-permute-start | bytes 1966088 | tf_op jit(solution)/shard_map/ppermute | solution.py:654
  269.5 17.5 %collective-permute-start.16 = (bf16[2,256,640]{2,1,0:T(8,128)(2,1)S(1)}, bf16[2,256,640]{2,1,0:T(8,128)(2,1)S(1)}, u32[]{:S(2)}, u32[]{:S(2)}) collective-permute-start(bf16[2,256,640]{2,1,0:T(8,128)(2,1)S(1)} %get-tuple-element.217), channel_id=1, source_target_pairs={{2,0},{4,2},{6,4},{8,6},{10,8},{12,10},{14,12},{16,14},{18,16},{20... | collective-permute-start | bytes 1966088 | tf_op jit(solution)/shard_map/ppermute | solution.py:654
  287.8 49.0 %all-to-all-start.1 = ((bf16[64,40,384]{2,1,0:T(8,128)(2,1)}), bf16[64,40,384]{2,1,0:T(8,128)(2,1)S(1)}, u32[]{:S(2)}, u32[]{:S(2)}) async-start(bf16[64,40,384]{2,1,0:T(8,128)(2,1)} %get-tuple-element.152), calls=%async_computation.1 | async-start | bytes 3932160 | tf_op jit(solution)/shard_map/all_to_all | solution.py:746
  299.9 65.5 %all-gather.8.cloned.1.call-start = ((), (), s32[]{:S(2)}) async-start(), calls=%async_computation.4 | async-start | bytes 1740800 | tf_op jit(solution)/shard_map/all_gather | solution.py:747
  303.6 31.3 %collective-permute-start.17 = (bf16[2,256,640]{2,1,0:T(8,128)(2,1)}, bf16[2,256,640]{2,1,0:T(8,128)(2,1)S(1)}, u32[]{:S(2)}, u32[]{:S(2)}) collective-permute-start(bf16[2,256,640]{2,1,0:T(8,128)(2,1)} %get-tuple-element.216), channel_id=1, source_target_pairs={{0,2},{2,4},{4,6},{6,8},{8,10},{10,12},{12,14},{14,16},{16,18},{18... | collective-permute-start | bytes 1966088 | tf_op jit(solution)/shard_map/ppermute | solution.py:654
  306.5 30.3 %collective-permute-start.18 = (bf16[2,256,640]{2,1,0:T(8,128)(2,1)}, bf16[2,256,640]{2,1,0:T(8,128)(2,1)}, u32[]{:S(2)}, u32[]{:S(2)}) collective-permute-start(bf16[2,256,640]{2,1,0:T(8,128)(2,1)} %get-tuple-element.215), channel_id=1, source_target_pairs={{2,0},{4,2},{6,4},{8,6},{10,8},{12,10},{14,12},{16,14},{18,16},{20... | collective-permute-start | bytes 1966088 | tf_op jit(solution)/shard_map/ppermute | solution.py:654
  337.1 7.2 %collective-permute-start.19 = (bf16[40,384]{1,0:T(8,128)(2,1)S(1)}, bf16[40,384]{1,0:T(8,128)(2,1)S(1)}, u32[]{:S(2)}, u32[]{:S(2)}) collective-permute-start(bf16[40,384]{1,0:T(8,128)(2,1)S(1)} %reduce_sum.61), channel_id=1, source_target_pairs={{0,2},{2,4},{4,6},{6,0},{1,3},{3,5},{5,7},{7,1},{8,10},{10,12},{12... | collective-permute-start | bytes 92168 | tf_op jit(solution)/shard_map/ppermute | solution.py:649
  338.9 5.4 %collective-permute-start.20 = (bf16[40,384]{1,0:T(8,128)(2,1)S(1)}, bf16[40,384]{1,0:T(8,128)(2,1)S(1)}, u32[]{:S(2)}, u32[]{:S(2)}) collective-permute-start(bf16[40,384]{1,0:T(8,128)(2,1)S(1)} %reduce_sum.61), channel_id=1, source_target_pairs={{0,6},{2,0},{4,2},{6,4},{1,7},{3,1},{5,3},{7,5},{8,14},{10,8},{12,... | collective-permute-start | bytes 92168 | tf_op jit(solution)/shard_map/ppermute | solution.py:649
  345.0 6.4 %collective-permute-start.22 = (bf16[160,384]{1,0:T(8,128)(2,1)S(1)}, bf16[160,384]{1,0:T(8,128)(2,1)S(1)}, u32[]{:S(2)}, u32[]{:S(2)}) collective-permute-start(bf16[160,384]{1,0:T(8,128)(2,1)S(1)} %bitcast.115), channel_id=1, source_target_pairs={{0,8},{8,16},{16,24},{24,0},{1,9},{9,17},{17,25},{25,1},{2,10},{10... | collective-permute-start | bytes 368648 | tf_op jit(solution)/shard_map/ppermute | solution.py:649
  348.4 6.2 %collective-permute-start.23 = (bf16[160,384]{1,0:T(8,128)(2,1)S(1)}, bf16[160,384]{1,0:T(8,128)(2,1)S(1)}, u32[]{:S(2)}, u32[]{:S(2)}) collective-permute-start(bf16[160,384]{1,0:T(8,128)(2,1)S(1)} %bitcast.116), channel_id=1, source_target_pairs={{0,24},{8,0},{16,8},{24,16},{1,25},{9,1},{17,9},{25,17},{2,26},{10... | collective-permute-start | bytes 368648 | tf_op jit(solution)/shard_map/ppermute | solution.py:649
  350.2 8.3 %collective-permute-start.24 = (bf16[160,384]{1,0:T(8,128)(2,1)S(1)}, bf16[160,384]{1,0:T(8,128)(2,1)S(1)}, u32[]{:S(2)}, u32[]{:S(2)}) collective-permute-start(bf16[160,384]{1,0:T(8,128)(2,1)S(1)} %bitcast.117), channel_id=1, source_target_pairs={{0,16},{8,24},{16,0},{24,8},{1,17},{9,25},{17,1},{25,9},{2,18},{10... | collective-permute-start | bytes 368648 | tf_op jit(solution)/shard_map/ppermute | solution.py:649
  365.4 8.0 %collective-permute-start.26 = (bf16[16,80,640]{2,1,0:T(8,128)(2,1)}, bf16[16,80,640]{2,1,0:T(8,128)(2,1)S(1)}, u32[]{:S(2)}, u32[]{:S(2)}) collective-permute-start(bf16[16,80,640]{2,1,0:T(8,128)(2,1)} %bitcast.111), channel_id=1, source_target_pairs={{0,1},{1,0},{2,3},{3,2},{4,5},{5,4},{6,7},{7,6},{8,9},{9,8},{10,11... | collective-permute-start | bytes 4915208 | tf_op jit(solution)/shard_map/ppermute | solution.py:658
  (38 other events, 407.3 us)
Sparse Core Ops, SparseCore 0:
  18.9 30.7 all-gather.3
  52.0 74.5 all-gather.5
  308.3 57.0 all-gather.7
